TPU v7x, 256 devices: a whole 4x4x8 slice. The times are simulated.
256 devices in a mesh: ctx: 32 (over z, x), tp: 8 (over y, core).
Axes of the slice: x: 4, y: 4, z: 8, core: 2. Of those that a mesh axis runs over, the one named last changes fastest.
Arguments:
- query_in: bfloat16 [16384, 8192], P('ctx', 'tp'), may hold values from -6 to 6
- key_in: bfloat16 [16384, 8192], P('ctx', 'tp'), may hold values from -6 to 6
- value_in: bfloat16 [16384, 8192], P('ctx', 'tp'), may hold values from -6 to 6
- filters: bfloat16 [512, 128], P('tp'), may hold values from -0.5 to 0.5
- proj_out: bfloat16 [4096, 8192], P('ctx', 'tp'), may hold values from -0.0625 to 0.0625
- cotangent: bfloat16 [16384, 4096], P('ctx', 'tp'), may hold values from -6 to 6
Outputs:
- grad_query: bfloat16 [16384, 8192], P('ctx', 'tp')
- grad_key: bfloat16 [16384, 8192], P('ctx', 'tp')
- grad_value: bfloat16 [16384, 8192], P('ctx', 'tp')
- grad_filter: float32 [512, 128], P('tp')
- grad_proj: float32 [4096, 8192], P('ctx', 'tp')
All inputs are finite; a program needn't handle non-finite values.
Results may differ from a plain program's by a relative error of at most 0.005.
Values may be sent and summed in bfloat16 or wider, within the bound.
No kernel may reach another device: no remote copies, remote signals or barrier semaphores. Data moves between devices by JAX's collectives and lax.ppermute only.
A program may use at most 192 MiB of HBM per device.

v0:
```python
import jax
import jax.numpy as jnp
from jax import lax
from jax.sharding import PartitionSpec as P


def from_behind(value, axis, by):
    count = lax.axis_size(axis)
    pairs = [(i, i + by) for i in range(count) if 0 <= i + by < count]
    return lax.ppermute(value, axis, pairs)


def toeplitz_rows(filters):
    group_count, tap_count = filters.shape
    padded = jnp.concatenate(
        [
            jnp.zeros((group_count, 1), filters.dtype),
            jnp.flip(filters, 1),
            jnp.zeros((group_count, 2 * tap_count - 1), filters.dtype),
        ],
        1,
    )
    tiled = jnp.tile(padded, (1, tap_count))[:, : tap_count * (3 * tap_count - 1)]
    return tiled.reshape(group_count, tap_count, 3 * tap_count - 1)[:, :, : 2 * tap_count]


def on_device(query_in, key_in, value_in, filters, proj_out, cotangent):
    tok_rows, chan_width = query_in.shape
    group_count, tap_count = filters.shape
    group_size = chan_width // group_count
    blocks = tok_rows // tap_count
    table = toeplitz_rows(filters)
    mixed_in = (key_in.astype(jnp.float32) * value_in.astype(jnp.float32)).astype(jnp.bfloat16)
    left_rim = from_behind(mixed_in[tok_rows - tap_count + 1 :], "ctx", 1)
    extended = jnp.concatenate(
        [jnp.zeros((1, chan_width), jnp.bfloat16), left_rim, mixed_in[: tok_rows - tap_count]], 0
    )
    window = jnp.concatenate(
        [
            extended.reshape(blocks, tap_count, group_count, group_size),
            mixed_in.reshape(blocks, tap_count, group_count, group_size),
        ],
        1,
    )
    conv_out = jnp.einsum(
        "gts,bsgc->btgc", table, window, preferred_element_type=jnp.float32
    ).reshape(tok_rows, chan_width)
    gated = (query_in.astype(jnp.float32) * conv_out).astype(jnp.bfloat16)
    cot_full = lax.all_gather(cotangent, "tp", axis=1, tiled=True)
    columns = cot_full
    grad_all = jnp.dot(
        columns,
        lax.all_gather(proj_out, "ctx", axis=0, tiled=True),
        preferred_element_type=jnp.float32,
    )
    grad_query = (grad_all * conv_out).astype(jnp.bfloat16)
    grad_inner = (grad_all * query_in.astype(jnp.float32)).astype(jnp.bfloat16)
    next_rows = from_behind(grad_inner[: tap_count - 1], "ctx", -1)
    ahead = jnp.concatenate(
        [grad_inner[tap_count:], next_rows, jnp.zeros((1, chan_width), jnp.bfloat16)], 0
    )
    inner_blocks = grad_inner.reshape(blocks, tap_count, group_count, group_size)
    ahead_blocks = ahead.reshape(blocks, tap_count, group_count, group_size)
    grad_mixed = jnp.einsum(
        "gts,btgc->bsgc", table[:, :, tap_count:], inner_blocks, preferred_element_type=jnp.float32
    )
    grad_mixed = grad_mixed + jnp.einsum(
        "gts,btgc->bsgc", table[:, :, :tap_count], ahead_blocks, preferred_element_type=jnp.float32
    )
    grad_mixed = grad_mixed.reshape(tok_rows, chan_width)
    grad_key = (grad_mixed * value_in.astype(jnp.float32)).astype(jnp.bfloat16)
    grad_value = (grad_mixed * key_in.astype(jnp.float32)).astype(jnp.bfloat16)
    corr = jnp.einsum("btgc,bsgc->gts", inner_blocks, window, preferred_element_type=jnp.float32)
    skewed = jnp.pad(corr.reshape(group_count, -1), ((0, 0), (0, tap_count))).reshape(
        group_count, tap_count, 2 * tap_count + 1
    )
    filter_part = jnp.flip(jnp.sum(skewed, axis=1)[:, 1 : tap_count + 1], 1)
    columns = cot_full
    grad_proj = lax.psum_scatter(
        lax.dot_general(
            columns, gated, (((0,), (0,)), ((), ())), preferred_element_type=jnp.float32
        ),
        "ctx",
        scatter_dimension=0,
        tiled=True,
    )
    grad_filter = lax.psum(filter_part, "ctx")
    return (grad_query, grad_key, grad_value, grad_filter, grad_proj)


def solution(mesh):
    placed = (
        P("ctx", "tp"),
        P("ctx", "tp"),
        P("ctx", "tp"),
        P("tp", None),
        P("ctx", "tp"),
        P("ctx", "tp"),
    )
    return jax.shard_map(
        on_device,
        mesh=mesh,
        in_specs=placed,
        out_specs=(P("ctx", "tp"), P("ctx", "tp"), P("ctx", "tp"), P("tp", None), P("ctx", "tp")),
        check_vma=False,
    )
```

profile of v0, /device:TPU:6, one launch (start us, length us, event | category | flops | bytes accessed | tf_op | source)
XLA Modules:
  0.0 495.5 jit_solution(13362791816464786184)
XLA Ops:
  7.2 0.7 all-gather.3.cloned.1.call-update
  7.9 0.7 all-gather.5.cloned.1.call-update
  8.7 38.7 %all-gather.3.cloned.1.call-done = bf16[512,4096]{1,0:T(8,128)(2,1)} async-done(((bf16[512,512]{1,0:T(8,128)(2,1)}), bf16[512,4096]{1,0:T(8,128)(2,1)}) %all-gather.3.cloned.1.call-update) | async-done | bytes 4194320 | tf_op jit(solution)/shard_map/all_gather | solution.py:49
  47.5 99.1 %all-gather.5.cloned.1.call-done = bf16[4096,1024]{1,0:T(8,128)(2,1)} async-done(((bf16[128,1024]{1,0:T(8,128)(2,1)}), bf16[4096,1024]{1,0:T(8,128)(2,1)}) %all-gather.5.cloned.1.call-update) | async-done | bytes 8388624 | tf_op jit(solution)/shard_map/all_gather | solution.py:53
  146.5 10.6 %fusion.4 = (bf16[512,1024]{1,0:T(8,128)(2,1)S(1)}, f32[512,1024]{1,0:T(8,128)}) fusion(bf16[512,1024]{1,0:T(8,128)(2,1)} %param.6, bf16[512,4096]{1,0:T(8,128)(2,1)} %all-gather.3.cloned.1.call-done, bf16[4096,1024]{1,0:T(8,128)(2,1)} %all-gather.5.cloned.1.call-done), kind=kOutput, calls=%fused_computation.11 | convolution fusion | flops 4296540160 | bytes 16777216 | tf_op jit(solution)/shard_map/dot_general | solution.py:51
  157.1 3.3 collective-permute-start.1
  160.7 0.5 copy.16
  161.2 2.3 copy.17
  163.6 0.5 tile.4
  164.1 4.1 copy.37
  168.2 3.1 slice.40
  171.3 16.4 %reshape.43 = bf16[64,128,383]{2,1,0:T(8,128)(2,1)} reshape(bf16[64,49024]{1,0:T(8,128)(2,1)} %slice.40) | data formatting | bytes 12550144 | tf_op jit(solution)/shard_map/reshape | solution.py:24
  187.7 0.9 slice.43
  188.6 1.3 copy.23
  189.9 1.3 reshape.45
  191.3 1.5 maximum_maximum_fusion
  192.8 1.3 copy.25
  194.1 1.3 reshape.46
  195.4 2.3 fusion.6
  197.7 2.3 add_bitcast_fusion
  200.0 1.0 copy.27
  201.0 0.2 copy-done.1
  201.2 2.0 fusion.1
  203.2 0.1 slice.38
  203.3 5.1 %collective-permute-start = (bf16[127,1024]{0,1:T(8,128)(2,1)S(1)}, bf16[127,1024]{0,1:T(8,128)(2,1)}, u32[]{:S(2)}, u32[]{:S(2)}) collective-permute-start(bf16[127,1024]{0,1:T(8,128)(2,1)S(1)} %slice.38), channel_id=1, source_target_pairs={{0,8},{8,16},{16,24},{24,32},{32,40},{40,48},{48,56},{56,64},{64,7... | collective-permute-start | bytes 780296 | tf_op jit(solution)/shard_map/ppermute | solution.py:10
  208.5 1.0 slice.39
  209.4 0.3 reshape.42
  209.7 3.4 collective-permute-done
  213.1 2.5 pad_maximum_fusion
  215.6 1.3 reshape.41
  216.9 0.3 copy_dynamic-update-slice_fusion.1
  217.2 0.4 copy_dynamic-update-slice_fusion
  217.6 4.5 fusion.8
  222.2 1.0 copy.21
  223.1 1.5 copy.52
  224.7 1.9 copy.22
  226.6 12.8 %convolution_bitcast_fusion = f32[4096,1024]{0,1:T(8,128)} fusion(bf16[512,4096]{1,0:T(8,128)(2,1)} %all-gather.3.cloned.1.call-done, f32[512,1024]{1,0:T(8,128)S(1)} %copy.22, bf16[512,1024]{1,0:T(8,128)(2,1)} %param.6), kind=kOutput, calls=%fused_computation | convolution fusion | flops 4296540160 | bytes 24117248 | tf_op jit(solution)/shard_map/dot_general | solution.py:80
  239.5 2.3 copy.31
  241.7 2.3 copy.30
  244.0 2.9 fusion.11
  246.9 4.7 copy.40
  251.6 3.9 pad.4
  255.5 14.2 %reshape.49 = f32[64,128,257]{2,1,0:T(8,128)} reshape(f32[64,32896]{1,0:T(8,128)} %pad.4) | data formatting | bytes 16842752 | tf_op jit(solution)/shard_map/reshape | solution.py:74
  269.7 6.2 %reduce_sum.9 = f32[64,257]{1,0:T(8,128)S(1)} reduce(f32[64,128,257]{2,1,0:T(8,128)} %reshape.49, f32[]{:T(128)} %constant.3.clone.1), dimensions={1}, to_apply=%region_0.1 | reduce | flops 2088896 | bytes 8487172 | tf_op jit(solution)/shard_map/reduce_sum | solution.py:77
  276.1 133.6 %psum.7 = f32[64,128]{1,0:T(8,128)} all-reduce(f32[64,128]{1,0:T(8,128)S(1)} %rev.9), channel_id=1, replica_groups=mesh['ctx'=32,'tp'=8] {'ctx'}, use_global_device_ids=true, to_apply=%region_1.2 | all-reduce | flops 8192 | bytes 65536 | tf_op jit(solution)/shard_map/psum | solution.py:87
  409.7 2.9 multiply_convert_fusion
  412.5 74.4 %reduce-scatter.2.cloned.1.call-done = f32[128,1024]{0,1:T(8,128)} async-done(((f32[4096,1024]{0,1:T(8,128)}), f32[128,1024]{0,1:T(8,128)}) %reduce-scatter.2.cloned.1.call-update) | async-done | bytes 524304 | tf_op jit(solution)/shard_map/reduce_scatter | solution.py:79
  487.0 2.0 copy.32
  (22 shorter events, 0.7 us)
Async XLA Ops:
  7.2 40.3 %all-gather.3.cloned.1.call-start = ((), (), s32[]{:S(2)}) async-start(), calls=%async_computation.1 | async-start | bytes 4718592 | tf_op jit(solution)/shard_map/all_gather | solution.py:49
  7.9 138.6 %all-gather.5.cloned.1.call-start = ((), (), s32[]{:S(2)}) async-start(), calls=%async_computation.2 | async-start | bytes 8650752 | tf_op jit(solution)/shard_map/all_gather | solution.py:53
  8.6 151.9 %copy-start.3 = (bf16[64,128]{1,0:T(8,128)(2,1)S(1)}, bf16[64,128]{1,0:T(8,128)(2,1)}, u32[]{:S(2)}) copy-start(bf16[64,128]{1,0:T(8,128)(2,1)} %param.9) | copy-start | bytes 49156
  8.7 152.0 %copy-start.2 = (bf16[512,1024]{1,0:T(8,128)(2,1)S(1)}, bf16[512,1024]{1,0:T(8,128)(2,1)}, u32[]{:S(2)}) copy-start(bf16[512,1024]{1,0:T(8,128)(2,1)} %param.7) | copy-start | bytes 3145732
  8.7 478.3 %reduce-scatter.2.cloned.1.call-start = ((), (), s32[]{:S(2)}) async-start(), calls=%async_computation.3 | async-start | bytes 17301504 | tf_op jit(solution)/shard_map/reduce_scatter | solution.py:79
  157.1 34.1 %collective-permute-start.1 = (bf16[127,1024]{1,0:T(8,128)(2,1)S(1)}, bf16[127,1024]{1,0:T(8,128)(2,1)}, u32[]{:S(2)}, u32[]{:S(2)}) collective-permute-start(bf16[127,1024]{1,0:T(8,128)(2,1)S(1)} %slice.44), channel_id=1, source_target_pairs={{8,0},{16,8},{24,16},{32,24},{40,32},{48,40},{56,48},{64,56},{72,6... | collective-permute-start | bytes 780296 | tf_op jit(solution)/shard_map/ppermute | solution.py:10
  200.0 1.2 copy-start.1
  203.3 9.7 %collective-permute-start = (bf16[127,1024]{0,1:T(8,128)(2,1)S(1)}, bf16[127,1024]{0,1:T(8,128)(2,1)}, u32[]{:S(2)}, u32[]{:S(2)}) collective-permute-start(bf16[127,1024]{0,1:T(8,128)(2,1)S(1)} %slice.38), channel_id=1, source_target_pairs={{0,8},{8,16},{16,24},{24,32},{32,40},{40,48},{48,56},{56,64},{64,7... | collective-permute-start | bytes 780296 | tf_op jit(solution)/shard_map/ppermute | solution.py:10
  217.6 4.5 copy-start
Sparse Core Ops, SparseCore 0:
  9.8 37.5 all-gather.2
  50.0 96.4 all-gather.4
  239.6 247.3 reduce-scatter.1
where the time goes:
time: 497 us; the launch traced here: 496 us
  waiting for transfers between devices  217 us (44%)
  blocking collectives  134 us (27%)
  local copies, waits for them, and re-layouts  72 us (14%)
  matrix products  35.4 us (7%)
  other arithmetic  15.1 us (3%)
  between operations  14 us (3%)
  starting transfers between devices  8.47 us (2%)
    psum x1, blocking collectives, on_device(): grad_filter = lax.psum(filter_part, 'ctx')  134 us
    all_gather x1, waiting for transfers between devices, on_device(): lax.all_gather(proj_out, 'ctx', axis=0, tiled=True)  99.1 us
    reduce_scatter x1, waiting for transfers between devices, on_device(): lax.psum_scatter(lax.dot_general(columns, gated, (((0,), (0,)), ((), ()))...  74.4 us
    all_gather x1, waiting for transfers between devices, on_device(): cot_full = lax.all_gather(cotangent, 'tp', axis=1, tiled=True)  38.7 us
    unnamed x17, local copies, waits for them, and re-layouts  20.2 us
    reshape x1, local copies, waits for them, and re-layouts, toeplitz_rows(): tiled.reshape(group_count, tap_count, 3 * tap_count - 1)  16.4 us
    reshape x1, local copies, waits for them, and re-layouts, on_device(): jnp.pad(corr.reshape(group_count, -1), ((0, 0), (0, tap_count)))  14.2 us
    dot_general x1, matrix products, on_device(): lax.dot_general(columns, gated, (((0,), (0,)), ((), ())), preferred_eleme...  12.8 us
  transfers between devices with their start and end apart: 5, of which 4 were waited for; matrix products, arithmetic and copies ran while one was open for 14% of the time, Pallas kernels for 0%

commit v1 on v0

v1 whole, which is shorter than its diff:
```python
import functools

import jax
import jax.numpy as jnp
from jax import lax
from jax.experimental import pallas as pl
from jax.experimental.pallas import tpu as pltpu
from jax.sharding import Mesh
from jax.sharding import PartitionSpec as P

F32, BF16 = jnp.float32, jnp.bfloat16
LANES = 128
AXES = ("z", "x", "y", "c")
SIZE = {"x": 4, "y": 4, "c": 2}
MIB = 1 << 20


def send(value, axis, by):
    count = lax.axis_size(axis)
    return lax.ppermute(value, axis, [(i, (i + by) % count) for i in range(count)])


def send_along_tokens(value, by):
    count = lax.axis_size("z") * lax.axis_size("x")
    pairs = [(i, i + by) for i in range(count) if 0 <= i + by < count]
    return lax.ppermute(value, ("z", "x"), pairs)


def product(a, b):
    return (a.astype(F32) * b.astype(F32)).astype(BF16)


def group_tables(rows, width):
    tables = [
        pltpu.roll(
            jnp.broadcast_to(rows[g : g + 1], (width // 2, width)), 0, 1, stride=1, stride_axis=0
        )
        for g in range(rows.shape[0])
    ]
    return jnp.concatenate(tables, 0).astype(BF16)


def banded(tables, window, taps, groups):
    lane_group = lax.broadcasted_iota(jnp.int32, (taps, LANES), 1) // (LANES // groups)
    blocks = window.shape[0] // taps - 1
    out = []
    for b in range(0, blocks, 2):
        pair = jnp.concatenate(
            [window[(b + i) * taps : (b + i + 2) * taps] for i in range(2)], 1
        )
        res = jnp.dot(tables, pair, preferred_element_type=F32)
        for i in range(2):
            cols = slice(i * LANES, (i + 1) * LANES)
            acc = res[:taps, cols]
            for g in range(1, groups):
                acc = jnp.where(lane_group == g, res[g * taps : (g + 1) * taps, cols], acc)
            out.append(acc)
    return jnp.concatenate(out, 0)


def forward_body(taps, groups, rows_ref, k_ref, v_ref, q_ref, rim_ref, *refs):
    conv_ref, mixed_ref, gated_ref = refs[-3:]
    mixed = product(k_ref[...], v_ref[...])
    window = jnp.concatenate([rim_ref[...], mixed], 0)
    conv = banded(group_tables(rows_ref[...], 2 * taps), window, taps, groups)
    conv_ref[...] = conv
    mixed_ref[...] = mixed
    gated_ref[...] = (q_ref[...].astype(F32) * conv).astype(BF16)


def forward(half, rows, k, v, q, rim, earlier):
    tokens, width = k.shape
    taps = rim.shape[0]
    groups = LANES * rows.shape[0] // width
    steps = width // LANES // 2
    at = lambda i: (0, i + half * steps)
    column = pl.BlockSpec((tokens, LANES), at)
    in_specs = [
        pl.BlockSpec((groups, 2 * taps), lambda i: (i + half * steps, 0)),
        column,
        column,
        column,
        pl.BlockSpec((taps, LANES), at),
    ]
    args = [rows, k, v, q, rim]
    aliases = {}
    if earlier is not None:
        in_specs += [pl.BlockSpec(memory_space=pl.ANY)] * 2
        args += list(earlier)
        aliases = {5: 0, 6: 1}
    return pl.pallas_call(
        functools.partial(forward_body, taps, groups),
        grid=(steps,),
        in_specs=in_specs,
        out_specs=[column, column, pl.BlockSpec((tokens, LANES), lambda i: (0, i))],
        out_shape=[
            jax.ShapeDtypeStruct((tokens, width), F32),
            jax.ShapeDtypeStruct((tokens, width), BF16),
            jax.ShapeDtypeStruct((tokens, width // 2), BF16),
        ],
        input_output_aliases=aliases,
        compiler_params=pltpu.CompilerParams(vmem_limit_bytes=24 * MIB),
        cost_estimate=pl.CostEstimate(
            flops=tokens * width * 2 * taps * groups, bytes_accessed=tokens * width * 7, transcendentals=0
        ),
        name="conv_forward",
    )(*args)


def gate_body(place_ref, mine_ref, sib_ref, proj_ref, *refs):
    out_ref = refs[-1]
    rows = proj_ref.shape[0] // 8
    acc = None
    for dy in range(4):
        at = pl.ds(dy * rows, rows)
        lhs = jnp.concatenate([mine_ref[:, at], sib_ref[:, at]], 1)
        rhs = jnp.concatenate(
            [
                proj_ref[pl.ds(pl.multiple_of(place_ref[2 * dy + i] * rows, rows), rows), :]
                for i in range(2)
            ],
            0,
        )
        term = jnp.dot(lhs, rhs, preferred_element_type=F32)
        acc = term if acc is None else acc + term
    for ref in refs[:-1]:
        acc = acc + ref[...].astype(F32)
    out_ref[...] = acc.astype(out_ref.dtype)


def gate_part(place, mine, sib, proj, block, half, dtype, *addends):
    depth, width = proj.shape
    tokens = mine.shape[0] // 4
    tile = 256
    steps = width // 2 // tile
    spec = pltpu.PrefetchScalarGridSpec(
        num_scalar_prefetch=1,
        grid=(steps,),
        in_specs=[
            pl.BlockSpec((tokens, depth // 2), lambda i, p: (block, 0)),
            pl.BlockSpec((tokens, depth // 2), lambda i, p: (block, 0)),
            pl.BlockSpec((depth, tile), lambda i, p: (0, i + half * steps)),
        ]
        + [pl.BlockSpec((tokens, tile), lambda i, p: (0, i))] * len(addends),
        out_specs=pl.BlockSpec((tokens, tile), lambda i, p: (0, i)),
    )
    return pl.pallas_call(
        gate_body,
        grid_spec=spec,
        out_shape=jax.ShapeDtypeStruct((tokens, width // 2), dtype),
        compiler_params=pltpu.CompilerParams(vmem_limit_bytes=24 * MIB),
        cost_estimate=pl.CostEstimate(
            flops=tokens * depth * width, bytes_accessed=depth * width + 2 * tokens * depth, transcendentals=0
        ),
        name="grad_gate_part",
    )(place, mine, sib, proj, *addends)


def proj_body(place_ref, mine_ref, sib_ref, *refs):
    gated_refs, out_ref = refs[:-1], refs[-1]
    rows = mine_ref.shape[1]
    tokens, half = gated_refs[0].shape
    core = place_ref[0] % 2
    for h in range(2):
        acc = None
        for d in range(4):
            at = pl.ds(d * tokens, tokens)
            lhs = jnp.concatenate([mine_ref[at, :], sib_ref[at, :]], 1)
            term = lax.dot_general(
                lhs, gated_refs[2 * d + h][...], (((0,), (0,)), ((), ())), preferred_element_type=F32
            )
            acc = term if acc is None else acc + term
        acc = acc.astype(BF16)
        cols = pl.ds(h * half, half)
        out_ref[pl.ds(pl.multiple_of(core * rows, rows), rows), cols] = acc[:rows]
        out_ref[pl.ds(pl.multiple_of((1 - core) * rows, rows), rows), cols] = acc[rows:]


def proj_part(place, mine, sib, gated):
    depth = 2 * mine.shape[1]
    tokens, half = gated[0].shape
    rows = depth // 8
    spec = pltpu.PrefetchScalarGridSpec(
        num_scalar_prefetch=1,
        grid=(4,),
        in_specs=[pl.BlockSpec((4 * tokens, rows), lambda i, p: (0, i))] * 2
        + [pl.BlockSpec((tokens, half), lambda i, p: (0, 0))] * 8,
        out_specs=pl.BlockSpec((2 * rows, 2 * half), lambda i, p: (p[2 * i] // 2, 0)),
    )
    return pl.pallas_call(
        proj_body,
        grid_spec=spec,
        out_shape=jax.ShapeDtypeStruct((depth, 2 * half), BF16),
        compiler_params=pltpu.CompilerParams(vmem_limit_bytes=40 * MIB),
        cost_estimate=pl.CostEstimate(
            flops=16 * tokens * depth * half, bytes_accessed=20 * tokens * half, transcendentals=0
        ),
        name="grad_proj_part",
    )(place, mine, sib, *gated)


def inner_body(taps, groups, *refs):
    own, from_left, from_right = refs[0:2], refs[2:4], refs[4:6]
    q_ref, conv_ref, mixed_ref, rim_ref, query_ref, inner_ref, filter_ref = refs[6:]
    second = pl.program_id(0) >= pl.num_programs(0) // 2
    pick = lambda pair: jnp.where(second, pair[1][...], pair[0][...]).astype(F32)
    gate = pick(own) + pick(from_left) + pick(from_right)
    query_ref[...] = (gate * conv_ref[...]).astype(BF16)
    inner = (gate * q_ref[...].astype(F32)).astype(BF16)
    inner_ref[...] = inner
    window = jnp.concatenate([rim_ref[...], mixed_ref[...]], 0)
    blocks = inner.shape[0] // taps
    left = jnp.concatenate([inner[b * taps : (b + 1) * taps] for b in range(blocks)], 1)
    turn = sum(lax.broadcasted_iota(jnp.int32, (taps, taps), i) for i in range(2)) == taps - 1
    left = jnp.dot(turn.astype(F32).astype(BF16), left, preferred_element_type=F32).astype(BF16)
    right = jnp.concatenate([window[b * taps : (b + 2) * taps] for b in range(blocks)], 1)
    lane_group = (lax.broadcasted_iota(jnp.int32, left.shape, 1) % LANES) // (LANES // groups)
    zero = jnp.zeros_like(left)
    stacked = jnp.concatenate([jnp.where(lane_group == g, left, zero) for g in range(groups)], 0)
    corr = lax.dot_general(stacked, right, (((1,), (1,)), ((), ())), preferred_element_type=F32)
    sums = [
        jnp.sum(
            pltpu.roll(corr[g * taps : (g + 1) * taps], 0, 1, stride=1, stride_axis=0),
            axis=0,
            keepdims=True,
        )[:, taps:]
        for g in range(groups)
    ]
    filter_ref[...] = jnp.concatenate(sums, 0)


def gate_gradients(own, from_left, from_right, q, conv, mixed, rim, group_count):
    tokens, width = q.shape
    taps = rim.shape[0]
    groups = LANES * group_count // width
    steps = width // LANES
    column = pl.BlockSpec((tokens, LANES), lambda i: (0, i))
    first = pl.BlockSpec((tokens, LANES), lambda i: (0, jnp.minimum(i, steps // 2 - 1)))
    last = pl.BlockSpec((tokens, LANES), lambda i: (0, jnp.maximum(i - steps // 2, 0)))
    return pl.pallas_call(
        functools.partial(inner_body, taps, groups),
        grid=(steps,),
        in_specs=[first, last] * 3
        + [column, column, column, pl.BlockSpec((taps, LANES), lambda i: (0, i))],
        out_specs=[column, column, pl.BlockSpec((groups, taps), lambda i: (i, 0))],
        out_shape=[
            jax.ShapeDtypeStruct((tokens, width), BF16),
            jax.ShapeDtypeStruct((tokens, width), BF16),
            jax.ShapeDtypeStruct((group_count, taps), F32),
        ],
        compiler_params=pltpu.CompilerParams(vmem_limit_bytes=32 * MIB),
        cost_estimate=pl.CostEstimate(
            flops=tokens * width * 4 * taps * groups, bytes_accessed=tokens * width * 20, transcendentals=0
        ),
        name="gate_gradients",
    )(*own, *from_left, *from_right, q, conv, mixed, rim)


def backward_body(taps, groups, rows_ref, inner_ref, ahead_ref, k_ref, v_ref, gk_ref, gv_ref):
    window = jnp.concatenate([inner_ref[...], ahead_ref[...]], 0)
    grad = banded(group_tables(rows_ref[...], 2 * taps), window, taps, groups)
    gk_ref[...] = (grad * v_ref[...].astype(F32)).astype(BF16)
    gv_ref[...] = (grad * k_ref[...].astype(F32)).astype(BF16)


def backward(rows, inner, ahead, k, v):
    tokens, width = k.shape
    taps = ahead.shape[0]
    groups = LANES * rows.shape[0] // width
    column = pl.BlockSpec((tokens, LANES), lambda i: (0, i))
    return pl.pallas_call(
        functools.partial(backward_body, taps, groups),
        grid=(width // LANES,),
        in_specs=[
            pl.BlockSpec((groups, 2 * taps), lambda i: (i, 0)),
            column,
            pl.BlockSpec((taps, LANES), lambda i: (0, i)),
            column,
            column,
        ],
        out_specs=[column, column],
        out_shape=[jax.ShapeDtypeStruct((tokens, width), BF16)] * 2,
        compiler_params=pltpu.CompilerParams(vmem_limit_bytes=24 * MIB),
        cost_estimate=pl.CostEstimate(
            flops=tokens * width * 4 * taps * groups, bytes_accessed=tokens * width * 10, transcendentals=0
        ),
        name="conv_backward",
    )(rows, inner, ahead, k, v)


def sum_over(value, axis):
    count = lax.axis_size(axis)
    copies = jnp.broadcast_to(value[None], (count, *value.shape))
    return jnp.sum(lax.all_to_all(copies, axis, split_axis=0, concat_axis=0, tiled=True), 0)


def on_device(query_in, key_in, value_in, filters, proj_out, cotangent):
    tokens, width = query_in.shape
    group_count, taps = filters.shape
    half = width // 2
    x, y, c = (lax.axis_index(a) for a in ("x", "y", "c"))
    part = cotangent.shape[1] // 4

    proj = lax.all_gather(proj_out, "z", axis=0, tiled=True)

    rim = send_along_tokens(product(key_in[tokens - taps :], value_in[tokens - taps :]), 1)
    own_cols = lambda d: lax.dynamic_slice_in_dim(cotangent, ((x + d) % 4) * part, part, 1)
    pieces = [own_cols(0), None, None, None]
    for d in (2, 1, 3):
        pieces[(-d) % 4] = send(own_cols(d), "x", d)
    column = jnp.concatenate(pieces, 0)
    below, above = send(column, "y", 1), send(column, "y", -1)
    middle = column.shape[0] // 2
    far = jnp.concatenate([send(below[:middle], "y", 1), send(above[middle:], "y", -1)], 0)
    mine = jnp.concatenate([column, above, far, below], 1)
    sib = send(mine, "c", 1)
    place = jnp.stack([2 * ((y + dy) % 4) + (c if i == 0 else 1 - c) for dy in range(4) for i in range(2)])
    place = place.astype(jnp.int32)

    taps32 = filters.astype(F32)
    rows = jnp.concatenate(
        [jnp.zeros((group_count, 1), F32), jnp.flip(taps32, 1), jnp.zeros((group_count, taps - 1), F32)], 1
    )
    back_rows = jnp.concatenate([taps32, jnp.zeros((group_count, taps), F32)], 1)
    conv, mixed, gated_a = forward(0, rows, key_in, value_in, query_in, rim, None)
    conv, mixed, gated_b = forward(1, rows, key_in, value_in, query_in, rim, (conv, mixed))
    left_a, right_b = send(gated_a, "x", 1), send(gated_b, "x", -1)
    right_a, left_b = send(gated_a, "x", -1), send(gated_b, "x", 1)
    far_a, far_b = send(left_a, "x", 1), send(right_b, "x", -1)
    gated = [gated_a, gated_b, right_a, right_b, far_a, far_b, left_a, left_b]
    proj_sums = proj_part(place, mine, sib, gated)
    grad_proj = lax.psum_scatter(proj_sums, "z", scatter_dimension=0, tiled=True).astype(F32)

    share = lambda d, h, dtype, *addends: gate_part(place, mine, sib, proj, d, h, dtype, *addends)
    far_a = send(share(2, 0, BF16), "x", 1)
    far_b = send(share(2, 1, BF16), "x", -1)
    from_left_b = send(share(1, 1, BF16), "x", 1)
    from_right_a = send(share(3, 0, BF16), "x", -1)
    from_left_a = send(share(1, 0, BF16, far_a), "x", 1)
    from_right_b = send(share(3, 1, BF16, far_b), "x", -1)
    own = share(0, 0, F32), share(0, 1, F32)
    from_left, from_right = (from_left_a, from_left_b), (from_right_a, from_right_b)

    first = [
        (
            (own[h][:taps] + from_left[h][:taps].astype(F32) + from_right[h][:taps].astype(F32))
            * query_in[:taps, h * half : (h + 1) * half].astype(F32)
        ).astype(BF16)
        for h in range(2)
    ]
    ahead = send_along_tokens(jnp.concatenate(first, 1), -1)
    grad_query, inner, sums = gate_gradients(
        own, from_left, from_right, query_in, conv, mixed, rim, group_count
    )
    grad_filter = sum_over(sum_over(jnp.flip(sums, 1), "x"), "z")
    grad_key, grad_value = backward(back_rows, inner, ahead, key_in, value_in)
    return grad_query, grad_key, grad_value, grad_filter, grad_proj


def solution(mesh):
    ctx, tp = mesh.devices.shape
    shape = (ctx // SIZE["x"], SIZE["x"], tp // SIZE["c"], SIZE["c"])
    fine = Mesh(mesh.devices.reshape(shape), AXES)
    spec, along = P(("z", "x"), ("y", "c")), P(("y", "c"), None)
    return jax.shard_map(
        on_device,
        mesh=fine,
        in_specs=(spec, spec, spec, along, spec, spec),
        out_specs=(spec, spec, spec, along, spec),
        check_vma=False,
    )
```

time: 497 us -> 222 us (0.45)
  waiting for transfers between devices: 217 us -> 71.1 us
  blocking collectives: 134 us -> 0 us
  local copies, waits for them, and re-layouts: 72 us -> 14.7 us
  Pallas kernels: 0 us -> 51.2 us
  starting transfers between devices: 8.47 us -> 54.5 us
  matrix products: 35.4 us -> 0 us
    all_gather x2 -> x1, waiting for transfers between devices: 138 us -> 0.02 us  [on_device(): proj = lax.all_gather(proj_out, 'z', axis=0, tiled=True)]
    psum x1 -> x0, blocking collectives: 134 us -> none  [on_device(): grad_filter = lax.psum(filter_part, 'ctx')]
    reduce_scatter x1, waiting for transfers between devices: 74.4 us -> 0.01 us  [on_device(): lax.psum_scatter(proj_sums, 'z', scatter_dimension=0, tiled=True)]
    ppermute x2 -> x22, waiting for transfers between devices: 3.37 us -> 67.3 us  [the longest x20 58.4 us: send(): lax.ppermute(value, axis, [(i, (i + by) % count) for i in range(count)])]
    pallas_call x0 -> x13, Pallas kernels: none -> 51.2 us  [the longest x8 21.6 us: gate_part(): pl.pallas_call(gate_body, grid_spec=spec, out_shape=jax.ShapeDtypeStruct(...]
    reshape x7 -> x0, local copies, waits for them, and re-layouts: 36.8 us -> none  [the longest x1 16.4 us: toeplitz_rows(): tiled.reshape(group_count, tap_count, 3 * tap_count - 1)]
    dot_general x6 -> x0, matrix products: 35.4 us -> none  [the longest x1 12.8 us: on_device(): lax.dot_general(columns, gated, (((0,), (0,)), ((), ())), preferred_eleme...]
    ppermute x2 -> x22, starting transfers between devices: 8.35 us -> 40.1 us  [the longest x20 29.4 us: send(): lax.ppermute(value, axis, [(i, (i + by) % count) for i in range(count)])]
  transfers between devices with their start and end apart: 5 -> 26, of which waited for: 4 -> 15; matrix products, arithmetic and copies ran while one was open for 14% -> 6% of each run, Pallas kernels for 0% -> 23%
where the time goes in v1:
time: 222 us; the launch traced here: 219 us
  waiting for transfers between devices  71.1 us (32%)
  starting transfers between devices  54.5 us (25%)
  Pallas kernels  51.2 us (23%)
  local copies, waits for them, and re-layouts  14.7 us (7%)
  between operations  14.5 us (7%)
  other arithmetic  13 us (6%)
    ppermute x20, waiting for transfers between devices, send(): lax.ppermute(value, axis, [(i, (i + by) % count) for i in range(count)])  58.4 us
    ppermute x20, starting transfers between devices, send(): lax.ppermute(value, axis, [(i, (i + by) % count) for i in range(count)])  29.4 us
    pallas_call x8, Pallas kernels, gate_part(): pl.pallas_call(gate_body, grid_spec=spec, out_shape=jax.ShapeDtypeStruct(...  21.6 us
    all_to_all x2, starting transfers between devices, sum_over(): lax.all_to_all(copies, axis, split_axis=0, concat_axis=0, tiled=True)  14.4 us
    unnamed x48, local copies, waits for them, and re-layouts  11.8 us
    ppermute x2, starting transfers between devices, send_along_tokens(): return lax.ppermute(value, ('z', 'x'), pairs)  10.6 us
    ppermute x2, waiting for transfers between devices, send_along_tokens(): return lax.ppermute(value, ('z', 'x'), pairs)  8.94 us
    pallas_call x1, Pallas kernels, proj_part(): pl.pallas_call(proj_body, grid_spec=spec, out_shape=jax.ShapeDtypeStruct(...  8.38 us
  transfers between devices with their start and end apart: 26, of which 15 were waited for; matrix products, arithmetic and copies ran while one was open for 6% of the time, Pallas kernels for 23%

profile of v1, /device:TPU:6, one launch (start us, length us, event | category | flops | bytes accessed | tf_op | source)
XLA Modules:
  0.0 219.1 jit_solution(9176169988722789628)
XLA Ops:
  9.3 2.8 %collective-permute-start.1 = (bf16[512,128]{1,0:T(8,128)(2,1)S(1)}, bf16[512,128]{1,0:T(8,128)(2,1)S(1)}, u32[]{:S(2)}, u32[]{:S(2)}) collective-permute-start(bf16[512,128]{1,0:T(8,128)(2,1)S(1)} %get-tuple-element.32), channel_id=1, source_target_pairs={{0,16},{8,24},{16,0},{24,8},{1,17},{9,25},{17,1},{25,9},{2,18},{10... | collective-permute-start | bytes 393224 | tf_op jit(solution)/shard_map/ppermute | solution.py:20
  12.5 5.2 %collective-permute-done = bf16[512,128]{1,0:T(8,128)(2,1)S(1)} collective-permute-done((bf16[512,128]{1,0:T(8,128)(2,1)S(1)}, bf16[512,128]{1,0:T(8,128)(2,1)S(1)}, u32[]{:S(2)}, u32[]{:S(2)}) %collective-permute-start) | collective-permute-done | bytes 131104 | tf_op jit(solution)/shard_map/ppermute | solution.py:20
  19.0 1.7 collective-permute-start.4
  20.7 1.7 collective-permute-start.3
  22.4 10.5 %collective-permute-done.4 = bf16[2048,128]{1,0:T(8,128)(2,1)S(1)} collective-permute-done((bf16[2048,128]{1,0:T(8,128)(2,1)S(1)}, bf16[2048,128]{1,0:T(8,128)(2,1)S(1)}, u32[]{:S(2)}, u32[]{:S(2)}) %collective-permute-start.4) | collective-permute-done | bytes 524320 | tf_op jit(solution)/shard_map/ppermute | solution.py:20
  34.5 2.6 %collective-permute-start.6 = (bf16[1024,128]{1,0:T(8,128)(2,1)S(1)}, bf16[1024,128]{1,0:T(8,128)(2,1)S(1)}, u32[]{:S(2)}, u32[]{:S(2)}) collective-permute-start(bf16[1024,128]{1,0:T(8,128)(2,1)S(1)} %slice.49), channel_id=1, source_target_pairs={{0,6},{2,0},{4,2},{6,4},{1,7},{3,1},{5,3},{7,5},{8,14},{10,8},{12,... | collective-permute-start | bytes 786440 | tf_op jit(solution)/shard_map/ppermute | solution.py:20
  37.1 3.4 %collective-permute-done.5 = bf16[1024,128]{1,0:T(8,128)(2,1)S(1)} collective-permute-done((bf16[1024,128]{1,0:T(8,128)(2,1)S(1)}, bf16[1024,128]{1,0:T(8,128)(2,1)S(1)}, u32[]{:S(2)}, u32[]{:S(2)}) %collective-permute-start.5) | collective-permute-done | bytes 262176 | tf_op jit(solution)/shard_map/ppermute | solution.py:20
  41.0 6.3 %pad_maximum_fusion.mine_ref = bf16[2048,512]{1,0:T(8,128)(2,1)S(1)} fusion(bf16[2048,128]{1,0:T(8,128)(2,1)} %copy-done.19, bf16[1024,128]{1,0:T(8,128)(2,1)S(1)} %collective-permute-done.6, bf16[1024,128]{1,0:T(8,128)(2,1)S(1)} %collective-permute-done.5, bf16[2048,128]{1,0:T(8,128)(2,1)} %copy-done.20, bf16[512,128]{1,0:T(8,128)(2,1)} %copy-done.22, ...), kind=kLoop, calls=%fused_computation | loop fusion | flops 16777216 | bytes 4194304 | tf_op jit(solution)/shard_map/concatenate | solution.py:315
  47.4 1.8 multiply_convert_fusion
  49.2 7.9 %collective-permute-start.14 = (bf16[128,1024]{1,0:T(8,128)(2,1)}, bf16[128,1024]{1,0:T(8,128)(2,1)S(1)}, u32[]{:S(2)}, u32[]{:S(2)}) collective-permute-start(bf16[128,1024]{1,0:T(8,128)(2,1)} %multiply_convert_fusion), channel_id=1, source_target_pairs={{0,8},{8,16},{16,24},{24,32},{32,40},{40,48},{48,56},{56,64},{64,7... | collective-permute-start | bytes 786440 | tf_op jit(solution)/shard_map/ppermute | solution.py:26
  57.4 8.9 %collective-permute-done.14.rim_ref.refs_9_ = bf16[128,1024]{1,0:T(8,128)(2,1)S(1)} collective-permute-done((bf16[128,1024]{1,0:T(8,128)(2,1)}, bf16[128,1024]{1,0:T(8,128)(2,1)S(1)}, u32[]{:S(2)}, u32[]{:S(2)}) %collective-permute-start.14) | collective-permute-done | bytes 262176 | tf_op jit(solution)/shard_map/ppermute | solution.py:26
  66.3 1.2 copy-done.9
  67.6 1.2 copy-done.11
  68.8 3.5 %conv_forward.2 = (f32[512,1024]{1,0:T(8,128)S(1)}, bf16[512,1024]{1,0:T(8,128)(2,1)S(1)}, bf16[512,512]{1,0:T(8,128)(2,1)}) custom-call(f32[64,256]{1,0:T(8,128)S(1)} %maximum_maximum_fusion.rows_ref, bf16[512,1024]{1,0:T(8,128)(2,1)S(1)} %copy-done.9, bf16[512,1024]{1,0:T(8,128)(2,1)S(1)} %copy-done.11, bf16[512,1024]{1,0:T(8,128)(2,1)S(1)} %copy-done.3, ...), custom_call_target="tpu_custom_call" | custom-call | flops 1073741824 | bytes 3670016 | tf_op jit(solution)/shard_map/conv_forward/pallas_call | solution.py:91
  72.3 3.5 %conv_forward.3 = (f32[512,1024]{1,0:T(8,128)S(1)}, bf16[512,1024]{1,0:T(8,128)(2,1)S(1)}, bf16[512,512]{1,0:T(8,128)(2,1)}) custom-call(f32[64,256]{1,0:T(8,128)S(1)} %maximum_maximum_fusion.rows_ref, bf16[512,1024]{1,0:T(8,128)(2,1)S(1)} %copy-done.9, bf16[512,1024]{1,0:T(8,128)(2,1)S(1)} %copy-done.11, ...), custom_call_target="tpu_custom_call", output_to_operand_aliasing={{0}: (5, {}), {1}: (6, {})} | custom-call | flops 1073741824 | bytes 3670016 | tf_op jit(solution)/shard_map/conv_forward/pallas_call | solution.py:91
  75.7 1.3 copy-done.1
  78.0 3.2 %collective-permute-start.18 = (bf16[512,512]{1,0:T(8,128)(2,1)}, bf16[512,512]{1,0:T(8,128)(2,1)}, u32[]{:S(2)}, u32[]{:S(2)}) collective-permute-start(bf16[512,512]{1,0:T(8,128)(2,1)} %get-tuple-element.25.refs_0_), channel_id=1, source_target_pairs={{0,8},{8,16},{16,24},{24,0},{1,9},{9,17},{17,25},{25,1},{2,10},{10... | collective-permute-start | bytes 1572872 | tf_op jit(solution)/shard_map/ppermute | solution.py:20
  81.3 2.0 collective-permute-start.16
  83.3 11.1 %collective-permute-done.17.refs_3_ = bf16[512,512]{1,0:T(8,128)(2,1)} collective-permute-done((bf16[512,512]{1,0:T(8,128)(2,1)}, bf16[512,512]{1,0:T(8,128)(2,1)}, u32[]{:S(2)}, u32[]{:S(2)}) %collective-permute-start.17) | collective-permute-done | bytes 524320 | tf_op jit(solution)/shard_map/ppermute | solution.py:20
  94.3 3.3 %collective-permute-start.19 = (bf16[512,512]{1,0:T(8,128)(2,1)}, bf16[512,512]{1,0:T(8,128)(2,1)}, u32[]{:S(2)}, u32[]{:S(2)}) collective-permute-start(bf16[512,512]{1,0:T(8,128)(2,1)} %collective-permute-done.18.refs_6_), channel_id=1, source_target_pairs={{0,8},{8,16},{16,24},{24,0},{1,9},{9,17},{17,25},{25,1},{2,10},{10... | collective-permute-start | bytes 1572872 | tf_op jit(solution)/shard_map/ppermute | solution.py:20
  97.7 7.5 %collective-permute-done.21.refs_7_ = bf16[512,512]{1,0:T(8,128)(2,1)} collective-permute-done((bf16[512,512]{1,0:T(8,128)(2,1)}, bf16[512,512]{1,0:T(8,128)(2,1)}, u32[]{:S(2)}, u32[]{:S(2)}) %collective-permute-start.21) | collective-permute-done | bytes 524320 | tf_op jit(solution)/shard_map/ppermute | solution.py:20
  105.6 10.2 %collective-permute-done.20.refs_5_ = bf16[512,512]{1,0:T(8,128)(2,1)} collective-permute-done((bf16[512,512]{1,0:T(8,128)(2,1)}, bf16[512,512]{1,0:T(8,128)(2,1)}, u32[]{:S(2)}, u32[]{:S(2)}) %collective-permute-start.20) | collective-permute-done | bytes 524320 | tf_op jit(solution)/shard_map/ppermute | solution.py:20
  115.8 8.4 %grad_proj_part.1 = bf16[1024,1024]{1,0:T(8,128)(2,1)S(1)} custom-call(s32[8]{0:T(128)S(1)} %stack.35.place_ref, bf16[2048,512]{1,0:T(8,128)(2,1)S(1)} %pad_maximum_fusion.mine_ref, bf16[2048,512]{1,0:T(8,128)(2,1)} %collective-permute-done.7.sib_ref, bf16[512,512]{1,0:T(8,128)(2,1)} %get-tuple-element.25.refs_0_, ...), custom_call_target="tpu_custom_call" | custom-call | flops 4294967296 | bytes 5242880 | tf_op jit(solution)/shard_map/grad_proj_part/pallas_call | solution.py:190
  124.2 1.4 copy-done.8
  125.6 1.6 copy-done
  127.2 2.6 %grad_gate_part.14 = bf16[512,512]{1,0:T(8,128)(2,1)S(1)} custom-call(s32[8]{0:T(128)S(1)} %stack.35.place_ref, bf16[2048,512]{1,0:T(8,128)(2,1)S(1)} %pad_maximum_fusion.mine_ref, bf16[2048,512]{1,0:T(8,128)(2,1)} %collective-permute-done.7.sib_ref, bf16[1024,1024]{1,0:T(8,128)(2,1)S(1)} %copy-done), custom_call_target="tpu_custom_call" | custom-call | flops 536870912 | bytes 2097152 | tf_op jit(solution)/shard_map/grad_gate_part/pallas_call | solution.py:147
  129.9 2.6 %grad_gate_part.10 = bf16[512,512]{1,0:T(8,128)(2,1)S(1)} custom-call(s32[8]{0:T(128)S(1)} %stack.35.place_ref, bf16[2048,512]{1,0:T(8,128)(2,1)S(1)} %pad_maximum_fusion.mine_ref, bf16[2048,512]{1,0:T(8,128)(2,1)} %collective-permute-done.7.sib_ref, bf16[1024,1024]{1,0:T(8,128)(2,1)S(1)} %copy-done), custom_call_target="tpu_custom_call" | custom-call | flops 536870912 | bytes 2097152 | tf_op jit(solution)/shard_map/grad_gate_part/pallas_call | solution.py:147
  132.5 3.3 %collective-permute-start.8 = (bf16[512,512]{1,0:T(8,128)(2,1)S(1)}, bf16[512,512]{1,0:T(8,128)(2,1)S(1)}, u32[]{:S(2)}, u32[]{:S(2)}) collective-permute-start(bf16[512,512]{1,0:T(8,128)(2,1)S(1)} %grad_gate_part.10), channel_id=1, source_target_pairs={{0,8},{8,16},{16,24},{24,0},{1,9},{9,17},{17,25},{25,1},{2,10},{10... | collective-permute-start | bytes 1572872 | tf_op jit(solution)/shard_map/ppermute | solution.py:20
  135.8 2.6 %grad_gate_part.13 = bf16[512,512]{1,0:T(8,128)(2,1)S(1)} custom-call(s32[8]{0:T(128)S(1)} %stack.35.place_ref, bf16[2048,512]{1,0:T(8,128)(2,1)S(1)} %pad_maximum_fusion.mine_ref, bf16[2048,512]{1,0:T(8,128)(2,1)} %collective-permute-done.7.sib_ref, bf16[1024,1024]{1,0:T(8,128)(2,1)S(1)} %copy-done), custom_call_target="tpu_custom_call" | custom-call | flops 536870912 | bytes 2097152 | tf_op jit(solution)/shard_map/grad_gate_part/pallas_call | solution.py:147
  138.5 2.6 %grad_gate_part.12 = bf16[512,512]{1,0:T(8,128)(2,1)S(1)} custom-call(s32[8]{0:T(128)S(1)} %stack.35.place_ref, bf16[2048,512]{1,0:T(8,128)(2,1)S(1)} %pad_maximum_fusion.mine_ref, bf16[2048,512]{1,0:T(8,128)(2,1)} %collective-permute-done.7.sib_ref, bf16[1024,1024]{1,0:T(8,128)(2,1)S(1)} %copy-done), custom_call_target="tpu_custom_call" | custom-call | flops 536870912 | bytes 2097152 | tf_op jit(solution)/shard_map/grad_gate_part/pallas_call | solution.py:147
  141.2 3.3 %collective-permute-start.10 = (bf16[512,512]{1,0:T(8,128)(2,1)S(1)}, bf16[512,512]{1,0:T(8,128)(2,1)S(1)}, u32[]{:S(2)}, u32[]{:S(2)}) collective-permute-start(bf16[512,512]{1,0:T(8,128)(2,1)S(1)} %grad_gate_part.12), channel_id=1, source_target_pairs={{0,8},{8,16},{16,24},{24,0},{1,9},{9,17},{17,25},{25,1},{2,10},{10... | collective-permute-start | bytes 1572872 | tf_op jit(solution)/shard_map/ppermute | solution.py:20
  144.4 1.5 collective-permute-done.12.refs_0_
  146.0 2.6 %grad_gate_part.15 = bf16[512,512]{1,0:T(8,128)(2,1)S(1)} custom-call(s32[8]{0:T(128)S(1)} %stack.35.place_ref, bf16[2048,512]{1,0:T(8,128)(2,1)S(1)} %pad_maximum_fusion.mine_ref, bf16[2048,512]{1,0:T(8,128)(2,1)} %collective-permute-done.7.sib_ref, bf16[1024,1024]{1,0:T(8,128)(2,1)S(1)} %copy-done, bf16[512,512]{1,0:T(8,128)(2,1)S(1)} %collective-permute-done.12.refs_0_), custom_call_target="tpu_custom_call" | custom-call | flops 536870912 | bytes 2097152 | tf_op jit(solution)/shard_map/grad_gate_part/pallas_call | solution.py:147
  148.7 2.6 %grad_gate_part.11 = bf16[512,512]{1,0:T(8,128)(2,1)S(1)} custom-call(s32[8]{0:T(128)S(1)} %stack.35.place_ref, bf16[2048,512]{1,0:T(8,128)(2,1)S(1)} %pad_maximum_fusion.mine_ref, bf16[2048,512]{1,0:T(8,128)(2,1)} %collective-permute-done.7.sib_ref, bf16[1024,1024]{1,0:T(8,128)(2,1)S(1)} %copy-done, bf16[512,512]{1,0:T(8,128)(2,1)S(1)} %collective-permute-done.8.refs_0_), custom_call_target="tpu_custom_call" | custom-call | flops 536870912 | bytes 2097152 | tf_op jit(solution)/shard_map/grad_gate_part/pallas_call | solution.py:147
  151.4 3.5 %collective-permute-start.9 = (bf16[512,512]{1,0:T(8,128)(2,1)S(1)}, bf16[512,512]{1,0:T(8,128)(2,1)S(1)}, u32[]{:S(2)}, u32[]{:S(2)}) collective-permute-start(bf16[512,512]{1,0:T(8,128)(2,1)S(1)} %grad_gate_part.11), channel_id=1, source_target_pairs={{0,8},{8,16},{16,24},{24,0},{1,9},{9,17},{17,25},{25,1},{2,10},{10... | collective-permute-start | bytes 1572872 | tf_op jit(solution)/shard_map/ppermute | solution.py:20
  154.9 2.6 %grad_gate_part.9.refs_1_ = f32[512,512]{1,0:T(8,128)S(1)} custom-call(s32[8]{0:T(128)S(1)} %stack.35.place_ref, bf16[2048,512]{1,0:T(8,128)(2,1)S(1)} %pad_maximum_fusion.mine_ref, bf16[2048,512]{1,0:T(8,128)(2,1)} %collective-permute-done.7.sib_ref, bf16[1024,1024]{1,0:T(8,128)(2,1)S(1)} %copy-done), custom_call_target="tpu_custom_call" | custom-call | flops 536870912 | bytes 2097152 | tf_op jit(solution)/shard_map/grad_gate_part/pallas_call | solution.py:147
  157.6 3.3 %grad_gate_part.8.refs_0_ = f32[512,512]{1,0:T(8,128)S(1)} custom-call(s32[8]{0:T(128)S(1)} %stack.35.place_ref, bf16[2048,512]{1,0:T(8,128)(2,1)S(1)} %pad_maximum_fusion.mine_ref, bf16[2048,512]{1,0:T(8,128)(2,1)} %collective-permute-done.7.sib_ref, bf16[1024,1024]{1,0:T(8,128)(2,1)S(1)} %copy-done), custom_call_target="tpu_custom_call" | custom-call | flops 536870912 | bytes 2097152 | tf_op jit(solution)/shard_map/grad_gate_part/pallas_call | solution.py:147
  160.9 5.6 %collective-permute-done.13.refs_5_ = bf16[512,512]{1,0:T(8,128)(2,1)S(1)} collective-permute-done((bf16[512,512]{1,0:T(8,128)(2,1)S(1)}, bf16[512,512]{1,0:T(8,128)(2,1)S(1)}, u32[]{:S(2)}, u32[]{:S(2)}) %collective-permute-start.13) | collective-permute-done | bytes 524320 | tf_op jit(solution)/shard_map/ppermute | solution.py:20
  166.5 1.9 collective-permute-done.9.refs_2_
  168.5 8.4 %gate_gradients.1 = (bf16[512,1024]{1,0:T(8,128)(2,1)}, bf16[512,1024]{1,0:T(8,128)(2,1)S(1)}, f32[64,128]{1,0:T(8,128)S(1)}) custom-call(f32[512,512]{1,0:T(8,128)S(1)} %grad_gate_part.8.refs_0_, f32[512,512]{1,0:T(8,128)S(1)} %grad_gate_part.9.refs_1_, bf16[512,512]{1,0:T(8,128)(2,1)S(1)} %collective-permute-done.9.refs_2_, ...), custom_call_target="tpu_custom_call" | custom-call | flops 2147483648 | bytes 10485760 | tf_op jit(solution)/shard_map/gate_gradients/pallas_call | solution.py:240
  178.6 7.0 %all-to-all-start = ((f32[4,64,128]{2,1,0:T(8,128)}), f32[4,64,128]{2,1,0:T(8,128)S(1)}, u32[]{:S(2)}, u32[]{:S(2)}) async-start(f32[4,64,128]{2,1,0:T(8,128)} %broadcast_in_dim.10), calls=%async_computation | async-start | bytes 262144 | tf_op jit(solution)/shard_map/all_to_all | solution.py:294
  185.6 1.4 fusion.5
  187.0 2.8 %collective-permute-start.15 = (bf16[128,1024]{1,0:T(8,128)(2,1)S(1)}, bf16[128,1024]{1,0:T(8,128)(2,1)S(1)}, u32[]{:S(2)}, u32[]{:S(2)}) collective-permute-start(bf16[128,1024]{1,0:T(8,128)(2,1)S(1)} %pad_maximum_fusion.2), channel_id=1, source_target_pairs={{8,0},{16,8},{24,16},{32,24},{40,32},{48,40},{56,48},{64,56},{72,6... | collective-permute-start | bytes 786440 | tf_op jit(solution)/shard_map/ppermute | solution.py:26
  190.8 7.4 %all-to-all-start.1 = ((f32[8,64,128]{2,1,0:T(8,128)}), f32[8,64,128]{2,1,0:T(8,128)}, u32[]{:S(2)}, u32[]{:S(2)}) async-start(f32[8,64,128]{2,1,0:T(8,128)} %broadcast_in_dim.22), calls=%async_computation.1 | async-start | bytes 524288 | tf_op jit(solution)/shard_map/all_to_all | solution.py:294
  199.5 6.0 %conv_backward.1 = (bf16[512,1024]{1,0:T(8,128)(2,1)}, bf16[512,1024]{1,0:T(8,128)(2,1)}) custom-call(f32[64,256]{1,0:T(8,128)S(1)} %concatenate.22.rows_ref, bf16[512,1024]{1,0:T(8,128)(2,1)S(1)} %copy-done.18, bf16[128,1024]{1,0:T(8,128)(2,1)S(1)} %collective-permute-done.15.ahead_ref, bf16[512,1024]{1,0:T(8,128)(2,1)S(1)} %copy-done.10, ...), custom_call_target="tpu_custom_call" | custom-call | flops 2147483648 | bytes 5242880 | tf_op jit(solution)/shard_map/conv_backward/pallas_call | solution.py:271
  205.5 3.4 %all-to-all-done.1 = f32[8,64,128]{2,1,0:T(8,128)} async-done(((f32[8,64,128]{2,1,0:T(8,128)}), f32[8,64,128]{2,1,0:T(8,128)}, u32[]{:S(2)}, u32[]{:S(2)}) %all-to-all-start.1) | async-done | bytes 262176 | tf_op jit(solution)/shard_map/all_to_all | solution.py:294
  208.8 1.6 reduce_sum.19
  210.4 1.8 convert_element_type.51
  (88 shorter events, 12.1 us)
Async XLA Ops:
  7.2 118.5 %all-gather.2.cloned.1.call-start = ((), (), s32[]{:S(2)}) async-start(), calls=%async_computation.3 | async-start | bytes 2359296 | tf_op jit(solution)/shard_map/all_gather | solution.py:304
  8.4 9.3 %collective-permute-start = (bf16[512,128]{1,0:T(8,128)(2,1)S(1)}, bf16[512,128]{1,0:T(8,128)(2,1)S(1)}, u32[]{:S(2)}, u32[]{:S(2)}) collective-permute-start(bf16[512,128]{1,0:T(8,128)(2,1)S(1)} %get-tuple-element.30), channel_id=1, source_target_pairs={{0,24},{8,0},{16,8},{24,16},{1,25},{9,1},{17,9},{25,17},{2,26},{10... | collective-permute-start | bytes 393224 | tf_op jit(solution)/shard_map/ppermute | solution.py:20
  9.3 8.4 %collective-permute-start.1 = (bf16[512,128]{1,0:T(8,128)(2,1)S(1)}, bf16[512,128]{1,0:T(8,128)(2,1)S(1)}, u32[]{:S(2)}, u32[]{:S(2)}) collective-permute-start(bf16[512,128]{1,0:T(8,128)(2,1)S(1)} %get-tuple-element.32), channel_id=1, source_target_pairs={{0,16},{8,24},{16,0},{24,8},{1,17},{9,25},{17,1},{25,9},{2,18},{10... | collective-permute-start | bytes 393224 | tf_op jit(solution)/shard_map/ppermute | solution.py:20
  12.2 6.2 %collective-permute-start.2 = (bf16[512,128]{1,0:T(8,128)(2,1)S(1)}, bf16[512,128]{1,0:T(8,128)(2,1)S(1)}, u32[]{:S(2)}, u32[]{:S(2)}) collective-permute-start(bf16[512,128]{1,0:T(8,128)(2,1)S(1)} %get-tuple-element.31), channel_id=1, source_target_pairs={{0,8},{8,16},{16,24},{24,0},{1,9},{9,17},{17,25},{25,1},{2,10},{10... | collective-permute-start | bytes 393224 | tf_op jit(solution)/shard_map/ppermute | solution.py:20
  19.0 13.8 %collective-permute-start.4 = (bf16[2048,128]{1,0:T(8,128)(2,1)S(1)}, bf16[2048,128]{1,0:T(8,128)(2,1)S(1)}, u32[]{:S(2)}, u32[]{:S(2)}) collective-permute-start(bf16[2048,128]{1,0:T(8,128)(2,1)S(1)} %pad_maximum_fusion.1), channel_id=1, source_target_pairs={{0,2},{2,4},{4,6},{6,0},{1,3},{3,5},{5,7},{7,1},{8,10},{10,12},{12... | collective-permute-start | bytes 1572872 | tf_op jit(solution)/shard_map/ppermute | solution.py:20
  20.7 12.6 %collective-permute-start.3 = (bf16[2048,128]{1,0:T(8,128)(2,1)S(1)}, bf16[2048,128]{1,0:T(8,128)(2,1)S(1)}, u32[]{:S(2)}, u32[]{:S(2)}) collective-permute-start(bf16[2048,128]{1,0:T(8,128)(2,1)S(1)} %pad_maximum_fusion.1), channel_id=1, source_target_pairs={{0,6},{2,0},{4,2},{6,4},{1,7},{3,1},{5,3},{7,5},{8,14},{10,8},{12,... | collective-permute-start | bytes 1572872 | tf_op jit(solution)/shard_map/ppermute | solution.py:20
  22.4 188.0 %reduce-scatter.2.cloned.1.call-start = ((), (), s32[]{:S(2)}) async-start(), calls=%async_computation.4 | async-start | bytes 2359296 | tf_op jit(solution)/shard_map/reduce_scatter | solution.py:332
  32.9 0.8 copy-start.19
  32.9 7.7 %collective-permute-start.5 = (bf16[1024,128]{1,0:T(8,128)(2,1)S(1)}, bf16[1024,128]{1,0:T(8,128)(2,1)S(1)}, u32[]{:S(2)}, u32[]{:S(2)}) collective-permute-start(bf16[1024,128]{1,0:T(8,128)(2,1)S(1)} %slice.48), channel_id=1, source_target_pairs={{0,2},{2,4},{4,6},{6,0},{1,3},{3,5},{5,7},{7,1},{8,10},{10,12},{12... | collective-permute-start | bytes 786440 | tf_op jit(solution)/shard_map/ppermute | solution.py:20
  33.7 0.8 copy-start.20
  34.5 22.7 %copy-start.23 = (bf16[64,128]{1,0:T(8,128)(2,1)S(1)}, bf16[64,128]{1,0:T(8,128)(2,1)}, u32[]{:S(2)}) copy-start(bf16[64,128]{1,0:T(8,128)(2,1)} %param.9) | copy-start | bytes 49156
  34.5 31.8 %copy-start.3 = (bf16[512,1024]{1,0:T(8,128)(2,1)S(1)}, bf16[512,1024]{1,0:T(8,128)(2,1)}, u32[]{:S(2)}) copy-start(bf16[512,1024]{1,0:T(8,128)(2,1)} %refs_6_.1) | copy-start | bytes 3145732
  34.5 6.5 %collective-permute-start.6 = (bf16[1024,128]{1,0:T(8,128)(2,1)S(1)}, bf16[1024,128]{1,0:T(8,128)(2,1)S(1)}, u32[]{:S(2)}, u32[]{:S(2)}) collective-permute-start(bf16[1024,128]{1,0:T(8,128)(2,1)S(1)} %slice.49), channel_id=1, source_target_pairs={{0,6},{2,0},{4,2},{6,4},{1,7},{3,1},{5,3},{7,5},{8,14},{10,8},{12,... | collective-permute-start | bytes 786440 | tf_op jit(solution)/shard_map/ppermute | solution.py:20
  47.3 68.5 %collective-permute-start.7 = (bf16[2048,512]{1,0:T(8,128)(2,1)S(1)}, bf16[2048,512]{1,0:T(8,128)(2,1)}, u32[]{:S(2)}, u32[]{:S(2)}) collective-permute-start(bf16[2048,512]{1,0:T(8,128)(2,1)S(1)} %pad_maximum_fusion.mine_ref), channel_id=1, source_target_pairs={{0,1},{1,0},{2,3},{3,2},{4,5},{5,4},{6,7},{7,6},{8,9},{9,8},{10,11... | collective-permute-start | bytes 6291464 | tf_op jit(solution)/shard_map/ppermute | solution.py:20
  49.2 17.1 %collective-permute-start.14 = (bf16[128,1024]{1,0:T(8,128)(2,1)}, bf16[128,1024]{1,0:T(8,128)(2,1)S(1)}, u32[]{:S(2)}, u32[]{:S(2)}) collective-permute-start(bf16[128,1024]{1,0:T(8,128)(2,1)} %multiply_convert_fusion), channel_id=1, source_target_pairs={{0,8},{8,16},{16,24},{24,32},{32,40},{40,48},{48,56},{56,64},{64,7... | collective-permute-start | bytes 786440 | tf_op jit(solution)/shard_map/ppermute | solution.py:26
  66.3 1.2 copy-start.9
  67.6 1.2 copy-start.11
  75.7 1.3 copy-start.1
  77.1 1.0 copy-start.6
  78.0 16.3 %collective-permute-start.17 = (bf16[512,512]{1,0:T(8,128)(2,1)}, bf16[512,512]{1,0:T(8,128)(2,1)}, u32[]{:S(2)}, u32[]{:S(2)}) collective-permute-start(bf16[512,512]{1,0:T(8,128)(2,1)} %get-tuple-element.26.refs_1_), channel_id=1, source_target_pairs={{0,24},{8,0},{16,8},{24,16},{1,25},{9,1},{17,9},{25,17},{2,26},{10... | collective-permute-start | bytes 1572872 | tf_op jit(solution)/shard_map/ppermute | solution.py:20
  78.0 16.3 %collective-permute-start.18 = (bf16[512,512]{1,0:T(8,128)(2,1)}, bf16[512,512]{1,0:T(8,128)(2,1)}, u32[]{:S(2)}, u32[]{:S(2)}) collective-permute-start(bf16[512,512]{1,0:T(8,128)(2,1)} %get-tuple-element.25.refs_0_), channel_id=1, source_target_pairs={{0,8},{8,16},{16,24},{24,0},{1,9},{9,17},{17,25},{25,1},{2,10},{10... | collective-permute-start | bytes 1572872 | tf_op jit(solution)/shard_map/ppermute | solution.py:20
  81.3 23.9 %collective-permute-start.21 = (bf16[512,512]{1,0:T(8,128)(2,1)}, bf16[512,512]{1,0:T(8,128)(2,1)}, u32[]{:S(2)}, u32[]{:S(2)}) collective-permute-start(bf16[512,512]{1,0:T(8,128)(2,1)} %get-tuple-element.26.refs_1_), channel_id=1, source_target_pairs={{0,8},{8,16},{16,24},{24,0},{1,9},{9,17},{17,25},{25,1},{2,10},{10... | collective-permute-start | bytes 1572872 | tf_op jit(solution)/shard_map/ppermute | solution.py:20
  81.3 24.3 %collective-permute-start.16 = (bf16[512,512]{1,0:T(8,128)(2,1)}, bf16[512,512]{1,0:T(8,128)(2,1)}, u32[]{:S(2)}, u32[]{:S(2)}) collective-permute-start(bf16[512,512]{1,0:T(8,128)(2,1)} %get-tuple-element.25.refs_0_), channel_id=1, source_target_pairs={{0,24},{8,0},{16,8},{24,16},{1,25},{9,1},{17,9},{25,17},{2,26},{10... | collective-permute-start | bytes 1572872 | tf_op jit(solution)/shard_map/ppermute | solution.py:20
  94.3 21.4 %collective-permute-start.20 = (bf16[512,512]{1,0:T(8,128)(2,1)}, bf16[512,512]{1,0:T(8,128)(2,1)}, u32[]{:S(2)}, u32[]{:S(2)}) collective-permute-start(bf16[512,512]{1,0:T(8,128)(2,1)} %collective-permute-done.17.refs_3_), channel_id=1, source_target_pairs={{0,24},{8,0},{16,8},{24,16},{1,25},{9,1},{17,9},{25,17},{2,26},{10... | collective-permute-start | bytes 1572872 | tf_op jit(solution)/shard_map/ppermute | solution.py:20
  94.3 21.4 %collective-permute-start.19 = (bf16[512,512]{1,0:T(8,128)(2,1)}, bf16[512,512]{1,0:T(8,128)(2,1)}, u32[]{:S(2)}, u32[]{:S(2)}) collective-permute-start(bf16[512,512]{1,0:T(8,128)(2,1)} %collective-permute-done.18.refs_6_), channel_id=1, source_target_pairs={{0,8},{8,16},{16,24},{24,0},{1,9},{9,17},{17,25},{25,1},{2,10},{10... | collective-permute-start | bytes 1572872 | tf_op jit(solution)/shard_map/ppermute | solution.py:20
  124.2 1.4 copy-start.8
  125.6 1.6 copy-start
  129.8 16.2 %collective-permute-start.12 = (bf16[512,512]{1,0:T(8,128)(2,1)S(1)}, bf16[512,512]{1,0:T(8,128)(2,1)S(1)}, u32[]{:S(2)}, u32[]{:S(2)}) collective-permute-start(bf16[512,512]{1,0:T(8,128)(2,1)S(1)} %grad_gate_part.14), channel_id=1, source_target_pairs={{0,24},{8,0},{16,8},{24,16},{1,25},{9,1},{17,9},{25,17},{2,26},{10... | collective-permute-start | bytes 1572872 | tf_op jit(solution)/shard_map/ppermute | solution.py:20
  132.5 16.2 %collective-permute-start.8 = (bf16[512,512]{1,0:T(8,128)(2,1)S(1)}, bf16[512,512]{1,0:T(8,128)(2,1)S(1)}, u32[]{:S(2)}, u32[]{:S(2)}) collective-permute-start(bf16[512,512]{1,0:T(8,128)(2,1)S(1)} %grad_gate_part.10), channel_id=1, source_target_pairs={{0,8},{8,16},{16,24},{24,0},{1,9},{9,17},{17,25},{25,1},{2,10},{10... | collective-permute-start | bytes 1572872 | tf_op jit(solution)/shard_map/ppermute | solution.py:20
  138.4 22.5 %collective-permute-start.11 = (bf16[512,512]{1,0:T(8,128)(2,1)S(1)}, bf16[512,512]{1,0:T(8,128)(2,1)S(1)}, u32[]{:S(2)}, u32[]{:S(2)}) collective-permute-start(bf16[512,512]{1,0:T(8,128)(2,1)S(1)} %grad_gate_part.13), channel_id=1, source_target_pairs={{0,24},{8,0},{16,8},{24,16},{1,25},{9,1},{17,9},{25,17},{2,26},{10... | collective-permute-start | bytes 1572872 | tf_op jit(solution)/shard_map/ppermute | solution.py:20
  141.2 19.8 %collective-permute-start.10 = (bf16[512,512]{1,0:T(8,128)(2,1)S(1)}, bf16[512,512]{1,0:T(8,128)(2,1)S(1)}, u32[]{:S(2)}, u32[]{:S(2)}) collective-permute-start(bf16[512,512]{1,0:T(8,128)(2,1)S(1)} %grad_gate_part.12), channel_id=1, source_target_pairs={{0,8},{8,16},{16,24},{24,0},{1,9},{9,17},{17,25},{25,1},{2,10},{10... | collective-permute-start | bytes 1572872 | tf_op jit(solution)/shard_map/ppermute | solution.py:20
  148.6 17.9 %collective-permute-start.13 = (bf16[512,512]{1,0:T(8,128)(2,1)S(1)}, bf16[512,512]{1,0:T(8,128)(2,1)S(1)}, u32[]{:S(2)}, u32[]{:S(2)}) collective-permute-start(bf16[512,512]{1,0:T(8,128)(2,1)S(1)} %grad_gate_part.15), channel_id=1, source_target_pairs={{0,24},{8,0},{16,8},{24,16},{1,25},{9,1},{17,9},{25,17},{2,26},{10... | collective-permute-start | bytes 1572872 | tf_op jit(solution)/shard_map/ppermute | solution.py:20
  151.4 17.1 %collective-permute-start.9 = (bf16[512,512]{1,0:T(8,128)(2,1)S(1)}, bf16[512,512]{1,0:T(8,128)(2,1)S(1)}, u32[]{:S(2)}, u32[]{:S(2)}) collective-permute-start(bf16[512,512]{1,0:T(8,128)(2,1)S(1)} %grad_gate_part.11), channel_id=1, source_target_pairs={{0,8},{8,16},{16,24},{24,0},{1,9},{9,17},{17,25},{25,1},{2,10},{10... | collective-permute-start | bytes 1572872 | tf_op jit(solution)/shard_map/ppermute | solution.py:20
  157.5 10.9 %copy-start.4 = (f32[512,512]{1,0:T(8,128)}, f32[512,512]{1,0:T(8,128)S(1)}, u32[]{:S(2)}) copy-start(f32[512,512]{1,0:T(8,128)S(1)} %grad_gate_part.9.refs_1_) | copy-start | bytes 3145732
  157.5 10.9 %copy-start.2 = (f32[512,1024]{1,0:T(8,128)S(1)}, f32[512,1024]{1,0:T(8,128)}, u32[]{:S(2)}) copy-start(f32[512,1024]{1,0:T(8,128)} %copy-done.1) | copy-start | bytes 6291460
  157.5 10.9 %copy-start.7 = (bf16[512,1024]{1,0:T(8,128)(2,1)S(1)}, bf16[512,1024]{1,0:T(8,128)(2,1)}, u32[]{:S(2)}) copy-start(bf16[512,1024]{1,0:T(8,128)(2,1)} %copy-done.6) | copy-start | bytes 3145732
  160.9 16.0 %copy-start.5 = (f32[512,512]{1,0:T(8,128)}, f32[512,512]{1,0:T(8,128)S(1)}, u32[]{:S(2)}) copy-start(f32[512,512]{1,0:T(8,128)S(1)} %grad_gate_part.8.refs_0_) | copy-start | bytes 3145732
  160.9 15.9 %copy-start.13 = (bf16[512,512]{1,0:T(8,128)(2,1)}, bf16[512,512]{1,0:T(8,128)(2,1)S(1)}, u32[]{:S(2)}) copy-start(bf16[512,512]{1,0:T(8,128)(2,1)S(1)} %collective-permute-done.11.refs_4_) | copy-start | bytes 1572868
  160.9 15.9 %copy-start.14 = (bf16[512,512]{1,0:T(8,128)(2,1)}, bf16[512,512]{1,0:T(8,128)(2,1)S(1)}, u32[]{:S(2)}) copy-start(bf16[512,512]{1,0:T(8,128)(2,1)S(1)} %collective-permute-done.10.refs_3_) | copy-start | bytes 1572868
  166.5 10.3 %copy-start.15 = (bf16[512,512]{1,0:T(8,128)(2,1)}, bf16[512,512]{1,0:T(8,128)(2,1)S(1)}, u32[]{:S(2)}) copy-start(bf16[512,512]{1,0:T(8,128)(2,1)S(1)} %collective-permute-done.13.refs_5_) | copy-start | bytes 1572868
  168.5 8.4 %copy-start.16 = (bf16[512,512]{1,0:T(8,128)(2,1)}, bf16[512,512]{1,0:T(8,128)(2,1)S(1)}, u32[]{:S(2)}) copy-start(bf16[512,512]{1,0:T(8,128)(2,1)S(1)} %collective-permute-done.9.refs_2_) | copy-start | bytes 1572868
  176.9 1.0 copy-start.17
  177.8 20.4 %copy-start.10 = (bf16[512,1024]{1,0:T(8,128)(2,1)S(1)}, bf16[512,1024]{1,0:T(8,128)(2,1)}, u32[]{:S(2)}) copy-start(bf16[512,1024]{1,0:T(8,128)(2,1)} %k_ref.5) | copy-start | bytes 3145732
  177.8 20.4 %copy-start.12 = (bf16[512,1024]{1,0:T(8,128)(2,1)S(1)}, bf16[512,1024]{1,0:T(8,128)(2,1)}, u32[]{:S(2)}) copy-start(bf16[512,1024]{1,0:T(8,128)(2,1)} %v_ref.5) | copy-start | bytes 3145732
  178.6 11.5 %all-to-all-start = ((f32[4,64,128]{2,1,0:T(8,128)}), f32[4,64,128]{2,1,0:T(8,128)S(1)}, u32[]{:S(2)}, u32[]{:S(2)}) async-start(f32[4,64,128]{2,1,0:T(8,128)} %broadcast_in_dim.10), calls=%async_computation | async-start | bytes 262144 | tf_op jit(solution)/shard_map/all_to_all | solution.py:294
  187.0 11.3 %collective-permute-start.15 = (bf16[128,1024]{1,0:T(8,128)(2,1)S(1)}, bf16[128,1024]{1,0:T(8,128)(2,1)S(1)}, u32[]{:S(2)}, u32[]{:S(2)}) collective-permute-start(bf16[128,1024]{1,0:T(8,128)(2,1)S(1)} %pad_maximum_fusion.2), channel_id=1, source_target_pairs={{8,0},{16,8},{24,16},{32,24},{40,32},{48,40},{56,48},{64,56},{72,6... | collective-permute-start | bytes 786440 | tf_op jit(solution)/shard_map/ppermute | solution.py:26
  190.8 18.0 %all-to-all-start.1 = ((f32[8,64,128]{2,1,0:T(8,128)}), f32[8,64,128]{2,1,0:T(8,128)}, u32[]{:S(2)}, u32[]{:S(2)}) async-start(f32[8,64,128]{2,1,0:T(8,128)} %broadcast_in_dim.22), calls=%async_computation.1 | async-start | bytes 524288 | tf_op jit(solution)/shard_map/all_to_all | solution.py:294
  198.3 1.2 copy-start.18
  (2 other events, 1.3 us)
Sparse Core Ops, SparseCore 0:
  22.5 43.9 all-gather.1
  125.7 43.9 reduce-scatter.1

commit v2 on v1

--- a/solution.py
+++ b/solution.py
@@ -13,6 +13,7 @@
 AXES = ("z", "x", "y", "c")
 SIZE = {"x": 4, "y": 4, "c": 2}
 MIB = 1 << 20
+LIGHT = pl.CostEstimate(flops=1 << 20, bytes_accessed=1 << 18, transcendentals=0)
 
 
 def send(value, axis, by):
@@ -24,6 +25,10 @@
     count = lax.axis_size("z") * lax.axis_size("x")
     pairs = [(i, i + by) for i in range(count) if 0 <= i + by < count]
     return lax.ppermute(value, ("z", "x"), pairs)
+
+
+def after(value, *others):
+    return lax.optimization_barrier((value, *others))[0]
 
 
 def product(a, b):
@@ -100,9 +105,7 @@
         ],
         input_output_aliases=aliases,
         compiler_params=pltpu.CompilerParams(vmem_limit_bytes=24 * MIB),
-        cost_estimate=pl.CostEstimate(
-            flops=tokens * width * 2 * taps * groups, bytes_accessed=tokens * width * 7, transcendentals=0
-        ),
+        cost_estimate=LIGHT,
         name="conv_forward",
     )(*args)
 
@@ -112,8 +115,7 @@
     rows = proj_ref.shape[0] // 8
     acc = None
     for dy in range(4):
-        at = pl.ds(dy * rows, rows)
-        lhs = jnp.concatenate([mine_ref[:, at], sib_ref[:, at]], 1)
+        lhs = jnp.concatenate([mine_ref[dy], sib_ref[dy]], 1)
         rhs = jnp.concatenate(
             [
                 proj_ref[pl.ds(pl.multiple_of(place_ref[2 * dy + i] * rows, rows), rows), :]
@@ -130,15 +132,15 @@
 
 def gate_part(place, mine, sib, proj, block, half, dtype, *addends):
     depth, width = proj.shape
-    tokens = mine.shape[0] // 4
+    tokens = mine.shape[1] // 4
     tile = 256
     steps = width // 2 // tile
     spec = pltpu.PrefetchScalarGridSpec(
         num_scalar_prefetch=1,
         grid=(steps,),
         in_specs=[
-            pl.BlockSpec((tokens, depth // 2), lambda i, p: (block, 0)),
-            pl.BlockSpec((tokens, depth // 2), lambda i, p: (block, 0)),
+            pl.BlockSpec((4, tokens, depth // 8), lambda i, p: (0, block, 0)),
+            pl.BlockSpec((4, tokens, depth // 8), lambda i, p: (0, block, 0)),
             pl.BlockSpec((depth, tile), lambda i, p: (0, i + half * steps)),
         ]
         + [pl.BlockSpec((tokens, tile), lambda i, p: (0, i))] * len(addends),
@@ -149,9 +151,7 @@
         grid_spec=spec,
         out_shape=jax.ShapeDtypeStruct((tokens, width // 2), dtype),
         compiler_params=pltpu.CompilerParams(vmem_limit_bytes=24 * MIB),
-        cost_estimate=pl.CostEstimate(
-            flops=tokens * depth * width, bytes_accessed=depth * width + 2 * tokens * depth, transcendentals=0
-        ),
+        cost_estimate=LIGHT,
         name="grad_gate_part",
     )(place, mine, sib, proj, *addends)
 
@@ -177,13 +177,13 @@
 
 
 def proj_part(place, mine, sib, gated):
-    depth = 2 * mine.shape[1]
+    rows = mine.shape[2]
+    depth = 8 * rows
     tokens, half = gated[0].shape
-    rows = depth // 8
     spec = pltpu.PrefetchScalarGridSpec(
         num_scalar_prefetch=1,
         grid=(4,),
-        in_specs=[pl.BlockSpec((4 * tokens, rows), lambda i, p: (0, i))] * 2
+        in_specs=[pl.BlockSpec((None, 4 * tokens, rows), lambda i, p: (i, 0, 0))] * 2
         + [pl.BlockSpec((tokens, half), lambda i, p: (0, 0))] * 8,
         out_specs=pl.BlockSpec((2 * rows, 2 * half), lambda i, p: (p[2 * i] // 2, 0)),
     )
@@ -192,22 +192,42 @@
         grid_spec=spec,
         out_shape=jax.ShapeDtypeStruct((depth, 2 * half), BF16),
         compiler_params=pltpu.CompilerParams(vmem_limit_bytes=40 * MIB),
-        cost_estimate=pl.CostEstimate(
-            flops=16 * tokens * depth * half, bytes_accessed=20 * tokens * half, transcendentals=0
-        ),
+        cost_estimate=LIGHT,
         name="grad_proj_part",
     )(place, mine, sib, *gated)
 
 
-def inner_body(taps, groups, *refs):
+def inner_body(*refs):
     own, from_left, from_right = refs[0:2], refs[2:4], refs[4:6]
-    q_ref, conv_ref, mixed_ref, rim_ref, query_ref, inner_ref, filter_ref = refs[6:]
+    q_ref, conv_ref, query_ref, inner_ref = refs[6:]
     second = pl.program_id(0) >= pl.num_programs(0) // 2
     pick = lambda pair: jnp.where(second, pair[1][...], pair[0][...]).astype(F32)
     gate = pick(own) + pick(from_left) + pick(from_right)
     query_ref[...] = (gate * conv_ref[...]).astype(BF16)
-    inner = (gate * q_ref[...].astype(F32)).astype(BF16)
-    inner_ref[...] = inner
+    inner_ref[...] = (gate * q_ref[...].astype(F32)).astype(BF16)
+
+
+def gate_gradients(own, from_left, from_right, q, conv):
+    tokens, width = q.shape
+    wide = 2 * LANES
+    steps = width // wide
+    column = pl.BlockSpec((tokens, wide), lambda i: (0, i))
+    first = pl.BlockSpec((tokens, wide), lambda i: (0, jnp.minimum(i, steps // 2 - 1)))
+    last = pl.BlockSpec((tokens, wide), lambda i: (0, jnp.maximum(i - steps // 2, 0)))
+    return pl.pallas_call(
+        inner_body,
+        grid=(steps,),
+        in_specs=[first, last] * 3 + [column, column],
+        out_specs=[column, column],
+        out_shape=[jax.ShapeDtypeStruct((tokens, width), BF16)] * 2,
+        compiler_params=pltpu.CompilerParams(vmem_limit_bytes=32 * MIB),
+        cost_estimate=LIGHT,
+        name="gate_gradients",
+    )(*own, *from_left, *from_right, q, conv)
+
+
+def filter_body(taps, groups, inner_ref, mixed_ref, rim_ref, filter_ref):
+    inner = inner_ref[...]
     window = jnp.concatenate([rim_ref[...], mixed_ref[...]], 0)
     blocks = inner.shape[0] // taps
     left = jnp.concatenate([inner[b * taps : (b + 1) * taps] for b in range(blocks)], 1)
@@ -229,31 +249,21 @@
     filter_ref[...] = jnp.concatenate(sums, 0)
 
 
-def gate_gradients(own, from_left, from_right, q, conv, mixed, rim, group_count):
-    tokens, width = q.shape
+def filter_part(inner, mixed, rim, group_count):
+    tokens, width = inner.shape
     taps = rim.shape[0]
     groups = LANES * group_count // width
-    steps = width // LANES
     column = pl.BlockSpec((tokens, LANES), lambda i: (0, i))
-    first = pl.BlockSpec((tokens, LANES), lambda i: (0, jnp.minimum(i, steps // 2 - 1)))
-    last = pl.BlockSpec((tokens, LANES), lambda i: (0, jnp.maximum(i - steps // 2, 0)))
-    return pl.pallas_call(
-        functools.partial(inner_body, taps, groups),
-        grid=(steps,),
-        in_specs=[first, last] * 3
-        + [column, column, column, pl.BlockSpec((taps, LANES), lambda i: (0, i))],
-        out_specs=[column, column, pl.BlockSpec((groups, taps), lambda i: (i, 0))],
-        out_shape=[
-            jax.ShapeDtypeStruct((tokens, width), BF16),
-            jax.ShapeDtypeStruct((tokens, width), BF16),
-            jax.ShapeDtypeStruct((group_count, taps), F32),
-        ],
+    return pl.pallas_call(
+        functools.partial(filter_body, taps, groups),
+        grid=(width // LANES,),
+        in_specs=[column, column, pl.BlockSpec((taps, LANES), lambda i: (0, i))],
+        out_specs=pl.BlockSpec((groups, taps), lambda i: (i, 0)),
+        out_shape=jax.ShapeDtypeStruct((group_count, taps), F32),
         compiler_params=pltpu.CompilerParams(vmem_limit_bytes=32 * MIB),
-        cost_estimate=pl.CostEstimate(
-            flops=tokens * width * 4 * taps * groups, bytes_accessed=tokens * width * 20, transcendentals=0
-        ),
-        name="gate_gradients",
-    )(*own, *from_left, *from_right, q, conv, mixed, rim)
+        cost_estimate=LIGHT,
+        name="filter_part",
+    )(inner, mixed, rim)
 
 
 def backward_body(taps, groups, rows_ref, inner_ref, ahead_ref, k_ref, v_ref, gk_ref, gv_ref):
@@ -281,9 +291,7 @@
         out_specs=[column, column],
         out_shape=[jax.ShapeDtypeStruct((tokens, width), BF16)] * 2,
         compiler_params=pltpu.CompilerParams(vmem_limit_bytes=24 * MIB),
-        cost_estimate=pl.CostEstimate(
-            flops=tokens * width * 4 * taps * groups, bytes_accessed=tokens * width * 10, transcendentals=0
-        ),
+        cost_estimate=LIGHT,
         name="conv_backward",
     )(rows, inner, ahead, k, v)
 
@@ -311,11 +319,7 @@
     column = jnp.concatenate(pieces, 0)
     below, above = send(column, "y", 1), send(column, "y", -1)
     middle = column.shape[0] // 2
-    far = jnp.concatenate([send(below[:middle], "y", 1), send(above[middle:], "y", -1)], 0)
-    mine = jnp.concatenate([column, above, far, below], 1)
-    sib = send(mine, "c", 1)
-    place = jnp.stack([2 * ((y + dy) % 4) + (c if i == 0 else 1 - c) for dy in range(4) for i in range(2)])
-    place = place.astype(jnp.int32)
+    far = send(below[:middle], "y", 1), send(above[middle:], "y", -1)
 
     taps32 = filters.astype(F32)
     rows = jnp.concatenate(
@@ -328,14 +332,22 @@
     right_a, left_b = send(gated_a, "x", -1), send(gated_b, "x", 1)
     far_a, far_b = send(left_a, "x", 1), send(right_b, "x", -1)
     gated = [gated_a, gated_b, right_a, right_b, far_a, far_b, left_a, left_b]
+
+    far = after(far[0], left_a, right_b), far[1]
+    mine = jnp.concatenate([column, above, *far, below], 0).reshape(4, 4 * tokens, part)
+    sib = send(after(mine, right_a, left_b), "c", 1)
+    place = jnp.stack([2 * ((y + dy) % 4) + (c if i == 0 else 1 - c) for dy in range(4) for i in range(2)])
+    place = place.astype(jnp.int32)
+
+    share = lambda d, h, dtype, *addends: gate_part(place, mine, sib, proj, d, h, dtype, *addends)
+    far_a, far_b = send(share(2, 0, BF16), "x", 1), send(share(2, 1, BF16), "x", -1)
+    proj = after(proj, *gated[4:6])
+    early = share(1, 1, BF16), share(3, 0, BF16)
+    from_left_b, from_right_a = send(early[0], "x", 1), send(early[1], "x", -1)
+    gated[0] = after(gated[0], far_a, far_b, *early)
     proj_sums = proj_part(place, mine, sib, gated)
     grad_proj = lax.psum_scatter(proj_sums, "z", scatter_dimension=0, tiled=True).astype(F32)
 
-    share = lambda d, h, dtype, *addends: gate_part(place, mine, sib, proj, d, h, dtype, *addends)
-    far_a = send(share(2, 0, BF16), "x", 1)
-    far_b = send(share(2, 1, BF16), "x", -1)
-    from_left_b = send(share(1, 1, BF16), "x", 1)
-    from_right_a = send(share(3, 0, BF16), "x", -1)
     from_left_a = send(share(1, 0, BF16, far_a), "x", 1)
     from_right_b = send(share(3, 1, BF16, far_b), "x", -1)
     own = share(0, 0, F32), share(0, 1, F32)
@@ -348,12 +360,15 @@
         ).astype(BF16)
         for h in range(2)
     ]
-    ahead = send_along_tokens(jnp.concatenate(first, 1), -1)
-    grad_query, inner, sums = gate_gradients(
-        own, from_left, from_right, query_in, conv, mixed, rim, group_count
-    )
-    grad_filter = sum_over(sum_over(jnp.flip(sums, 1), "x"), "z")
+    first = jnp.concatenate(first, 1)
+    ahead = send_along_tokens(first, -1)
+    grad_query, inner = gate_gradients(
+        (after(own[0], first), own[1]), from_left, from_right, query_in, conv
+    )
+    sums = filter_part(after(inner, ahead), mixed, rim, group_count)
+    sums = sum_over(sums, "x")
     grad_key, grad_value = backward(back_rows, inner, ahead, key_in, value_in)
+    grad_filter = jnp.flip(sum_over(sums, "z"), 1)
     return grad_query, grad_key, grad_value, grad_filter, grad_proj
 
 

time: 222 us -> 187 us (0.84)
  waiting for transfers between devices: 71.1 us -> 38.9 us
  starting transfers between devices: 54.5 us -> 42.2 us
  local copies, waits for them, and re-layouts: 14.7 us -> 24.8 us
  blocking collectives: 0 us -> 8.22 us
  other arithmetic: 13 us -> 6.64 us
  Pallas kernels: 51.2 us -> 48.6 us
    ppermute x20, waiting for transfers between devices: 58.4 us -> 26.7 us  [send(): lax.ppermute(value, axis, [(i, (i + by) % count) for i in range(count)])]
    unnamed x48 -> x76, local copies, waits for them, and re-layouts: 11.8 us -> 20.5 us
    all_to_all x2 -> x1, starting transfers between devices: 14.4 us -> 6.07 us  [sum_over(): lax.all_to_all(copies, axis, split_axis=0, concat_axis=0, tiled=True)]
    all_to_all x0 -> x1, blocking collectives: none -> 8.22 us  [sum_over(): lax.all_to_all(copies, axis, split_axis=0, concat_axis=0, tiled=True)]
    concatenate x2 -> x1, other arithmetic: 6.32 us -> 0.02 us  [on_device(): first = jnp.concatenate(first, 1)]
    ppermute x2, starting transfers between devices: 10.6 us -> 6.06 us  [send_along_tokens(): return lax.ppermute(value, ('z', 'x'), pairs)]
    all_to_all x2 -> x1, waiting for transfers between devices: 3.73 us -> 0.01 us  [sum_over(): lax.all_to_all(copies, axis, split_axis=0, concat_axis=0, tiled=True)]
    ppermute x2, waiting for transfers between devices: 8.94 us -> 12.2 us  [send_along_tokens(): return lax.ppermute(value, ('z', 'x'), pairs)]
  transfers between devices with their start and end apart: 26 -> 25, of which waited for: 15 -> 8; matrix products, arithmetic and copies ran while one was open for 6% -> 6% of each run, Pallas kernels for 23% -> 23%
where the time goes in v2:
time: 187 us; the launch traced here: 184 us
  Pallas kernels  48.6 us (26%)
  starting transfers between devices  42.2 us (23%)
  waiting for transfers between devices  38.9 us (21%)
  local copies, waits for them, and re-layouts  24.8 us (13%)
  between operations  14.6 us (8%)
  blocking collectives  8.22 us (4%)
  other arithmetic  6.64 us (4%)
    ppermute x20, starting transfers between devices, send(): lax.ppermute(value, axis, [(i, (i + by) % count) for i in range(count)])  30 us
    ppermute x20, waiting for transfers between devices, send(): lax.ppermute(value, axis, [(i, (i + by) % count) for i in range(count)])  26.7 us
    pallas_call x8, Pallas kernels, gate_part(): pl.pallas_call(gate_body, grid_spec=spec, out_shape=jax.ShapeDtypeStruct(...  21.6 us
    unnamed x76, local copies, waits for them, and re-layouts  20.5 us
    ppermute x2, waiting for transfers between devices, send_along_tokens(): return lax.ppermute(value, ('z', 'x'), pairs)  12.2 us
    all_to_all x1, blocking collectives, sum_over(): lax.all_to_all(copies, axis, split_axis=0, concat_axis=0, tiled=True)  8.22 us
    pallas_call x1, Pallas kernels, proj_part(): pl.pallas_call(proj_body, grid_spec=spec, out_shape=jax.ShapeDtypeStruct(...  7.07 us
    all_to_all x1, starting transfers between devices, sum_over(): lax.all_to_all(copies, axis, split_axis=0, concat_axis=0, tiled=True)  6.07 us
  transfers between devices with their start and end apart: 25, of which 8 were waited for; matrix products, arithmetic and copies ran while one was open for 6% of the time, Pallas kernels for 23%

profile of v2, /device:TPU:6, one launch (start us, length us, event | category | flops | bytes accessed | tf_op | source)
XLA Modules:
  0.0 184.0 jit_solution(5763216031289515528)
XLA Ops:
  7.3 1.9 %constant_dynamic-slice_fusion = (bf16[512,128]{1,0:T(8,128)(2,1)}, bf16[512,128]{1,0:T(8,128)(2,1)}, bf16[8192,128]{1,0:T(8,128)(2,1)S(1)}, bf16[512,128]{1,0:T(8,128)(2,1)S(1)}, bf16[512,128]{1,0:T(8,128)(2,1)}) fusion(bf16[512,512]{1,0:T(8,128)(2,1)} %param.11, s32[]{:T(128)S(6)} %select_n.66, s32[]{:T(128)S(6)} %select_n.62, s32[]{:T(128)S(6)} %select_n.60, ...), kind=kLoop, calls=%fused_computation.20 | loop fusion | bytes 1179664 | tf_op jit(solution)/shard_map/dynamic_slice | solution.py:315
  10.1 2.8 %collective-permute-start.1 = (bf16[512,128]{1,0:T(8,128)(2,1)}, bf16[512,128]{1,0:T(8,128)(2,1)}, u32[]{:S(2)}, u32[]{:S(2)}) collective-permute-start(bf16[512,128]{1,0:T(8,128)(2,1)} %get-tuple-element.45), channel_id=1, source_target_pairs={{0,16},{8,24},{16,0},{24,8},{1,17},{9,25},{17,1},{25,9},{2,18},{10... | collective-permute-start | bytes 393224 | tf_op jit(solution)/shard_map/ppermute | solution.py:21
  13.3 1.8 multiply_convert_fusion
  15.1 4.1 %collective-permute-start.6 = (bf16[128,1024]{1,0:T(8,128)(2,1)}, bf16[128,1024]{1,0:T(8,128)(2,1)S(1)}, u32[]{:S(2)}, u32[]{:S(2)}) collective-permute-start(bf16[128,1024]{1,0:T(8,128)(2,1)} %multiply_convert_fusion), channel_id=1, source_target_pairs={{0,8},{8,16},{16,24},{24,32},{32,40},{40,48},{48,56},{56,64},{64,7... | collective-permute-start | bytes 786440 | tf_op jit(solution)/shard_map/ppermute | solution.py:27
  21.2 1.7 collective-permute-start.4
  23.7 1.7 collective-permute-start.3
  25.4 1.2 copy-done.3
  26.6 1.2 copy-done.5
  27.9 2.9 %conv_forward.2 = (f32[512,1024]{1,0:T(8,128)S(1)}, bf16[512,1024]{1,0:T(8,128)(2,1)S(1)}, bf16[512,512]{1,0:T(8,128)(2,1)S(1)}) custom-call(f32[64,256]{1,0:T(8,128)S(1)} %maximum_maximum_fusion.rows_ref, bf16[512,1024]{1,0:T(8,128)(2,1)S(1)} %copy-done.3, bf16[512,1024]{1,0:T(8,128)(2,1)S(1)} %copy-done.5, bf16[512,1024]{1,0:T(8,128)(2,1)S(1)} %copy-done.2, ...), custom_call_target="tpu_custom_call" | custom-call | flops 1048576 | bytes 262144 | tf_op jit(solution)/shard_map/conv_forward/pallas_call | solution.py:96
  30.8 2.9 %conv_forward.3 = (f32[512,1024]{1,0:T(8,128)S(1)}, bf16[512,1024]{1,0:T(8,128)(2,1)S(1)}, bf16[512,512]{1,0:T(8,128)(2,1)S(1)}) custom-call(f32[64,256]{1,0:T(8,128)S(1)} %maximum_maximum_fusion.rows_ref, bf16[512,1024]{1,0:T(8,128)(2,1)S(1)} %copy-done.3, bf16[512,1024]{1,0:T(8,128)(2,1)S(1)} %copy-done.5, ...), custom_call_target="tpu_custom_call", output_to_operand_aliasing={{0}: (5, {}), {1}: (6, {})} | custom-call | flops 1048576 | bytes 262144 | tf_op jit(solution)/shard_map/conv_forward/pallas_call | solution.py:96
  34.6 2.4 %collective-permute-start.7 = (bf16[512,512]{1,0:T(8,128)(2,1)S(1)}, bf16[512,512]{1,0:T(8,128)(2,1)S(1)}, u32[]{:S(2)}, u32[]{:S(2)}) collective-permute-start(bf16[512,512]{1,0:T(8,128)(2,1)S(1)} %get-tuple-element.36.refs_0_), channel_id=1, source_target_pairs={{0,8},{8,16},{16,24},{24,0},{1,9},{9,17},{17,25},{25,1},{2,10},{10... | collective-permute-start | bytes 1572872 | tf_op jit(solution)/shard_map/ppermute | solution.py:21
  41.1 2.0 %collective-permute-start.10 = (bf16[512,512]{1,0:T(8,128)(2,1)S(1)}, bf16[512,512]{1,0:T(8,128)(2,1)S(1)}, u32[]{:S(2)}, u32[]{:S(2)}) collective-permute-start(bf16[512,512]{1,0:T(8,128)(2,1)S(1)} %get-tuple-element.36.refs_0_), channel_id=1, source_target_pairs={{0,24},{8,0},{16,8},{24,16},{1,25},{9,1},{17,9},{25,17},{2,26},{10... | collective-permute-start | bytes 1572872 | tf_op jit(solution)/shard_map/ppermute | solution.py:21
  43.1 6.7 %collective-permute-done.8.refs_3_ = bf16[512,512]{1,0:T(8,128)(2,1)S(1)} collective-permute-done((bf16[512,512]{1,0:T(8,128)(2,1)S(1)}, bf16[512,512]{1,0:T(8,128)(2,1)S(1)}, u32[]{:S(2)}, u32[]{:S(2)}) %collective-permute-start.8) | collective-permute-done | bytes 524320 | tf_op jit(solution)/shard_map/ppermute | solution.py:21
  49.9 2.5 %collective-permute-start.9 = (bf16[1024,128]{1,0:T(8,128)(2,1)S(1)}, bf16[1024,128]{1,0:T(8,128)(2,1)S(1)}, u32[]{:S(2)}, u32[]{:S(2)}) collective-permute-start(bf16[1024,128]{1,0:T(8,128)(2,1)S(1)} %slice.49), channel_id=1, source_target_pairs={{0,6},{2,0},{4,2},{6,4},{1,7},{3,1},{5,3},{7,5},{8,14},{10,8},{12,... | collective-permute-start | bytes 786440 | tf_op jit(solution)/shard_map/ppermute | solution.py:21
  52.5 3.7 %collective-permute-done.9 = bf16[1024,128]{1,0:T(8,128)(2,1)S(1)} collective-permute-done((bf16[1024,128]{1,0:T(8,128)(2,1)S(1)}, bf16[1024,128]{1,0:T(8,128)(2,1)S(1)}, u32[]{:S(2)}, u32[]{:S(2)}) %collective-permute-start.9) | collective-permute-done | bytes 262176 | tf_op jit(solution)/shard_map/ppermute | solution.py:21
  56.4 1.4 collective-permute-done.11.refs_7_
  59.5 1.8 collective-permute-start.14
  61.2 2.2 %collective-permute-start.13 = (bf16[512,512]{1,0:T(8,128)(2,1)}, bf16[512,512]{1,0:T(8,128)(2,1)}, u32[]{:S(2)}, u32[]{:S(2)}) collective-permute-start(bf16[512,512]{1,0:T(8,128)(2,1)} %copy-done.26), channel_id=1, source_target_pairs={{0,8},{8,16},{16,24},{24,0},{1,9},{9,17},{17,25},{25,1},{2,10},{10... | collective-permute-start | bytes 1572872 | tf_op jit(solution)/shard_map/ppermute | solution.py:21
  63.7 1.6 copy-done
  65.3 2.7 %grad_gate_part.14 = bf16[512,512]{1,0:T(8,128)(2,1)S(1)} custom-call(s32[8]{0:T(128)S(1)} %stack.35.place_ref, bf16[4,2048,128]{2,1,0:T(8,128)(2,1)S(1)} %bitcast.11, bf16[4,2048,128]{2,1,0:T(8,128)(2,1)} %collective-permute-done.12.sib_ref, bf16[1024,1024]{1,0:T(8,128)(2,1)S(1)} %copy-done), custom_call_target="tpu_custom_call" | custom-call | flops 1048576 | bytes 262144 | tf_op jit(solution)/shard_map/grad_gate_part/pallas_call | solution.py:149
  68.0 1.9 %collective-permute-start.19 = (bf16[512,512]{1,0:T(8,128)(2,1)S(1)}, bf16[512,512]{1,0:T(8,128)(2,1)S(1)}, u32[]{:S(2)}, u32[]{:S(2)}) collective-permute-start(bf16[512,512]{1,0:T(8,128)(2,1)S(1)} %grad_gate_part.14), channel_id=1, source_target_pairs={{0,24},{8,0},{16,8},{24,16},{1,25},{9,1},{17,9},{25,17},{2,26},{10... | collective-permute-start | bytes 1572872 | tf_op jit(solution)/shard_map/ppermute | solution.py:21
  69.9 2.6 %grad_gate_part.9 = bf16[512,512]{1,0:T(8,128)(2,1)S(1)} custom-call(s32[8]{0:T(128)S(1)} %stack.35.place_ref, bf16[4,2048,128]{2,1,0:T(8,128)(2,1)S(1)} %bitcast.12, bf16[4,2048,128]{2,1,0:T(8,128)(2,1)} %collective-permute-done.12.sib_ref, bf16[1024,1024]{1,0:T(8,128)(2,1)S(1)} %copy-done), custom_call_target="tpu_custom_call" | custom-call | flops 1048576 | bytes 262144 | tf_op jit(solution)/shard_map/grad_gate_part/pallas_call | solution.py:149
  72.5 2.0 %collective-permute-start.15 = (bf16[512,512]{1,0:T(8,128)(2,1)S(1)}, bf16[512,512]{1,0:T(8,128)(2,1)S(1)}, u32[]{:S(2)}, u32[]{:S(2)}) collective-permute-start(bf16[512,512]{1,0:T(8,128)(2,1)S(1)} %grad_gate_part.9), channel_id=1, source_target_pairs={{0,8},{8,16},{16,24},{24,0},{1,9},{9,17},{17,25},{25,1},{2,10},{10... | collective-permute-start | bytes 1572872 | tf_op jit(solution)/shard_map/ppermute | solution.py:21
  74.5 1.7 collective-permute-done.14.refs_5_
  76.2 2.7 %grad_gate_part.13 = bf16[512,512]{1,0:T(8,128)(2,1)S(1)} custom-call(s32[8]{0:T(128)S(1)} %stack.35.place_ref, bf16[4,2048,128]{2,1,0:T(8,128)(2,1)S(1)} %bitcast.13, bf16[4,2048,128]{2,1,0:T(8,128)(2,1)} %collective-permute-done.12.sib_ref, bf16[1024,1024]{1,0:T(8,128)(2,1)S(1)} %copy-done), custom_call_target="tpu_custom_call" | custom-call | flops 1048576 | bytes 262144 | tf_op jit(solution)/shard_map/grad_gate_part/pallas_call | solution.py:149
  79.7 2.9 %grad_gate_part.11 = bf16[512,512]{1,0:T(8,128)(2,1)S(1)} custom-call(s32[8]{0:T(128)S(1)} %stack.35.place_ref, bf16[4,2048,128]{2,1,0:T(8,128)(2,1)S(1)} %bitcast.14, bf16[4,2048,128]{2,1,0:T(8,128)(2,1)} %collective-permute-done.12.sib_ref, bf16[1024,1024]{1,0:T(8,128)(2,1)S(1)} %copy-done), custom_call_target="tpu_custom_call" | custom-call | flops 1048576 | bytes 262144 | tf_op jit(solution)/shard_map/grad_gate_part/pallas_call | solution.py:149
  83.4 3.8 %collective-permute-done.19.refs_0_ = bf16[512,512]{1,0:T(8,128)(2,1)S(1)} collective-permute-done((bf16[512,512]{1,0:T(8,128)(2,1)S(1)}, bf16[512,512]{1,0:T(8,128)(2,1)S(1)}, u32[]{:S(2)}, u32[]{:S(2)}) %collective-permute-start.19) | collective-permute-done | bytes 524320 | tf_op jit(solution)/shard_map/ppermute | solution.py:21
  88.8 7.1 %grad_proj_part.1 = bf16[1024,1024]{1,0:T(8,128)(2,1)S(1)} custom-call(s32[8]{0:T(128)S(1)} %stack.35.place_ref, bf16[4,2048,128]{2,1,0:T(8,128)(2,1)S(1)} %bitcast.15, bf16[4,2048,128]{2,1,0:T(8,128)(2,1)} %collective-permute-done.12.sib_ref, bf16[512,512]{1,0:T(8,128)(2,1)S(1)} %copy-done.21, bf16[512,512]{1,0:T(8,128)(2,1)S(1)} %copy-done.23, ...), custom_call_target="tpu_custom_call" | custom-call | flops 1048576 | bytes 262144 | tf_op jit(solution)/shard_map/grad_proj_part/pallas_call | solution.py:190
  95.9 1.4 copy-done.9
  97.3 2.3 %collective-permute-start.18 = (bf16[512,512]{1,0:T(8,128)(2,1)}, bf16[512,512]{1,0:T(8,128)(2,1)S(1)}, u32[]{:S(2)}, u32[]{:S(2)}) collective-permute-start(bf16[512,512]{1,0:T(8,128)(2,1)} %copy-done.15), channel_id=1, source_target_pairs={{0,8},{8,16},{16,24},{24,0},{1,9},{9,17},{17,25},{25,1},{2,10},{10... | collective-permute-start | bytes 1572872 | tf_op jit(solution)/shard_map/ppermute | solution.py:21
  99.6 1.6 copy-done.1
  102.2 2.7 %grad_gate_part.15 = bf16[512,512]{1,0:T(8,128)(2,1)S(1)} custom-call(s32[8]{0:T(128)S(1)} %stack.35.place_ref, bf16[4,2048,128]{2,1,0:T(8,128)(2,1)S(1)} %bitcast.16, bf16[4,2048,128]{2,1,0:T(8,128)(2,1)} %collective-permute-done.12.sib_ref, bf16[1024,1024]{1,0:T(8,128)(2,1)S(1)} %copy-done.1, bf16[512,512]{1,0:T(8,128)(2,1)S(1)} %copy-done.19), custom_call_target="tpu_custom_call" | custom-call | flops 1048576 | bytes 262144 | tf_op jit(solution)/shard_map/grad_gate_part/pallas_call | solution.py:149
  105.3 2.7 %grad_gate_part.10 = bf16[512,512]{1,0:T(8,128)(2,1)S(1)} custom-call(s32[8]{0:T(128)S(1)} %stack.35.place_ref, bf16[4,2048,128]{2,1,0:T(8,128)(2,1)S(1)} %bitcast.17, bf16[4,2048,128]{2,1,0:T(8,128)(2,1)} %collective-permute-done.12.sib_ref, bf16[1024,1024]{1,0:T(8,128)(2,1)S(1)} %copy-done.1, bf16[512,512]{1,0:T(8,128)(2,1)S(1)} %copy-done.17), custom_call_target="tpu_custom_call" | custom-call | flops 1048576 | bytes 262144 | tf_op jit(solution)/shard_map/grad_gate_part/pallas_call | solution.py:149
  108.0 3.0 %collective-permute-start.16 = (bf16[512,512]{1,0:T(8,128)(2,1)S(1)}, bf16[512,512]{1,0:T(8,128)(2,1)S(1)}, u32[]{:S(2)}, u32[]{:S(2)}) collective-permute-start(bf16[512,512]{1,0:T(8,128)(2,1)S(1)} %grad_gate_part.10), channel_id=1, source_target_pairs={{0,8},{8,16},{16,24},{24,0},{1,9},{9,17},{17,25},{25,1},{2,10},{10... | collective-permute-start | bytes 1572872 | tf_op jit(solution)/shard_map/ppermute | solution.py:21
  111.0 2.7 %grad_gate_part.12.refs_1_ = f32[512,512]{1,0:T(8,128)S(1)} custom-call(s32[8]{0:T(128)S(1)} %stack.35.place_ref, bf16[4,2048,128]{2,1,0:T(8,128)(2,1)S(1)} %bitcast.18, bf16[4,2048,128]{2,1,0:T(8,128)(2,1)} %collective-permute-done.12.sib_ref, bf16[1024,1024]{1,0:T(8,128)(2,1)S(1)} %copy-done.1), custom_call_target="tpu_custom_call" | custom-call | flops 1048576 | bytes 262144 | tf_op jit(solution)/shard_map/grad_gate_part/pallas_call | solution.py:149
  113.7 2.7 %grad_gate_part.8.refs_0_ = f32[512,512]{1,0:T(8,128)S(1)} custom-call(s32[8]{0:T(128)S(1)} %stack.35.place_ref, bf16[4,2048,128]{2,1,0:T(8,128)(2,1)S(1)} %bitcast.19, bf16[4,2048,128]{2,1,0:T(8,128)(2,1)} %collective-permute-done.12.sib_ref, bf16[1024,1024]{1,0:T(8,128)(2,1)S(1)} %copy-done.1), custom_call_target="tpu_custom_call" | custom-call | flops 1048576 | bytes 262144 | tf_op jit(solution)/shard_map/grad_gate_part/pallas_call | solution.py:149
  116.4 9.1 %collective-permute-done.20.refs_5_ = bf16[512,512]{1,0:T(8,128)(2,1)S(1)} collective-permute-done((bf16[512,512]{1,0:T(8,128)(2,1)S(1)}, bf16[512,512]{1,0:T(8,128)(2,1)S(1)}, u32[]{:S(2)}, u32[]{:S(2)}) %collective-permute-start.20) | collective-permute-done | bytes 524320 | tf_op jit(solution)/shard_map/ppermute | solution.py:21
  125.7 1.9 %collective-permute-start.21 = (bf16[128,1024]{1,0:T(8,128)(2,1)S(1)}, bf16[128,1024]{1,0:T(8,128)(2,1)S(1)}, u32[]{:S(2)}, u32[]{:S(2)}) collective-permute-start(bf16[128,1024]{1,0:T(8,128)(2,1)S(1)} %pad_maximum_fusion.1), channel_id=1, source_target_pairs={{8,0},{16,8},{24,16},{32,24},{40,32},{48,40},{56,48},{64,56},{72,6... | collective-permute-start | bytes 786440 | tf_op jit(solution)/shard_map/ppermute | solution.py:27
  127.6 2.5 %gate_gradients.1 = (bf16[512,1024]{1,0:T(8,128)(2,1)}, bf16[512,1024]{1,0:T(8,128)(2,1)S(1)}) custom-call(f32[512,512]{1,0:T(8,128)S(1)} %grad_gate_part.8.refs_0_, f32[512,512]{1,0:T(8,128)S(1)} %grad_gate_part.12.refs_1_, bf16[512,512]{1,0:T(8,128)(2,1)S(1)} %collective-permute-done.16.refs_2_, bf16[512,512]{1,0:T(8,128)(2,1)S(1)} %collective-permute-done.18.refs_3_, ...), custom_call_target="tpu_custom_call" | custom-call | flops 1048576 | bytes 262144 | tf_op jit(solution)/shard_map/gate_gradients/pallas_call | solution.py:217
  130.1 12.2 %collective-permute-done.21.ahead_ref = bf16[128,1024]{1,0:T(8,128)(2,1)S(1)} collective-permute-done((bf16[128,1024]{1,0:T(8,128)(2,1)S(1)}, bf16[128,1024]{1,0:T(8,128)(2,1)S(1)}, u32[]{:S(2)}, u32[]{:S(2)}) %collective-permute-start.21) | collective-permute-done | bytes 262176 | tf_op jit(solution)/shard_map/ppermute | solution.py:27
  142.3 5.7 %filter_part.1 = f32[64,128]{1,0:T(8,128)S(1)} custom-call(bf16[512,1024]{1,0:T(8,128)(2,1)S(1)} %get-tuple-element.34.inner_ref, bf16[512,1024]{1,0:T(8,128)(2,1)S(1)} %copy-done.11, bf16[128,1024]{1,0:T(8,128)(2,1)S(1)} %collective-permute-done.6.rim_ref), custom_call_target="tpu_custom_call" | custom-call | flops 1048576 | bytes 262144 | tf_op jit(solution)/shard_map/filter_part/pallas_call | solution.py:257
  148.1 8.2 %all_to_all.10 = f32[4,64,128]{2,1,0:T(8,128)S(1)} all-to-all(f32[4,64,128]{2,1,0:T(8,128)S(1)} %broadcast_in_dim.10), channel_id=1, replica_groups=mesh['z'=8,'x'=4,'y'=4,'c'=2] {'x'}, dimensions={0} | all-to-all | bytes 262144 | tf_op jit(solution)/shard_map/all_to_all | solution.py:302
  157.0 6.1 %all-to-all-start.1 = ((f32[8,64,128]{2,1,0:T(8,128)}), f32[8,64,128]{2,1,0:T(8,128)}, u32[]{:S(2)}, u32[]{:S(2)}) async-start(f32[8,64,128]{2,1,0:T(8,128)} %broadcast_in_dim.22), calls=%async_computation.1 | async-start | bytes 524288 | tf_op jit(solution)/shard_map/all_to_all | solution.py:302
  163.1 1.2 copy-done.4
  164.3 1.2 copy-done.6
  165.6 1.2 copy-done.13
  167.7 6.0 %conv_backward.1 = (bf16[512,1024]{1,0:T(8,128)(2,1)}, bf16[512,1024]{1,0:T(8,128)(2,1)}) custom-call(f32[64,256]{1,0:T(8,128)S(1)} %concatenate.20.rows_ref, bf16[512,1024]{1,0:T(8,128)(2,1)S(1)} %copy-done.13, bf16[128,1024]{1,0:T(8,128)(2,1)S(1)} %copy-done.33, bf16[512,1024]{1,0:T(8,128)(2,1)S(1)} %copy-done.4, bf16[512,1024]{1,0:T(8,128)(2,1)S(1)} %copy-done.6), custom_call_target="tpu_custom_call" | custom-call | flops 1048576 | bytes 262144 | tf_op jit(solution)/shard_map/conv_backward/pallas_call | solution.py:281
  175.4 1.8 convert_element_type.51
  (116 shorter events, 19.5 us)
Async XLA Ops:
  7.2 12.1 %copy-start.34 = (bf16[64,128]{1,0:T(8,128)(2,1)S(1)}, bf16[64,128]{1,0:T(8,128)(2,1)}, u32[]{:S(2)}) copy-start(bf16[64,128]{1,0:T(8,128)(2,1)} %param.9) | copy-start | bytes 49156
  7.2 18.2 %copy-start.2 = (bf16[512,1024]{1,0:T(8,128)(2,1)S(1)}, bf16[512,1024]{1,0:T(8,128)(2,1)}, u32[]{:S(2)}) copy-start(bf16[512,1024]{1,0:T(8,128)(2,1)} %refs_6_.1) | copy-start | bytes 3145732
  7.2 56.6 %all-gather.2.cloned.1.call-start = ((), (), s32[]{:S(2)}) async-start(), calls=%async_computation.3 | async-start | bytes 2359296 | tf_op jit(solution)/shard_map/all_gather | solution.py:312
  9.2 10.8 %collective-permute-start = (bf16[512,128]{1,0:T(8,128)(2,1)}, bf16[512,128]{1,0:T(8,128)(2,1)}, u32[]{:S(2)}, u32[]{:S(2)}) collective-permute-start(bf16[512,128]{1,0:T(8,128)(2,1)} %get-tuple-element.42), channel_id=1, source_target_pairs={{0,24},{8,0},{16,8},{24,16},{1,25},{9,1},{17,9},{25,17},{2,26},{10... | collective-permute-start | bytes 393224 | tf_op jit(solution)/shard_map/ppermute | solution.py:21
  10.1 10.0 %collective-permute-start.1 = (bf16[512,128]{1,0:T(8,128)(2,1)}, bf16[512,128]{1,0:T(8,128)(2,1)}, u32[]{:S(2)}, u32[]{:S(2)}) collective-permute-start(bf16[512,128]{1,0:T(8,128)(2,1)} %get-tuple-element.45), channel_id=1, source_target_pairs={{0,16},{8,24},{16,0},{24,8},{1,17},{9,25},{17,1},{25,9},{2,18},{10... | collective-permute-start | bytes 393224 | tf_op jit(solution)/shard_map/ppermute | solution.py:21
  12.9 7.2 %collective-permute-start.2 = (bf16[512,128]{1,0:T(8,128)(2,1)}, bf16[512,128]{1,0:T(8,128)(2,1)}, u32[]{:S(2)}, u32[]{:S(2)}) collective-permute-start(bf16[512,128]{1,0:T(8,128)(2,1)} %get-tuple-element.41), channel_id=1, source_target_pairs={{0,8},{8,16},{16,24},{24,0},{1,9},{9,17},{17,25},{25,1},{2,10},{10... | collective-permute-start | bytes 393224 | tf_op jit(solution)/shard_map/ppermute | solution.py:21
  15.1 10.3 %collective-permute-start.6 = (bf16[128,1024]{1,0:T(8,128)(2,1)}, bf16[128,1024]{1,0:T(8,128)(2,1)S(1)}, u32[]{:S(2)}, u32[]{:S(2)}) collective-permute-start(bf16[128,1024]{1,0:T(8,128)(2,1)} %multiply_convert_fusion), channel_id=1, source_target_pairs={{0,8},{8,16},{16,24},{24,32},{32,40},{40,48},{48,56},{56,64},{64,7... | collective-permute-start | bytes 786440 | tf_op jit(solution)/shard_map/ppermute | solution.py:27
  19.2 156.1 %reduce-scatter.2.cloned.1.call-start = ((), (), s32[]{:S(2)}) async-start(), calls=%async_computation.4 | async-start | bytes 2359296 | tf_op jit(solution)/shard_map/reduce_scatter | solution.py:349
  21.2 17.7 %collective-permute-start.4 = (bf16[2048,128]{1,0:T(8,128)(2,1)S(1)}, bf16[2048,128]{1,0:T(8,128)(2,1)S(1)}, u32[]{:S(2)}, u32[]{:S(2)}) collective-permute-start(bf16[2048,128]{1,0:T(8,128)(2,1)S(1)} %pad_maximum_fusion), channel_id=1, source_target_pairs={{0,2},{2,4},{4,6},{6,0},{1,3},{3,5},{5,7},{7,1},{8,10},{10,12},{12... | collective-permute-start | bytes 1572872 | tf_op jit(solution)/shard_map/ppermute | solution.py:21
  23.7 17.5 %collective-permute-start.3 = (bf16[2048,128]{1,0:T(8,128)(2,1)S(1)}, bf16[2048,128]{1,0:T(8,128)(2,1)S(1)}, u32[]{:S(2)}, u32[]{:S(2)}) collective-permute-start(bf16[2048,128]{1,0:T(8,128)(2,1)S(1)} %pad_maximum_fusion), channel_id=1, source_target_pairs={{0,6},{2,0},{4,2},{6,4},{1,7},{3,1},{5,3},{7,5},{8,14},{10,8},{12,... | collective-permute-start | bytes 1572872 | tf_op jit(solution)/shard_map/ppermute | solution.py:21
  30.7 10.4 %copy-start.20 = (bf16[512,512]{1,0:T(8,128)(2,1)}, bf16[512,512]{1,0:T(8,128)(2,1)S(1)}, u32[]{:S(2)}) copy-start(bf16[512,512]{1,0:T(8,128)(2,1)S(1)} %get-tuple-element.36.refs_0_) | copy-start | bytes 1572868
  33.7 22.7 %copy-start.7 = (f32[512,1024]{1,0:T(8,128)}, f32[512,1024]{1,0:T(8,128)S(1)}, u32[]{:S(2)}) copy-start(f32[512,1024]{1,0:T(8,128)S(1)} %get-tuple-element.29.refs_7_) | copy-start | bytes 6291460
  33.7 22.7 %copy-start.10 = (bf16[512,1024]{1,0:T(8,128)(2,1)}, bf16[512,1024]{1,0:T(8,128)(2,1)S(1)}, u32[]{:S(2)}) copy-start(bf16[512,1024]{1,0:T(8,128)(2,1)S(1)} %get-tuple-element.35.mixed_ref) | copy-start | bytes 3145732
  33.7 22.7 %copy-start.22 = (bf16[512,512]{1,0:T(8,128)(2,1)}, bf16[512,512]{1,0:T(8,128)(2,1)S(1)}, u32[]{:S(2)}) copy-start(bf16[512,512]{1,0:T(8,128)(2,1)S(1)} %get-tuple-element.24.refs_1_) | copy-start | bytes 1572868
  33.7 16.1 %collective-permute-start.8 = (bf16[512,512]{1,0:T(8,128)(2,1)S(1)}, bf16[512,512]{1,0:T(8,128)(2,1)S(1)}, u32[]{:S(2)}, u32[]{:S(2)}) collective-permute-start(bf16[512,512]{1,0:T(8,128)(2,1)S(1)} %get-tuple-element.24.refs_1_), channel_id=1, source_target_pairs={{0,24},{8,0},{16,8},{24,16},{1,25},{9,1},{17,9},{25,17},{2,26},{10... | collective-permute-start | bytes 1572872 | tf_op jit(solution)/shard_map/ppermute | solution.py:21
  34.6 17.8 %collective-permute-start.7 = (bf16[512,512]{1,0:T(8,128)(2,1)S(1)}, bf16[512,512]{1,0:T(8,128)(2,1)S(1)}, u32[]{:S(2)}, u32[]{:S(2)}) collective-permute-start(bf16[512,512]{1,0:T(8,128)(2,1)S(1)} %get-tuple-element.36.refs_0_), channel_id=1, source_target_pairs={{0,8},{8,16},{16,24},{24,0},{1,9},{9,17},{17,25},{25,1},{2,10},{10... | collective-permute-start | bytes 1572872 | tf_op jit(solution)/shard_map/ppermute | solution.py:21
  38.9 13.5 %collective-permute-start.5 = (bf16[1024,128]{1,0:T(8,128)(2,1)S(1)}, bf16[1024,128]{1,0:T(8,128)(2,1)S(1)}, u32[]{:S(2)}, u32[]{:S(2)}) collective-permute-start(bf16[1024,128]{1,0:T(8,128)(2,1)S(1)} %slice.48), channel_id=1, source_target_pairs={{0,2},{2,4},{4,6},{6,0},{1,3},{3,5},{5,7},{7,1},{8,10},{10,12},{12... | collective-permute-start | bytes 786440 | tf_op jit(solution)/shard_map/ppermute | solution.py:21
  41.0 16.8 %collective-permute-start.11 = (bf16[512,512]{1,0:T(8,128)(2,1)S(1)}, bf16[512,512]{1,0:T(8,128)(2,1)S(1)}, u32[]{:S(2)}, u32[]{:S(2)}) collective-permute-start(bf16[512,512]{1,0:T(8,128)(2,1)S(1)} %get-tuple-element.24.refs_1_), channel_id=1, source_target_pairs={{0,8},{8,16},{16,24},{24,0},{1,9},{9,17},{17,25},{25,1},{2,10},{10... | collective-permute-start | bytes 1572872 | tf_op jit(solution)/shard_map/ppermute | solution.py:21
  41.1 17.4 %collective-permute-start.10 = (bf16[512,512]{1,0:T(8,128)(2,1)S(1)}, bf16[512,512]{1,0:T(8,128)(2,1)S(1)}, u32[]{:S(2)}, u32[]{:S(2)}) collective-permute-start(bf16[512,512]{1,0:T(8,128)(2,1)S(1)} %get-tuple-element.36.refs_0_), channel_id=1, source_target_pairs={{0,24},{8,0},{16,8},{24,16},{1,25},{9,1},{17,9},{25,17},{2,26},{10... | collective-permute-start | bytes 1572872 | tf_op jit(solution)/shard_map/ppermute | solution.py:21
  49.9 8.7 %copy-start.24 = (bf16[512,512]{1,0:T(8,128)(2,1)}, bf16[512,512]{1,0:T(8,128)(2,1)S(1)}, u32[]{:S(2)}) copy-start(bf16[512,512]{1,0:T(8,128)(2,1)S(1)} %collective-permute-done.8.refs_3_) | copy-start | bytes 1572868
  49.9 6.4 %collective-permute-start.9 = (bf16[1024,128]{1,0:T(8,128)(2,1)S(1)}, bf16[1024,128]{1,0:T(8,128)(2,1)S(1)}, u32[]{:S(2)}, u32[]{:S(2)}) collective-permute-start(bf16[1024,128]{1,0:T(8,128)(2,1)S(1)} %slice.49), channel_id=1, source_target_pairs={{0,6},{2,0},{4,2},{6,4},{1,7},{3,1},{5,3},{7,5},{8,14},{10,8},{12,... | collective-permute-start | bytes 786440 | tf_op jit(solution)/shard_map/ppermute | solution.py:21
  52.5 7.0 %copy-start.26 = (bf16[512,512]{1,0:T(8,128)(2,1)}, bf16[512,512]{1,0:T(8,128)(2,1)S(1)}, u32[]{:S(2)}) copy-start(bf16[512,512]{1,0:T(8,128)(2,1)S(1)} %collective-permute-done.7.refs_6_) | copy-start | bytes 1572868
  59.5 4.3 %collective-permute-start.12 = (bf16[4,2048,128]{2,1,0:T(8,128)(2,1)S(1)}, bf16[4,2048,128]{2,1,0:T(8,128)(2,1)}, u32[]{:S(2)}, u32[]{:S(2)}) collective-permute-start(bf16[4,2048,128]{2,1,0:T(8,128)(2,1)S(1)} %bitcast.10), channel_id=1, source_target_pairs={{0,1},{1,0},{2,3},{3,2},{4,5},{5,4},{6,7},{7,6},{8,9},{9,8},{10,11... | collective-permute-start | bytes 6291464 | tf_op jit(solution)/shard_map/ppermute | solution.py:21
  59.5 16.8 %collective-permute-start.14 = (bf16[512,512]{1,0:T(8,128)(2,1)}, bf16[512,512]{1,0:T(8,128)(2,1)}, u32[]{:S(2)}, u32[]{:S(2)}) collective-permute-start(bf16[512,512]{1,0:T(8,128)(2,1)} %copy-done.24), channel_id=1, source_target_pairs={{0,24},{8,0},{16,8},{24,16},{1,25},{9,1},{17,9},{25,17},{2,26},{10... | collective-permute-start | bytes 1572872 | tf_op jit(solution)/shard_map/ppermute | solution.py:21
  61.2 15.0 %collective-permute-start.13 = (bf16[512,512]{1,0:T(8,128)(2,1)}, bf16[512,512]{1,0:T(8,128)(2,1)}, u32[]{:S(2)}, u32[]{:S(2)}) collective-permute-start(bf16[512,512]{1,0:T(8,128)(2,1)} %copy-done.26), channel_id=1, source_target_pairs={{0,8},{8,16},{16,24},{24,0},{1,9},{9,17},{17,25},{25,1},{2,10},{10... | collective-permute-start | bytes 1572872 | tf_op jit(solution)/shard_map/ppermute | solution.py:21
  63.7 1.6 copy-start
  68.0 19.2 %collective-permute-start.19 = (bf16[512,512]{1,0:T(8,128)(2,1)S(1)}, bf16[512,512]{1,0:T(8,128)(2,1)S(1)}, u32[]{:S(2)}, u32[]{:S(2)}) collective-permute-start(bf16[512,512]{1,0:T(8,128)(2,1)S(1)} %grad_gate_part.14), channel_id=1, source_target_pairs={{0,24},{8,0},{16,8},{24,16},{1,25},{9,1},{17,9},{25,17},{2,26},{10... | collective-permute-start | bytes 1572872 | tf_op jit(solution)/shard_map/ppermute | solution.py:21
  72.5 15.5 %collective-permute-start.15 = (bf16[512,512]{1,0:T(8,128)(2,1)S(1)}, bf16[512,512]{1,0:T(8,128)(2,1)S(1)}, u32[]{:S(2)}, u32[]{:S(2)}) collective-permute-start(bf16[512,512]{1,0:T(8,128)(2,1)S(1)} %grad_gate_part.9), channel_id=1, source_target_pairs={{0,8},{8,16},{16,24},{24,0},{1,9},{9,17},{17,25},{25,1},{2,10},{10... | collective-permute-start | bytes 1572872 | tf_op jit(solution)/shard_map/ppermute | solution.py:21
  79.7 9.1 %copy-start.21 = (bf16[512,512]{1,0:T(8,128)(2,1)S(1)}, bf16[512,512]{1,0:T(8,128)(2,1)}, u32[]{:S(2)}) copy-start(bf16[512,512]{1,0:T(8,128)(2,1)} %copy-done.20) | copy-start | bytes 1572868
  79.7 9.1 %copy-start.23 = (bf16[512,512]{1,0:T(8,128)(2,1)S(1)}, bf16[512,512]{1,0:T(8,128)(2,1)}, u32[]{:S(2)}) copy-start(bf16[512,512]{1,0:T(8,128)(2,1)} %copy-done.22) | copy-start | bytes 1572868
  79.7 9.1 %copy-start.25 = (bf16[512,512]{1,0:T(8,128)(2,1)S(1)}, bf16[512,512]{1,0:T(8,128)(2,1)}, u32[]{:S(2)}) copy-start(bf16[512,512]{1,0:T(8,128)(2,1)} %copy-done.24) | copy-start | bytes 1572868
  79.7 9.1 %copy-start.27 = (bf16[512,512]{1,0:T(8,128)(2,1)S(1)}, bf16[512,512]{1,0:T(8,128)(2,1)}, u32[]{:S(2)}) copy-start(bf16[512,512]{1,0:T(8,128)(2,1)} %copy-done.26) | copy-start | bytes 1572868
  79.7 9.1 %copy-start.29 = (bf16[512,512]{1,0:T(8,128)(2,1)S(1)}, bf16[512,512]{1,0:T(8,128)(2,1)}, u32[]{:S(2)}) copy-start(bf16[512,512]{1,0:T(8,128)(2,1)} %copy-done.28) | copy-start | bytes 1572868
  79.7 9.1 %copy-start.31 = (bf16[512,512]{1,0:T(8,128)(2,1)S(1)}, bf16[512,512]{1,0:T(8,128)(2,1)}, u32[]{:S(2)}) copy-start(bf16[512,512]{1,0:T(8,128)(2,1)} %copy-done.30) | copy-start | bytes 1572868
  95.9 1.4 copy-start.9
  97.3 19.1 %collective-permute-start.18 = (bf16[512,512]{1,0:T(8,128)(2,1)}, bf16[512,512]{1,0:T(8,128)(2,1)S(1)}, u32[]{:S(2)}, u32[]{:S(2)}) collective-permute-start(bf16[512,512]{1,0:T(8,128)(2,1)} %copy-done.15), channel_id=1, source_target_pairs={{0,8},{8,16},{16,24},{24,0},{1,9},{9,17},{17,25},{25,1},{2,10},{10... | collective-permute-start | bytes 1572872 | tf_op jit(solution)/shard_map/ppermute | solution.py:21
  99.6 16.9 %collective-permute-start.17 = (bf16[512,512]{1,0:T(8,128)(2,1)}, bf16[512,512]{1,0:T(8,128)(2,1)S(1)}, u32[]{:S(2)}, u32[]{:S(2)}) collective-permute-start(bf16[512,512]{1,0:T(8,128)(2,1)} %copy-done.14), channel_id=1, source_target_pairs={{0,24},{8,0},{16,8},{24,16},{1,25},{9,1},{17,9},{25,17},{2,26},{10... | collective-permute-start | bytes 1572872 | tf_op jit(solution)/shard_map/ppermute | solution.py:21
  99.6 1.6 copy-start.1
  102.2 3.1 %copy-start.17 = (bf16[512,512]{1,0:T(8,128)(2,1)S(1)}, bf16[512,512]{1,0:T(8,128)(2,1)}, u32[]{:S(2)}) copy-start(bf16[512,512]{1,0:T(8,128)(2,1)} %copy-done.16) | copy-start | bytes 1572868
  104.9 20.6 %collective-permute-start.20 = (bf16[512,512]{1,0:T(8,128)(2,1)S(1)}, bf16[512,512]{1,0:T(8,128)(2,1)S(1)}, u32[]{:S(2)}, u32[]{:S(2)}) collective-permute-start(bf16[512,512]{1,0:T(8,128)(2,1)S(1)} %grad_gate_part.15), channel_id=1, source_target_pairs={{0,24},{8,0},{16,8},{24,16},{1,25},{9,1},{17,9},{25,17},{2,26},{10... | collective-permute-start | bytes 1572872 | tf_op jit(solution)/shard_map/ppermute | solution.py:21
  108.0 17.5 %collective-permute-start.16 = (bf16[512,512]{1,0:T(8,128)(2,1)S(1)}, bf16[512,512]{1,0:T(8,128)(2,1)S(1)}, u32[]{:S(2)}, u32[]{:S(2)}) collective-permute-start(bf16[512,512]{1,0:T(8,128)(2,1)S(1)} %grad_gate_part.10), channel_id=1, source_target_pairs={{0,8},{8,16},{16,24},{24,0},{1,9},{9,17},{17,25},{25,1},{2,10},{10... | collective-permute-start | bytes 1572872 | tf_op jit(solution)/shard_map/ppermute | solution.py:21
  116.4 11.2 %copy-start.8 = (f32[512,1024]{1,0:T(8,128)S(1)}, f32[512,1024]{1,0:T(8,128)}, u32[]{:S(2)}) copy-start(f32[512,1024]{1,0:T(8,128)} %copy-done.7) | copy-start | bytes 6291460
  125.7 16.6 %collective-permute-start.21 = (bf16[128,1024]{1,0:T(8,128)(2,1)S(1)}, bf16[128,1024]{1,0:T(8,128)(2,1)S(1)}, u32[]{:S(2)}, u32[]{:S(2)}) collective-permute-start(bf16[128,1024]{1,0:T(8,128)(2,1)S(1)} %pad_maximum_fusion.1), channel_id=1, source_target_pairs={{8,0},{16,8},{24,16},{32,24},{40,32},{48,40},{56,48},{64,56},{72,6... | collective-permute-start | bytes 786440 | tf_op jit(solution)/shard_map/ppermute | solution.py:27
  127.6 14.7 %copy-start.11 = (bf16[512,1024]{1,0:T(8,128)(2,1)S(1)}, bf16[512,1024]{1,0:T(8,128)(2,1)}, u32[]{:S(2)}) copy-start(bf16[512,1024]{1,0:T(8,128)(2,1)} %copy-done.10) | copy-start | bytes 3145732
  130.1 17.9 %copy-start.12 = (bf16[512,1024]{1,0:T(8,128)(2,1)}, bf16[512,1024]{1,0:T(8,128)(2,1)S(1)}, u32[]{:S(2)}) copy-start(bf16[512,1024]{1,0:T(8,128)(2,1)S(1)} %get-tuple-element.34.inner_ref) | copy-start | bytes 3145732
  142.3 5.7 %copy-start.32 = (bf16[128,1024]{1,0:T(8,128)(2,1)}, bf16[128,1024]{1,0:T(8,128)(2,1)S(1)}, u32[]{:S(2)}) copy-start(bf16[128,1024]{1,0:T(8,128)(2,1)S(1)} %collective-permute-done.21.ahead_ref) | copy-start | bytes 786436
  157.0 16.7 %all-to-all-start.1 = ((f32[8,64,128]{2,1,0:T(8,128)}), f32[8,64,128]{2,1,0:T(8,128)}, u32[]{:S(2)}, u32[]{:S(2)}) async-start(f32[8,64,128]{2,1,0:T(8,128)} %broadcast_in_dim.22), calls=%async_computation.1 | async-start | bytes 524288 | tf_op jit(solution)/shard_map/all_to_all | solution.py:302
  163.1 1.2 copy-start.4
  (12 other events, 11.7 us)
Sparse Core Ops, SparseCore 0:
  19.4 42.9 all-gather.1
  97.4 44.8 reduce-scatter.1

commit v3 on v2

--- a/solution.py
+++ b/solution.py
@@ -35,10 +35,19 @@
     return (a.astype(F32) * b.astype(F32)).astype(BF16)
 
 
-def group_tables(rows, width):
+def anti_identity(size):
+    at = sum(lax.broadcasted_iota(jnp.int32, (size, size), i) for i in range(2))
+    return (at == size - 1).astype(F32).astype(BF16)
+
+
+def group_tables(filters, reverse):
+    taps = filters.shape[1]
+    if reverse:
+        filters = jnp.dot(filters, anti_identity(taps), preferred_element_type=F32)
+    rows = jnp.concatenate([filters.astype(F32), jnp.zeros(filters.shape, F32)], 1)
     tables = [
         pltpu.roll(
-            jnp.broadcast_to(rows[g : g + 1], (width // 2, width)), 0, 1, stride=1, stride_axis=0
+            jnp.broadcast_to(rows[g : g + 1], (taps, 2 * taps)), int(reverse), 1, stride=1, stride_axis=0
         )
         for g in range(rows.shape[0])
     ]
@@ -63,31 +72,31 @@
     return jnp.concatenate(out, 0)
 
 
-def forward_body(taps, groups, rows_ref, k_ref, v_ref, q_ref, rim_ref, *refs):
+def forward_body(taps, groups, filters_ref, k_ref, v_ref, q_ref, rim_ref, *refs):
     conv_ref, mixed_ref, gated_ref = refs[-3:]
     mixed = product(k_ref[...], v_ref[...])
     window = jnp.concatenate([rim_ref[...], mixed], 0)
-    conv = banded(group_tables(rows_ref[...], 2 * taps), window, taps, groups)
+    conv = banded(group_tables(filters_ref[...], True), window, taps, groups)
     conv_ref[...] = conv
     mixed_ref[...] = mixed
     gated_ref[...] = (q_ref[...].astype(F32) * conv).astype(BF16)
 
 
-def forward(half, rows, k, v, q, rim, earlier):
+def forward(half, filters, k, v, q, rim, earlier):
     tokens, width = k.shape
     taps = rim.shape[0]
-    groups = LANES * rows.shape[0] // width
+    groups = LANES * filters.shape[0] // width
     steps = width // LANES // 2
     at = lambda i: (0, i + half * steps)
     column = pl.BlockSpec((tokens, LANES), at)
     in_specs = [
-        pl.BlockSpec((groups, 2 * taps), lambda i: (i + half * steps, 0)),
+        pl.BlockSpec((groups, taps), lambda i: (i + half * steps, 0)),
         column,
         column,
         column,
         pl.BlockSpec((taps, LANES), at),
     ]
-    args = [rows, k, v, q, rim]
+    args = [filters, k, v, q, rim]
     aliases = {}
     if earlier is not None:
         in_specs += [pl.BlockSpec(memory_space=pl.ANY)] * 2
@@ -104,14 +113,14 @@
             jax.ShapeDtypeStruct((tokens, width // 2), BF16),
         ],
         input_output_aliases=aliases,
-        compiler_params=pltpu.CompilerParams(vmem_limit_bytes=24 * MIB),
+        compiler_params=pltpu.CompilerParams(vmem_limit_bytes=16 * MIB),
         cost_estimate=LIGHT,
         name="conv_forward",
     )(*args)
 
 
 def gate_body(place_ref, mine_ref, sib_ref, proj_ref, *refs):
-    out_ref = refs[-1]
+    added, outs = refs[:-2], refs[-2:]
     rows = proj_ref.shape[0] // 8
     acc = None
     for dy in range(4):
@@ -125,35 +134,51 @@
         )
         term = jnp.dot(lhs, rhs, preferred_element_type=F32)
         acc = term if acc is None else acc + term
-    for ref in refs[:-1]:
-        acc = acc + ref[...].astype(F32)
-    out_ref[...] = acc.astype(out_ref.dtype)
-
-
-def gate_part(place, mine, sib, proj, block, half, dtype, *addends):
+    second = pl.program_id(0) >= pl.num_programs(0) // 2
+    if added:
+        acc = acc + jnp.where(second, added[1][...], added[0][...]).astype(F32)
+    acc = acc.astype(outs[0].dtype)
+
+    @pl.when(jnp.logical_not(second))
+    def _():
+        outs[0][...] = acc
+
+    @pl.when(second)
+    def _():
+        outs[1][...] = acc
+
+
+def gate_parts(place, mine, sib, proj, wanted, dtype, *added):
     depth, width = proj.shape
     tokens = mine.shape[1] // 4
     tile = 256
     steps = width // 2 // tile
+    (block0, half0), (block1, half1) = wanted
+    choose = lambda i, first, second: jnp.where(i < steps, first, second)
+    cot = pl.BlockSpec((4, tokens, depth // 8), lambda i, p: (0, choose(i, block0, block1), 0))
+    pair = [
+        pl.BlockSpec((tokens, tile), lambda i, p: (0, jnp.minimum(i, steps - 1))),
+        pl.BlockSpec((tokens, tile), lambda i, p: (0, jnp.maximum(i - steps, 0))),
+    ]
     spec = pltpu.PrefetchScalarGridSpec(
         num_scalar_prefetch=1,
-        grid=(steps,),
+        grid=(2 * steps,),
         in_specs=[
-            pl.BlockSpec((4, tokens, depth // 8), lambda i, p: (0, block, 0)),
-            pl.BlockSpec((4, tokens, depth // 8), lambda i, p: (0, block, 0)),
-            pl.BlockSpec((depth, tile), lambda i, p: (0, i + half * steps)),
+            cot,
+            cot,
+            pl.BlockSpec((depth, tile), lambda i, p: (0, i % steps + choose(i, half0, half1) * steps)),
         ]
-        + [pl.BlockSpec((tokens, tile), lambda i, p: (0, i))] * len(addends),
-        out_specs=pl.BlockSpec((tokens, tile), lambda i, p: (0, i)),
+        + pair[: len(added)],
+        out_specs=pair,
     )
     return pl.pallas_call(
         gate_body,
         grid_spec=spec,
-        out_shape=jax.ShapeDtypeStruct((tokens, width // 2), dtype),
-        compiler_params=pltpu.CompilerParams(vmem_limit_bytes=24 * MIB),
-        cost_estimate=LIGHT,
-        name="grad_gate_part",
-    )(place, mine, sib, proj, *addends)
+        out_shape=[jax.ShapeDtypeStruct((tokens, width // 2), dtype)] * 2,
+        compiler_params=pltpu.CompilerParams(vmem_limit_bytes=16 * MIB),
+        cost_estimate=LIGHT,
+        name="grad_gate_parts",
+    )(place, mine, sib, proj, *added)
 
 
 def proj_body(place_ref, mine_ref, sib_ref, *refs):
@@ -191,7 +216,7 @@
         proj_body,
         grid_spec=spec,
         out_shape=jax.ShapeDtypeStruct((depth, 2 * half), BF16),
-        compiler_params=pltpu.CompilerParams(vmem_limit_bytes=40 * MIB),
+        compiler_params=pltpu.CompilerParams(vmem_limit_bytes=24 * MIB),
         cost_estimate=LIGHT,
         name="grad_proj_part",
     )(place, mine, sib, *gated)
@@ -220,7 +245,7 @@
         in_specs=[first, last] * 3 + [column, column],
         out_specs=[column, column],
         out_shape=[jax.ShapeDtypeStruct((tokens, width), BF16)] * 2,
-        compiler_params=pltpu.CompilerParams(vmem_limit_bytes=32 * MIB),
+        compiler_params=pltpu.CompilerParams(vmem_limit_bytes=16 * MIB),
         cost_estimate=LIGHT,
         name="gate_gradients",
     )(*own, *from_left, *from_right, q, conv)
@@ -231,8 +256,7 @@
     window = jnp.concatenate([rim_ref[...], mixed_ref[...]], 0)
     blocks = inner.shape[0] // taps
     left = jnp.concatenate([inner[b * taps : (b + 1) * taps] for b in range(blocks)], 1)
-    turn = sum(lax.broadcasted_iota(jnp.int32, (taps, taps), i) for i in range(2)) == taps - 1
-    left = jnp.dot(turn.astype(F32).astype(BF16), left, preferred_element_type=F32).astype(BF16)
+    left = jnp.dot(anti_identity(taps), left, preferred_element_type=F32).astype(BF16)
     right = jnp.concatenate([window[b * taps : (b + 2) * taps] for b in range(blocks)], 1)
     lane_group = (lax.broadcasted_iota(jnp.int32, left.shape, 1) % LANES) // (LANES // groups)
     zero = jnp.zeros_like(left)
@@ -260,29 +284,29 @@
         in_specs=[column, column, pl.BlockSpec((taps, LANES), lambda i: (0, i))],
         out_specs=pl.BlockSpec((groups, taps), lambda i: (i, 0)),
         out_shape=jax.ShapeDtypeStruct((group_count, taps), F32),
-        compiler_params=pltpu.CompilerParams(vmem_limit_bytes=32 * MIB),
+        compiler_params=pltpu.CompilerParams(vmem_limit_bytes=16 * MIB),
         cost_estimate=LIGHT,
         name="filter_part",
     )(inner, mixed, rim)
 
 
-def backward_body(taps, groups, rows_ref, inner_ref, ahead_ref, k_ref, v_ref, gk_ref, gv_ref):
+def backward_body(taps, groups, filters_ref, inner_ref, ahead_ref, k_ref, v_ref, gk_ref, gv_ref):
     window = jnp.concatenate([inner_ref[...], ahead_ref[...]], 0)
-    grad = banded(group_tables(rows_ref[...], 2 * taps), window, taps, groups)
+    grad = banded(group_tables(filters_ref[...], False), window, taps, groups)
     gk_ref[...] = (grad * v_ref[...].astype(F32)).astype(BF16)
     gv_ref[...] = (grad * k_ref[...].astype(F32)).astype(BF16)
 
 
-def backward(rows, inner, ahead, k, v):
+def backward(filters, inner, ahead, k, v):
     tokens, width = k.shape
     taps = ahead.shape[0]
-    groups = LANES * rows.shape[0] // width
+    groups = LANES * filters.shape[0] // width
     column = pl.BlockSpec((tokens, LANES), lambda i: (0, i))
     return pl.pallas_call(
         functools.partial(backward_body, taps, groups),
         grid=(width // LANES,),
         in_specs=[
-            pl.BlockSpec((groups, 2 * taps), lambda i: (i, 0)),
+            pl.BlockSpec((groups, taps), lambda i: (i, 0)),
             column,
             pl.BlockSpec((taps, LANES), lambda i: (0, i)),
             column,
@@ -290,16 +314,22 @@
         ],
         out_specs=[column, column],
         out_shape=[jax.ShapeDtypeStruct((tokens, width), BF16)] * 2,
-        compiler_params=pltpu.CompilerParams(vmem_limit_bytes=24 * MIB),
+        compiler_params=pltpu.CompilerParams(vmem_limit_bytes=16 * MIB),
         cost_estimate=LIGHT,
         name="conv_backward",
-    )(rows, inner, ahead, k, v)
-
-
-def sum_over(value, axis):
-    count = lax.axis_size(axis)
-    copies = jnp.broadcast_to(value[None], (count, *value.shape))
-    return jnp.sum(lax.all_to_all(copies, axis, split_axis=0, concat_axis=0, tiled=True), 0)
+    )(filters, inner, ahead, k, v)
+
+
+def sum_over(value, axis, *beside):
+    count, me = lax.axis_size(axis), lax.axis_index(axis)
+    terms = [after(value, *beside)] + [send(value, axis, d) for d in range(1, count)]
+    total = None
+    for source in range(count):
+        term = terms[0]
+        for d in range(1, count):
+            term = jnp.where((me - source) % count == d, terms[d], term)
+        total = term if total is None else total + term
+    return total
 
 
 def on_device(query_in, key_in, value_in, filters, proj_out, cotangent):
@@ -311,23 +341,20 @@
 
     proj = lax.all_gather(proj_out, "z", axis=0, tiled=True)
 
-    rim = send_along_tokens(product(key_in[tokens - taps :], value_in[tokens - taps :]), 1)
-    own_cols = lambda d: lax.dynamic_slice_in_dim(cotangent, ((x + d) % 4) * part, part, 1)
+    last = product(key_in[tokens - taps :], value_in[tokens - taps :])
+    rim = send_along_tokens(last, 1)
+    base = after(x, last)
+    own_cols = lambda d: lax.dynamic_slice_in_dim(cotangent, ((base + d) % 4) * part, part, 1)
     pieces = [own_cols(0), None, None, None]
     for d in (2, 1, 3):
         pieces[(-d) % 4] = send(own_cols(d), "x", d)
-    column = jnp.concatenate(pieces, 0)
+    column = jnp.concatenate([after(pieces[0], rim), *pieces[1:]], 0)
     below, above = send(column, "y", 1), send(column, "y", -1)
     middle = column.shape[0] // 2
     far = send(below[:middle], "y", 1), send(above[middle:], "y", -1)
 
-    taps32 = filters.astype(F32)
-    rows = jnp.concatenate(
-        [jnp.zeros((group_count, 1), F32), jnp.flip(taps32, 1), jnp.zeros((group_count, taps - 1), F32)], 1
-    )
-    back_rows = jnp.concatenate([taps32, jnp.zeros((group_count, taps), F32)], 1)
-    conv, mixed, gated_a = forward(0, rows, key_in, value_in, query_in, rim, None)
-    conv, mixed, gated_b = forward(1, rows, key_in, value_in, query_in, rim, (conv, mixed))
+    conv, mixed, gated_a = forward(0, filters, key_in, value_in, query_in, rim, None)
+    conv, mixed, gated_b = forward(1, filters, key_in, value_in, query_in, rim, (conv, mixed))
     left_a, right_b = send(gated_a, "x", 1), send(gated_b, "x", -1)
     right_a, left_b = send(gated_a, "x", -1), send(gated_b, "x", 1)
     far_a, far_b = send(left_a, "x", 1), send(right_b, "x", -1)
@@ -339,18 +366,19 @@
     place = jnp.stack([2 * ((y + dy) % 4) + (c if i == 0 else 1 - c) for dy in range(4) for i in range(2)])
     place = place.astype(jnp.int32)
 
-    share = lambda d, h, dtype, *addends: gate_part(place, mine, sib, proj, d, h, dtype, *addends)
-    far_a, far_b = send(share(2, 0, BF16), "x", 1), send(share(2, 1, BF16), "x", -1)
-    proj = after(proj, *gated[4:6])
-    early = share(1, 1, BF16), share(3, 0, BF16)
-    from_left_b, from_right_a = send(early[0], "x", 1), send(early[1], "x", -1)
-    gated[0] = after(gated[0], far_a, far_b, *early)
+    across = gate_parts(place, mine, sib, proj, ((2, 0), (2, 1)), BF16)
+    far_a, far_b = send(across[0], "x", 1), send(across[1], "x", -1)
+    proj = after(proj, *across, *gated[4:6])
+    beside = gate_parts(place, mine, sib, proj, ((1, 1), (3, 0)), BF16)
+    from_left_b, from_right_a = send(beside[0], "x", 1), send(beside[1], "x", -1)
+    gated[0] = after(gated[0], *beside)
     proj_sums = proj_part(place, mine, sib, gated)
+    proj_sums = after(proj_sums, far_a, far_b)
     grad_proj = lax.psum_scatter(proj_sums, "z", scatter_dimension=0, tiled=True).astype(F32)
 
-    from_left_a = send(share(1, 0, BF16, far_a), "x", 1)
-    from_right_b = send(share(3, 1, BF16, far_b), "x", -1)
-    own = share(0, 0, F32), share(0, 1, F32)
+    joined = gate_parts(place, mine, sib, proj, ((1, 0), (3, 1)), BF16, far_a, far_b)
+    from_left_a, from_right_b = send(joined[0], "x", 1), send(joined[1], "x", -1)
+    own = gate_parts(place, mine, sib, proj, ((0, 0), (0, 1)), F32)
     from_left, from_right = (from_left_a, from_left_b), (from_right_a, from_right_b)
 
     first = [
@@ -365,9 +393,9 @@
     grad_query, inner = gate_gradients(
         (after(own[0], first), own[1]), from_left, from_right, query_in, conv
     )
-    sums = filter_part(after(inner, ahead), mixed, rim, group_count)
-    sums = sum_over(sums, "x")
-    grad_key, grad_value = backward(back_rows, inner, ahead, key_in, value_in)
+    sums = filter_part(inner, mixed, rim, group_count)
+    grad_key, grad_value = backward(filters, after(inner, sums), ahead, key_in, value_in)
+    sums = sum_over(sums, "x", grad_key)
     grad_filter = jnp.flip(sum_over(sums, "z"), 1)
     return grad_query, grad_key, grad_value, grad_filter, grad_proj
 

time: 187 us -> 179 us (0.957); the launches traced: 184 us -> 178 us
  starting transfers between devices: 42.2 us -> 58.2 us
  local copies, waits for them, and re-layouts: 24.8 us -> 14.9 us
  blocking collectives: 8.22 us -> 0 us
  other arithmetic: 6.64 us -> 4.06 us
  Pallas kernels: 48.6 us -> 46.7 us
    ppermute x20 -> x30, starting transfers between devices: 30 us -> 51.6 us  [send(): lax.ppermute(value, axis, [(i, (i + by) % count) for i in range(count)])]
    ppermute x20 -> x30, waiting for transfers between devices: 26.7 us -> 39.1 us  [send(): lax.ppermute(value, axis, [(i, (i + by) % count) for i in range(count)])]
    ppermute x2, waiting for transfers between devices: 12.2 us -> 0.53 us  [send_along_tokens(): return lax.ppermute(value, ('z', 'x'), pairs)]
    unnamed x76 -> x60, local copies, waits for them, and re-layouts: 20.5 us -> 11.2 us
    all_to_all x1 -> x0, blocking collectives: 8.22 us -> none  [sum_over(): lax.all_to_all(copies, axis, split_axis=0, concat_axis=0, tiled=True)]
    all_to_all x1 -> x0, starting transfers between devices: 6.07 us -> none  [sum_over(): lax.all_to_all(copies, axis, split_axis=0, concat_axis=0, tiled=True)]
    pallas_call x8 -> x4, Pallas kernels: 21.6 us -> 17.8 us  [gate_parts(): pl.pallas_call(gate_body, grid_spec=spec, out_shape=[jax.ShapeDtypeStruct...]
    concatenate x2 -> x0, other arithmetic: 1.91 us -> none  [the longest x1 1.07 us: on_device(): column = jnp.concatenate(pieces, 0)]
  transfers between devices with their start and end apart: 25 -> 34, of which waited for: 8 -> 15; matrix products, arithmetic and copies ran while one was open for 6% -> 4% of each run, Pallas kernels for 23% -> 26%
where the time goes in v3:
time: 179 us; the launch traced here: 178 us
  starting transfers between devices  58.2 us (33%)
  Pallas kernels  46.7 us (26%)
  waiting for transfers between devices  39.7 us (22%)
  local copies, waits for them, and re-layouts  14.9 us (8%)
  between operations  14.5 us (8%)
  other arithmetic  4.06 us (2%)
    ppermute x30, starting transfers between devices, send(): lax.ppermute(value, axis, [(i, (i + by) % count) for i in range(count)])  51.6 us
    ppermute x30, waiting for transfers between devices, send(): lax.ppermute(value, axis, [(i, (i + by) % count) for i in range(count)])  39.1 us
    pallas_call x4, Pallas kernels, gate_parts(): pl.pallas_call(gate_body, grid_spec=spec, out_shape=[jax.ShapeDtypeStruct...  17.8 us
    unnamed x60, local copies, waits for them, and re-layouts  11.2 us
    pallas_call x1, Pallas kernels, proj_part(): pl.pallas_call(proj_body, grid_spec=spec, out_shape=jax.ShapeDtypeStruct(...  7.09 us
    pallas_call x2, Pallas kernels, forward(): pl.pallas_call(functools.partial(forward_body, taps, groups), grid=(steps...  6.91 us
    pallas_call x1, Pallas kernels, backward(): pl.pallas_call(functools.partial(backward_body, taps, groups), grid=(widt...  6.77 us
    ppermute x2, starting transfers between devices, send_along_tokens(): return lax.ppermute(value, ('z', 'x'), pairs)  6.58 us
  transfers between devices with their start and end apart: 34, of which 15 were waited for; matrix products, arithmetic and copies ran while one was open for 4% of the time, Pallas kernels for 26%

profile of v3, /device:TPU:6, one launch (start us, length us, event | category | flops | bytes accessed | tf_op | source)
XLA Modules:
  0.0 178.1 jit_solution(10877830933979218924)
XLA Ops:
  7.2 1.2 multiply_convert_fusion
  8.4 3.7 %collective-permute-start = (bf16[128,1024]{1,0:T(8,128)(2,1)S(1)}, bf16[128,1024]{1,0:T(8,128)(2,1)S(1)}, u32[]{:S(2)}, u32[]{:S(2)}) collective-permute-start(bf16[128,1024]{1,0:T(8,128)(2,1)S(1)} %multiply_convert_fusion), channel_id=1, source_target_pairs={{0,8},{8,16},{16,24},{24,32},{32,40},{40,48},{48,56},{56,64},{64,7... | collective-permute-start | bytes 786440 | tf_op jit(solution)/shard_map/ppermute | solution.py:27
  12.2 1.9 %constant_dynamic-slice_fusion = (bf16[512,128]{1,0:T(8,128)(2,1)}, bf16[512,128]{1,0:T(8,128)(2,1)}, bf16[512,128]{1,0:T(8,128)(2,1)S(1)}, bf16[512,128]{1,0:T(8,128)(2,1)}) fusion(bf16[512,512]{1,0:T(8,128)(2,1)} %param.11, s32[]{:T(128)S(6)} %select_n.636, s32[]{:T(128)S(6)} %select_n.632, s32[]{:T(128)S(6)} %select_n.630, s32[]{:T(128)S(6)} %select_n.634), kind=kLoop, calls=%fused_computation.18 | loop fusion | bytes 1048592 | tf_op jit(solution)/shard_map/dynamic_slice | solution.py:347
  14.3 1.4 collective-permute-start.2
  15.7 2.1 %collective-permute-start.3 = (bf16[512,128]{1,0:T(8,128)(2,1)}, bf16[512,128]{1,0:T(8,128)(2,1)}, u32[]{:S(2)}, u32[]{:S(2)}) collective-permute-start(bf16[512,128]{1,0:T(8,128)(2,1)} %get-tuple-element.63), channel_id=1, source_target_pairs={{0,8},{8,16},{16,24},{24,0},{1,9},{9,17},{17,25},{25,1},{2,10},{10... | collective-permute-start | bytes 393224 | tf_op jit(solution)/shard_map/ppermute | solution.py:21
  18.4 5.0 %collective-permute-done.1 = bf16[512,128]{1,0:T(8,128)(2,1)} collective-permute-done((bf16[512,128]{1,0:T(8,128)(2,1)}, bf16[512,128]{1,0:T(8,128)(2,1)}, u32[]{:S(2)}, u32[]{:S(2)}) %collective-permute-start.1) | collective-permute-done | bytes 131104 | tf_op jit(solution)/shard_map/ppermute | solution.py:21
  26.3 1.7 collective-permute-start.5
  27.9 1.7 collective-permute-start.4
  29.6 1.2 copy-done.5
  30.8 3.4 %conv_forward.2 = (f32[512,1024]{1,0:T(8,128)S(1)}, bf16[512,1024]{1,0:T(8,128)(2,1)S(1)}, bf16[512,512]{1,0:T(8,128)(2,1)S(1)}) custom-call(bf16[64,128]{1,0:T(8,128)(2,1)S(1)} %copy-done.24, bf16[512,1024]{1,0:T(8,128)(2,1)S(1)} %copy-done.3, bf16[512,1024]{1,0:T(8,128)(2,1)S(1)} %copy-done.5, bf16[512,1024]{1,0:T(8,128)(2,1)S(1)} %copy-done.2, ...), custom_call_target="tpu_custom_call" | custom-call | flops 1048576 | bytes 262144 | tf_op jit(solution)/shard_map/conv_forward/pallas_call | solution.py:105
  34.3 3.5 %conv_forward.3 = (f32[512,1024]{1,0:T(8,128)S(1)}, bf16[512,1024]{1,0:T(8,128)(2,1)S(1)}, bf16[512,512]{1,0:T(8,128)(2,1)S(1)}) custom-call(bf16[64,128]{1,0:T(8,128)(2,1)S(1)} %copy-done.24, bf16[512,1024]{1,0:T(8,128)(2,1)S(1)} %copy-done.3, bf16[512,1024]{1,0:T(8,128)(2,1)S(1)} %copy-done.5, ...), custom_call_target="tpu_custom_call", output_to_operand_aliasing={{0}: (5, {}), {1}: (6, {})} | custom-call | flops 1048576 | bytes 262144 | tf_op jit(solution)/shard_map/conv_forward/pallas_call | solution.py:105
  37.9 3.2 %collective-permute-start.7 = (bf16[512,512]{1,0:T(8,128)(2,1)S(1)}, bf16[512,512]{1,0:T(8,128)(2,1)S(1)}, u32[]{:S(2)}, u32[]{:S(2)}) collective-permute-start(bf16[512,512]{1,0:T(8,128)(2,1)S(1)} %get-tuple-element.59.refs_0_), channel_id=1, source_target_pairs={{0,8},{8,16},{16,24},{24,0},{1,9},{9,17},{17,25},{25,1},{2,10},{10... | collective-permute-start | bytes 1572872 | tf_op jit(solution)/shard_map/ppermute | solution.py:21
  41.6 1.0 collective-permute-start.11
  42.6 1.0 collective-permute-start.10
  43.6 10.3 %collective-permute-done.8.refs_3_ = bf16[512,512]{1,0:T(8,128)(2,1)S(1)} collective-permute-done((bf16[512,512]{1,0:T(8,128)(2,1)S(1)}, bf16[512,512]{1,0:T(8,128)(2,1)S(1)}, u32[]{:S(2)}, u32[]{:S(2)}) %collective-permute-start.8) | collective-permute-done | bytes 524320 | tf_op jit(solution)/shard_map/ppermute | solution.py:21
  53.9 1.8 %collective-permute-start.9 = (bf16[1024,128]{1,0:T(8,128)(2,1)S(1)}, bf16[1024,128]{1,0:T(8,128)(2,1)S(1)}, u32[]{:S(2)}, u32[]{:S(2)}) collective-permute-start(bf16[1024,128]{1,0:T(8,128)(2,1)S(1)} %slice.49), channel_id=1, source_target_pairs={{0,6},{2,0},{4,2},{6,4},{1,7},{3,1},{5,3},{7,5},{8,14},{10,8},{12,... | collective-permute-start | bytes 786440 | tf_op jit(solution)/shard_map/ppermute | solution.py:21
  55.9 4.4 %collective-permute-done.9 = bf16[1024,128]{1,0:T(8,128)(2,1)S(1)} collective-permute-done((bf16[1024,128]{1,0:T(8,128)(2,1)S(1)}, bf16[1024,128]{1,0:T(8,128)(2,1)S(1)}, u32[]{:S(2)}, u32[]{:S(2)}) %collective-permute-start.9) | collective-permute-done | bytes 262176 | tf_op jit(solution)/shard_map/ppermute | solution.py:21
  60.5 1.8 collective-permute-done.11.refs_7_
  64.3 3.3 %collective-permute-start.13 = (bf16[512,512]{1,0:T(8,128)(2,1)}, bf16[512,512]{1,0:T(8,128)(2,1)}, u32[]{:S(2)}, u32[]{:S(2)}) collective-permute-start(bf16[512,512]{1,0:T(8,128)(2,1)} %copy-done.18), channel_id=1, source_target_pairs={{0,8},{8,16},{16,24},{24,0},{1,9},{9,17},{17,25},{25,1},{2,10},{10... | collective-permute-start | bytes 1572872 | tf_op jit(solution)/shard_map/ppermute | solution.py:21
  68.2 1.6 copy-done
  69.8 4.8 %grad_gate_parts.4 = (bf16[512,512]{1,0:T(8,128)(2,1)}, bf16[512,512]{1,0:T(8,128)(2,1)}) custom-call(s32[8]{0:T(128)S(1)} %stack.35.place_ref, bf16[4,2048,128]{2,1,0:T(8,128)(2,1)S(1)} %bitcast.10, bf16[4,2048,128]{2,1,0:T(8,128)(2,1)} %collective-permute-done.12.sib_ref, bf16[1024,1024]{1,0:T(8,128)(2,1)S(1)} %copy-done), custom_call_target="tpu_custom_call" | custom-call | flops 1048576 | bytes 262144 | tf_op jit(solution)/shard_map/grad_gate_parts/pallas_call | solution.py:174
  74.5 3.7 %collective-permute-start.15 = (bf16[512,512]{1,0:T(8,128)(2,1)}, bf16[512,512]{1,0:T(8,128)(2,1)}, u32[]{:S(2)}, u32[]{:S(2)}) collective-permute-start(bf16[512,512]{1,0:T(8,128)(2,1)} %get-tuple-element.41), channel_id=1, source_target_pairs={{0,8},{8,16},{16,24},{24,0},{1,9},{9,17},{17,25},{25,1},{2,10},{10... | collective-permute-start | bytes 1572872 | tf_op jit(solution)/shard_map/ppermute | solution.py:21
  78.3 2.1 %collective-permute-done.14.refs_5_ = bf16[512,512]{1,0:T(8,128)(2,1)} collective-permute-done((bf16[512,512]{1,0:T(8,128)(2,1)}, bf16[512,512]{1,0:T(8,128)(2,1)}, u32[]{:S(2)}, u32[]{:S(2)}) %collective-permute-start.14) | collective-permute-done | bytes 524320 | tf_op jit(solution)/shard_map/ppermute | solution.py:21
  80.5 4.3 %grad_gate_parts.7 = (bf16[512,512]{1,0:T(8,128)(2,1)S(1)}, bf16[512,512]{1,0:T(8,128)(2,1)S(1)}) custom-call(s32[8]{0:T(128)S(1)} %stack.35.place_ref, bf16[4,2048,128]{2,1,0:T(8,128)(2,1)S(1)} %bitcast.11, bf16[4,2048,128]{2,1,0:T(8,128)(2,1)} %collective-permute-done.12.sib_ref, bf16[1024,1024]{1,0:T(8,128)(2,1)S(1)} %copy-done), custom_call_target="tpu_custom_call" | custom-call | flops 1048576 | bytes 262144 | tf_op jit(solution)/shard_map/grad_gate_parts/pallas_call | solution.py:174
  86.5 7.1 %grad_proj_part.1 = bf16[1024,1024]{1,0:T(8,128)(2,1)S(1)} custom-call(s32[8]{0:T(128)S(1)} %stack.35.place_ref, bf16[4,2048,128]{2,1,0:T(8,128)(2,1)S(1)} %bitcast.12, bf16[4,2048,128]{2,1,0:T(8,128)(2,1)} %collective-permute-done.12.sib_ref, bf16[512,512]{1,0:T(8,128)(2,1)S(1)} %copy-done.13, bf16[512,512]{1,0:T(8,128)(2,1)S(1)} %copy-done.15, ...), custom_call_target="tpu_custom_call" | custom-call | flops 1048576 | bytes 262144 | tf_op jit(solution)/shard_map/grad_proj_part/pallas_call | solution.py:215
  93.6 1.4 copy-done.9
  95.0 1.6 collective-permute-start.18
  96.6 1.9 %collective-permute-start.19 = (bf16[512,512]{1,0:T(8,128)(2,1)}, bf16[512,512]{1,0:T(8,128)(2,1)S(1)}, u32[]{:S(2)}, u32[]{:S(2)}) collective-permute-start(bf16[512,512]{1,0:T(8,128)(2,1)} %copy-done.25), channel_id=1, source_target_pairs={{0,8},{8,16},{16,24},{24,0},{1,9},{9,17},{17,25},{25,1},{2,10},{10... | collective-permute-start | bytes 1572872 | tf_op jit(solution)/shard_map/ppermute | solution.py:21
  98.5 1.6 copy-done.1
  100.1 4.6 %grad_gate_parts.6 = (bf16[512,512]{1,0:T(8,128)(2,1)S(1)}, bf16[512,512]{1,0:T(8,128)(2,1)S(1)}) custom-call(s32[8]{0:T(128)S(1)} %stack.35.place_ref, bf16[4,2048,128]{2,1,0:T(8,128)(2,1)S(1)} %bitcast.13, bf16[4,2048,128]{2,1,0:T(8,128)(2,1)} %collective-permute-done.12.sib_ref, bf16[1024,1024]{1,0:T(8,128)(2,1)S(1)} %copy-done.1, ...), custom_call_target="tpu_custom_call" | custom-call | flops 1048576 | bytes 262144 | tf_op jit(solution)/shard_map/grad_gate_parts/pallas_call | solution.py:174
  104.7 2.0 %collective-permute-start.17 = (bf16[512,512]{1,0:T(8,128)(2,1)S(1)}, bf16[512,512]{1,0:T(8,128)(2,1)S(1)}, u32[]{:S(2)}, u32[]{:S(2)}) collective-permute-start(bf16[512,512]{1,0:T(8,128)(2,1)S(1)} %get-tuple-element.45), channel_id=1, source_target_pairs={{0,8},{8,16},{16,24},{24,0},{1,9},{9,17},{17,25},{25,1},{2,10},{10... | collective-permute-start | bytes 1572872 | tf_op jit(solution)/shard_map/ppermute | solution.py:21
  106.8 4.1 %grad_gate_parts.5 = (f32[512,512]{1,0:T(8,128)S(1)}, f32[512,512]{1,0:T(8,128)S(1)}) custom-call(s32[8]{0:T(128)S(1)} %stack.35.place_ref, bf16[4,2048,128]{2,1,0:T(8,128)(2,1)S(1)} %bitcast.14, bf16[4,2048,128]{2,1,0:T(8,128)(2,1)} %collective-permute-done.12.sib_ref, bf16[1024,1024]{1,0:T(8,128)(2,1)S(1)} %copy-done.1), custom_call_target="tpu_custom_call" | custom-call | flops 1048576 | bytes 262144 | tf_op jit(solution)/shard_map/grad_gate_parts/pallas_call | solution.py:174
  111.7 9.2 %collective-permute-done.17.refs_2_ = bf16[512,512]{1,0:T(8,128)(2,1)S(1)} collective-permute-done((bf16[512,512]{1,0:T(8,128)(2,1)S(1)}, bf16[512,512]{1,0:T(8,128)(2,1)S(1)}, u32[]{:S(2)}, u32[]{:S(2)}) %collective-permute-start.17) | collective-permute-done | bytes 524320 | tf_op jit(solution)/shard_map/ppermute | solution.py:21
  122.3 2.8 %collective-permute-start.21 = (bf16[128,1024]{1,0:T(8,128)(2,1)}, bf16[128,1024]{1,0:T(8,128)(2,1)}, u32[]{:S(2)}, u32[]{:S(2)}) collective-permute-start(bf16[128,1024]{1,0:T(8,128)(2,1)} %pad_maximum_fusion), channel_id=1, source_target_pairs={{8,0},{16,8},{24,16},{32,24},{40,32},{48,40},{56,48},{64,56},{72,6... | collective-permute-start | bytes 786440 | tf_op jit(solution)/shard_map/ppermute | solution.py:27
  125.2 2.5 %gate_gradients.1 = (bf16[512,1024]{1,0:T(8,128)(2,1)}, bf16[512,1024]{1,0:T(8,128)(2,1)S(1)}) custom-call(f32[512,512]{1,0:T(8,128)S(1)} %get-tuple-element.50.refs_0_, f32[512,512]{1,0:T(8,128)S(1)} %get-tuple-element.47.refs_1_, bf16[512,512]{1,0:T(8,128)(2,1)S(1)} %collective-permute-done.17.refs_2_, ...), custom_call_target="tpu_custom_call" | custom-call | flops 1048576 | bytes 262144 | tf_op jit(solution)/shard_map/gate_gradients/pallas_call | solution.py:242
  127.7 5.7 %filter_part.1 = f32[64,128]{1,0:T(8,128)S(1)} custom-call(bf16[512,1024]{1,0:T(8,128)(2,1)S(1)} %get-tuple-element.55.inner_ref, bf16[512,1024]{1,0:T(8,128)(2,1)S(1)} %copy-done.11, bf16[128,1024]{1,0:T(8,128)(2,1)S(1)} %collective-permute-done.rim_ref), custom_call_target="tpu_custom_call" | custom-call | flops 1048576 | bytes 262144 | tf_op jit(solution)/shard_map/filter_part/pallas_call | solution.py:281
  133.4 1.8 %collective-permute-start.22 = (f32[64,128]{1,0:T(8,128)S(1)}, f32[64,128]{1,0:T(8,128)S(1)}, u32[]{:S(2)}, u32[]{:S(2)}) collective-permute-start(f32[64,128]{1,0:T(8,128)S(1)} %filter_part.1), channel_id=1, source_target_pairs={{0,24},{8,0},{16,8},{24,16},{1,25},{9,1},{17,9},{25,17},{2,26},{10... | collective-permute-start | bytes 98312 | tf_op jit(solution)/shard_map/ppermute | solution.py:21
  135.2 1.8 %collective-permute-start.23 = (f32[64,128]{1,0:T(8,128)S(1)}, f32[64,128]{1,0:T(8,128)S(1)}, u32[]{:S(2)}, u32[]{:S(2)}) collective-permute-start(f32[64,128]{1,0:T(8,128)S(1)} %filter_part.1), channel_id=1, source_target_pairs={{0,16},{8,24},{16,0},{24,8},{1,17},{9,25},{17,1},{25,9},{2,18},{10... | collective-permute-start | bytes 98312 | tf_op jit(solution)/shard_map/ppermute | solution.py:21
  137.1 2.5 %collective-permute-start.24 = (f32[64,128]{1,0:T(8,128)S(1)}, f32[64,128]{1,0:T(8,128)S(1)}, u32[]{:S(2)}, u32[]{:S(2)}) collective-permute-start(f32[64,128]{1,0:T(8,128)S(1)} %filter_part.1), channel_id=1, source_target_pairs={{0,8},{8,16},{16,24},{24,0},{1,9},{9,17},{17,25},{25,1},{2,10},{10... | collective-permute-start | bytes 98312 | tf_op jit(solution)/shard_map/ppermute | solution.py:21
  139.6 6.8 %conv_backward.1 = (bf16[512,1024]{1,0:T(8,128)(2,1)}, bf16[512,1024]{1,0:T(8,128)(2,1)}) custom-call(bf16[64,128]{1,0:T(8,128)(2,1)S(1)} %copy-done.24, bf16[512,1024]{1,0:T(8,128)(2,1)S(1)} %get-tuple-element.55.inner_ref, bf16[128,1024]{1,0:T(8,128)(2,1)} %collective-permute-done.21.ahead_ref, bf16[512,1024]{1,0:T(8,128)(2,1)S(1)} %copy-done.4, ...), custom_call_target="tpu_custom_call" | custom-call | flops 1048576 | bytes 262144 | tf_op jit(solution)/shard_map/conv_backward/pallas_call | solution.py:305
  146.4 5.1 %collective-permute-start.25 = (f32[64,128]{1,0:T(8,128)S(1)}, f32[64,128]{1,0:T(8,128)S(1)}, u32[]{:S(2)}, u32[]{:S(2)}) collective-permute-start(f32[64,128]{1,0:T(8,128)S(1)} %select_add_fusion.1), channel_id=1, source_target_pairs={{0,224},{32,0},{64,32},{96,64},{128,96},{160,128},{192,160},{224,1... | collective-permute-start | bytes 98312 | tf_op jit(solution)/shard_map/ppermute | solution.py:21
  151.6 1.4 collective-permute-start.26
  153.0 2.5 %collective-permute-start.27 = (f32[64,128]{1,0:T(8,128)S(1)}, f32[64,128]{1,0:T(8,128)S(1)}, u32[]{:S(2)}, u32[]{:S(2)}) collective-permute-start(f32[64,128]{1,0:T(8,128)S(1)} %select_add_fusion.1), channel_id=1, source_target_pairs={{0,160},{32,192},{64,224},{96,0},{128,32},{160,64},{192,96},{224,1... | collective-permute-start | bytes 98312 | tf_op jit(solution)/shard_map/ppermute | solution.py:21
  155.5 3.0 %collective-permute-start.28 = (f32[64,128]{1,0:T(8,128)S(1)}, f32[64,128]{1,0:T(8,128)S(1)}, u32[]{:S(2)}, u32[]{:S(2)}) collective-permute-start(f32[64,128]{1,0:T(8,128)S(1)} %select_add_fusion.1), channel_id=1, source_target_pairs={{0,128},{32,160},{64,192},{96,224},{128,0},{160,32},{192,64},{224,... | collective-permute-start | bytes 98312 | tf_op jit(solution)/shard_map/ppermute | solution.py:21
  159.3 4.1 %collective-permute-start.30 = (f32[64,128]{1,0:T(8,128)S(1)}, f32[64,128]{1,0:T(8,128)S(1)}, u32[]{:S(2)}, u32[]{:S(2)}) collective-permute-start(f32[64,128]{1,0:T(8,128)S(1)} %select_add_fusion.1), channel_id=1, source_target_pairs={{0,64},{32,96},{64,128},{96,160},{128,192},{160,224},{192,0},{224,... | collective-permute-start | bytes 98312 | tf_op jit(solution)/shard_map/ppermute | solution.py:21
  164.3 1.1 collective-permute-done.29
  166.2 2.3 %collective-permute-done.31 = f32[64,128]{1,0:T(8,128)S(1)} collective-permute-done((f32[64,128]{1,0:T(8,128)S(1)}, f32[64,128]{1,0:T(8,128)S(1)}, u32[]{:S(2)}, u32[]{:S(2)}) %collective-permute-start.31) | collective-permute-done | bytes 32800 | tf_op jit(solution)/shard_map/ppermute | solution.py:21
  169.4 1.8 %convert_element_type.47 = f32[128,1024]{1,0:T(8,128)} convert(bf16[128,1024]{1,0:T(8,128)(2,1)} %reduce-scatter.2.cloned.1.call-done) | non-fusion elementwise | flops 131072 | bytes 786432 | tf_op jit(solution)/shard_map/convert_element_type | solution.py:377
  (105 shorter events, 14.6 us)
Async XLA Ops:
  7.2 22.4 %copy-start.2 = (bf16[512,1024]{1,0:T(8,128)(2,1)S(1)}, bf16[512,1024]{1,0:T(8,128)(2,1)}, u32[]{:S(2)}) copy-start(bf16[512,1024]{1,0:T(8,128)(2,1)} %refs_6_.1) | copy-start | bytes 3145732
  7.2 22.4 %copy-start.24 = (bf16[64,128]{1,0:T(8,128)(2,1)S(1)}, bf16[64,128]{1,0:T(8,128)(2,1)}, u32[]{:S(2)}) copy-start(bf16[64,128]{1,0:T(8,128)(2,1)} %filters_ref.5) | copy-start | bytes 49156
  7.2 61.0 %all-gather.2.cloned.1.call-start = ((), (), s32[]{:S(2)}) async-start(), calls=%async_computation.1 | async-start | bytes 2359296 | tf_op jit(solution)/shard_map/all_gather | solution.py:342
  8.4 10.0 %collective-permute-start = (bf16[128,1024]{1,0:T(8,128)(2,1)S(1)}, bf16[128,1024]{1,0:T(8,128)(2,1)S(1)}, u32[]{:S(2)}, u32[]{:S(2)}) collective-permute-start(bf16[128,1024]{1,0:T(8,128)(2,1)S(1)} %multiply_convert_fusion), channel_id=1, source_target_pairs={{0,8},{8,16},{16,24},{24,32},{32,40},{40,48},{48,56},{56,64},{64,7... | collective-permute-start | bytes 786440 | tf_op jit(solution)/shard_map/ppermute | solution.py:27
  14.1 9.3 %collective-permute-start.1 = (bf16[512,128]{1,0:T(8,128)(2,1)}, bf16[512,128]{1,0:T(8,128)(2,1)}, u32[]{:S(2)}, u32[]{:S(2)}) collective-permute-start(bf16[512,128]{1,0:T(8,128)(2,1)} %get-tuple-element.64), channel_id=1, source_target_pairs={{0,24},{8,0},{16,8},{24,16},{1,25},{9,1},{17,9},{25,17},{2,26},{10... | collective-permute-start | bytes 393224 | tf_op jit(solution)/shard_map/ppermute | solution.py:21
  14.3 10.1 %collective-permute-start.2 = (bf16[512,128]{1,0:T(8,128)(2,1)}, bf16[512,128]{1,0:T(8,128)(2,1)}, u32[]{:S(2)}, u32[]{:S(2)}) collective-permute-start(bf16[512,128]{1,0:T(8,128)(2,1)} %get-tuple-element.66), channel_id=1, source_target_pairs={{0,16},{8,24},{16,0},{24,8},{1,17},{9,25},{17,1},{25,9},{2,18},{10... | collective-permute-start | bytes 393224 | tf_op jit(solution)/shard_map/ppermute | solution.py:21
  15.7 9.6 %collective-permute-start.3 = (bf16[512,128]{1,0:T(8,128)(2,1)}, bf16[512,128]{1,0:T(8,128)(2,1)}, u32[]{:S(2)}, u32[]{:S(2)}) collective-permute-start(bf16[512,128]{1,0:T(8,128)(2,1)} %get-tuple-element.63), channel_id=1, source_target_pairs={{0,8},{8,16},{16,24},{24,0},{1,9},{9,17},{17,25},{25,1},{2,10},{10... | collective-permute-start | bytes 393224 | tf_op jit(solution)/shard_map/ppermute | solution.py:21
  17.8 151.6 %reduce-scatter.2.cloned.1.call-start = ((), (), s32[]{:S(2)}) async-start(), calls=%async_computation.2 | async-start | bytes 2359296 | tf_op jit(solution)/shard_map/reduce_scatter | solution.py:377
  17.9 11.7 %copy-start.3 = (bf16[512,1024]{1,0:T(8,128)(2,1)S(1)}, bf16[512,1024]{1,0:T(8,128)(2,1)}, u32[]{:S(2)}) copy-start(bf16[512,1024]{1,0:T(8,128)(2,1)} %k_ref.5) | copy-start | bytes 3145732
  26.3 14.8 %collective-permute-start.5 = (bf16[2048,128]{1,0:T(8,128)(2,1)S(1)}, bf16[2048,128]{1,0:T(8,128)(2,1)S(1)}, u32[]{:S(2)}, u32[]{:S(2)}) collective-permute-start(bf16[2048,128]{1,0:T(8,128)(2,1)S(1)} %get-tuple-element.67), channel_id=1, source_target_pairs={{0,2},{2,4},{4,6},{6,0},{1,3},{3,5},{5,7},{7,1},{8,10},{10,12},{12... | collective-permute-start | bytes 1572872 | tf_op jit(solution)/shard_map/ppermute | solution.py:21
  27.9 14.7 %collective-permute-start.4 = (bf16[2048,128]{1,0:T(8,128)(2,1)S(1)}, bf16[2048,128]{1,0:T(8,128)(2,1)S(1)}, u32[]{:S(2)}, u32[]{:S(2)}) collective-permute-start(bf16[2048,128]{1,0:T(8,128)(2,1)S(1)} %get-tuple-element.67), channel_id=1, source_target_pairs={{0,6},{2,0},{4,2},{6,4},{1,7},{3,1},{5,3},{7,5},{8,14},{10,8},{12,... | collective-permute-start | bytes 1572872 | tf_op jit(solution)/shard_map/ppermute | solution.py:21
  34.2 8.3 %copy-start.12 = (bf16[512,512]{1,0:T(8,128)(2,1)}, bf16[512,512]{1,0:T(8,128)(2,1)S(1)}, u32[]{:S(2)}) copy-start(bf16[512,512]{1,0:T(8,128)(2,1)S(1)} %get-tuple-element.59.refs_0_) | copy-start | bytes 1572868
  37.8 22.7 %copy-start.7 = (f32[512,1024]{1,0:T(8,128)}, f32[512,1024]{1,0:T(8,128)S(1)}, u32[]{:S(2)}) copy-start(f32[512,1024]{1,0:T(8,128)S(1)} %get-tuple-element.51.refs_7_) | copy-start | bytes 6291460
  37.8 22.7 %copy-start.10 = (bf16[512,1024]{1,0:T(8,128)(2,1)}, bf16[512,1024]{1,0:T(8,128)(2,1)S(1)}, u32[]{:S(2)}) copy-start(bf16[512,1024]{1,0:T(8,128)(2,1)S(1)} %get-tuple-element.54.mixed_ref) | copy-start | bytes 3145732
  37.8 22.7 %copy-start.14 = (bf16[512,512]{1,0:T(8,128)(2,1)}, bf16[512,512]{1,0:T(8,128)(2,1)S(1)}, u32[]{:S(2)}) copy-start(bf16[512,512]{1,0:T(8,128)(2,1)S(1)} %get-tuple-element.38.refs_1_) | copy-start | bytes 1572868
  37.8 16.1 %collective-permute-start.8 = (bf16[512,512]{1,0:T(8,128)(2,1)S(1)}, bf16[512,512]{1,0:T(8,128)(2,1)S(1)}, u32[]{:S(2)}, u32[]{:S(2)}) collective-permute-start(bf16[512,512]{1,0:T(8,128)(2,1)S(1)} %get-tuple-element.38.refs_1_), channel_id=1, source_target_pairs={{0,24},{8,0},{16,8},{24,16},{1,25},{9,1},{17,9},{25,17},{2,26},{10... | collective-permute-start | bytes 1572872 | tf_op jit(solution)/shard_map/ppermute | solution.py:21
  37.9 17.9 %collective-permute-start.7 = (bf16[512,512]{1,0:T(8,128)(2,1)S(1)}, bf16[512,512]{1,0:T(8,128)(2,1)S(1)}, u32[]{:S(2)}, u32[]{:S(2)}) collective-permute-start(bf16[512,512]{1,0:T(8,128)(2,1)S(1)} %get-tuple-element.59.refs_0_), channel_id=1, source_target_pairs={{0,8},{8,16},{16,24},{24,0},{1,9},{9,17},{17,25},{25,1},{2,10},{10... | collective-permute-start | bytes 1572872 | tf_op jit(solution)/shard_map/ppermute | solution.py:21
  41.1 14.7 %collective-permute-start.6 = (bf16[1024,128]{1,0:T(8,128)(2,1)S(1)}, bf16[1024,128]{1,0:T(8,128)(2,1)S(1)}, u32[]{:S(2)}, u32[]{:S(2)}) collective-permute-start(bf16[1024,128]{1,0:T(8,128)(2,1)S(1)} %slice.48), channel_id=1, source_target_pairs={{0,2},{2,4},{4,6},{6,0},{1,3},{3,5},{5,7},{7,1},{8,10},{10,12},{12... | collective-permute-start | bytes 786440 | tf_op jit(solution)/shard_map/ppermute | solution.py:21
  41.6 20.7 %collective-permute-start.11 = (bf16[512,512]{1,0:T(8,128)(2,1)S(1)}, bf16[512,512]{1,0:T(8,128)(2,1)S(1)}, u32[]{:S(2)}, u32[]{:S(2)}) collective-permute-start(bf16[512,512]{1,0:T(8,128)(2,1)S(1)} %get-tuple-element.38.refs_1_), channel_id=1, source_target_pairs={{0,8},{8,16},{16,24},{24,0},{1,9},{9,17},{17,25},{25,1},{2,10},{10... | collective-permute-start | bytes 1572872 | tf_op jit(solution)/shard_map/ppermute | solution.py:21
  42.6 20.5 %collective-permute-start.10 = (bf16[512,512]{1,0:T(8,128)(2,1)S(1)}, bf16[512,512]{1,0:T(8,128)(2,1)S(1)}, u32[]{:S(2)}, u32[]{:S(2)}) collective-permute-start(bf16[512,512]{1,0:T(8,128)(2,1)S(1)} %get-tuple-element.59.refs_0_), channel_id=1, source_target_pairs={{0,24},{8,0},{16,8},{24,16},{1,25},{9,1},{17,9},{25,17},{2,26},{10... | collective-permute-start | bytes 1572872 | tf_op jit(solution)/shard_map/ppermute | solution.py:21
  53.9 6.4 %collective-permute-start.9 = (bf16[1024,128]{1,0:T(8,128)(2,1)S(1)}, bf16[1024,128]{1,0:T(8,128)(2,1)S(1)}, u32[]{:S(2)}, u32[]{:S(2)}) collective-permute-start(bf16[1024,128]{1,0:T(8,128)(2,1)S(1)} %slice.49), channel_id=1, source_target_pairs={{0,6},{2,0},{4,2},{6,4},{1,7},{3,1},{5,3},{7,5},{8,14},{10,8},{12,... | collective-permute-start | bytes 786440 | tf_op jit(solution)/shard_map/ppermute | solution.py:21
  63.9 4.3 %collective-permute-start.12 = (bf16[4,2048,128]{2,1,0:T(8,128)(2,1)S(1)}, bf16[4,2048,128]{2,1,0:T(8,128)(2,1)}, u32[]{:S(2)}, u32[]{:S(2)}) collective-permute-start(bf16[4,2048,128]{2,1,0:T(8,128)(2,1)S(1)} %bitcast.9), channel_id=1, source_target_pairs={{0,1},{1,0},{2,3},{3,2},{4,5},{5,4},{6,7},{7,6},{8,9},{9,8},{10,11... | collective-permute-start | bytes 6291464 | tf_op jit(solution)/shard_map/ppermute | solution.py:21
  63.9 16.6 %collective-permute-start.14 = (bf16[512,512]{1,0:T(8,128)(2,1)}, bf16[512,512]{1,0:T(8,128)(2,1)}, u32[]{:S(2)}, u32[]{:S(2)}) collective-permute-start(bf16[512,512]{1,0:T(8,128)(2,1)} %copy-done.16), channel_id=1, source_target_pairs={{0,24},{8,0},{16,8},{24,16},{1,25},{9,1},{17,9},{25,17},{2,26},{10... | collective-permute-start | bytes 1572872 | tf_op jit(solution)/shard_map/ppermute | solution.py:21
  64.3 16.2 %collective-permute-start.13 = (bf16[512,512]{1,0:T(8,128)(2,1)}, bf16[512,512]{1,0:T(8,128)(2,1)}, u32[]{:S(2)}, u32[]{:S(2)}) collective-permute-start(bf16[512,512]{1,0:T(8,128)(2,1)} %copy-done.18), channel_id=1, source_target_pairs={{0,8},{8,16},{16,24},{24,0},{1,9},{9,17},{17,25},{25,1},{2,10},{10... | collective-permute-start | bytes 1572872 | tf_op jit(solution)/shard_map/ppermute | solution.py:21
  74.5 20.4 %collective-permute-start.15 = (bf16[512,512]{1,0:T(8,128)(2,1)}, bf16[512,512]{1,0:T(8,128)(2,1)}, u32[]{:S(2)}, u32[]{:S(2)}) collective-permute-start(bf16[512,512]{1,0:T(8,128)(2,1)} %get-tuple-element.41), channel_id=1, source_target_pairs={{0,8},{8,16},{16,24},{24,0},{1,9},{9,17},{17,25},{25,1},{2,10},{10... | collective-permute-start | bytes 1572872 | tf_op jit(solution)/shard_map/ppermute | solution.py:21
  78.2 8.2 %copy-start.17 = (bf16[512,512]{1,0:T(8,128)(2,1)S(1)}, bf16[512,512]{1,0:T(8,128)(2,1)}, u32[]{:S(2)}) copy-start(bf16[512,512]{1,0:T(8,128)(2,1)} %copy-done.16) | copy-start | bytes 1572868
  78.2 8.2 %copy-start.19 = (bf16[512,512]{1,0:T(8,128)(2,1)S(1)}, bf16[512,512]{1,0:T(8,128)(2,1)}, u32[]{:S(2)}) copy-start(bf16[512,512]{1,0:T(8,128)(2,1)} %copy-done.18) | copy-start | bytes 1572868
  78.2 8.2 %copy-start.21 = (bf16[512,512]{1,0:T(8,128)(2,1)S(1)}, bf16[512,512]{1,0:T(8,128)(2,1)}, u32[]{:S(2)}) copy-start(bf16[512,512]{1,0:T(8,128)(2,1)} %copy-done.20) | copy-start | bytes 1572868
  78.2 8.2 %copy-start.23 = (bf16[512,512]{1,0:T(8,128)(2,1)S(1)}, bf16[512,512]{1,0:T(8,128)(2,1)}, u32[]{:S(2)}) copy-start(bf16[512,512]{1,0:T(8,128)(2,1)} %copy-done.22) | copy-start | bytes 1572868
  78.2 16.7 %collective-permute-start.16 = (bf16[512,512]{1,0:T(8,128)(2,1)}, bf16[512,512]{1,0:T(8,128)(2,1)}, u32[]{:S(2)}, u32[]{:S(2)}) collective-permute-start(bf16[512,512]{1,0:T(8,128)(2,1)} %get-tuple-element.42), channel_id=1, source_target_pairs={{0,24},{8,0},{16,8},{24,16},{1,25},{9,1},{17,9},{25,17},{2,26},{10... | collective-permute-start | bytes 1572872 | tf_op jit(solution)/shard_map/ppermute | solution.py:21
  95.0 16.4 %collective-permute-start.18 = (bf16[512,512]{1,0:T(8,128)(2,1)}, bf16[512,512]{1,0:T(8,128)(2,1)S(1)}, u32[]{:S(2)}, u32[]{:S(2)}) collective-permute-start(bf16[512,512]{1,0:T(8,128)(2,1)} %copy-done.26), channel_id=1, source_target_pairs={{0,24},{8,0},{16,8},{24,16},{1,25},{9,1},{17,9},{25,17},{2,26},{10... | collective-permute-start | bytes 1572872 | tf_op jit(solution)/shard_map/ppermute | solution.py:21
  96.6 15.1 %collective-permute-start.19 = (bf16[512,512]{1,0:T(8,128)(2,1)}, bf16[512,512]{1,0:T(8,128)(2,1)S(1)}, u32[]{:S(2)}, u32[]{:S(2)}) collective-permute-start(bf16[512,512]{1,0:T(8,128)(2,1)} %copy-done.25), channel_id=1, source_target_pairs={{0,8},{8,16},{16,24},{24,0},{1,9},{9,17},{17,25},{25,1},{2,10},{10... | collective-permute-start | bytes 1572872 | tf_op jit(solution)/shard_map/ppermute | solution.py:21
  104.7 16.2 %collective-permute-start.17 = (bf16[512,512]{1,0:T(8,128)(2,1)S(1)}, bf16[512,512]{1,0:T(8,128)(2,1)S(1)}, u32[]{:S(2)}, u32[]{:S(2)}) collective-permute-start(bf16[512,512]{1,0:T(8,128)(2,1)S(1)} %get-tuple-element.45), channel_id=1, source_target_pairs={{0,8},{8,16},{16,24},{24,0},{1,9},{9,17},{17,25},{25,1},{2,10},{10... | collective-permute-start | bytes 1572872 | tf_op jit(solution)/shard_map/ppermute | solution.py:21
  106.7 14.8 %collective-permute-start.20 = (bf16[512,512]{1,0:T(8,128)(2,1)S(1)}, bf16[512,512]{1,0:T(8,128)(2,1)S(1)}, u32[]{:S(2)}, u32[]{:S(2)}) collective-permute-start(bf16[512,512]{1,0:T(8,128)(2,1)S(1)} %get-tuple-element.49), channel_id=1, source_target_pairs={{0,24},{8,0},{16,8},{24,16},{1,25},{9,1},{17,9},{25,17},{2,26},{10... | collective-permute-start | bytes 1572872 | tf_op jit(solution)/shard_map/ppermute | solution.py:21
  110.9 14.3 %copy-start.8 = (f32[512,1024]{1,0:T(8,128)S(1)}, f32[512,1024]{1,0:T(8,128)}, u32[]{:S(2)}) copy-start(f32[512,1024]{1,0:T(8,128)} %copy-done.7) | copy-start | bytes 6291460
  122.3 17.2 %collective-permute-start.21 = (bf16[128,1024]{1,0:T(8,128)(2,1)}, bf16[128,1024]{1,0:T(8,128)(2,1)}, u32[]{:S(2)}, u32[]{:S(2)}) collective-permute-start(bf16[128,1024]{1,0:T(8,128)(2,1)} %pad_maximum_fusion), channel_id=1, source_target_pairs={{8,0},{16,8},{24,16},{32,24},{40,32},{48,40},{56,48},{64,56},{72,6... | collective-permute-start | bytes 786440 | tf_op jit(solution)/shard_map/ppermute | solution.py:27
  127.7 11.9 %copy-start.4 = (bf16[512,1024]{1,0:T(8,128)(2,1)S(1)}, bf16[512,1024]{1,0:T(8,128)(2,1)}, u32[]{:S(2)}) copy-start(bf16[512,1024]{1,0:T(8,128)(2,1)} %k_ref.5) | copy-start | bytes 3145732
  127.7 11.9 %copy-start.6 = (bf16[512,1024]{1,0:T(8,128)(2,1)S(1)}, bf16[512,1024]{1,0:T(8,128)(2,1)}, u32[]{:S(2)}) copy-start(bf16[512,1024]{1,0:T(8,128)(2,1)} %v_ref.5) | copy-start | bytes 3145732
  133.4 13.0 %collective-permute-start.22 = (f32[64,128]{1,0:T(8,128)S(1)}, f32[64,128]{1,0:T(8,128)S(1)}, u32[]{:S(2)}, u32[]{:S(2)}) collective-permute-start(f32[64,128]{1,0:T(8,128)S(1)} %filter_part.1), channel_id=1, source_target_pairs={{0,24},{8,0},{16,8},{24,16},{1,25},{9,1},{17,9},{25,17},{2,26},{10... | collective-permute-start | bytes 98312 | tf_op jit(solution)/shard_map/ppermute | solution.py:21
  135.2 11.2 %collective-permute-start.23 = (f32[64,128]{1,0:T(8,128)S(1)}, f32[64,128]{1,0:T(8,128)S(1)}, u32[]{:S(2)}, u32[]{:S(2)}) collective-permute-start(f32[64,128]{1,0:T(8,128)S(1)} %filter_part.1), channel_id=1, source_target_pairs={{0,16},{8,24},{16,0},{24,8},{1,17},{9,25},{17,1},{25,9},{2,18},{10... | collective-permute-start | bytes 98312 | tf_op jit(solution)/shard_map/ppermute | solution.py:21
  137.1 9.3 %collective-permute-start.24 = (f32[64,128]{1,0:T(8,128)S(1)}, f32[64,128]{1,0:T(8,128)S(1)}, u32[]{:S(2)}, u32[]{:S(2)}) collective-permute-start(f32[64,128]{1,0:T(8,128)S(1)} %filter_part.1), channel_id=1, source_target_pairs={{0,8},{8,16},{16,24},{24,0},{1,9},{9,17},{17,25},{25,1},{2,10},{10... | collective-permute-start | bytes 98312 | tf_op jit(solution)/shard_map/ppermute | solution.py:21
  146.4 12.9 %collective-permute-start.25 = (f32[64,128]{1,0:T(8,128)S(1)}, f32[64,128]{1,0:T(8,128)S(1)}, u32[]{:S(2)}, u32[]{:S(2)}) collective-permute-start(f32[64,128]{1,0:T(8,128)S(1)} %select_add_fusion.1), channel_id=1, source_target_pairs={{0,224},{32,0},{64,32},{96,64},{128,96},{160,128},{192,160},{224,1... | collective-permute-start | bytes 98312 | tf_op jit(solution)/shard_map/ppermute | solution.py:21
  151.6 11.9 %collective-permute-start.26 = (f32[64,128]{1,0:T(8,128)S(1)}, f32[64,128]{1,0:T(8,128)S(1)}, u32[]{:S(2)}, u32[]{:S(2)}) collective-permute-start(f32[64,128]{1,0:T(8,128)S(1)} %select_add_fusion.1), channel_id=1, source_target_pairs={{0,192},{32,224},{64,0},{96,32},{128,64},{160,96},{192,128},{224,1... | collective-permute-start | bytes 98312 | tf_op jit(solution)/shard_map/ppermute | solution.py:21
  153.0 11.1 %collective-permute-start.27 = (f32[64,128]{1,0:T(8,128)S(1)}, f32[64,128]{1,0:T(8,128)S(1)}, u32[]{:S(2)}, u32[]{:S(2)}) collective-permute-start(f32[64,128]{1,0:T(8,128)S(1)} %select_add_fusion.1), channel_id=1, source_target_pairs={{0,160},{32,192},{64,224},{96,0},{128,32},{160,64},{192,96},{224,1... | collective-permute-start | bytes 98312 | tf_op jit(solution)/shard_map/ppermute | solution.py:21
  155.5 8.8 %collective-permute-start.28 = (f32[64,128]{1,0:T(8,128)S(1)}, f32[64,128]{1,0:T(8,128)S(1)}, u32[]{:S(2)}, u32[]{:S(2)}) collective-permute-start(f32[64,128]{1,0:T(8,128)S(1)} %select_add_fusion.1), channel_id=1, source_target_pairs={{0,128},{32,160},{64,192},{96,224},{128,0},{160,32},{192,64},{224,... | collective-permute-start | bytes 98312 | tf_op jit(solution)/shard_map/ppermute | solution.py:21
  158.5 6.9 %collective-permute-start.29 = (f32[64,128]{1,0:T(8,128)S(1)}, f32[64,128]{1,0:T(8,128)S(1)}, u32[]{:S(2)}, u32[]{:S(2)}) collective-permute-start(f32[64,128]{1,0:T(8,128)S(1)} %select_add_fusion.1), channel_id=1, source_target_pairs={{0,96},{32,128},{64,160},{96,192},{128,224},{160,0},{192,32},{224,... | collective-permute-start | bytes 98312 | tf_op jit(solution)/shard_map/ppermute | solution.py:21
  159.3 7.0 %collective-permute-start.30 = (f32[64,128]{1,0:T(8,128)S(1)}, f32[64,128]{1,0:T(8,128)S(1)}, u32[]{:S(2)}, u32[]{:S(2)}) collective-permute-start(f32[64,128]{1,0:T(8,128)S(1)} %select_add_fusion.1), channel_id=1, source_target_pairs={{0,64},{32,96},{64,128},{96,160},{128,192},{160,224},{192,0},{224,... | collective-permute-start | bytes 98312 | tf_op jit(solution)/shard_map/ppermute | solution.py:21
  163.4 5.1 %collective-permute-start.31 = (f32[64,128]{1,0:T(8,128)S(1)}, f32[64,128]{1,0:T(8,128)S(1)}, u32[]{:S(2)}, u32[]{:S(2)}) collective-permute-start(f32[64,128]{1,0:T(8,128)S(1)} %select_add_fusion.1), channel_id=1, source_target_pairs={{0,32},{32,64},{64,96},{96,128},{128,160},{160,192},{192,224},{224... | collective-permute-start | bytes 98312 | tf_op jit(solution)/shard_map/ppermute | solution.py:21
  (13 other events, 37.0 us)
Sparse Core Ops, SparseCore 0:
  17.9 44.1 all-gather.1
  95.1 45.2 reduce-scatter.1

commit v4 on v3

--- a/solution.py
+++ b/solution.py
@@ -270,7 +270,10 @@
         )[:, taps:]
         for g in range(groups)
     ]
-    filter_ref[...] = jnp.concatenate(sums, 0)
+    turn = anti_identity(taps).astype(F32)
+    filter_ref[...] = jnp.dot(
+        jnp.concatenate(sums, 0), turn, precision=lax.Precision.HIGHEST, preferred_element_type=F32
+    )
 
 
 def filter_part(inner, mixed, rim, group_count):
@@ -320,9 +323,9 @@
     )(filters, inner, ahead, k, v)
 
 
-def sum_over(value, axis, *beside):
-    count, me = lax.axis_size(axis), lax.axis_index(axis)
-    terms = [after(value, *beside)] + [send(value, axis, d) for d in range(1, count)]
+def sum_over(value, axis, stride, *beside):
+    count, me = lax.axis_size(axis) // stride, lax.axis_index(axis) // stride
+    terms = [after(value, *beside)] + [send(value, axis, d * stride) for d in range(1, count)]
     total = None
     for source in range(count):
         term = terms[0]
@@ -348,15 +351,14 @@
     pieces = [own_cols(0), None, None, None]
     for d in (2, 1, 3):
         pieces[(-d) % 4] = send(own_cols(d), "x", d)
-    column = jnp.concatenate([after(pieces[0], rim), *pieces[1:]], 0)
+    conv, mixed, gated_a = forward(0, filters, key_in, value_in, query_in, rim, None)
+    conv, mixed, gated_b = forward(1, filters, key_in, value_in, query_in, rim, (conv, mixed))
+    column = after(jnp.concatenate(pieces, 0), gated_a)
     below, above = send(column, "y", 1), send(column, "y", -1)
     middle = column.shape[0] // 2
     far = send(below[:middle], "y", 1), send(above[middle:], "y", -1)
-
-    conv, mixed, gated_a = forward(0, filters, key_in, value_in, query_in, rim, None)
-    conv, mixed, gated_b = forward(1, filters, key_in, value_in, query_in, rim, (conv, mixed))
-    left_a, right_b = send(gated_a, "x", 1), send(gated_b, "x", -1)
-    right_a, left_b = send(gated_a, "x", -1), send(gated_b, "x", 1)
+    left_a, right_a = send(gated_a, "x", 1), send(gated_a, "x", -1)
+    right_b, left_b = send(gated_b, "x", -1), send(after(gated_b, left_a, right_a), "x", 1)
     far_a, far_b = send(left_a, "x", 1), send(right_b, "x", -1)
     gated = [gated_a, gated_b, right_a, right_b, far_a, far_b, left_a, left_b]
 
@@ -395,8 +397,9 @@
     )
     sums = filter_part(inner, mixed, rim, group_count)
     grad_key, grad_value = backward(filters, after(inner, sums), ahead, key_in, value_in)
-    sums = sum_over(sums, "x", grad_key)
-    grad_filter = jnp.flip(sum_over(sums, "z"), 1)
+    sums = sum_over(sum_over(sums, "x", 1, grad_key), "z", 2)
+    odd = lax.ppermute(sums, "z", [(i, i ^ 1) for i in range(lax.axis_size("z"))])
+    grad_filter = after(sums, grad_proj) + odd
     return grad_query, grad_key, grad_value, grad_filter, grad_proj
 
 

time: 179 us -> 175 us (0.978)
  starting transfers between devices: 58.2 us -> 52.4 us
  local copies, waits for them, and re-layouts: 14.9 us -> 9.3 us
  waiting for transfers between devices: 39.7 us -> 42.3 us
  other arithmetic: 4.06 us -> 6.35 us
  Pallas kernels: 46.7 us -> 48.8 us
    ppermute x30 -> x26, starting transfers between devices: 51.6 us -> 44.3 us  [send(): lax.ppermute(value, axis, [(i, (i + by) % count) for i in range(count)])]
    ppermute x2, waiting for transfers between devices: 0.53 us -> 4.87 us  [send_along_tokens(): return lax.ppermute(value, ('z', 'x'), pairs)]
    unnamed x60 -> x58, local copies, waits for them, and re-layouts: 11.2 us -> 7.25 us
    ppermute x30 -> x26, waiting for transfers between devices: 39.1 us -> 36.4 us  [send(): lax.ppermute(value, axis, [(i, (i + by) % count) for i in range(count)])]
    pallas_call x1, Pallas kernels: 5.68 us -> 7.74 us  [filter_part(): pl.pallas_call(functools.partial(filter_body, taps, groups), grid=(width...]
  transfers between devices with their start and end apart: 34 -> 31, of which waited for: 15 -> 16; matrix products, arithmetic and copies ran while one was open for 4% -> 2% of each run, Pallas kernels for 26% -> 28%
where the time goes in v4:
time: 175 us; the launch traced here: 174 us
  starting transfers between devices  52.4 us (30%)
  Pallas kernels  48.8 us (28%)
  waiting for transfers between devices  42.3 us (24%)
  between operations  14.5 us (8%)
  local copies, waits for them, and re-layouts  9.3 us (5%)
  other arithmetic  6.35 us (4%)
    ppermute x26, starting transfers between devices, send(): lax.ppermute(value, axis, [(i, (i + by) % count) for i in range(count)])  44.3 us
    ppermute x26, waiting for transfers between devices, send(): lax.ppermute(value, axis, [(i, (i + by) % count) for i in range(count)])  36.4 us
    pallas_call x4, Pallas kernels, gate_parts(): pl.pallas_call(gate_body, grid_spec=spec, out_shape=[jax.ShapeDtypeStruct...  17.8 us
    pallas_call x1, Pallas kernels, filter_part(): pl.pallas_call(functools.partial(filter_body, taps, groups), grid=(width...  7.74 us
    unnamed x58, local copies, waits for them, and re-layouts  7.25 us
    pallas_call x1, Pallas kernels, proj_part(): pl.pallas_call(proj_body, grid_spec=spec, out_shape=jax.ShapeDtypeStruct(...  7.08 us
    pallas_call x2, Pallas kernels, forward(): pl.pallas_call(functools.partial(forward_body, taps, groups), grid=(steps...  6.9 us
    ppermute x2, starting transfers between devices, send_along_tokens(): return lax.ppermute(value, ('z', 'x'), pairs)  6.86 us
  transfers between devices with their start and end apart: 31, of which 16 were waited for; matrix products, arithmetic and copies ran while one was open for 2% of the time, Pallas kernels for 28%

profile of v4, /device:TPU:6, one launch (start us, length us, event | category | flops | bytes accessed | tf_op | source)
XLA Modules:
  0.0 173.6 jit_solution(17859852185860443368)
XLA Ops:
  7.3 2.0 %multiply_convert_fusion = bf16[128,1024]{1,0:T(8,128)(2,1)} fusion(bf16[512,1024]{1,0:T(8,128)(2,1)} %v_ref.5, bf16[512,1024]{1,0:T(8,128)(2,1)} %k_ref.5), kind=kLoop, calls=%fused_computation.1 | loop fusion | flops 524288 | bytes 786432 | tf_op jit(solution)/shard_map/convert_element_type | solution.py:35
  9.2 1.9 %constant_dynamic-slice_fusion.3 = (bf16[512,128]{1,0:T(8,128)(2,1)S(1)}, bf16[512,128]{1,0:T(8,128)(2,1)}, bf16[512,128]{1,0:T(8,128)(2,1)}, bf16[512,128]{1,0:T(8,128)(2,1)}) fusion(bf16[512,512]{1,0:T(8,128)(2,1)} %param.11, s32[]{:T(128)S(6)} %select_n.275, s32[]{:T(128)S(6)} %select_n.277, s32[]{:T(128)S(6)} %select_n.281, s32[]{:T(128)S(6)} %select_n.279), kind=kLoop, calls=%fused_computation.15 | loop fusion | bytes 1048592 | tf_op jit(solution)/shard_map/dynamic_slice | solution.py:350
  11.9 2.8 %collective-permute-start.1 = (bf16[512,128]{1,0:T(8,128)(2,1)}, bf16[512,128]{1,0:T(8,128)(2,1)}, u32[]{:S(2)}, u32[]{:S(2)}) collective-permute-start(bf16[512,128]{1,0:T(8,128)(2,1)} %get-tuple-element.70), channel_id=1, source_target_pairs={{0,16},{8,24},{16,0},{24,8},{1,17},{9,25},{17,1},{25,9},{2,18},{10... | collective-permute-start | bytes 393224 | tf_op jit(solution)/shard_map/ppermute | solution.py:21
  15.1 4.1 %collective-permute-start.3 = (bf16[128,1024]{1,0:T(8,128)(2,1)}, bf16[128,1024]{1,0:T(8,128)(2,1)S(1)}, u32[]{:S(2)}, u32[]{:S(2)}) collective-permute-start(bf16[128,1024]{1,0:T(8,128)(2,1)} %multiply_convert_fusion), channel_id=1, source_target_pairs={{0,8},{8,16},{16,24},{24,32},{32,40},{40,48},{48,56},{56,64},{64,7... | collective-permute-start | bytes 786440 | tf_op jit(solution)/shard_map/ppermute | solution.py:27
  19.3 1.3 collective-permute-done
  20.6 2.0 %collective-permute-done.2 = bf16[512,128]{1,0:T(8,128)(2,1)} collective-permute-done((bf16[512,128]{1,0:T(8,128)(2,1)}, bf16[512,128]{1,0:T(8,128)(2,1)}, u32[]{:S(2)}, u32[]{:S(2)}) %collective-permute-start.2) | collective-permute-done | bytes 131104 | tf_op jit(solution)/shard_map/ppermute | solution.py:21
  22.7 1.1 pad_maximum_fusion
  23.8 3.0 %collective-permute-done.3.rim_ref = bf16[128,1024]{1,0:T(8,128)(2,1)S(1)} collective-permute-done((bf16[128,1024]{1,0:T(8,128)(2,1)}, bf16[128,1024]{1,0:T(8,128)(2,1)S(1)}, u32[]{:S(2)}, u32[]{:S(2)}) %collective-permute-start.3) | collective-permute-done | bytes 262176 | tf_op jit(solution)/shard_map/ppermute | solution.py:27
  26.8 3.4 %conv_forward.2 = (f32[512,1024]{1,0:T(8,128)S(1)}, bf16[512,1024]{1,0:T(8,128)(2,1)S(1)}, bf16[512,512]{1,0:T(8,128)(2,1)S(1)}) custom-call(bf16[64,128]{1,0:T(8,128)(2,1)S(1)} %copy-done.24, bf16[512,1024]{1,0:T(8,128)(2,1)S(1)} %copy-done.3, bf16[512,1024]{1,0:T(8,128)(2,1)S(1)} %copy-done.5, bf16[512,1024]{1,0:T(8,128)(2,1)S(1)} %copy-done.2, ...), custom_call_target="tpu_custom_call" | custom-call | flops 1048576 | bytes 262144 | tf_op jit(solution)/shard_map/conv_forward/pallas_call | solution.py:105
  30.2 1.7 collective-permute-start.5
  31.9 1.7 collective-permute-start.4
  33.5 2.0 %collective-permute-start.10 = (bf16[512,512]{1,0:T(8,128)(2,1)S(1)}, bf16[512,512]{1,0:T(8,128)(2,1)S(1)}, u32[]{:S(2)}, u32[]{:S(2)}) collective-permute-start(bf16[512,512]{1,0:T(8,128)(2,1)S(1)} %get-tuple-element.62.refs_0_), channel_id=1, source_target_pairs={{0,24},{8,0},{16,8},{24,16},{1,25},{9,1},{17,9},{25,17},{2,26},{10... | collective-permute-start | bytes 1572872 | tf_op jit(solution)/shard_map/ppermute | solution.py:21
  35.5 3.5 %conv_forward.3 = (f32[512,1024]{1,0:T(8,128)S(1)}, bf16[512,1024]{1,0:T(8,128)(2,1)S(1)}, bf16[512,512]{1,0:T(8,128)(2,1)S(1)}) custom-call(bf16[64,128]{1,0:T(8,128)(2,1)S(1)} %copy-done.24, bf16[512,1024]{1,0:T(8,128)(2,1)S(1)} %copy-done.3, bf16[512,1024]{1,0:T(8,128)(2,1)S(1)} %copy-done.5, ...), custom_call_target="tpu_custom_call", output_to_operand_aliasing={{0}: (5, {}), {1}: (6, {})} | custom-call | flops 1048576 | bytes 262144 | tf_op jit(solution)/shard_map/conv_forward/pallas_call | solution.py:105
  39.9 4.1 %collective-permute-done.5 = bf16[2048,128]{1,0:T(8,128)(2,1)S(1)} collective-permute-done((bf16[2048,128]{1,0:T(8,128)(2,1)S(1)}, bf16[2048,128]{1,0:T(8,128)(2,1)S(1)}, u32[]{:S(2)}, u32[]{:S(2)}) %collective-permute-start.5) | collective-permute-done | bytes 524320 | tf_op jit(solution)/shard_map/ppermute | solution.py:21
  44.5 3.0 %collective-permute-start.9 = (bf16[1024,128]{1,0:T(8,128)(2,1)S(1)}, bf16[1024,128]{1,0:T(8,128)(2,1)S(1)}, u32[]{:S(2)}, u32[]{:S(2)}) collective-permute-start(bf16[1024,128]{1,0:T(8,128)(2,1)S(1)} %slice.49), channel_id=1, source_target_pairs={{0,6},{2,0},{4,2},{6,4},{1,7},{3,1},{5,3},{7,5},{8,14},{10,8},{12,... | collective-permute-start | bytes 786440 | tf_op jit(solution)/shard_map/ppermute | solution.py:21
  47.5 2.1 %collective-permute-done.10.refs_2_ = bf16[512,512]{1,0:T(8,128)(2,1)S(1)} collective-permute-done((bf16[512,512]{1,0:T(8,128)(2,1)S(1)}, bf16[512,512]{1,0:T(8,128)(2,1)S(1)}, u32[]{:S(2)}, u32[]{:S(2)}) %collective-permute-start.10) | collective-permute-done | bytes 524320 | tf_op jit(solution)/shard_map/ppermute | solution.py:21
  50.4 7.6 %collective-permute-done.8.refs_3_ = bf16[512,512]{1,0:T(8,128)(2,1)S(1)} collective-permute-done((bf16[512,512]{1,0:T(8,128)(2,1)S(1)}, bf16[512,512]{1,0:T(8,128)(2,1)S(1)}, u32[]{:S(2)}, u32[]{:S(2)}) %collective-permute-start.8) | collective-permute-done | bytes 524320 | tf_op jit(solution)/shard_map/ppermute | solution.py:21
  60.1 1.8 %collective-permute-start.14 = (bf16[512,512]{1,0:T(8,128)(2,1)}, bf16[512,512]{1,0:T(8,128)(2,1)}, u32[]{:S(2)}, u32[]{:S(2)}) collective-permute-start(bf16[512,512]{1,0:T(8,128)(2,1)} %copy-done.20), channel_id=1, source_target_pairs={{0,24},{8,0},{16,8},{24,16},{1,25},{9,1},{17,9},{25,17},{2,26},{10... | collective-permute-start | bytes 1572872 | tf_op jit(solution)/shard_map/ppermute | solution.py:21
  62.0 1.5 collective-permute-start.13
  64.4 1.6 copy-done
  66.0 4.8 %grad_gate_parts.4 = (bf16[512,512]{1,0:T(8,128)(2,1)}, bf16[512,512]{1,0:T(8,128)(2,1)}) custom-call(s32[8]{0:T(128)S(1)} %stack.35.place_ref, bf16[4,2048,128]{2,1,0:T(8,128)(2,1)S(1)} %bitcast.10, bf16[4,2048,128]{2,1,0:T(8,128)(2,1)} %collective-permute-done.12.sib_ref, bf16[1024,1024]{1,0:T(8,128)(2,1)S(1)} %copy-done), custom_call_target="tpu_custom_call" | custom-call | flops 1048576 | bytes 262144 | tf_op jit(solution)/shard_map/grad_gate_parts/pallas_call | solution.py:174
  70.7 1.5 collective-permute-start.15
  72.8 3.1 %collective-permute-done.14.refs_5_ = bf16[512,512]{1,0:T(8,128)(2,1)} collective-permute-done((bf16[512,512]{1,0:T(8,128)(2,1)}, bf16[512,512]{1,0:T(8,128)(2,1)}, u32[]{:S(2)}, u32[]{:S(2)}) %collective-permute-start.14) | collective-permute-done | bytes 524320 | tf_op jit(solution)/shard_map/ppermute | solution.py:21
  75.9 1.1 collective-permute-done.13.refs_4_
  77.1 4.3 %grad_gate_parts.7 = (bf16[512,512]{1,0:T(8,128)(2,1)S(1)}, bf16[512,512]{1,0:T(8,128)(2,1)S(1)}) custom-call(s32[8]{0:T(128)S(1)} %stack.35.place_ref, bf16[4,2048,128]{2,1,0:T(8,128)(2,1)S(1)} %bitcast.11, bf16[4,2048,128]{2,1,0:T(8,128)(2,1)} %collective-permute-done.12.sib_ref, bf16[1024,1024]{1,0:T(8,128)(2,1)S(1)} %copy-done), custom_call_target="tpu_custom_call" | custom-call | flops 1048576 | bytes 262144 | tf_op jit(solution)/shard_map/grad_gate_parts/pallas_call | solution.py:174
  83.0 7.1 %grad_proj_part.1 = bf16[1024,1024]{1,0:T(8,128)(2,1)S(1)} custom-call(s32[8]{0:T(128)S(1)} %stack.35.place_ref, bf16[4,2048,128]{2,1,0:T(8,128)(2,1)S(1)} %bitcast.12, bf16[4,2048,128]{2,1,0:T(8,128)(2,1)} %collective-permute-done.12.sib_ref, bf16[512,512]{1,0:T(8,128)(2,1)S(1)} %copy-done.13, bf16[512,512]{1,0:T(8,128)(2,1)S(1)} %copy-done.19, ...), custom_call_target="tpu_custom_call" | custom-call | flops 1048576 | bytes 262144 | tf_op jit(solution)/shard_map/grad_proj_part/pallas_call | solution.py:215
  90.1 1.4 copy-done.9
  91.9 3.0 %collective-permute-start.19 = (bf16[512,512]{1,0:T(8,128)(2,1)}, bf16[512,512]{1,0:T(8,128)(2,1)S(1)}, u32[]{:S(2)}, u32[]{:S(2)}) collective-permute-start(bf16[512,512]{1,0:T(8,128)(2,1)} %copy-done.25), channel_id=1, source_target_pairs={{0,8},{8,16},{16,24},{24,0},{1,9},{9,17},{17,25},{25,1},{2,10},{10... | collective-permute-start | bytes 1572872 | tf_op jit(solution)/shard_map/ppermute | solution.py:21
  94.8 1.6 copy-done.1
  96.4 4.6 %grad_gate_parts.6 = (bf16[512,512]{1,0:T(8,128)(2,1)S(1)}, bf16[512,512]{1,0:T(8,128)(2,1)S(1)}) custom-call(s32[8]{0:T(128)S(1)} %stack.35.place_ref, bf16[4,2048,128]{2,1,0:T(8,128)(2,1)S(1)} %bitcast.13, bf16[4,2048,128]{2,1,0:T(8,128)(2,1)} %collective-permute-done.12.sib_ref, bf16[1024,1024]{1,0:T(8,128)(2,1)S(1)} %copy-done.1, ...), custom_call_target="tpu_custom_call" | custom-call | flops 1048576 | bytes 262144 | tf_op jit(solution)/shard_map/grad_gate_parts/pallas_call | solution.py:174
  101.1 1.6 collective-permute-start.17
  103.2 4.1 %grad_gate_parts.5 = (f32[512,512]{1,0:T(8,128)S(1)}, f32[512,512]{1,0:T(8,128)S(1)}) custom-call(s32[8]{0:T(128)S(1)} %stack.35.place_ref, bf16[4,2048,128]{2,1,0:T(8,128)(2,1)S(1)} %bitcast.14, bf16[4,2048,128]{2,1,0:T(8,128)(2,1)} %collective-permute-done.12.sib_ref, bf16[1024,1024]{1,0:T(8,128)(2,1)S(1)} %copy-done.1), custom_call_target="tpu_custom_call" | custom-call | flops 1048576 | bytes 262144 | tf_op jit(solution)/shard_map/grad_gate_parts/pallas_call | solution.py:174
  107.5 8.3 %collective-permute-done.17.refs_2_ = bf16[512,512]{1,0:T(8,128)(2,1)S(1)} collective-permute-done((bf16[512,512]{1,0:T(8,128)(2,1)S(1)}, bf16[512,512]{1,0:T(8,128)(2,1)S(1)}, u32[]{:S(2)}, u32[]{:S(2)}) %collective-permute-start.17) | collective-permute-done | bytes 524320 | tf_op jit(solution)/shard_map/ppermute | solution.py:21
  117.4 2.7 %collective-permute-start.21 = (bf16[128,1024]{1,0:T(8,128)(2,1)}, bf16[128,1024]{1,0:T(8,128)(2,1)}, u32[]{:S(2)}, u32[]{:S(2)}) collective-permute-start(bf16[128,1024]{1,0:T(8,128)(2,1)} %pad_maximum_fusion.1), channel_id=1, source_target_pairs={{8,0},{16,8},{24,16},{32,24},{40,32},{48,40},{56,48},{64,56},{72,6... | collective-permute-start | bytes 786440 | tf_op jit(solution)/shard_map/ppermute | solution.py:27
  120.2 2.5 %gate_gradients.1 = (bf16[512,1024]{1,0:T(8,128)(2,1)}, bf16[512,1024]{1,0:T(8,128)(2,1)S(1)}) custom-call(f32[512,512]{1,0:T(8,128)S(1)} %get-tuple-element.53.refs_0_, f32[512,512]{1,0:T(8,128)S(1)} %get-tuple-element.50.refs_1_, bf16[512,512]{1,0:T(8,128)(2,1)S(1)} %collective-permute-done.17.refs_2_, ...), custom_call_target="tpu_custom_call" | custom-call | flops 1048576 | bytes 262144 | tf_op jit(solution)/shard_map/gate_gradients/pallas_call | solution.py:242
  122.7 7.7 %filter_part.1 = f32[64,128]{1,0:T(8,128)S(1)} custom-call(bf16[512,1024]{1,0:T(8,128)(2,1)S(1)} %get-tuple-element.58.inner_ref, bf16[512,1024]{1,0:T(8,128)(2,1)S(1)} %copy-done.11, bf16[128,1024]{1,0:T(8,128)(2,1)S(1)} %collective-permute-done.3.rim_ref), custom_call_target="tpu_custom_call" | custom-call | flops 1048576 | bytes 262144 | tf_op jit(solution)/shard_map/filter_part/pallas_call | solution.py:284
  130.4 1.8 %collective-permute-start.22 = (f32[64,128]{1,0:T(8,128)S(1)}, f32[64,128]{1,0:T(8,128)S(1)}, u32[]{:S(2)}, u32[]{:S(2)}) collective-permute-start(f32[64,128]{1,0:T(8,128)S(1)} %filter_part.1), channel_id=1, source_target_pairs={{0,24},{8,0},{16,8},{24,16},{1,25},{9,1},{17,9},{25,17},{2,26},{10... | collective-permute-start | bytes 98312 | tf_op jit(solution)/shard_map/ppermute | solution.py:21
  132.2 1.9 %collective-permute-start.23 = (f32[64,128]{1,0:T(8,128)S(1)}, f32[64,128]{1,0:T(8,128)S(1)}, u32[]{:S(2)}, u32[]{:S(2)}) collective-permute-start(f32[64,128]{1,0:T(8,128)S(1)} %filter_part.1), channel_id=1, source_target_pairs={{0,16},{8,24},{16,0},{24,8},{1,17},{9,25},{17,1},{25,9},{2,18},{10... | collective-permute-start | bytes 98312 | tf_op jit(solution)/shard_map/ppermute | solution.py:21
  134.1 2.5 %collective-permute-start.24 = (f32[64,128]{1,0:T(8,128)S(1)}, f32[64,128]{1,0:T(8,128)S(1)}, u32[]{:S(2)}, u32[]{:S(2)}) collective-permute-start(f32[64,128]{1,0:T(8,128)S(1)} %filter_part.1), channel_id=1, source_target_pairs={{0,8},{8,16},{16,24},{24,0},{1,9},{9,17},{17,25},{25,1},{2,10},{10... | collective-permute-start | bytes 98312 | tf_op jit(solution)/shard_map/ppermute | solution.py:21
  136.7 1.9 %collective-permute-done.21.ahead_ref = bf16[128,1024]{1,0:T(8,128)(2,1)} collective-permute-done((bf16[128,1024]{1,0:T(8,128)(2,1)}, bf16[128,1024]{1,0:T(8,128)(2,1)}, u32[]{:S(2)}, u32[]{:S(2)}) %collective-permute-start.21) | collective-permute-done | bytes 262176 | tf_op jit(solution)/shard_map/ppermute | solution.py:27
  138.5 6.8 %conv_backward.1 = (bf16[512,1024]{1,0:T(8,128)(2,1)}, bf16[512,1024]{1,0:T(8,128)(2,1)}) custom-call(bf16[64,128]{1,0:T(8,128)(2,1)S(1)} %copy-done.24, bf16[512,1024]{1,0:T(8,128)(2,1)S(1)} %get-tuple-element.58.inner_ref, bf16[128,1024]{1,0:T(8,128)(2,1)} %collective-permute-done.21.ahead_ref, bf16[512,1024]{1,0:T(8,128)(2,1)S(1)} %copy-done.4, ...), custom_call_target="tpu_custom_call" | custom-call | flops 1048576 | bytes 262144 | tf_op jit(solution)/shard_map/conv_backward/pallas_call | solution.py:308
  145.4 8.9 %collective-permute-start.25 = (f32[64,128]{1,0:T(8,128)S(1)}, f32[64,128]{1,0:T(8,128)S(1)}, u32[]{:S(2)}, u32[]{:S(2)}) collective-permute-start(f32[64,128]{1,0:T(8,128)S(1)} %select_add_fusion.1), channel_id=1, source_target_pairs={{0,192},{32,224},{64,0},{96,32},{128,64},{160,96},{192,128},{224,1... | collective-permute-start | bytes 98312 | tf_op jit(solution)/shard_map/ppermute | solution.py:21
  154.3 1.1 collective-permute-start.26
  155.3 2.8 %collective-permute-start.27 = (f32[64,128]{1,0:T(8,128)S(1)}, f32[64,128]{1,0:T(8,128)S(1)}, u32[]{:S(2)}, u32[]{:S(2)}) collective-permute-start(f32[64,128]{1,0:T(8,128)S(1)} %select_add_fusion.1), channel_id=1, source_target_pairs={{0,64},{32,96},{64,128},{96,160},{128,192},{160,224},{192,0},{224,... | collective-permute-start | bytes 98312 | tf_op jit(solution)/shard_map/ppermute | solution.py:21
  158.2 4.0 %collective-permute-done.26 = f32[64,128]{1,0:T(8,128)S(1)} collective-permute-done((f32[64,128]{1,0:T(8,128)S(1)}, f32[64,128]{1,0:T(8,128)S(1)}, u32[]{:S(2)}, u32[]{:S(2)}) %collective-permute-start.26) | collective-permute-done | bytes 32800 | tf_op jit(solution)/shard_map/ppermute | solution.py:21
  162.1 1.2 collective-permute-start.28
  163.3 1.8 %convert_element_type.47 = f32[128,1024]{1,0:T(8,128)} convert(bf16[128,1024]{1,0:T(8,128)(2,1)} %reduce-scatter.2.cloned.1.call-done) | non-fusion elementwise | flops 131072 | bytes 786432 | tf_op jit(solution)/shard_map/convert_element_type | solution.py:379
  165.1 1.0 collective-permute-done.28
  (97 shorter events, 12.0 us)
Async XLA Ops:
  7.2 19.6 %copy-start.3 = (bf16[512,1024]{1,0:T(8,128)(2,1)S(1)}, bf16[512,1024]{1,0:T(8,128)(2,1)}, u32[]{:S(2)}) copy-start(bf16[512,1024]{1,0:T(8,128)(2,1)} %k_ref.5) | copy-start | bytes 3145732
  7.2 19.6 %copy-start.5 = (bf16[512,1024]{1,0:T(8,128)(2,1)S(1)}, bf16[512,1024]{1,0:T(8,128)(2,1)}, u32[]{:S(2)}) copy-start(bf16[512,1024]{1,0:T(8,128)(2,1)} %v_ref.5) | copy-start | bytes 3145732
  7.2 19.6 %copy-start.2 = (bf16[512,1024]{1,0:T(8,128)(2,1)S(1)}, bf16[512,1024]{1,0:T(8,128)(2,1)}, u32[]{:S(2)}) copy-start(bf16[512,1024]{1,0:T(8,128)(2,1)} %refs_6_.1) | copy-start | bytes 3145732
  7.2 19.5 %copy-start.24 = (bf16[64,128]{1,0:T(8,128)(2,1)S(1)}, bf16[64,128]{1,0:T(8,128)(2,1)}, u32[]{:S(2)}) copy-start(bf16[64,128]{1,0:T(8,128)(2,1)} %filters_ref.5) | copy-start | bytes 49156
  7.2 57.2 %all-gather.2.cloned.1.call-start = ((), (), s32[]{:S(2)}) async-start(), calls=%async_computation.1 | async-start | bytes 2359296 | tf_op jit(solution)/shard_map/all_gather | solution.py:345
  11.1 9.6 %collective-permute-start = (bf16[512,128]{1,0:T(8,128)(2,1)}, bf16[512,128]{1,0:T(8,128)(2,1)}, u32[]{:S(2)}, u32[]{:S(2)}) collective-permute-start(bf16[512,128]{1,0:T(8,128)(2,1)} %get-tuple-element.68), channel_id=1, source_target_pairs={{0,24},{8,0},{16,8},{24,16},{1,25},{9,1},{17,9},{25,17},{2,26},{10... | collective-permute-start | bytes 393224 | tf_op jit(solution)/shard_map/ppermute | solution.py:21
  11.9 8.7 %collective-permute-start.1 = (bf16[512,128]{1,0:T(8,128)(2,1)}, bf16[512,128]{1,0:T(8,128)(2,1)}, u32[]{:S(2)}, u32[]{:S(2)}) collective-permute-start(bf16[512,128]{1,0:T(8,128)(2,1)} %get-tuple-element.70), channel_id=1, source_target_pairs={{0,16},{8,24},{16,0},{24,8},{1,17},{9,25},{17,1},{25,9},{2,18},{10... | collective-permute-start | bytes 393224 | tf_op jit(solution)/shard_map/ppermute | solution.py:21
  14.7 7.9 %collective-permute-start.2 = (bf16[512,128]{1,0:T(8,128)(2,1)}, bf16[512,128]{1,0:T(8,128)(2,1)}, u32[]{:S(2)}, u32[]{:S(2)}) collective-permute-start(bf16[512,128]{1,0:T(8,128)(2,1)} %get-tuple-element.69), channel_id=1, source_target_pairs={{0,8},{8,16},{16,24},{24,0},{1,9},{9,17},{17,25},{25,1},{2,10},{10... | collective-permute-start | bytes 393224 | tf_op jit(solution)/shard_map/ppermute | solution.py:21
  15.1 11.6 %collective-permute-start.3 = (bf16[128,1024]{1,0:T(8,128)(2,1)}, bf16[128,1024]{1,0:T(8,128)(2,1)S(1)}, u32[]{:S(2)}, u32[]{:S(2)}) collective-permute-start(bf16[128,1024]{1,0:T(8,128)(2,1)} %multiply_convert_fusion), channel_id=1, source_target_pairs={{0,8},{8,16},{16,24},{24,32},{32,40},{40,48},{48,56},{56,64},{64,7... | collective-permute-start | bytes 786440 | tf_op jit(solution)/shard_map/ppermute | solution.py:27
  19.3 144.1 %reduce-scatter.2.cloned.1.call-start = ((), (), s32[]{:S(2)}) async-start(), calls=%async_computation.2 | async-start | bytes 2359296 | tf_op jit(solution)/shard_map/reduce_scatter | solution.py:379
  30.2 13.8 %collective-permute-start.5 = (bf16[2048,128]{1,0:T(8,128)(2,1)S(1)}, bf16[2048,128]{1,0:T(8,128)(2,1)S(1)}, u32[]{:S(2)}, u32[]{:S(2)}) collective-permute-start(bf16[2048,128]{1,0:T(8,128)(2,1)S(1)} %pad_maximum_fusion), channel_id=1, source_target_pairs={{0,2},{2,4},{4,6},{6,0},{1,3},{3,5},{5,7},{7,1},{8,10},{10,12},{12... | collective-permute-start | bytes 1572872 | tf_op jit(solution)/shard_map/ppermute | solution.py:21
  31.9 12.6 %collective-permute-start.4 = (bf16[2048,128]{1,0:T(8,128)(2,1)S(1)}, bf16[2048,128]{1,0:T(8,128)(2,1)S(1)}, u32[]{:S(2)}, u32[]{:S(2)}) collective-permute-start(bf16[2048,128]{1,0:T(8,128)(2,1)S(1)} %pad_maximum_fusion), channel_id=1, source_target_pairs={{0,6},{2,0},{4,2},{6,4},{1,7},{3,1},{5,3},{7,5},{8,14},{10,8},{12,... | collective-permute-start | bytes 1572872 | tf_op jit(solution)/shard_map/ppermute | solution.py:21
  33.5 14.0 %collective-permute-start.7 = (bf16[512,512]{1,0:T(8,128)(2,1)S(1)}, bf16[512,512]{1,0:T(8,128)(2,1)S(1)}, u32[]{:S(2)}, u32[]{:S(2)}) collective-permute-start(bf16[512,512]{1,0:T(8,128)(2,1)S(1)} %get-tuple-element.62.refs_0_), channel_id=1, source_target_pairs={{0,8},{8,16},{16,24},{24,0},{1,9},{9,17},{17,25},{25,1},{2,10},{10... | collective-permute-start | bytes 1572872 | tf_op jit(solution)/shard_map/ppermute | solution.py:21
  33.5 16.1 %collective-permute-start.10 = (bf16[512,512]{1,0:T(8,128)(2,1)S(1)}, bf16[512,512]{1,0:T(8,128)(2,1)S(1)}, u32[]{:S(2)}, u32[]{:S(2)}) collective-permute-start(bf16[512,512]{1,0:T(8,128)(2,1)S(1)} %get-tuple-element.62.refs_0_), channel_id=1, source_target_pairs={{0,24},{8,0},{16,8},{24,16},{1,25},{9,1},{17,9},{25,17},{2,26},{10... | collective-permute-start | bytes 1572872 | tf_op jit(solution)/shard_map/ppermute | solution.py:21
  39.0 19.1 %copy-start.7 = (f32[512,1024]{1,0:T(8,128)}, f32[512,1024]{1,0:T(8,128)S(1)}, u32[]{:S(2)}) copy-start(f32[512,1024]{1,0:T(8,128)S(1)} %get-tuple-element.54.refs_7_) | copy-start | bytes 6291460
  39.0 19.1 %copy-start.10 = (bf16[512,1024]{1,0:T(8,128)(2,1)}, bf16[512,1024]{1,0:T(8,128)(2,1)S(1)}, u32[]{:S(2)}) copy-start(bf16[512,1024]{1,0:T(8,128)(2,1)S(1)} %get-tuple-element.57.mixed_ref) | copy-start | bytes 3145732
  39.1 19.1 %copy-start.18 = (bf16[512,512]{1,0:T(8,128)(2,1)}, bf16[512,512]{1,0:T(8,128)(2,1)S(1)}, u32[]{:S(2)}) copy-start(bf16[512,512]{1,0:T(8,128)(2,1)S(1)} %get-tuple-element.42.refs_1_) | copy-start | bytes 1572868
  39.1 19.0 %collective-permute-start.8 = (bf16[512,512]{1,0:T(8,128)(2,1)S(1)}, bf16[512,512]{1,0:T(8,128)(2,1)S(1)}, u32[]{:S(2)}, u32[]{:S(2)}) collective-permute-start(bf16[512,512]{1,0:T(8,128)(2,1)S(1)} %get-tuple-element.42.refs_1_), channel_id=1, source_target_pairs={{0,24},{8,0},{16,8},{24,16},{1,25},{9,1},{17,9},{25,17},{2,26},{10... | collective-permute-start | bytes 1572872 | tf_op jit(solution)/shard_map/ppermute | solution.py:21
  44.0 14.0 %collective-permute-start.6 = (bf16[1024,128]{1,0:T(8,128)(2,1)S(1)}, bf16[1024,128]{1,0:T(8,128)(2,1)S(1)}, u32[]{:S(2)}, u32[]{:S(2)}) collective-permute-start(bf16[1024,128]{1,0:T(8,128)(2,1)S(1)} %slice.48), channel_id=1, source_target_pairs={{0,2},{2,4},{4,6},{6,0},{1,3},{3,5},{5,7},{7,1},{8,10},{10,12},{12... | collective-permute-start | bytes 786440 | tf_op jit(solution)/shard_map/ppermute | solution.py:21
  44.5 13.6 %collective-permute-start.9 = (bf16[1024,128]{1,0:T(8,128)(2,1)S(1)}, bf16[1024,128]{1,0:T(8,128)(2,1)S(1)}, u32[]{:S(2)}, u32[]{:S(2)}) collective-permute-start(bf16[1024,128]{1,0:T(8,128)(2,1)S(1)} %slice.49), channel_id=1, source_target_pairs={{0,6},{2,0},{4,2},{6,4},{1,7},{3,1},{5,3},{7,5},{8,14},{10,8},{12,... | collective-permute-start | bytes 786440 | tf_op jit(solution)/shard_map/ppermute | solution.py:21
  47.5 11.7 %copy-start.14 = (bf16[512,512]{1,0:T(8,128)(2,1)}, bf16[512,512]{1,0:T(8,128)(2,1)S(1)}, u32[]{:S(2)}) copy-start(bf16[512,512]{1,0:T(8,128)(2,1)S(1)} %collective-permute-done.7.refs_6_) | copy-start | bytes 1572868
  49.6 9.6 %collective-permute-start.11 = (bf16[512,512]{1,0:T(8,128)(2,1)S(1)}, bf16[512,512]{1,0:T(8,128)(2,1)S(1)}, u32[]{:S(2)}, u32[]{:S(2)}) collective-permute-start(bf16[512,512]{1,0:T(8,128)(2,1)S(1)} %get-tuple-element.42.refs_1_), channel_id=1, source_target_pairs={{0,8},{8,16},{16,24},{24,0},{1,9},{9,17},{17,25},{25,1},{2,10},{10... | collective-permute-start | bytes 1572872 | tf_op jit(solution)/shard_map/ppermute | solution.py:21
  60.1 4.3 %collective-permute-start.12 = (bf16[4,2048,128]{2,1,0:T(8,128)(2,1)S(1)}, bf16[4,2048,128]{2,1,0:T(8,128)(2,1)}, u32[]{:S(2)}, u32[]{:S(2)}) collective-permute-start(bf16[4,2048,128]{2,1,0:T(8,128)(2,1)S(1)} %bitcast.9), channel_id=1, source_target_pairs={{0,1},{1,0},{2,3},{3,2},{4,5},{5,4},{6,7},{7,6},{8,9},{9,8},{10,11... | collective-permute-start | bytes 6291464 | tf_op jit(solution)/shard_map/ppermute | solution.py:21
  60.1 15.8 %collective-permute-start.14 = (bf16[512,512]{1,0:T(8,128)(2,1)}, bf16[512,512]{1,0:T(8,128)(2,1)}, u32[]{:S(2)}, u32[]{:S(2)}) collective-permute-start(bf16[512,512]{1,0:T(8,128)(2,1)} %copy-done.20), channel_id=1, source_target_pairs={{0,24},{8,0},{16,8},{24,16},{1,25},{9,1},{17,9},{25,17},{2,26},{10... | collective-permute-start | bytes 1572872 | tf_op jit(solution)/shard_map/ppermute | solution.py:21
  62.0 15.1 %collective-permute-start.13 = (bf16[512,512]{1,0:T(8,128)(2,1)}, bf16[512,512]{1,0:T(8,128)(2,1)}, u32[]{:S(2)}, u32[]{:S(2)}) collective-permute-start(bf16[512,512]{1,0:T(8,128)(2,1)} %copy-done.14), channel_id=1, source_target_pairs={{0,8},{8,16},{16,24},{24,0},{1,9},{9,17},{17,25},{25,1},{2,10},{10... | collective-permute-start | bytes 1572872 | tf_op jit(solution)/shard_map/ppermute | solution.py:21
  70.7 20.8 %collective-permute-start.15 = (bf16[512,512]{1,0:T(8,128)(2,1)}, bf16[512,512]{1,0:T(8,128)(2,1)}, u32[]{:S(2)}, u32[]{:S(2)}) collective-permute-start(bf16[512,512]{1,0:T(8,128)(2,1)} %get-tuple-element.44), channel_id=1, source_target_pairs={{0,8},{8,16},{16,24},{24,0},{1,9},{9,17},{17,25},{25,1},{2,10},{10... | collective-permute-start | bytes 1572872 | tf_op jit(solution)/shard_map/ppermute | solution.py:21
  72.2 10.8 %copy-start.13 = (bf16[512,512]{1,0:T(8,128)(2,1)S(1)}, bf16[512,512]{1,0:T(8,128)(2,1)}, u32[]{:S(2)}) copy-start(bf16[512,512]{1,0:T(8,128)(2,1)} %copy-done.12) | copy-start | bytes 1572868
  72.2 10.8 %copy-start.15 = (bf16[512,512]{1,0:T(8,128)(2,1)S(1)}, bf16[512,512]{1,0:T(8,128)(2,1)}, u32[]{:S(2)}) copy-start(bf16[512,512]{1,0:T(8,128)(2,1)} %copy-done.14) | copy-start | bytes 1572868
  72.2 10.8 %copy-start.17 = (bf16[512,512]{1,0:T(8,128)(2,1)S(1)}, bf16[512,512]{1,0:T(8,128)(2,1)}, u32[]{:S(2)}) copy-start(bf16[512,512]{1,0:T(8,128)(2,1)} %copy-done.16) | copy-start | bytes 1572868
  72.2 10.8 %copy-start.19 = (bf16[512,512]{1,0:T(8,128)(2,1)S(1)}, bf16[512,512]{1,0:T(8,128)(2,1)}, u32[]{:S(2)}) copy-start(bf16[512,512]{1,0:T(8,128)(2,1)} %copy-done.18) | copy-start | bytes 1572868
  72.2 10.8 %copy-start.21 = (bf16[512,512]{1,0:T(8,128)(2,1)S(1)}, bf16[512,512]{1,0:T(8,128)(2,1)}, u32[]{:S(2)}) copy-start(bf16[512,512]{1,0:T(8,128)(2,1)} %copy-done.20) | copy-start | bytes 1572868
  72.2 10.8 %copy-start.23 = (bf16[512,512]{1,0:T(8,128)(2,1)S(1)}, bf16[512,512]{1,0:T(8,128)(2,1)}, u32[]{:S(2)}) copy-start(bf16[512,512]{1,0:T(8,128)(2,1)} %copy-done.22) | copy-start | bytes 1572868
  72.3 19.2 %collective-permute-start.16 = (bf16[512,512]{1,0:T(8,128)(2,1)}, bf16[512,512]{1,0:T(8,128)(2,1)}, u32[]{:S(2)}, u32[]{:S(2)}) collective-permute-start(bf16[512,512]{1,0:T(8,128)(2,1)} %get-tuple-element.45), channel_id=1, source_target_pairs={{0,24},{8,0},{16,8},{24,16},{1,25},{9,1},{17,9},{25,17},{2,26},{10... | collective-permute-start | bytes 1572872 | tf_op jit(solution)/shard_map/ppermute | solution.py:21
  91.5 15.8 %collective-permute-start.18 = (bf16[512,512]{1,0:T(8,128)(2,1)}, bf16[512,512]{1,0:T(8,128)(2,1)S(1)}, u32[]{:S(2)}, u32[]{:S(2)}) collective-permute-start(bf16[512,512]{1,0:T(8,128)(2,1)} %copy-done.26), channel_id=1, source_target_pairs={{0,24},{8,0},{16,8},{24,16},{1,25},{9,1},{17,9},{25,17},{2,26},{10... | collective-permute-start | bytes 1572872 | tf_op jit(solution)/shard_map/ppermute | solution.py:21
  91.9 15.7 %collective-permute-start.19 = (bf16[512,512]{1,0:T(8,128)(2,1)}, bf16[512,512]{1,0:T(8,128)(2,1)S(1)}, u32[]{:S(2)}, u32[]{:S(2)}) collective-permute-start(bf16[512,512]{1,0:T(8,128)(2,1)} %copy-done.25), channel_id=1, source_target_pairs={{0,8},{8,16},{16,24},{24,0},{1,9},{9,17},{17,25},{25,1},{2,10},{10... | collective-permute-start | bytes 1572872 | tf_op jit(solution)/shard_map/ppermute | solution.py:21
  101.1 14.7 %collective-permute-start.17 = (bf16[512,512]{1,0:T(8,128)(2,1)S(1)}, bf16[512,512]{1,0:T(8,128)(2,1)S(1)}, u32[]{:S(2)}, u32[]{:S(2)}) collective-permute-start(bf16[512,512]{1,0:T(8,128)(2,1)S(1)} %get-tuple-element.48), channel_id=1, source_target_pairs={{0,8},{8,16},{16,24},{24,0},{1,9},{9,17},{17,25},{25,1},{2,10},{10... | collective-permute-start | bytes 1572872 | tf_op jit(solution)/shard_map/ppermute | solution.py:21
  102.6 13.9 %collective-permute-start.20 = (bf16[512,512]{1,0:T(8,128)(2,1)S(1)}, bf16[512,512]{1,0:T(8,128)(2,1)S(1)}, u32[]{:S(2)}, u32[]{:S(2)}) collective-permute-start(bf16[512,512]{1,0:T(8,128)(2,1)S(1)} %get-tuple-element.52), channel_id=1, source_target_pairs={{0,24},{8,0},{16,8},{24,16},{1,25},{9,1},{17,9},{25,17},{2,26},{10... | collective-permute-start | bytes 1572872 | tf_op jit(solution)/shard_map/ppermute | solution.py:21
  107.3 12.9 %copy-start.8 = (f32[512,1024]{1,0:T(8,128)S(1)}, f32[512,1024]{1,0:T(8,128)}, u32[]{:S(2)}) copy-start(f32[512,1024]{1,0:T(8,128)} %copy-done.7) | copy-start | bytes 6291460
  117.4 21.1 %collective-permute-start.21 = (bf16[128,1024]{1,0:T(8,128)(2,1)}, bf16[128,1024]{1,0:T(8,128)(2,1)}, u32[]{:S(2)}, u32[]{:S(2)}) collective-permute-start(bf16[128,1024]{1,0:T(8,128)(2,1)} %pad_maximum_fusion.1), channel_id=1, source_target_pairs={{8,0},{16,8},{24,16},{32,24},{40,32},{48,40},{56,48},{64,56},{72,6... | collective-permute-start | bytes 786440 | tf_op jit(solution)/shard_map/ppermute | solution.py:27
  122.7 15.9 %copy-start.4 = (bf16[512,1024]{1,0:T(8,128)(2,1)S(1)}, bf16[512,1024]{1,0:T(8,128)(2,1)}, u32[]{:S(2)}) copy-start(bf16[512,1024]{1,0:T(8,128)(2,1)} %k_ref.5) | copy-start | bytes 3145732
  122.7 15.9 %copy-start.6 = (bf16[512,1024]{1,0:T(8,128)(2,1)S(1)}, bf16[512,1024]{1,0:T(8,128)(2,1)}, u32[]{:S(2)}) copy-start(bf16[512,1024]{1,0:T(8,128)(2,1)} %v_ref.5) | copy-start | bytes 3145732
  130.4 14.9 %collective-permute-start.22 = (f32[64,128]{1,0:T(8,128)S(1)}, f32[64,128]{1,0:T(8,128)S(1)}, u32[]{:S(2)}, u32[]{:S(2)}) collective-permute-start(f32[64,128]{1,0:T(8,128)S(1)} %filter_part.1), channel_id=1, source_target_pairs={{0,24},{8,0},{16,8},{24,16},{1,25},{9,1},{17,9},{25,17},{2,26},{10... | collective-permute-start | bytes 98312 | tf_op jit(solution)/shard_map/ppermute | solution.py:21
  132.2 13.1 %collective-permute-start.23 = (f32[64,128]{1,0:T(8,128)S(1)}, f32[64,128]{1,0:T(8,128)S(1)}, u32[]{:S(2)}, u32[]{:S(2)}) collective-permute-start(f32[64,128]{1,0:T(8,128)S(1)} %filter_part.1), channel_id=1, source_target_pairs={{0,16},{8,24},{16,0},{24,8},{1,17},{9,25},{17,1},{25,9},{2,18},{10... | collective-permute-start | bytes 98312 | tf_op jit(solution)/shard_map/ppermute | solution.py:21
  134.1 11.2 %collective-permute-start.24 = (f32[64,128]{1,0:T(8,128)S(1)}, f32[64,128]{1,0:T(8,128)S(1)}, u32[]{:S(2)}, u32[]{:S(2)}) collective-permute-start(f32[64,128]{1,0:T(8,128)S(1)} %filter_part.1), channel_id=1, source_target_pairs={{0,8},{8,16},{16,24},{24,0},{1,9},{9,17},{17,25},{25,1},{2,10},{10... | collective-permute-start | bytes 98312 | tf_op jit(solution)/shard_map/ppermute | solution.py:21
  145.4 12.8 %collective-permute-start.25 = (f32[64,128]{1,0:T(8,128)S(1)}, f32[64,128]{1,0:T(8,128)S(1)}, u32[]{:S(2)}, u32[]{:S(2)}) collective-permute-start(f32[64,128]{1,0:T(8,128)S(1)} %select_add_fusion.1), channel_id=1, source_target_pairs={{0,192},{32,224},{64,0},{96,32},{128,64},{160,96},{192,128},{224,1... | collective-permute-start | bytes 98312 | tf_op jit(solution)/shard_map/ppermute | solution.py:21
  154.3 7.8 %collective-permute-start.26 = (f32[64,128]{1,0:T(8,128)S(1)}, f32[64,128]{1,0:T(8,128)S(1)}, u32[]{:S(2)}, u32[]{:S(2)}) collective-permute-start(f32[64,128]{1,0:T(8,128)S(1)} %select_add_fusion.1), channel_id=1, source_target_pairs={{0,128},{32,160},{64,192},{96,224},{128,0},{160,32},{192,64},{224,... | collective-permute-start | bytes 98312 | tf_op jit(solution)/shard_map/ppermute | solution.py:21
  155.3 6.8 %collective-permute-start.27 = (f32[64,128]{1,0:T(8,128)S(1)}, f32[64,128]{1,0:T(8,128)S(1)}, u32[]{:S(2)}, u32[]{:S(2)}) collective-permute-start(f32[64,128]{1,0:T(8,128)S(1)} %select_add_fusion.1), channel_id=1, source_target_pairs={{0,64},{32,96},{64,128},{96,160},{128,192},{160,224},{192,0},{224,... | collective-permute-start | bytes 98312 | tf_op jit(solution)/shard_map/ppermute | solution.py:21
  162.1 4.0 %collective-permute-start.28 = (f32[64,128]{1,0:T(8,128)S(1)}, f32[64,128]{1,0:T(8,128)S(1)}, u32[]{:S(2)}, u32[]{:S(2)}) collective-permute-start(f32[64,128]{1,0:T(8,128)S(1)} %select_add_fusion), channel_id=1, source_target_pairs={{0,32},{32,0},{64,96},{96,64},{128,160},{160,128},{192,224},{224,1... | collective-permute-start | bytes 98312 | tf_op jit(solution)/shard_map/ppermute | solution.py:401
  (10 other events, 30.9 us)
Sparse Core Ops, SparseCore 0:
  19.4 43.1 all-gather.1
  91.7 47.6 reduce-scatter.1

commit v5 on v4

--- a/solution.py
+++ b/solution.py
@@ -270,10 +270,7 @@
         )[:, taps:]
         for g in range(groups)
     ]
-    turn = anti_identity(taps).astype(F32)
-    filter_ref[...] = jnp.dot(
-        jnp.concatenate(sums, 0), turn, precision=lax.Precision.HIGHEST, preferred_element_type=F32
-    )
+    filter_ref[...] = jnp.concatenate(sums, 0)
 
 
 def filter_part(inner, mixed, rim, group_count):
@@ -293,34 +290,45 @@
     )(inner, mixed, rim)
 
 
-def backward_body(taps, groups, filters_ref, inner_ref, ahead_ref, k_ref, v_ref, gk_ref, gv_ref):
+def backward_body(taps, groups, filters_ref, inner_ref, ahead_ref, k_ref, v_ref, *refs):
+    gk_ref, gv_ref = refs[-2:]
     window = jnp.concatenate([inner_ref[...], ahead_ref[...]], 0)
     grad = banded(group_tables(filters_ref[...], False), window, taps, groups)
     gk_ref[...] = (grad * v_ref[...].astype(F32)).astype(BF16)
     gv_ref[...] = (grad * k_ref[...].astype(F32)).astype(BF16)
 
 
-def backward(filters, inner, ahead, k, v):
+def backward(half, filters, inner, ahead, k, v, earlier):
     tokens, width = k.shape
     taps = ahead.shape[0]
     groups = LANES * filters.shape[0] // width
-    column = pl.BlockSpec((tokens, LANES), lambda i: (0, i))
+    steps = width // LANES // 2
+    at = lambda i: (0, i + half * steps)
+    column = pl.BlockSpec((tokens, LANES), at)
+    in_specs = [
+        pl.BlockSpec((groups, taps), lambda i: (i + half * steps, 0)),
+        column,
+        pl.BlockSpec((taps, LANES), at),
+        column,
+        column,
+    ]
+    args = [filters, inner, ahead, k, v]
+    aliases = {}
+    if earlier is not None:
+        in_specs += [pl.BlockSpec(memory_space=pl.ANY)] * 2
+        args += list(earlier)
+        aliases = {5: 0, 6: 1}
     return pl.pallas_call(
         functools.partial(backward_body, taps, groups),
-        grid=(width // LANES,),
-        in_specs=[
-            pl.BlockSpec((groups, taps), lambda i: (i, 0)),
-            column,
-            pl.BlockSpec((taps, LANES), lambda i: (0, i)),
-            column,
-            column,
-        ],
+        grid=(steps,),
+        in_specs=in_specs,
         out_specs=[column, column],
         out_shape=[jax.ShapeDtypeStruct((tokens, width), BF16)] * 2,
+        input_output_aliases=aliases,
         compiler_params=pltpu.CompilerParams(vmem_limit_bytes=16 * MIB),
         cost_estimate=LIGHT,
         name="conv_backward",
-    )(filters, inner, ahead, k, v)
+    )(*args)
 
 
 def sum_over(value, axis, stride, *beside):
@@ -375,11 +383,11 @@
     from_left_b, from_right_a = send(beside[0], "x", 1), send(beside[1], "x", -1)
     gated[0] = after(gated[0], *beside)
     proj_sums = proj_part(place, mine, sib, gated)
-    proj_sums = after(proj_sums, far_a, far_b)
-    grad_proj = lax.psum_scatter(proj_sums, "z", scatter_dimension=0, tiled=True).astype(F32)
 
     joined = gate_parts(place, mine, sib, proj, ((1, 0), (3, 1)), BF16, far_a, far_b)
     from_left_a, from_right_b = send(joined[0], "x", 1), send(joined[1], "x", -1)
+    proj_sums = after(proj_sums, from_left_b, from_right_a, joined[0])
+    grad_proj = lax.psum_scatter(proj_sums, "z", scatter_dimension=0, tiled=True).astype(F32)
     own = gate_parts(place, mine, sib, proj, ((0, 0), (0, 1)), F32)
     from_left, from_right = (from_left_a, from_left_b), (from_right_a, from_right_b)
 
@@ -396,10 +404,12 @@
         (after(own[0], first), own[1]), from_left, from_right, query_in, conv
     )
     sums = filter_part(inner, mixed, rim, group_count)
-    grad_key, grad_value = backward(filters, after(inner, sums), ahead, key_in, value_in)
-    sums = sum_over(sum_over(sums, "x", 1, grad_key), "z", 2)
+    grads = backward(0, filters, after(inner, sums), ahead, key_in, value_in, None)
+    sums = sum_over(sums, "x", 1, *grads)
+    grad_key, grad_value = backward(1, filters, after(inner, sums), ahead, key_in, value_in, grads)
+    sums = sum_over(sums, "z", 2, grad_key)
     odd = lax.ppermute(sums, "z", [(i, i ^ 1) for i in range(lax.axis_size("z"))])
-    grad_filter = after(sums, grad_proj) + odd
+    grad_filter = jnp.flip(after(sums, grad_proj) + odd, 1)
     return grad_query, grad_key, grad_value, grad_filter, grad_proj
 
 

time: 175 us -> 172 us (0.983)
  waiting for transfers between devices: 42.3 us -> 37.4 us
  starting transfers between devices: 52.4 us -> 50.1 us
  local copies, waits for them, and re-layouts: 9.3 us -> 11.5 us
    ppermute x26, waiting for transfers between devices: 36.4 us -> 30.5 us  [send(): lax.ppermute(value, axis, [(i, (i + by) % count) for i in range(count)])]
    ppermute x26, starting transfers between devices: 44.3 us -> 42.1 us  [send(): lax.ppermute(value, axis, [(i, (i + by) % count) for i in range(count)])]
    pallas_call x1, Pallas kernels: 7.74 us -> 5.68 us  [filter_part(): pl.pallas_call(functools.partial(filter_body, taps, groups), grid=(width...]
    ppermute x2, waiting for transfers between devices: 4.87 us -> 6.65 us  [send_along_tokens(): return lax.ppermute(value, ('z', 'x'), pairs)]
    unnamed x58 -> x52, local copies, waits for them, and re-layouts: 7.25 us -> 8.79 us
    pallas_call x1 -> x2, Pallas kernels: 6.76 us -> 8.05 us  [backward(): pl.pallas_call(functools.partial(backward_body, taps, groups), grid=(step...]
  transfers between devices with their start and end apart: 31 -> 31, of which waited for: 16 -> 15; matrix products, arithmetic and copies ran while one was open for 2% -> 3% of each run, Pallas kernels for 28% -> 30%
where the time goes in v5:
time: 172 us; the launch traced here: 171 us
  Pallas kernels  50.4 us (29%)
  starting transfers between devices  50.1 us (29%)
  waiting for transfers between devices  37.4 us (22%)
  between operations  14.4 us (8%)
  local copies, waits for them, and re-layouts  11.5 us (7%)
  other arithmetic  6.71 us (4%)
    ppermute x26, starting transfers between devices, send(): lax.ppermute(value, axis, [(i, (i + by) % count) for i in range(count)])  42.1 us
    ppermute x26, waiting for transfers between devices, send(): lax.ppermute(value, axis, [(i, (i + by) % count) for i in range(count)])  30.5 us
    pallas_call x4, Pallas kernels, gate_parts(): pl.pallas_call(gate_body, grid_spec=spec, out_shape=[jax.ShapeDtypeStruct...  18.5 us
    unnamed x52, local copies, waits for them, and re-layouts  8.79 us
    pallas_call x2, Pallas kernels, backward(): pl.pallas_call(functools.partial(backward_body, taps, groups), grid=(step...  8.05 us
    pallas_call x1, Pallas kernels, proj_part(): pl.pallas_call(proj_body, grid_spec=spec, out_shape=jax.ShapeDtypeStruct(...  7.42 us
    pallas_call x2, Pallas kernels, forward(): pl.pallas_call(functools.partial(forward_body, taps, groups), grid=(steps...  6.9 us
    ppermute x2, waiting for transfers between devices, send_along_tokens(): return lax.ppermute(value, ('z', 'x'), pairs)  6.65 us
  transfers between devices with their start and end apart: 31, of which 15 were waited for; matrix products, arithmetic and copies ran while one was open for 3% of the time, Pallas kernels for 30%

profile of v5, /device:TPU:6, one launch (start us, length us, event | category | flops | bytes accessed | tf_op | source)
XLA Modules:
  0.0 170.6 jit_solution(2910825149537724925)
XLA Ops:
  7.3 2.0 %multiply_convert_fusion = bf16[128,1024]{1,0:T(8,128)(2,1)} fusion(bf16[512,1024]{1,0:T(8,128)(2,1)} %v_ref.7, bf16[512,1024]{1,0:T(8,128)(2,1)} %k_ref.7), kind=kLoop, calls=%fused_computation.1 | loop fusion | flops 524288 | bytes 786432 | tf_op jit(solution)/shard_map/convert_element_type | solution.py:35
  9.2 1.9 %constant_dynamic-slice_fusion.3 = (bf16[512,128]{1,0:T(8,128)(2,1)S(1)}, bf16[512,128]{1,0:T(8,128)(2,1)}, bf16[512,128]{1,0:T(8,128)(2,1)}, bf16[512,128]{1,0:T(8,128)(2,1)}) fusion(bf16[512,512]{1,0:T(8,128)(2,1)} %param.11, s32[]{:T(128)S(6)} %select_n.275, s32[]{:T(128)S(6)} %select_n.277, s32[]{:T(128)S(6)} %select_n.281, s32[]{:T(128)S(6)} %select_n.279), kind=kLoop, calls=%fused_computation.15 | loop fusion | bytes 1048592 | tf_op jit(solution)/shard_map/dynamic_slice | solution.py:358
  11.9 2.8 %collective-permute-start.1 = (bf16[512,128]{1,0:T(8,128)(2,1)}, bf16[512,128]{1,0:T(8,128)(2,1)}, u32[]{:S(2)}, u32[]{:S(2)}) collective-permute-start(bf16[512,128]{1,0:T(8,128)(2,1)} %get-tuple-element.78), channel_id=1, source_target_pairs={{0,16},{8,24},{16,0},{24,8},{1,17},{9,25},{17,1},{25,9},{2,18},{10... | collective-permute-start | bytes 393224 | tf_op jit(solution)/shard_map/ppermute | solution.py:21
  15.1 4.1 %collective-permute-start.3 = (bf16[128,1024]{1,0:T(8,128)(2,1)}, bf16[128,1024]{1,0:T(8,128)(2,1)S(1)}, u32[]{:S(2)}, u32[]{:S(2)}) collective-permute-start(bf16[128,1024]{1,0:T(8,128)(2,1)} %multiply_convert_fusion), channel_id=1, source_target_pairs={{0,8},{8,16},{16,24},{24,32},{32,40},{40,48},{48,56},{56,64},{64,7... | collective-permute-start | bytes 786440 | tf_op jit(solution)/shard_map/ppermute | solution.py:27
  19.3 1.3 collective-permute-done
  20.6 2.0 %collective-permute-done.2 = bf16[512,128]{1,0:T(8,128)(2,1)} collective-permute-done((bf16[512,128]{1,0:T(8,128)(2,1)}, bf16[512,128]{1,0:T(8,128)(2,1)}, u32[]{:S(2)}, u32[]{:S(2)}) %collective-permute-start.2) | collective-permute-done | bytes 131104 | tf_op jit(solution)/shard_map/ppermute | solution.py:21
  22.7 1.1 pad_maximum_fusion
  23.8 3.0 %collective-permute-done.3.rim_ref = bf16[128,1024]{1,0:T(8,128)(2,1)S(1)} collective-permute-done((bf16[128,1024]{1,0:T(8,128)(2,1)}, bf16[128,1024]{1,0:T(8,128)(2,1)S(1)}, u32[]{:S(2)}, u32[]{:S(2)}) %collective-permute-start.3) | collective-permute-done | bytes 262176 | tf_op jit(solution)/shard_map/ppermute | solution.py:27
  26.8 3.4 %conv_forward.2 = (f32[512,1024]{1,0:T(8,128)S(1)}, bf16[512,1024]{1,0:T(8,128)(2,1)S(1)}, bf16[512,512]{1,0:T(8,128)(2,1)S(1)}) custom-call(bf16[64,128]{1,0:T(8,128)(2,1)S(1)} %copy-done.21, bf16[512,1024]{1,0:T(8,128)(2,1)S(1)} %copy-done.3, bf16[512,1024]{1,0:T(8,128)(2,1)S(1)} %copy-done.4, bf16[512,1024]{1,0:T(8,128)(2,1)S(1)} %copy-done.6, ...), custom_call_target="tpu_custom_call" | custom-call | flops 1048576 | bytes 262144 | tf_op jit(solution)/shard_map/conv_forward/pallas_call | solution.py:105
  30.2 1.7 collective-permute-start.5
  31.9 1.7 collective-permute-start.4
  33.5 2.0 %collective-permute-start.10 = (bf16[512,512]{1,0:T(8,128)(2,1)S(1)}, bf16[512,512]{1,0:T(8,128)(2,1)S(1)}, u32[]{:S(2)}, u32[]{:S(2)}) collective-permute-start(bf16[512,512]{1,0:T(8,128)(2,1)S(1)} %get-tuple-element.70.refs_0_), channel_id=1, source_target_pairs={{0,24},{8,0},{16,8},{24,16},{1,25},{9,1},{17,9},{25,17},{2,26},{10... | collective-permute-start | bytes 1572872 | tf_op jit(solution)/shard_map/ppermute | solution.py:21
  35.5 3.5 %conv_forward.3 = (f32[512,1024]{1,0:T(8,128)S(1)}, bf16[512,1024]{1,0:T(8,128)(2,1)S(1)}, bf16[512,512]{1,0:T(8,128)(2,1)S(1)}) custom-call(bf16[64,128]{1,0:T(8,128)(2,1)S(1)} %copy-done.21, bf16[512,1024]{1,0:T(8,128)(2,1)S(1)} %copy-done.3, bf16[512,1024]{1,0:T(8,128)(2,1)S(1)} %copy-done.4, ...), custom_call_target="tpu_custom_call", output_to_operand_aliasing={{0}: (5, {}), {1}: (6, {})} | custom-call | flops 1048576 | bytes 262144 | tf_op jit(solution)/shard_map/conv_forward/pallas_call | solution.py:105
  39.9 4.1 %collective-permute-done.5 = bf16[2048,128]{1,0:T(8,128)(2,1)S(1)} collective-permute-done((bf16[2048,128]{1,0:T(8,128)(2,1)S(1)}, bf16[2048,128]{1,0:T(8,128)(2,1)S(1)}, u32[]{:S(2)}, u32[]{:S(2)}) %collective-permute-start.5) | collective-permute-done | bytes 524320 | tf_op jit(solution)/shard_map/ppermute | solution.py:21
  44.5 3.0 %collective-permute-start.9 = (bf16[1024,128]{1,0:T(8,128)(2,1)S(1)}, bf16[1024,128]{1,0:T(8,128)(2,1)S(1)}, u32[]{:S(2)}, u32[]{:S(2)}) collective-permute-start(bf16[1024,128]{1,0:T(8,128)(2,1)S(1)} %slice.49), channel_id=1, source_target_pairs={{0,6},{2,0},{4,2},{6,4},{1,7},{3,1},{5,3},{7,5},{8,14},{10,8},{12,... | collective-permute-start | bytes 786440 | tf_op jit(solution)/shard_map/ppermute | solution.py:21
  47.5 2.1 %collective-permute-done.10.refs_2_ = bf16[512,512]{1,0:T(8,128)(2,1)S(1)} collective-permute-done((bf16[512,512]{1,0:T(8,128)(2,1)S(1)}, bf16[512,512]{1,0:T(8,128)(2,1)S(1)}, u32[]{:S(2)}, u32[]{:S(2)}) %collective-permute-start.10) | collective-permute-done | bytes 524320 | tf_op jit(solution)/shard_map/ppermute | solution.py:21
  50.4 7.7 %collective-permute-done.8.refs_3_ = bf16[512,512]{1,0:T(8,128)(2,1)} collective-permute-done((bf16[512,512]{1,0:T(8,128)(2,1)S(1)}, bf16[512,512]{1,0:T(8,128)(2,1)}, u32[]{:S(2)}, u32[]{:S(2)}) %collective-permute-start.8) | collective-permute-done | bytes 524320 | tf_op jit(solution)/shard_map/ppermute | solution.py:21
  60.0 1.7 %collective-permute-start.14 = (bf16[512,512]{1,0:T(8,128)(2,1)}, bf16[512,512]{1,0:T(8,128)(2,1)}, u32[]{:S(2)}, u32[]{:S(2)}) collective-permute-start(bf16[512,512]{1,0:T(8,128)(2,1)} %collective-permute-done.8.refs_3_), channel_id=1, source_target_pairs={{0,24},{8,0},{16,8},{24,16},{1,25},{9,1},{17,9},{25,17},{2,26},{10... | collective-permute-start | bytes 1572872 | tf_op jit(solution)/shard_map/ppermute | solution.py:21
  61.8 1.5 collective-permute-start.13
  63.4 1.0 collective-permute-done.12.sib_ref
  64.3 1.6 copy-done
  65.9 4.8 %grad_gate_parts.4 = (bf16[512,512]{1,0:T(8,128)(2,1)}, bf16[512,512]{1,0:T(8,128)(2,1)}) custom-call(s32[8]{0:T(128)S(1)} %stack.35.place_ref, bf16[4,2048,128]{2,1,0:T(8,128)(2,1)S(1)} %bitcast.10, bf16[4,2048,128]{2,1,0:T(8,128)(2,1)} %collective-permute-done.12.sib_ref, bf16[1024,1024]{1,0:T(8,128)(2,1)S(1)} %copy-done), custom_call_target="tpu_custom_call" | custom-call | flops 1048576 | bytes 262144 | tf_op jit(solution)/shard_map/grad_gate_parts/pallas_call | solution.py:174
  70.7 1.5 collective-permute-start.15
  72.8 3.1 %collective-permute-done.14.refs_5_ = bf16[512,512]{1,0:T(8,128)(2,1)} collective-permute-done((bf16[512,512]{1,0:T(8,128)(2,1)}, bf16[512,512]{1,0:T(8,128)(2,1)}, u32[]{:S(2)}, u32[]{:S(2)}) %collective-permute-start.14) | collective-permute-done | bytes 524320 | tf_op jit(solution)/shard_map/ppermute | solution.py:21
  76.9 5.0 %grad_gate_parts.7 = (bf16[512,512]{1,0:T(8,128)(2,1)}, bf16[512,512]{1,0:T(8,128)(2,1)}) custom-call(s32[8]{0:T(128)S(1)} %stack.35.place_ref, bf16[4,2048,128]{2,1,0:T(8,128)(2,1)S(1)} %bitcast.11, bf16[4,2048,128]{2,1,0:T(8,128)(2,1)} %collective-permute-done.12.sib_ref, bf16[1024,1024]{1,0:T(8,128)(2,1)S(1)} %copy-done), custom_call_target="tpu_custom_call" | custom-call | flops 1048576 | bytes 262144 | tf_op jit(solution)/shard_map/grad_gate_parts/pallas_call | solution.py:174
  81.9 3.2 %collective-permute-start.19 = (bf16[512,512]{1,0:T(8,128)(2,1)}, bf16[512,512]{1,0:T(8,128)(2,1)}, u32[]{:S(2)}, u32[]{:S(2)}) collective-permute-start(bf16[512,512]{1,0:T(8,128)(2,1)} %get-tuple-element.55), channel_id=1, source_target_pairs={{0,8},{8,16},{16,24},{24,0},{1,9},{9,17},{17,25},{25,1},{2,10},{10... | collective-permute-start | bytes 1572872 | tf_op jit(solution)/shard_map/ppermute | solution.py:21
  85.1 7.4 %grad_proj_part.1 = bf16[1024,1024]{1,0:T(8,128)(2,1)S(1)} custom-call(s32[8]{0:T(128)S(1)} %stack.35.place_ref, bf16[4,2048,128]{2,1,0:T(8,128)(2,1)S(1)} %bitcast.12, bf16[4,2048,128]{2,1,0:T(8,128)(2,1)} %collective-permute-done.12.sib_ref, bf16[512,512]{1,0:T(8,128)(2,1)S(1)} %copy-done.14, bf16[512,512]{1,0:T(8,128)(2,1)S(1)} %copy-done.18, ...), custom_call_target="tpu_custom_call" | custom-call | flops 1048576 | bytes 262144 | tf_op jit(solution)/shard_map/grad_proj_part/pallas_call | solution.py:215
  92.6 1.4 copy-done.10
  93.9 1.6 copy-done.1
  95.5 4.6 %grad_gate_parts.6 = (bf16[512,512]{1,0:T(8,128)(2,1)S(1)}, bf16[512,512]{1,0:T(8,128)(2,1)S(1)}) custom-call(s32[8]{0:T(128)S(1)} %stack.35.place_ref, bf16[4,2048,128]{2,1,0:T(8,128)(2,1)S(1)} %bitcast.13, bf16[4,2048,128]{2,1,0:T(8,128)(2,1)} %collective-permute-done.12.sib_ref, bf16[1024,1024]{1,0:T(8,128)(2,1)S(1)} %copy-done.1, ...), custom_call_target="tpu_custom_call" | custom-call | flops 1048576 | bytes 262144 | tf_op jit(solution)/shard_map/grad_gate_parts/pallas_call | solution.py:174
  101.8 1.6 collective-permute-start.17
  103.9 1.6 copy-done.2
  105.5 4.1 %grad_gate_parts.5 = (f32[512,512]{1,0:T(8,128)S(1)}, f32[512,512]{1,0:T(8,128)S(1)}) custom-call(s32[8]{0:T(128)S(1)} %stack.35.place_ref, bf16[4,2048,128]{2,1,0:T(8,128)(2,1)S(1)} %bitcast.14, bf16[4,2048,128]{2,1,0:T(8,128)(2,1)} %collective-permute-done.12.sib_ref, bf16[1024,1024]{1,0:T(8,128)(2,1)S(1)} %copy-done.2), custom_call_target="tpu_custom_call" | custom-call | flops 1048576 | bytes 262144 | tf_op jit(solution)/shard_map/grad_gate_parts/pallas_call | solution.py:174
  109.6 4.5 %collective-permute-done.17.refs_2_ = bf16[512,512]{1,0:T(8,128)(2,1)S(1)} collective-permute-done((bf16[512,512]{1,0:T(8,128)(2,1)}, bf16[512,512]{1,0:T(8,128)(2,1)S(1)}, u32[]{:S(2)}, u32[]{:S(2)}) %collective-permute-start.17) | collective-permute-done | bytes 524320 | tf_op jit(solution)/shard_map/ppermute | solution.py:21
  114.1 2.4 %collective-permute-done.20.refs_5_ = bf16[512,512]{1,0:T(8,128)(2,1)S(1)} collective-permute-done((bf16[512,512]{1,0:T(8,128)(2,1)}, bf16[512,512]{1,0:T(8,128)(2,1)S(1)}, u32[]{:S(2)}, u32[]{:S(2)}) %collective-permute-start.20) | collective-permute-done | bytes 524320 | tf_op jit(solution)/shard_map/ppermute | solution.py:21
  116.5 1.1 multiply_convert_fusion.2
  118.3 1.9 %collective-permute-start.24 = (bf16[128,1024]{1,0:T(8,128)(2,1)}, bf16[128,1024]{1,0:T(8,128)(2,1)}, u32[]{:S(2)}, u32[]{:S(2)}) collective-permute-start(bf16[128,1024]{1,0:T(8,128)(2,1)} %pad_maximum_fusion.1), channel_id=1, source_target_pairs={{8,0},{16,8},{24,16},{32,24},{40,32},{48,40},{56,48},{64,56},{72,6... | collective-permute-start | bytes 786440 | tf_op jit(solution)/shard_map/ppermute | solution.py:27
  120.3 3.9 %gate_gradients.1 = (bf16[512,1024]{1,0:T(8,128)(2,1)}, bf16[512,1024]{1,0:T(8,128)(2,1)S(1)}) custom-call(f32[512,512]{1,0:T(8,128)S(1)} %get-tuple-element.57.refs_0_, f32[512,512]{1,0:T(8,128)S(1)} %get-tuple-element.54.refs_1_, bf16[512,512]{1,0:T(8,128)(2,1)S(1)} %collective-permute-done.17.refs_2_, bf16[512,512]{1,0:T(8,128)(2,1)} %collective-permute-done.19.refs_3_, ...), custom_call_target="tpu_custom_call" | custom-call | flops 1048576 | bytes 262144 | tf_op jit(solution)/shard_map/gate_gradients/pallas_call | solution.py:242
  124.2 5.7 %filter_part.1 = f32[64,128]{1,0:T(8,128)S(1)} custom-call(bf16[512,1024]{1,0:T(8,128)(2,1)S(1)} %get-tuple-element.66.inner_ref, bf16[512,1024]{1,0:T(8,128)(2,1)S(1)} %copy-done.12, bf16[128,1024]{1,0:T(8,128)(2,1)S(1)} %collective-permute-done.3.rim_ref), custom_call_target="tpu_custom_call" | custom-call | flops 1048576 | bytes 262144 | tf_op jit(solution)/shard_map/filter_part/pallas_call | solution.py:281
  130.0 1.8 %collective-permute-start.22 = (f32[64,128]{1,0:T(8,128)S(1)}, f32[64,128]{1,0:T(8,128)S(1)}, u32[]{:S(2)}, u32[]{:S(2)}) collective-permute-start(f32[64,128]{1,0:T(8,128)S(1)} %filter_part.1), channel_id=1, source_target_pairs={{0,16},{8,24},{16,0},{24,8},{1,17},{9,25},{17,1},{25,9},{2,18},{10... | collective-permute-start | bytes 98312 | tf_op jit(solution)/shard_map/ppermute | solution.py:21
  131.8 2.5 %collective-permute-start.23 = (f32[64,128]{1,0:T(8,128)S(1)}, f32[64,128]{1,0:T(8,128)S(1)}, u32[]{:S(2)}, u32[]{:S(2)}) collective-permute-start(f32[64,128]{1,0:T(8,128)S(1)} %filter_part.1), channel_id=1, source_target_pairs={{0,8},{8,16},{16,24},{24,0},{1,9},{9,17},{17,25},{25,1},{2,10},{10... | collective-permute-start | bytes 98312 | tf_op jit(solution)/shard_map/ppermute | solution.py:21
  134.3 3.7 %collective-permute-done.24.ahead_ref = bf16[128,1024]{1,0:T(8,128)(2,1)} collective-permute-done((bf16[128,1024]{1,0:T(8,128)(2,1)}, bf16[128,1024]{1,0:T(8,128)(2,1)}, u32[]{:S(2)}, u32[]{:S(2)}) %collective-permute-start.24) | collective-permute-done | bytes 262176 | tf_op jit(solution)/shard_map/ppermute | solution.py:27
  138.0 4.0 %conv_backward.2 = (bf16[512,1024]{1,0:T(8,128)(2,1)}, bf16[512,1024]{1,0:T(8,128)(2,1)}) custom-call(bf16[64,128]{1,0:T(8,128)(2,1)S(1)} %copy-done.21, bf16[512,1024]{1,0:T(8,128)(2,1)S(1)} %get-tuple-element.66.inner_ref, bf16[128,1024]{1,0:T(8,128)(2,1)} %collective-permute-done.24.ahead_ref, bf16[512,1024]{1,0:T(8,128)(2,1)S(1)} %copy-done.3, ...), custom_call_target="tpu_custom_call" | custom-call | flops 1048576 | bytes 262144 | tf_op jit(solution)/shard_map/conv_backward/pallas_call | solution.py:321
  142.1 9.1 %collective-permute-start.25 = (f32[64,128]{1,0:T(8,128)S(1)}, f32[64,128]{1,0:T(8,128)S(1)}, u32[]{:S(2)}, u32[]{:S(2)}) collective-permute-start(f32[64,128]{1,0:T(8,128)S(1)} %select_add_fusion.1), channel_id=1, source_target_pairs={{0,192},{32,224},{64,0},{96,32},{128,64},{160,96},{192,128},{224,1... | collective-permute-start | bytes 98312 | tf_op jit(solution)/shard_map/ppermute | solution.py:21
  151.8 2.8 %collective-permute-start.27 = (f32[64,128]{1,0:T(8,128)S(1)}, f32[64,128]{1,0:T(8,128)S(1)}, u32[]{:S(2)}, u32[]{:S(2)}) collective-permute-start(f32[64,128]{1,0:T(8,128)S(1)} %select_add_fusion.1), channel_id=1, source_target_pairs={{0,64},{32,96},{64,128},{96,160},{128,192},{160,224},{192,0},{224,... | collective-permute-start | bytes 98312 | tf_op jit(solution)/shard_map/ppermute | solution.py:21
  154.6 4.0 %conv_backward.3 = (bf16[512,1024]{1,0:T(8,128)(2,1)}, bf16[512,1024]{1,0:T(8,128)(2,1)}) custom-call(bf16[64,128]{1,0:T(8,128)(2,1)S(1)} %copy-done.21, bf16[512,1024]{1,0:T(8,128)(2,1)S(1)} %get-tuple-element.66.inner_ref, bf16[128,1024]{1,0:T(8,128)(2,1)} %collective-permute-done.24.ahead_ref, ...), custom_call_target="tpu_custom_call", output_to_operand_aliasing={{0}: (5, {}), {1}: (6, {})} | custom-call | flops 1048576 | bytes 262144 | tf_op jit(solution)/shard_map/conv_backward/pallas_call | solution.py:321
  159.1 1.9 %collective-permute-start.28 = (f32[64,128]{1,0:T(8,128)S(1)}, f32[64,128]{1,0:T(8,128)S(1)}, u32[]{:S(2)}, u32[]{:S(2)}) collective-permute-start(f32[64,128]{1,0:T(8,128)S(1)} %select_add_fusion), channel_id=1, source_target_pairs={{0,32},{32,0},{64,96},{96,64},{128,160},{160,128},{192,224},{224,1... | collective-permute-start | bytes 98312 | tf_op jit(solution)/shard_map/ppermute | solution.py:411
  161.0 1.8 %convert_element_type.47 = f32[128,1024]{1,0:T(8,128)} convert(bf16[128,1024]{1,0:T(8,128)(2,1)} %reduce-scatter.2.cloned.1.call-done) | non-fusion elementwise | flops 131072 | bytes 786432 | tf_op jit(solution)/shard_map/convert_element_type | solution.py:390
  (93 shorter events, 12.0 us)
Async XLA Ops:
  7.2 19.6 %copy-start.3 = (bf16[512,1024]{1,0:T(8,128)(2,1)S(1)}, bf16[512,1024]{1,0:T(8,128)(2,1)}, u32[]{:S(2)}) copy-start(bf16[512,1024]{1,0:T(8,128)(2,1)} %k_ref.7) | copy-start | bytes 3145732
  7.2 19.6 %copy-start.4 = (bf16[512,1024]{1,0:T(8,128)(2,1)S(1)}, bf16[512,1024]{1,0:T(8,128)(2,1)}, u32[]{:S(2)}) copy-start(bf16[512,1024]{1,0:T(8,128)(2,1)} %v_ref.7) | copy-start | bytes 3145732
  7.2 19.6 %copy-start.6 = (bf16[512,1024]{1,0:T(8,128)(2,1)S(1)}, bf16[512,1024]{1,0:T(8,128)(2,1)}, u32[]{:S(2)}) copy-start(bf16[512,1024]{1,0:T(8,128)(2,1)} %refs_6_.1) | copy-start | bytes 3145732
  7.2 19.5 %copy-start.21 = (bf16[64,128]{1,0:T(8,128)(2,1)S(1)}, bf16[64,128]{1,0:T(8,128)(2,1)}, u32[]{:S(2)}) copy-start(bf16[64,128]{1,0:T(8,128)(2,1)} %filters_ref.7) | copy-start | bytes 49156
  7.2 57.1 %all-gather.2.cloned.1.call-start = ((), (), s32[]{:S(2)}) async-start(), calls=%async_computation.1 | async-start | bytes 2359296 | tf_op jit(solution)/shard_map/all_gather | solution.py:353
  11.1 9.6 %collective-permute-start = (bf16[512,128]{1,0:T(8,128)(2,1)}, bf16[512,128]{1,0:T(8,128)(2,1)}, u32[]{:S(2)}, u32[]{:S(2)}) collective-permute-start(bf16[512,128]{1,0:T(8,128)(2,1)} %get-tuple-element.76), channel_id=1, source_target_pairs={{0,24},{8,0},{16,8},{24,16},{1,25},{9,1},{17,9},{25,17},{2,26},{10... | collective-permute-start | bytes 393224 | tf_op jit(solution)/shard_map/ppermute | solution.py:21
  11.9 8.7 %collective-permute-start.1 = (bf16[512,128]{1,0:T(8,128)(2,1)}, bf16[512,128]{1,0:T(8,128)(2,1)}, u32[]{:S(2)}, u32[]{:S(2)}) collective-permute-start(bf16[512,128]{1,0:T(8,128)(2,1)} %get-tuple-element.78), channel_id=1, source_target_pairs={{0,16},{8,24},{16,0},{24,8},{1,17},{9,25},{17,1},{25,9},{2,18},{10... | collective-permute-start | bytes 393224 | tf_op jit(solution)/shard_map/ppermute | solution.py:21
  14.7 7.9 %collective-permute-start.2 = (bf16[512,128]{1,0:T(8,128)(2,1)}, bf16[512,128]{1,0:T(8,128)(2,1)}, u32[]{:S(2)}, u32[]{:S(2)}) collective-permute-start(bf16[512,128]{1,0:T(8,128)(2,1)} %get-tuple-element.77), channel_id=1, source_target_pairs={{0,8},{8,16},{16,24},{24,0},{1,9},{9,17},{17,25},{25,1},{2,10},{10... | collective-permute-start | bytes 393224 | tf_op jit(solution)/shard_map/ppermute | solution.py:21
  15.1 11.6 %collective-permute-start.3 = (bf16[128,1024]{1,0:T(8,128)(2,1)}, bf16[128,1024]{1,0:T(8,128)(2,1)S(1)}, u32[]{:S(2)}, u32[]{:S(2)}) collective-permute-start(bf16[128,1024]{1,0:T(8,128)(2,1)} %multiply_convert_fusion), channel_id=1, source_target_pairs={{0,8},{8,16},{16,24},{24,32},{32,40},{40,48},{48,56},{56,64},{64,7... | collective-permute-start | bytes 786440 | tf_op jit(solution)/shard_map/ppermute | solution.py:27
  19.3 141.7 %reduce-scatter.2.cloned.1.call-start = ((), (), s32[]{:S(2)}) async-start(), calls=%async_computation.2 | async-start | bytes 2359296 | tf_op jit(solution)/shard_map/reduce_scatter | solution.py:390
  30.2 8.8 %copy-start.13 = (bf16[512,512]{1,0:T(8,128)(2,1)}, bf16[512,512]{1,0:T(8,128)(2,1)S(1)}, u32[]{:S(2)}) copy-start(bf16[512,512]{1,0:T(8,128)(2,1)S(1)} %get-tuple-element.70.refs_0_) | copy-start | bytes 1572868
  30.2 13.8 %collective-permute-start.5 = (bf16[2048,128]{1,0:T(8,128)(2,1)S(1)}, bf16[2048,128]{1,0:T(8,128)(2,1)S(1)}, u32[]{:S(2)}, u32[]{:S(2)}) collective-permute-start(bf16[2048,128]{1,0:T(8,128)(2,1)S(1)} %pad_maximum_fusion), channel_id=1, source_target_pairs={{0,2},{2,4},{4,6},{6,0},{1,3},{3,5},{5,7},{7,1},{8,10},{10,12},{12... | collective-permute-start | bytes 1572872 | tf_op jit(solution)/shard_map/ppermute | solution.py:21
  31.9 12.6 %collective-permute-start.4 = (bf16[2048,128]{1,0:T(8,128)(2,1)S(1)}, bf16[2048,128]{1,0:T(8,128)(2,1)S(1)}, u32[]{:S(2)}, u32[]{:S(2)}) collective-permute-start(bf16[2048,128]{1,0:T(8,128)(2,1)S(1)} %pad_maximum_fusion), channel_id=1, source_target_pairs={{0,6},{2,0},{4,2},{6,4},{1,7},{3,1},{5,3},{7,5},{8,14},{10,8},{12,... | collective-permute-start | bytes 1572872 | tf_op jit(solution)/shard_map/ppermute | solution.py:21
  33.5 14.0 %collective-permute-start.7 = (bf16[512,512]{1,0:T(8,128)(2,1)S(1)}, bf16[512,512]{1,0:T(8,128)(2,1)}, u32[]{:S(2)}, u32[]{:S(2)}) collective-permute-start(bf16[512,512]{1,0:T(8,128)(2,1)S(1)} %get-tuple-element.70.refs_0_), channel_id=1, source_target_pairs={{0,8},{8,16},{16,24},{24,0},{1,9},{9,17},{17,25},{25,1},{2,10},{10... | collective-permute-start | bytes 1572872 | tf_op jit(solution)/shard_map/ppermute | solution.py:21
  33.5 16.1 %collective-permute-start.10 = (bf16[512,512]{1,0:T(8,128)(2,1)S(1)}, bf16[512,512]{1,0:T(8,128)(2,1)S(1)}, u32[]{:S(2)}, u32[]{:S(2)}) collective-permute-start(bf16[512,512]{1,0:T(8,128)(2,1)S(1)} %get-tuple-element.70.refs_0_), channel_id=1, source_target_pairs={{0,24},{8,0},{16,8},{24,16},{1,25},{9,1},{17,9},{25,17},{2,26},{10... | collective-permute-start | bytes 1572872 | tf_op jit(solution)/shard_map/ppermute | solution.py:21
  39.0 19.2 %copy-start.8 = (f32[512,1024]{1,0:T(8,128)}, f32[512,1024]{1,0:T(8,128)S(1)}, u32[]{:S(2)}) copy-start(f32[512,1024]{1,0:T(8,128)S(1)} %get-tuple-element.58.refs_7_) | copy-start | bytes 6291460
  39.0 19.2 %copy-start.11 = (bf16[512,1024]{1,0:T(8,128)(2,1)}, bf16[512,1024]{1,0:T(8,128)(2,1)S(1)}, u32[]{:S(2)}) copy-start(bf16[512,1024]{1,0:T(8,128)(2,1)S(1)} %get-tuple-element.61.mixed_ref) | copy-start | bytes 3145732
  39.1 19.2 %copy-start.17 = (bf16[512,512]{1,0:T(8,128)(2,1)}, bf16[512,512]{1,0:T(8,128)(2,1)S(1)}, u32[]{:S(2)}) copy-start(bf16[512,512]{1,0:T(8,128)(2,1)S(1)} %get-tuple-element.46.refs_1_) | copy-start | bytes 1572868
  39.1 19.1 %collective-permute-start.8 = (bf16[512,512]{1,0:T(8,128)(2,1)S(1)}, bf16[512,512]{1,0:T(8,128)(2,1)}, u32[]{:S(2)}, u32[]{:S(2)}) collective-permute-start(bf16[512,512]{1,0:T(8,128)(2,1)S(1)} %get-tuple-element.46.refs_1_), channel_id=1, source_target_pairs={{0,24},{8,0},{16,8},{24,16},{1,25},{9,1},{17,9},{25,17},{2,26},{10... | collective-permute-start | bytes 1572872 | tf_op jit(solution)/shard_map/ppermute | solution.py:21
  44.0 14.1 %collective-permute-start.6 = (bf16[1024,128]{1,0:T(8,128)(2,1)S(1)}, bf16[1024,128]{1,0:T(8,128)(2,1)S(1)}, u32[]{:S(2)}, u32[]{:S(2)}) collective-permute-start(bf16[1024,128]{1,0:T(8,128)(2,1)S(1)} %slice.48), channel_id=1, source_target_pairs={{0,2},{2,4},{4,6},{6,0},{1,3},{3,5},{5,7},{7,1},{8,10},{10,12},{12... | collective-permute-start | bytes 786440 | tf_op jit(solution)/shard_map/ppermute | solution.py:21
  44.5 13.7 %collective-permute-start.9 = (bf16[1024,128]{1,0:T(8,128)(2,1)S(1)}, bf16[1024,128]{1,0:T(8,128)(2,1)S(1)}, u32[]{:S(2)}, u32[]{:S(2)}) collective-permute-start(bf16[1024,128]{1,0:T(8,128)(2,1)S(1)} %slice.49), channel_id=1, source_target_pairs={{0,6},{2,0},{4,2},{6,4},{1,7},{3,1},{5,3},{7,5},{8,14},{10,8},{12,... | collective-permute-start | bytes 786440 | tf_op jit(solution)/shard_map/ppermute | solution.py:21
  49.6 9.6 %copy-start.15 = (bf16[512,512]{1,0:T(8,128)(2,1)}, bf16[512,512]{1,0:T(8,128)(2,1)S(1)}, u32[]{:S(2)}) copy-start(bf16[512,512]{1,0:T(8,128)(2,1)S(1)} %collective-permute-done.10.refs_2_) | copy-start | bytes 1572868
  49.6 9.6 %collective-permute-start.11 = (bf16[512,512]{1,0:T(8,128)(2,1)S(1)}, bf16[512,512]{1,0:T(8,128)(2,1)S(1)}, u32[]{:S(2)}, u32[]{:S(2)}) collective-permute-start(bf16[512,512]{1,0:T(8,128)(2,1)S(1)} %get-tuple-element.46.refs_1_), channel_id=1, source_target_pairs={{0,8},{8,16},{16,24},{24,0},{1,9},{9,17},{17,25},{25,1},{2,10},{10... | collective-permute-start | bytes 1572872 | tf_op jit(solution)/shard_map/ppermute | solution.py:21
  60.0 4.3 %collective-permute-start.12 = (bf16[4,2048,128]{2,1,0:T(8,128)(2,1)S(1)}, bf16[4,2048,128]{2,1,0:T(8,128)(2,1)}, u32[]{:S(2)}, u32[]{:S(2)}) collective-permute-start(bf16[4,2048,128]{2,1,0:T(8,128)(2,1)S(1)} %bitcast.9), channel_id=1, source_target_pairs={{0,1},{1,0},{2,3},{3,2},{4,5},{5,4},{6,7},{7,6},{8,9},{9,8},{10,11... | collective-permute-start | bytes 6291464 | tf_op jit(solution)/shard_map/ppermute | solution.py:21
  60.0 15.9 %collective-permute-start.14 = (bf16[512,512]{1,0:T(8,128)(2,1)}, bf16[512,512]{1,0:T(8,128)(2,1)}, u32[]{:S(2)}, u32[]{:S(2)}) collective-permute-start(bf16[512,512]{1,0:T(8,128)(2,1)} %collective-permute-done.8.refs_3_), channel_id=1, source_target_pairs={{0,24},{8,0},{16,8},{24,16},{1,25},{9,1},{17,9},{25,17},{2,26},{10... | collective-permute-start | bytes 1572872 | tf_op jit(solution)/shard_map/ppermute | solution.py:21
  61.8 15.1 %collective-permute-start.13 = (bf16[512,512]{1,0:T(8,128)(2,1)}, bf16[512,512]{1,0:T(8,128)(2,1)}, u32[]{:S(2)}, u32[]{:S(2)}) collective-permute-start(bf16[512,512]{1,0:T(8,128)(2,1)} %collective-permute-done.7.refs_6_), channel_id=1, source_target_pairs={{0,8},{8,16},{16,24},{24,0},{1,9},{9,17},{17,25},{25,1},{2,10},{10... | collective-permute-start | bytes 1572872 | tf_op jit(solution)/shard_map/ppermute | solution.py:21
  70.7 23.3 %collective-permute-start.15 = (bf16[512,512]{1,0:T(8,128)(2,1)}, bf16[512,512]{1,0:T(8,128)(2,1)}, u32[]{:S(2)}, u32[]{:S(2)}) collective-permute-start(bf16[512,512]{1,0:T(8,128)(2,1)} %get-tuple-element.48), channel_id=1, source_target_pairs={{0,8},{8,16},{16,24},{24,0},{1,9},{9,17},{17,25},{25,1},{2,10},{10... | collective-permute-start | bytes 1572872 | tf_op jit(solution)/shard_map/ppermute | solution.py:21
  72.2 12.9 %copy-start.14 = (bf16[512,512]{1,0:T(8,128)(2,1)S(1)}, bf16[512,512]{1,0:T(8,128)(2,1)}, u32[]{:S(2)}) copy-start(bf16[512,512]{1,0:T(8,128)(2,1)} %copy-done.13) | copy-start | bytes 1572868
  72.2 12.9 %copy-start.16 = (bf16[512,512]{1,0:T(8,128)(2,1)S(1)}, bf16[512,512]{1,0:T(8,128)(2,1)}, u32[]{:S(2)}) copy-start(bf16[512,512]{1,0:T(8,128)(2,1)} %copy-done.15) | copy-start | bytes 1572868
  72.2 12.9 %copy-start.18 = (bf16[512,512]{1,0:T(8,128)(2,1)S(1)}, bf16[512,512]{1,0:T(8,128)(2,1)}, u32[]{:S(2)}) copy-start(bf16[512,512]{1,0:T(8,128)(2,1)} %copy-done.17) | copy-start | bytes 1572868
  72.2 12.9 %copy-start.20 = (bf16[512,512]{1,0:T(8,128)(2,1)S(1)}, bf16[512,512]{1,0:T(8,128)(2,1)}, u32[]{:S(2)}) copy-start(bf16[512,512]{1,0:T(8,128)(2,1)} %copy-done.19) | copy-start | bytes 1572868
  72.2 21.7 %collective-permute-start.16 = (bf16[512,512]{1,0:T(8,128)(2,1)}, bf16[512,512]{1,0:T(8,128)(2,1)}, u32[]{:S(2)}, u32[]{:S(2)}) collective-permute-start(bf16[512,512]{1,0:T(8,128)(2,1)} %get-tuple-element.49), channel_id=1, source_target_pairs={{0,24},{8,0},{16,8},{24,16},{1,25},{9,1},{17,9},{25,17},{2,26},{10... | collective-permute-start | bytes 1572872 | tf_op jit(solution)/shard_map/ppermute | solution.py:21
  81.9 19.9 %collective-permute-start.18 = (bf16[512,512]{1,0:T(8,128)(2,1)}, bf16[512,512]{1,0:T(8,128)(2,1)}, u32[]{:S(2)}, u32[]{:S(2)}) collective-permute-start(bf16[512,512]{1,0:T(8,128)(2,1)} %get-tuple-element.53), channel_id=1, source_target_pairs={{0,24},{8,0},{16,8},{24,16},{1,25},{9,1},{17,9},{25,17},{2,26},{10... | collective-permute-start | bytes 1572872 | tf_op jit(solution)/shard_map/ppermute | solution.py:21
  81.9 19.9 %collective-permute-start.19 = (bf16[512,512]{1,0:T(8,128)(2,1)}, bf16[512,512]{1,0:T(8,128)(2,1)}, u32[]{:S(2)}, u32[]{:S(2)}) collective-permute-start(bf16[512,512]{1,0:T(8,128)(2,1)} %get-tuple-element.55), channel_id=1, source_target_pairs={{0,8},{8,16},{16,24},{24,0},{1,9},{9,17},{17,25},{25,1},{2,10},{10... | collective-permute-start | bytes 1572872 | tf_op jit(solution)/shard_map/ppermute | solution.py:21
  101.8 12.3 %collective-permute-start.17 = (bf16[512,512]{1,0:T(8,128)(2,1)}, bf16[512,512]{1,0:T(8,128)(2,1)S(1)}, u32[]{:S(2)}, u32[]{:S(2)}) collective-permute-start(bf16[512,512]{1,0:T(8,128)(2,1)} %copy-done.23), channel_id=1, source_target_pairs={{0,8},{8,16},{16,24},{24,0},{1,9},{9,17},{17,25},{25,1},{2,10},{10... | collective-permute-start | bytes 1572872 | tf_op jit(solution)/shard_map/ppermute | solution.py:21
  103.4 13.1 %collective-permute-start.20 = (bf16[512,512]{1,0:T(8,128)(2,1)}, bf16[512,512]{1,0:T(8,128)(2,1)S(1)}, u32[]{:S(2)}, u32[]{:S(2)}) collective-permute-start(bf16[512,512]{1,0:T(8,128)(2,1)} %copy-done.22), channel_id=1, source_target_pairs={{0,24},{8,0},{16,8},{24,16},{1,25},{9,1},{17,9},{25,17},{2,26},{10... | collective-permute-start | bytes 1572872 | tf_op jit(solution)/shard_map/ppermute | solution.py:21
  105.5 11.0 %copy-start.7 = (bf16[512,1024]{1,0:T(8,128)(2,1)S(1)}, bf16[512,1024]{1,0:T(8,128)(2,1)}, u32[]{:S(2)}) copy-start(bf16[512,1024]{1,0:T(8,128)(2,1)} %refs_6_.1) | copy-start | bytes 3145732
  109.6 10.7 %copy-start.9 = (f32[512,1024]{1,0:T(8,128)S(1)}, f32[512,1024]{1,0:T(8,128)}, u32[]{:S(2)}) copy-start(f32[512,1024]{1,0:T(8,128)} %copy-done.8) | copy-start | bytes 6291460
  118.3 19.6 %collective-permute-start.24 = (bf16[128,1024]{1,0:T(8,128)(2,1)}, bf16[128,1024]{1,0:T(8,128)(2,1)}, u32[]{:S(2)}, u32[]{:S(2)}) collective-permute-start(bf16[128,1024]{1,0:T(8,128)(2,1)} %pad_maximum_fusion.1), channel_id=1, source_target_pairs={{8,0},{16,8},{24,16},{32,24},{40,32},{48,40},{56,48},{64,56},{72,6... | collective-permute-start | bytes 786440 | tf_op jit(solution)/shard_map/ppermute | solution.py:27
  120.3 3.9 %copy-start.12 = (bf16[512,1024]{1,0:T(8,128)(2,1)S(1)}, bf16[512,1024]{1,0:T(8,128)(2,1)}, u32[]{:S(2)}) copy-start(bf16[512,1024]{1,0:T(8,128)(2,1)} %copy-done.11) | copy-start | bytes 3145732
  124.2 13.8 %copy-start.5 = (bf16[512,1024]{1,0:T(8,128)(2,1)S(1)}, bf16[512,1024]{1,0:T(8,128)(2,1)}, u32[]{:S(2)}) copy-start(bf16[512,1024]{1,0:T(8,128)(2,1)} %v_ref.7) | copy-start | bytes 3145732
  129.9 12.1 %collective-permute-start.21 = (f32[64,128]{1,0:T(8,128)S(1)}, f32[64,128]{1,0:T(8,128)S(1)}, u32[]{:S(2)}, u32[]{:S(2)}) collective-permute-start(f32[64,128]{1,0:T(8,128)S(1)} %filter_part.1), channel_id=1, source_target_pairs={{0,24},{8,0},{16,8},{24,16},{1,25},{9,1},{17,9},{25,17},{2,26},{10... | collective-permute-start | bytes 98312 | tf_op jit(solution)/shard_map/ppermute | solution.py:21
  130.0 12.1 %collective-permute-start.22 = (f32[64,128]{1,0:T(8,128)S(1)}, f32[64,128]{1,0:T(8,128)S(1)}, u32[]{:S(2)}, u32[]{:S(2)}) collective-permute-start(f32[64,128]{1,0:T(8,128)S(1)} %filter_part.1), channel_id=1, source_target_pairs={{0,16},{8,24},{16,0},{24,8},{1,17},{9,25},{17,1},{25,9},{2,18},{10... | collective-permute-start | bytes 98312 | tf_op jit(solution)/shard_map/ppermute | solution.py:21
  131.8 10.2 %collective-permute-start.23 = (f32[64,128]{1,0:T(8,128)S(1)}, f32[64,128]{1,0:T(8,128)S(1)}, u32[]{:S(2)}, u32[]{:S(2)}) collective-permute-start(f32[64,128]{1,0:T(8,128)S(1)} %filter_part.1), channel_id=1, source_target_pairs={{0,8},{8,16},{16,24},{24,0},{1,9},{9,17},{17,25},{25,1},{2,10},{10... | collective-permute-start | bytes 98312 | tf_op jit(solution)/shard_map/ppermute | solution.py:21
  142.1 16.6 %collective-permute-start.25 = (f32[64,128]{1,0:T(8,128)S(1)}, f32[64,128]{1,0:T(8,128)S(1)}, u32[]{:S(2)}, u32[]{:S(2)}) collective-permute-start(f32[64,128]{1,0:T(8,128)S(1)} %select_add_fusion.1), channel_id=1, source_target_pairs={{0,192},{32,224},{64,0},{96,32},{128,64},{160,96},{192,128},{224,1... | collective-permute-start | bytes 98312 | tf_op jit(solution)/shard_map/ppermute | solution.py:21
  151.2 7.8 %collective-permute-start.26 = (f32[64,128]{1,0:T(8,128)S(1)}, f32[64,128]{1,0:T(8,128)S(1)}, u32[]{:S(2)}, u32[]{:S(2)}) collective-permute-start(f32[64,128]{1,0:T(8,128)S(1)} %select_add_fusion.1), channel_id=1, source_target_pairs={{0,128},{32,160},{64,192},{96,224},{128,0},{160,32},{192,64},{224,... | collective-permute-start | bytes 98312 | tf_op jit(solution)/shard_map/ppermute | solution.py:21
  151.8 7.2 %collective-permute-start.27 = (f32[64,128]{1,0:T(8,128)S(1)}, f32[64,128]{1,0:T(8,128)S(1)}, u32[]{:S(2)}, u32[]{:S(2)}) collective-permute-start(f32[64,128]{1,0:T(8,128)S(1)} %select_add_fusion.1), channel_id=1, source_target_pairs={{0,64},{32,96},{64,128},{96,160},{128,192},{160,224},{192,0},{224,... | collective-permute-start | bytes 98312 | tf_op jit(solution)/shard_map/ppermute | solution.py:21
  159.1 4.0 %collective-permute-start.28 = (f32[64,128]{1,0:T(8,128)S(1)}, f32[64,128]{1,0:T(8,128)S(1)}, u32[]{:S(2)}, u32[]{:S(2)}) collective-permute-start(f32[64,128]{1,0:T(8,128)S(1)} %select_add_fusion), channel_id=1, source_target_pairs={{0,32},{32,0},{64,96},{96,64},{128,160},{160,128},{192,224},{224,1... | collective-permute-start | bytes 98312 | tf_op jit(solution)/shard_map/ppermute | solution.py:411
  (7 other events, 8.6 us)
Sparse Core Ops, SparseCore 0:
  19.4 43.1 all-gather.1
  101.9 47.1 reduce-scatter.1

commit v6 on v5

--- a/solution.py
+++ b/solution.py
@@ -117,6 +117,26 @@
         cost_estimate=LIGHT,
         name="conv_forward",
     )(*args)
+
+
+def join_body(*refs):
+    pieces, out_ref = refs[:-2], refs[-1]
+    rows = pieces[0].shape[0]
+    for i, ref in enumerate(pieces):
+        out_ref[i * rows : (i + 1) * rows] = ref[...]
+
+
+def join(pieces, later_than):
+    rows, width = pieces[0].shape
+    return pl.pallas_call(
+        join_body,
+        in_specs=[pl.BlockSpec(memory_space=pltpu.VMEM)] * len(pieces) + [pl.BlockSpec(memory_space=pl.ANY)],
+        out_specs=pl.BlockSpec(memory_space=pltpu.VMEM),
+        out_shape=jax.ShapeDtypeStruct((len(pieces) * rows, width), pieces[0].dtype),
+        compiler_params=pltpu.CompilerParams(vmem_limit_bytes=4 * MIB),
+        cost_estimate=LIGHT,
+        name="join",
+    )(*pieces, later_than)
 
 
 def gate_body(place_ref, mine_ref, sib_ref, proj_ref, *refs):
@@ -175,7 +195,7 @@
         gate_body,
         grid_spec=spec,
         out_shape=[jax.ShapeDtypeStruct((tokens, width // 2), dtype)] * 2,
-        compiler_params=pltpu.CompilerParams(vmem_limit_bytes=16 * MIB),
+        compiler_params=pltpu.CompilerParams(vmem_limit_bytes=(16 if dtype == F32 else 60) * MIB),
         cost_estimate=LIGHT,
         name="grad_gate_parts",
     )(place, mine, sib, proj, *added)
@@ -216,7 +236,7 @@
         proj_body,
         grid_spec=spec,
         out_shape=jax.ShapeDtypeStruct((depth, 2 * half), BF16),
-        compiler_params=pltpu.CompilerParams(vmem_limit_bytes=24 * MIB),
+        compiler_params=pltpu.CompilerParams(vmem_limit_bytes=60 * MIB),
         cost_estimate=LIGHT,
         name="grad_proj_part",
     )(place, mine, sib, *gated)
@@ -224,15 +244,17 @@
 
 def inner_body(*refs):
     own, from_left, from_right = refs[0:2], refs[2:4], refs[4:6]
-    q_ref, conv_ref, query_ref, inner_ref = refs[6:]
+    q_ref, conv_ref, query_ref, inner_ref, first_ref = refs[6:]
     second = pl.program_id(0) >= pl.num_programs(0) // 2
     pick = lambda pair: jnp.where(second, pair[1][...], pair[0][...]).astype(F32)
     gate = pick(own) + pick(from_left) + pick(from_right)
     query_ref[...] = (gate * conv_ref[...]).astype(BF16)
-    inner_ref[...] = (gate * q_ref[...].astype(F32)).astype(BF16)
-
-
-def gate_gradients(own, from_left, from_right, q, conv):
+    inner = (gate * q_ref[...].astype(F32)).astype(BF16)
+    inner_ref[...] = inner
+    first_ref[...] = inner[: first_ref.shape[0]]
+
+
+def gate_gradients(own, from_left, from_right, q, conv, taps):
     tokens, width = q.shape
     wide = 2 * LANES
     steps = width // wide
@@ -243,8 +265,8 @@
         inner_body,
         grid=(steps,),
         in_specs=[first, last] * 3 + [column, column],
-        out_specs=[column, column],
-        out_shape=[jax.ShapeDtypeStruct((tokens, width), BF16)] * 2,
+        out_specs=[column, column, pl.BlockSpec((taps, wide), lambda i: (0, i))],
+        out_shape=[jax.ShapeDtypeStruct((n, width), BF16) for n in (tokens, tokens, taps)],
         compiler_params=pltpu.CompilerParams(vmem_limit_bytes=16 * MIB),
         cost_estimate=LIGHT,
         name="gate_gradients",
@@ -361,7 +383,7 @@
         pieces[(-d) % 4] = send(own_cols(d), "x", d)
     conv, mixed, gated_a = forward(0, filters, key_in, value_in, query_in, rim, None)
     conv, mixed, gated_b = forward(1, filters, key_in, value_in, query_in, rim, (conv, mixed))
-    column = after(jnp.concatenate(pieces, 0), gated_a)
+    column = join(pieces, gated_b)
     below, above = send(column, "y", 1), send(column, "y", -1)
     middle = column.shape[0] // 2
     far = send(below[:middle], "y", 1), send(above[middle:], "y", -1)
@@ -391,18 +413,8 @@
     own = gate_parts(place, mine, sib, proj, ((0, 0), (0, 1)), F32)
     from_left, from_right = (from_left_a, from_left_b), (from_right_a, from_right_b)
 
-    first = [
-        (
-            (own[h][:taps] + from_left[h][:taps].astype(F32) + from_right[h][:taps].astype(F32))
-            * query_in[:taps, h * half : (h + 1) * half].astype(F32)
-        ).astype(BF16)
-        for h in range(2)
-    ]
-    first = jnp.concatenate(first, 1)
+    grad_query, inner, first = gate_gradients(own, from_left, from_right, query_in, conv, taps)
     ahead = send_along_tokens(first, -1)
-    grad_query, inner = gate_gradients(
-        (after(own[0], first), own[1]), from_left, from_right, query_in, conv
-    )
     sums = filter_part(inner, mixed, rim, group_count)
     grads = backward(0, filters, after(inner, sums), ahead, key_in, value_in, None)
     sums = sum_over(sums, "x", 1, *grads)

time: 172 us -> 175 us (1.017)
  Pallas kernels: 50.4 us -> 57.1 us
  starting transfers between devices: 50.1 us -> 55.4 us
  other arithmetic: 6.71 us -> 3.09 us
  local copies, waits for them, and re-layouts: 11.5 us -> 7.98 us
  waiting for transfers between devices: 37.4 us -> 35.4 us
    ppermute x26, starting transfers between devices: 42.1 us -> 49.4 us  [send(): lax.ppermute(value, axis, [(i, (i + by) % count) for i in range(count)])]
    ppermute x26, waiting for transfers between devices: 30.5 us -> 26.2 us  [send(): lax.ppermute(value, axis, [(i, (i + by) % count) for i in range(count)])]
    unnamed x52 -> x44, local copies, waits for them, and re-layouts: 8.79 us -> 5.4 us
    pallas_call x4, Pallas kernels: 18.5 us -> 21.7 us  [gate_parts(): pl.pallas_call(gate_body, grid_spec=spec, out_shape=[jax.ShapeDtypeStruct...]
    pallas_call x1, Pallas kernels: 7.42 us -> 9.27 us  [proj_part(): pl.pallas_call(proj_body, grid_spec=spec, out_shape=jax.ShapeDtypeStruct(...]
    ppermute x1, starting transfers between devices: 1.9 us -> 0.09 us  [on_device(): lax.ppermute(sums, 'z', [(i, i ^ 1) for i in range(lax.axis_size('z'))])]
    concatenate x2 -> x0, other arithmetic: 1.8 us -> none  [the longest x1 1.07 us: on_device(): column = after(jnp.concatenate(pieces, 0), gated_a)]
    ppermute x1, waiting for transfers between devices: 0.31 us -> 2.08 us  [on_device(): lax.ppermute(sums, 'z', [(i, i ^ 1) for i in range(lax.axis_size('z'))])]
  transfers between devices with their start and end apart: 31 -> 31, of which waited for: 15 -> 12; matrix products, arithmetic and copies ran while one was open for 3% -> 2% of each run, Pallas kernels for 30% -> 33%
where the time goes in v6:
time: 175 us; the launch traced here: 173 us
  Pallas kernels  57.1 us (33%)
  starting transfers between devices  55.4 us (32%)
  waiting for transfers between devices  35.4 us (20%)
  between operations  14.5 us (8%)
  local copies, waits for them, and re-layouts  7.98 us (5%)
  other arithmetic  3.09 us (2%)
    ppermute x26, starting transfers between devices, send(): lax.ppermute(value, axis, [(i, (i + by) % count) for i in range(count)])  49.4 us
    ppermute x26, waiting for transfers between devices, send(): lax.ppermute(value, axis, [(i, (i + by) % count) for i in range(count)])  26.2 us
    pallas_call x4, Pallas kernels, gate_parts(): pl.pallas_call(gate_body, grid_spec=spec, out_shape=[jax.ShapeDtypeStruct...  21.7 us
    pallas_call x1, Pallas kernels, proj_part(): pl.pallas_call(proj_body, grid_spec=spec, out_shape=jax.ShapeDtypeStruct(...  9.27 us
    pallas_call x2, Pallas kernels, backward(): pl.pallas_call(functools.partial(backward_body, taps, groups), grid=(step...  8.06 us
    ppermute x2, waiting for transfers between devices, send_along_tokens(): return lax.ppermute(value, ('z', 'x'), pairs)  7.08 us
    pallas_call x2, Pallas kernels, forward(): pl.pallas_call(functools.partial(forward_body, taps, groups), grid=(steps...  6.91 us
    ppermute x2, starting transfers between devices, send_along_tokens(): return lax.ppermute(value, ('z', 'x'), pairs)  5.78 us
  transfers between devices with their start and end apart: 31, of which 12 were waited for; matrix products, arithmetic and copies ran while one was open for 2% of the time, Pallas kernels for 33%

profile of v6, /device:TPU:6, one launch (start us, length us, event | category | flops | bytes accessed | tf_op | source)
XLA Modules:
  0.0 173.5 jit_solution(8704416051519452261)
XLA Ops:
  7.2 1.2 multiply_convert_fusion
  8.5 3.7 %collective-permute-start.3 = (bf16[128,1024]{1,0:T(8,128)(2,1)S(1)}, bf16[128,1024]{1,0:T(8,128)(2,1)S(1)}, u32[]{:S(2)}, u32[]{:S(2)}) collective-permute-start(bf16[128,1024]{1,0:T(8,128)(2,1)S(1)} %multiply_convert_fusion), channel_id=1, source_target_pairs={{0,8},{8,16},{16,24},{24,32},{32,40},{40,48},{48,56},{56,64},{64,7... | collective-permute-start | bytes 786440 | tf_op jit(solution)/shard_map/ppermute | solution.py:27
  12.3 1.2 constant_dynamic-slice_fusion
  13.7 1.4 collective-permute-start.1
  15.1 2.1 %collective-permute-start.2 = (bf16[512,128]{1,0:T(8,128)(2,1)S(1)}, bf16[512,128]{1,0:T(8,128)(2,1)}, u32[]{:S(2)}, u32[]{:S(2)}) collective-permute-start(bf16[512,128]{1,0:T(8,128)(2,1)S(1)} %get-tuple-element.71), channel_id=1, source_target_pairs={{0,8},{8,16},{16,24},{24,0},{1,9},{9,17},{17,25},{25,1},{2,10},{10... | collective-permute-start | bytes 393224 | tf_op jit(solution)/shard_map/ppermute | solution.py:21
  17.3 2.0 %collective-permute-done.3.rim_ref = bf16[128,1024]{1,0:T(8,128)(2,1)S(1)} collective-permute-done((bf16[128,1024]{1,0:T(8,128)(2,1)S(1)}, bf16[128,1024]{1,0:T(8,128)(2,1)S(1)}, u32[]{:S(2)}, u32[]{:S(2)}) %collective-permute-start.3) | collective-permute-done | bytes 262176 | tf_op jit(solution)/shard_map/ppermute | solution.py:27
  19.3 1.2 copy-done.6
  20.5 3.4 %conv_forward.2 = (f32[512,1024]{1,0:T(8,128)S(1)}, bf16[512,1024]{1,0:T(8,128)(2,1)S(1)}, bf16[512,512]{1,0:T(8,128)(2,1)S(1)}) custom-call(bf16[64,128]{1,0:T(8,128)(2,1)S(1)} %copy-done.14, bf16[512,1024]{1,0:T(8,128)(2,1)S(1)} %copy-done.3, bf16[512,1024]{1,0:T(8,128)(2,1)S(1)} %copy-done.4, bf16[512,1024]{1,0:T(8,128)(2,1)S(1)} %copy-done.6, ...), custom_call_target="tpu_custom_call" | custom-call | flops 1048576 | bytes 262144 | tf_op jit(solution)/shard_map/conv_forward/pallas_call | solution.py:105
  24.0 3.5 %conv_forward.3 = (f32[512,1024]{1,0:T(8,128)S(1)}, bf16[512,1024]{1,0:T(8,128)(2,1)S(1)}, bf16[512,512]{1,0:T(8,128)(2,1)S(1)}) custom-call(bf16[64,128]{1,0:T(8,128)(2,1)S(1)} %copy-done.14, bf16[512,1024]{1,0:T(8,128)(2,1)S(1)} %copy-done.3, bf16[512,1024]{1,0:T(8,128)(2,1)S(1)} %copy-done.4, ...), custom_call_target="tpu_custom_call", output_to_operand_aliasing={{0}: (5, {}), {1}: (6, {})} | custom-call | flops 1048576 | bytes 262144 | tf_op jit(solution)/shard_map/conv_forward/pallas_call | solution.py:105
  27.6 1.5 join.1
  29.1 1.7 collective-permute-start.5
  30.7 1.7 collective-permute-start.4
  32.4 2.7 %collective-permute-start.10 = (bf16[512,512]{1,0:T(8,128)(2,1)S(1)}, bf16[512,512]{1,0:T(8,128)(2,1)S(1)}, u32[]{:S(2)}, u32[]{:S(2)}) collective-permute-start(bf16[512,512]{1,0:T(8,128)(2,1)S(1)} %get-tuple-element.68.refs_0_), channel_id=1, source_target_pairs={{0,24},{8,0},{16,8},{24,16},{1,25},{9,1},{17,9},{25,17},{2,26},{10... | collective-permute-start | bytes 1572872 | tf_op jit(solution)/shard_map/ppermute | solution.py:21
  35.1 2.0 %collective-permute-start.8 = (bf16[512,512]{1,0:T(8,128)(2,1)S(1)}, bf16[512,512]{1,0:T(8,128)(2,1)}, u32[]{:S(2)}, u32[]{:S(2)}) collective-permute-start(bf16[512,512]{1,0:T(8,128)(2,1)S(1)} %get-tuple-element.44.refs_4_.refs_1_), channel_id=1, source_target_pairs={{0,24},{8,0},{16,8},{24,16},{1,25},{9,1},{17,9},{25,17},{2,26},{10... | collective-permute-start | bytes 1572872 | tf_op jit(solution)/shard_map/ppermute | solution.py:21
  37.1 5.2 %collective-permute-done.5 = bf16[2048,128]{1,0:T(8,128)(2,1)S(1)} collective-permute-done((bf16[2048,128]{1,0:T(8,128)(2,1)S(1)}, bf16[2048,128]{1,0:T(8,128)(2,1)S(1)}, u32[]{:S(2)}, u32[]{:S(2)}) %collective-permute-start.5) | collective-permute-done | bytes 524320 | tf_op jit(solution)/shard_map/ppermute | solution.py:21
  42.8 3.0 %collective-permute-start.9 = (bf16[1024,128]{1,0:T(8,128)(2,1)S(1)}, bf16[1024,128]{1,0:T(8,128)(2,1)S(1)}, u32[]{:S(2)}, u32[]{:S(2)}) collective-permute-start(bf16[1024,128]{1,0:T(8,128)(2,1)S(1)} %slice.17), channel_id=1, source_target_pairs={{0,6},{2,0},{4,2},{6,4},{1,7},{3,1},{5,3},{7,5},{8,14},{10,8},{12,... | collective-permute-start | bytes 786440 | tf_op jit(solution)/shard_map/ppermute | solution.py:21
  45.8 2.6 %collective-permute-done.10.refs_2_ = bf16[512,512]{1,0:T(8,128)(2,1)S(1)} collective-permute-done((bf16[512,512]{1,0:T(8,128)(2,1)S(1)}, bf16[512,512]{1,0:T(8,128)(2,1)S(1)}, u32[]{:S(2)}, u32[]{:S(2)}) %collective-permute-start.10) | collective-permute-done | bytes 524320 | tf_op jit(solution)/shard_map/ppermute | solution.py:21
  48.5 2.1 %collective-permute-start.11 = (bf16[512,512]{1,0:T(8,128)(2,1)S(1)}, bf16[512,512]{1,0:T(8,128)(2,1)S(1)}, u32[]{:S(2)}, u32[]{:S(2)}) collective-permute-start(bf16[512,512]{1,0:T(8,128)(2,1)S(1)} %get-tuple-element.44.refs_4_.refs_1_), channel_id=1, source_target_pairs={{0,8},{8,16},{16,24},{24,0},{1,9},{9,17},{17,25},{25,1},{2,10},{10... | collective-permute-start | bytes 1572872 | tf_op jit(solution)/shard_map/ppermute | solution.py:21
  50.7 5.8 %collective-permute-done.8.refs_3_ = bf16[512,512]{1,0:T(8,128)(2,1)} collective-permute-done((bf16[512,512]{1,0:T(8,128)(2,1)S(1)}, bf16[512,512]{1,0:T(8,128)(2,1)}, u32[]{:S(2)}, u32[]{:S(2)}) %collective-permute-start.8) | collective-permute-done | bytes 524320 | tf_op jit(solution)/shard_map/ppermute | solution.py:21
  56.6 1.0 collective-permute-done.11.refs_7_
  58.5 1.5 collective-permute-start.14
  60.0 1.8 %collective-permute-start.13 = (bf16[512,512]{1,0:T(8,128)(2,1)}, bf16[512,512]{1,0:T(8,128)(2,1)}, u32[]{:S(2)}, u32[]{:S(2)}) collective-permute-start(bf16[512,512]{1,0:T(8,128)(2,1)} %collective-permute-done.7.refs_6_), channel_id=1, source_target_pairs={{0,8},{8,16},{16,24},{24,0},{1,9},{9,17},{17,25},{25,1},{2,10},{10... | collective-permute-start | bytes 1572872 | tf_op jit(solution)/shard_map/ppermute | solution.py:21
  62.8 5.6 %grad_gate_parts.4 = (bf16[512,512]{1,0:T(8,128)(2,1)}, bf16[512,512]{1,0:T(8,128)(2,1)}) custom-call(s32[8]{0:T(128)} %stack.35.place_ref, bf16[4,2048,128]{2,1,0:T(8,128)(2,1)} %bitcast.10, bf16[4,2048,128]{2,1,0:T(8,128)(2,1)} %collective-permute-done.12.sib_ref, bf16[1024,1024]{1,0:T(8,128)(2,1)} %all-gather.2.cloned.1.call-done.proj_ref), custom_call_target="tpu_custom_call" | custom-call | flops 1048576 | bytes 262144 | tf_op jit(solution)/shard_map/grad_gate_parts/pallas_call | solution.py:194
  68.3 3.3 %collective-permute-start.15 = (bf16[512,512]{1,0:T(8,128)(2,1)}, bf16[512,512]{1,0:T(8,128)(2,1)S(1)}, u32[]{:S(2)}, u32[]{:S(2)}) collective-permute-start(bf16[512,512]{1,0:T(8,128)(2,1)} %get-tuple-element.46), channel_id=1, source_target_pairs={{0,8},{8,16},{16,24},{24,0},{1,9},{9,17},{17,25},{25,1},{2,10},{10... | collective-permute-start | bytes 1572872 | tf_op jit(solution)/shard_map/ppermute | solution.py:21
  71.6 3.0 %collective-permute-done.14.refs_5_ = bf16[512,512]{1,0:T(8,128)(2,1)} collective-permute-done((bf16[512,512]{1,0:T(8,128)(2,1)}, bf16[512,512]{1,0:T(8,128)(2,1)}, u32[]{:S(2)}, u32[]{:S(2)}) %collective-permute-start.14) | collective-permute-done | bytes 524320 | tf_op jit(solution)/shard_map/ppermute | solution.py:21
  75.0 5.8 %grad_gate_parts.7 = (bf16[512,512]{1,0:T(8,128)(2,1)}, bf16[512,512]{1,0:T(8,128)(2,1)}) custom-call(s32[8]{0:T(128)} %stack.35.place_ref, bf16[4,2048,128]{2,1,0:T(8,128)(2,1)} %bitcast.11, bf16[4,2048,128]{2,1,0:T(8,128)(2,1)} %collective-permute-done.12.sib_ref, bf16[1024,1024]{1,0:T(8,128)(2,1)} %all-gather.2.cloned.1.call-done.proj_ref), custom_call_target="tpu_custom_call" | custom-call | flops 1048576 | bytes 262144 | tf_op jit(solution)/shard_map/grad_gate_parts/pallas_call | solution.py:194
  80.8 3.0 %collective-permute-start.18 = (bf16[512,512]{1,0:T(8,128)(2,1)}, bf16[512,512]{1,0:T(8,128)(2,1)}, u32[]{:S(2)}, u32[]{:S(2)}) collective-permute-start(bf16[512,512]{1,0:T(8,128)(2,1)} %get-tuple-element.52), channel_id=1, source_target_pairs={{0,8},{8,16},{16,24},{24,0},{1,9},{9,17},{17,25},{25,1},{2,10},{10... | collective-permute-start | bytes 1572872 | tf_op jit(solution)/shard_map/ppermute | solution.py:21
  83.8 9.3 %grad_proj_part.1 = bf16[1024,1024]{1,0:T(8,128)(2,1)} custom-call(s32[8]{0:T(128)} %stack.35.place_ref, bf16[4,2048,128]{2,1,0:T(8,128)(2,1)} %bitcast.12, bf16[4,2048,128]{2,1,0:T(8,128)(2,1)} %collective-permute-done.12.sib_ref, bf16[512,512]{1,0:T(8,128)(2,1)} %copy-done.13, bf16[512,512]{1,0:T(8,128)(2,1)} %copy-done.12, bf16[512,512]{1,0:T(8,128)(2,1)} %copy-done.18, ...), custom_call_target="tpu_custom_call" | custom-call | flops 1048576 | bytes 262144 | tf_op jit(solution)/shard_map/grad_proj_part/pallas_call | solution.py:235
  93.9 0.8 copy-done.17
  94.7 6.0 %grad_gate_parts.6 = (bf16[512,512]{1,0:T(8,128)(2,1)}, bf16[512,512]{1,0:T(8,128)(2,1)}) custom-call(s32[8]{0:T(128)} %stack.35.place_ref, bf16[4,2048,128]{2,1,0:T(8,128)(2,1)} %bitcast.13, bf16[4,2048,128]{2,1,0:T(8,128)(2,1)} %collective-permute-done.12.sib_ref, bf16[1024,1024]{1,0:T(8,128)(2,1)} %all-gather.2.cloned.1.call-done.proj_ref, ...), custom_call_target="tpu_custom_call" | custom-call | flops 1048576 | bytes 262144 | tf_op jit(solution)/shard_map/grad_gate_parts/pallas_call | solution.py:194
  100.7 3.3 %collective-permute-start.17 = (bf16[512,512]{1,0:T(8,128)(2,1)}, bf16[512,512]{1,0:T(8,128)(2,1)S(1)}, u32[]{:S(2)}, u32[]{:S(2)}) collective-permute-start(bf16[512,512]{1,0:T(8,128)(2,1)} %get-tuple-element.51), channel_id=1, source_target_pairs={{0,8},{8,16},{16,24},{24,0},{1,9},{9,17},{17,25},{25,1},{2,10},{10... | collective-permute-start | bytes 1572872 | tf_op jit(solution)/shard_map/ppermute | solution.py:21
  104.1 1.6 copy-done.2
  105.7 4.3 %grad_gate_parts.5 = (f32[512,512]{1,0:T(8,128)S(1)}, f32[512,512]{1,0:T(8,128)S(1)}) custom-call(s32[8]{0:T(128)S(1)} %copy-done.15, bf16[4,2048,128]{2,1,0:T(8,128)(2,1)S(1)} %bitcast.14, bf16[4,2048,128]{2,1,0:T(8,128)(2,1)} %collective-permute-done.12.sib_ref, bf16[1024,1024]{1,0:T(8,128)(2,1)S(1)} %copy-done.2), custom_call_target="tpu_custom_call" | custom-call | flops 1048576 | bytes 262144 | tf_op jit(solution)/shard_map/grad_gate_parts/pallas_call | solution.py:194
  110.0 4.5 %collective-permute-done.17.refs_2_ = bf16[512,512]{1,0:T(8,128)(2,1)S(1)} collective-permute-done((bf16[512,512]{1,0:T(8,128)(2,1)}, bf16[512,512]{1,0:T(8,128)(2,1)S(1)}, u32[]{:S(2)}, u32[]{:S(2)}) %collective-permute-start.17) | collective-permute-done | bytes 524320 | tf_op jit(solution)/shard_map/ppermute | solution.py:21
  114.5 3.3 %collective-permute-done.20.refs_5_ = bf16[512,512]{1,0:T(8,128)(2,1)S(1)} collective-permute-done((bf16[512,512]{1,0:T(8,128)(2,1)}, bf16[512,512]{1,0:T(8,128)(2,1)S(1)}, u32[]{:S(2)}, u32[]{:S(2)}) %collective-permute-start.20) | collective-permute-done | bytes 524320 | tf_op jit(solution)/shard_map/ppermute | solution.py:21
  117.8 4.0 %gate_gradients.1 = (bf16[512,1024]{1,0:T(8,128)(2,1)}, bf16[512,1024]{1,0:T(8,128)(2,1)S(1)}, bf16[128,1024]{1,0:T(8,128)(2,1)}) custom-call(f32[512,512]{1,0:T(8,128)S(1)} %get-tuple-element.49.refs_0_, f32[512,512]{1,0:T(8,128)S(1)} %get-tuple-element.50.refs_1_, bf16[512,512]{1,0:T(8,128)(2,1)S(1)} %collective-permute-done.17.refs_2_, ...), custom_call_target="tpu_custom_call" | custom-call | flops 1048576 | bytes 262144 | tf_op jit(solution)/shard_map/gate_gradients/pallas_call | solution.py:264
  121.8 2.0 %collective-permute-start.24 = (bf16[128,1024]{1,0:T(8,128)(2,1)}, bf16[128,1024]{1,0:T(8,128)(2,1)}, u32[]{:S(2)}, u32[]{:S(2)}) collective-permute-start(bf16[128,1024]{1,0:T(8,128)(2,1)} %get-tuple-element.60), channel_id=1, source_target_pairs={{8,0},{16,8},{24,16},{32,24},{40,32},{48,40},{56,48},{64,56},{72,6... | collective-permute-start | bytes 786440 | tf_op jit(solution)/shard_map/ppermute | solution.py:27
  123.9 5.7 %filter_part.1 = f32[64,128]{1,0:T(8,128)S(1)} custom-call(bf16[512,1024]{1,0:T(8,128)(2,1)S(1)} %get-tuple-element.64.inner_ref, bf16[512,1024]{1,0:T(8,128)(2,1)S(1)} %copy-done.11, bf16[128,1024]{1,0:T(8,128)(2,1)S(1)} %collective-permute-done.3.rim_ref), custom_call_target="tpu_custom_call" | custom-call | flops 1048576 | bytes 262144 | tf_op jit(solution)/shard_map/filter_part/pallas_call | solution.py:303
  129.7 1.9 %collective-permute-start.22 = (f32[64,128]{1,0:T(8,128)S(1)}, f32[64,128]{1,0:T(8,128)S(1)}, u32[]{:S(2)}, u32[]{:S(2)}) collective-permute-start(f32[64,128]{1,0:T(8,128)S(1)} %filter_part.1), channel_id=1, source_target_pairs={{0,16},{8,24},{16,0},{24,8},{1,17},{9,25},{17,1},{25,9},{2,18},{10... | collective-permute-start | bytes 98312 | tf_op jit(solution)/shard_map/ppermute | solution.py:21
  131.6 2.5 %collective-permute-start.23 = (f32[64,128]{1,0:T(8,128)S(1)}, f32[64,128]{1,0:T(8,128)S(1)}, u32[]{:S(2)}, u32[]{:S(2)}) collective-permute-start(f32[64,128]{1,0:T(8,128)S(1)} %filter_part.1), channel_id=1, source_target_pairs={{0,8},{8,16},{16,24},{24,0},{1,9},{9,17},{17,25},{25,1},{2,10},{10... | collective-permute-start | bytes 98312 | tf_op jit(solution)/shard_map/ppermute | solution.py:21
  134.1 5.1 %collective-permute-done.24.ahead_ref = bf16[128,1024]{1,0:T(8,128)(2,1)} collective-permute-done((bf16[128,1024]{1,0:T(8,128)(2,1)}, bf16[128,1024]{1,0:T(8,128)(2,1)}, u32[]{:S(2)}, u32[]{:S(2)}) %collective-permute-start.24) | collective-permute-done | bytes 262176 | tf_op jit(solution)/shard_map/ppermute | solution.py:27
  139.2 4.0 %conv_backward.2 = (bf16[512,1024]{1,0:T(8,128)(2,1)}, bf16[512,1024]{1,0:T(8,128)(2,1)}) custom-call(bf16[64,128]{1,0:T(8,128)(2,1)S(1)} %copy-done.14, bf16[512,1024]{1,0:T(8,128)(2,1)S(1)} %get-tuple-element.64.inner_ref, bf16[128,1024]{1,0:T(8,128)(2,1)} %collective-permute-done.24.ahead_ref, bf16[512,1024]{1,0:T(8,128)(2,1)S(1)} %copy-done.3, ...), custom_call_target="tpu_custom_call" | custom-call | flops 1048576 | bytes 262144 | tf_op jit(solution)/shard_map/conv_backward/pallas_call | solution.py:343
  143.3 8.8 %collective-permute-start.25 = (f32[64,128]{1,0:T(8,128)S(1)}, f32[64,128]{1,0:T(8,128)S(1)}, u32[]{:S(2)}, u32[]{:S(2)}) collective-permute-start(f32[64,128]{1,0:T(8,128)S(1)} %select_add_fusion.1), channel_id=1, source_target_pairs={{0,192},{32,224},{64,0},{96,32},{128,64},{160,96},{192,128},{224,1... | collective-permute-start | bytes 98312 | tf_op jit(solution)/shard_map/ppermute | solution.py:21
  152.1 3.0 %collective-permute-start.26 = (f32[64,128]{1,0:T(8,128)S(1)}, f32[64,128]{1,0:T(8,128)S(1)}, u32[]{:S(2)}, u32[]{:S(2)}) collective-permute-start(f32[64,128]{1,0:T(8,128)S(1)} %select_add_fusion.1), channel_id=1, source_target_pairs={{0,128},{32,160},{64,192},{96,224},{128,0},{160,32},{192,64},{224,... | collective-permute-start | bytes 98312 | tf_op jit(solution)/shard_map/ppermute | solution.py:21
  155.0 2.8 %collective-permute-start.27 = (f32[64,128]{1,0:T(8,128)S(1)}, f32[64,128]{1,0:T(8,128)S(1)}, u32[]{:S(2)}, u32[]{:S(2)}) collective-permute-start(f32[64,128]{1,0:T(8,128)S(1)} %select_add_fusion.1), channel_id=1, source_target_pairs={{0,64},{32,96},{64,128},{96,160},{128,192},{160,224},{192,0},{224,... | collective-permute-start | bytes 98312 | tf_op jit(solution)/shard_map/ppermute | solution.py:21
  157.9 4.0 %conv_backward.3 = (bf16[512,1024]{1,0:T(8,128)(2,1)}, bf16[512,1024]{1,0:T(8,128)(2,1)}) custom-call(bf16[64,128]{1,0:T(8,128)(2,1)S(1)} %copy-done.14, bf16[512,1024]{1,0:T(8,128)(2,1)S(1)} %get-tuple-element.64.inner_ref, bf16[128,1024]{1,0:T(8,128)(2,1)} %collective-permute-done.24.ahead_ref, ...), custom_call_target="tpu_custom_call", output_to_operand_aliasing={{0}: (5, {}), {1}: (6, {})} | custom-call | flops 1048576 | bytes 262144 | tf_op jit(solution)/shard_map/conv_backward/pallas_call | solution.py:343
  162.1 1.8 %convert_element_type.15 = f32[128,1024]{1,0:T(8,128)} convert(bf16[128,1024]{1,0:T(8,128)(2,1)} %reduce-scatter.2.cloned.1.call-done) | non-fusion elementwise | flops 131072 | bytes 786432 | tf_op jit(solution)/shard_map/convert_element_type | solution.py:412
  163.9 2.1 %collective-permute-done.28 = f32[64,128]{1,0:T(8,128)S(1)} collective-permute-done((f32[64,128]{1,0:T(8,128)S(1)}, f32[64,128]{1,0:T(8,128)S(1)}, u32[]{:S(2)}, u32[]{:S(2)}) %collective-permute-start.28) | collective-permute-done | bytes 32800 | tf_op jit(solution)/shard_map/ppermute | solution.py:423
  (83 shorter events, 5.0 us)
Async XLA Ops:
  7.2 12.1 %copy-start.3 = (bf16[512,1024]{1,0:T(8,128)(2,1)S(1)}, bf16[512,1024]{1,0:T(8,128)(2,1)}, u32[]{:S(2)}) copy-start(bf16[512,1024]{1,0:T(8,128)(2,1)} %k_ref.7) | copy-start | bytes 3145732
  7.2 12.1 %copy-start.4 = (bf16[512,1024]{1,0:T(8,128)(2,1)S(1)}, bf16[512,1024]{1,0:T(8,128)(2,1)}, u32[]{:S(2)}) copy-start(bf16[512,1024]{1,0:T(8,128)(2,1)} %v_ref.7) | copy-start | bytes 3145732
  7.2 12.1 %copy-start.14 = (bf16[64,128]{1,0:T(8,128)(2,1)S(1)}, bf16[64,128]{1,0:T(8,128)(2,1)}, u32[]{:S(2)}) copy-start(bf16[64,128]{1,0:T(8,128)(2,1)} %filters_ref.7) | copy-start | bytes 49156
  7.2 55.6 %all-gather.2.cloned.1.call-start = ((), (), s32[]{:S(2)}) async-start(), calls=%async_computation.1 | async-start | bytes 2359296 | tf_op jit(solution)/shard_map/all_gather | solution.py:375
  8.5 10.8 %collective-permute-start.3 = (bf16[128,1024]{1,0:T(8,128)(2,1)S(1)}, bf16[128,1024]{1,0:T(8,128)(2,1)S(1)}, u32[]{:S(2)}, u32[]{:S(2)}) collective-permute-start(bf16[128,1024]{1,0:T(8,128)(2,1)S(1)} %multiply_convert_fusion), channel_id=1, source_target_pairs={{0,8},{8,16},{16,24},{24,32},{32,40},{40,48},{48,56},{56,64},{64,7... | collective-permute-start | bytes 786440 | tf_op jit(solution)/shard_map/ppermute | solution.py:27
  13.4 14.1 %collective-permute-start = (bf16[512,128]{1,0:T(8,128)(2,1)S(1)}, bf16[512,128]{1,0:T(8,128)(2,1)}, u32[]{:S(2)}, u32[]{:S(2)}) collective-permute-start(bf16[512,128]{1,0:T(8,128)(2,1)S(1)} %get-tuple-element.72), channel_id=1, source_target_pairs={{0,24},{8,0},{16,8},{24,16},{1,25},{9,1},{17,9},{25,17},{2,26},{10... | collective-permute-start | bytes 393224 | tf_op jit(solution)/shard_map/ppermute | solution.py:21
  13.7 13.8 %collective-permute-start.1 = (bf16[512,128]{1,0:T(8,128)(2,1)S(1)}, bf16[512,128]{1,0:T(8,128)(2,1)}, u32[]{:S(2)}, u32[]{:S(2)}) collective-permute-start(bf16[512,128]{1,0:T(8,128)(2,1)S(1)} %get-tuple-element.74), channel_id=1, source_target_pairs={{0,16},{8,24},{16,0},{24,8},{1,17},{9,25},{17,1},{25,9},{2,18},{10... | collective-permute-start | bytes 393224 | tf_op jit(solution)/shard_map/ppermute | solution.py:21
  15.1 12.4 %collective-permute-start.2 = (bf16[512,128]{1,0:T(8,128)(2,1)S(1)}, bf16[512,128]{1,0:T(8,128)(2,1)}, u32[]{:S(2)}, u32[]{:S(2)}) collective-permute-start(bf16[512,128]{1,0:T(8,128)(2,1)S(1)} %get-tuple-element.71), channel_id=1, source_target_pairs={{0,8},{8,16},{16,24},{24,0},{1,9},{9,17},{17,25},{25,1},{2,10},{10... | collective-permute-start | bytes 393224 | tf_op jit(solution)/shard_map/ppermute | solution.py:21
  17.2 144.8 %reduce-scatter.2.cloned.1.call-start = ((), (), s32[]{:S(2)}) async-start(), calls=%async_computation.2 | async-start | bytes 2359296 | tf_op jit(solution)/shard_map/reduce_scatter | solution.py:412
  19.3 1.2 copy-start.6
  24.0 8.4 %copy-start.13 = (bf16[512,512]{1,0:T(8,128)(2,1)}, bf16[512,512]{1,0:T(8,128)(2,1)S(1)}, u32[]{:S(2)}) copy-start(bf16[512,512]{1,0:T(8,128)(2,1)S(1)} %get-tuple-element.68.refs_0_) | copy-start | bytes 1572868
  27.5 23.2 %copy-start.8 = (f32[512,1024]{1,0:T(8,128)}, f32[512,1024]{1,0:T(8,128)S(1)}, u32[]{:S(2)}) copy-start(f32[512,1024]{1,0:T(8,128)S(1)} %get-tuple-element.55.refs_7_) | copy-start | bytes 6291460
  27.5 23.2 %copy-start.10 = (bf16[512,1024]{1,0:T(8,128)(2,1)}, bf16[512,1024]{1,0:T(8,128)(2,1)S(1)}, u32[]{:S(2)}) copy-start(bf16[512,1024]{1,0:T(8,128)(2,1)S(1)} %get-tuple-element.58.mixed_ref) | copy-start | bytes 3145732
  27.5 23.2 %copy-start.12 = (bf16[512,512]{1,0:T(8,128)(2,1)}, bf16[512,512]{1,0:T(8,128)(2,1)S(1)}, u32[]{:S(2)}) copy-start(bf16[512,512]{1,0:T(8,128)(2,1)S(1)} %get-tuple-element.44.refs_4_.refs_1_) | copy-start | bytes 1572868
  29.1 13.3 %collective-permute-start.5 = (bf16[2048,128]{1,0:T(8,128)(2,1)S(1)}, bf16[2048,128]{1,0:T(8,128)(2,1)S(1)}, u32[]{:S(2)}, u32[]{:S(2)}) collective-permute-start(bf16[2048,128]{1,0:T(8,128)(2,1)S(1)} %join.1), channel_id=1, source_target_pairs={{0,2},{2,4},{4,6},{6,0},{1,3},{3,5},{5,7},{7,1},{8,10},{10,12},{12... | collective-permute-start | bytes 1572872 | tf_op jit(solution)/shard_map/ppermute | solution.py:21
  30.7 12.0 %collective-permute-start.4 = (bf16[2048,128]{1,0:T(8,128)(2,1)S(1)}, bf16[2048,128]{1,0:T(8,128)(2,1)S(1)}, u32[]{:S(2)}, u32[]{:S(2)}) collective-permute-start(bf16[2048,128]{1,0:T(8,128)(2,1)S(1)} %join.1), channel_id=1, source_target_pairs={{0,6},{2,0},{4,2},{6,4},{1,7},{3,1},{5,3},{7,5},{8,14},{10,8},{12,... | collective-permute-start | bytes 1572872 | tf_op jit(solution)/shard_map/ppermute | solution.py:21
  32.4 13.4 %collective-permute-start.7 = (bf16[512,512]{1,0:T(8,128)(2,1)S(1)}, bf16[512,512]{1,0:T(8,128)(2,1)}, u32[]{:S(2)}, u32[]{:S(2)}) collective-permute-start(bf16[512,512]{1,0:T(8,128)(2,1)S(1)} %get-tuple-element.68.refs_0_), channel_id=1, source_target_pairs={{0,8},{8,16},{16,24},{24,0},{1,9},{9,17},{17,25},{25,1},{2,10},{10... | collective-permute-start | bytes 1572872 | tf_op jit(solution)/shard_map/ppermute | solution.py:21
  32.4 16.1 %collective-permute-start.10 = (bf16[512,512]{1,0:T(8,128)(2,1)S(1)}, bf16[512,512]{1,0:T(8,128)(2,1)S(1)}, u32[]{:S(2)}, u32[]{:S(2)}) collective-permute-start(bf16[512,512]{1,0:T(8,128)(2,1)S(1)} %get-tuple-element.68.refs_0_), channel_id=1, source_target_pairs={{0,24},{8,0},{16,8},{24,16},{1,25},{9,1},{17,9},{25,17},{2,26},{10... | collective-permute-start | bytes 1572872 | tf_op jit(solution)/shard_map/ppermute | solution.py:21
  35.1 21.3 %collective-permute-start.8 = (bf16[512,512]{1,0:T(8,128)(2,1)S(1)}, bf16[512,512]{1,0:T(8,128)(2,1)}, u32[]{:S(2)}, u32[]{:S(2)}) collective-permute-start(bf16[512,512]{1,0:T(8,128)(2,1)S(1)} %get-tuple-element.44.refs_4_.refs_1_), channel_id=1, source_target_pairs={{0,24},{8,0},{16,8},{24,16},{1,25},{9,1},{17,9},{25,17},{2,26},{10... | collective-permute-start | bytes 1572872 | tf_op jit(solution)/shard_map/ppermute | solution.py:21
  42.4 14.1 %collective-permute-start.6 = (bf16[1024,128]{1,0:T(8,128)(2,1)S(1)}, bf16[1024,128]{1,0:T(8,128)(2,1)S(1)}, u32[]{:S(2)}, u32[]{:S(2)}) collective-permute-start(bf16[1024,128]{1,0:T(8,128)(2,1)S(1)} %slice.16), channel_id=1, source_target_pairs={{0,2},{2,4},{4,6},{6,0},{1,3},{3,5},{5,7},{7,1},{8,10},{10,12},{12... | collective-permute-start | bytes 786440 | tf_op jit(solution)/shard_map/ppermute | solution.py:21
  42.8 13.7 %collective-permute-start.9 = (bf16[1024,128]{1,0:T(8,128)(2,1)S(1)}, bf16[1024,128]{1,0:T(8,128)(2,1)S(1)}, u32[]{:S(2)}, u32[]{:S(2)}) collective-permute-start(bf16[1024,128]{1,0:T(8,128)(2,1)S(1)} %slice.17), channel_id=1, source_target_pairs={{0,6},{2,0},{4,2},{6,4},{1,7},{3,1},{5,3},{7,5},{8,14},{10,8},{12,... | collective-permute-start | bytes 786440 | tf_op jit(solution)/shard_map/ppermute | solution.py:21
  48.5 9.2 %copy-start.18 = (bf16[512,512]{1,0:T(8,128)(2,1)}, bf16[512,512]{1,0:T(8,128)(2,1)S(1)}, u32[]{:S(2)}) copy-start(bf16[512,512]{1,0:T(8,128)(2,1)S(1)} %collective-permute-done.10.refs_2_) | copy-start | bytes 1572868
  48.5 9.2 %collective-permute-start.11 = (bf16[512,512]{1,0:T(8,128)(2,1)S(1)}, bf16[512,512]{1,0:T(8,128)(2,1)S(1)}, u32[]{:S(2)}, u32[]{:S(2)}) collective-permute-start(bf16[512,512]{1,0:T(8,128)(2,1)S(1)} %get-tuple-element.44.refs_4_.refs_1_), channel_id=1, source_target_pairs={{0,8},{8,16},{16,24},{24,0},{1,9},{9,17},{17,25},{25,1},{2,10},{10... | collective-permute-start | bytes 1572872 | tf_op jit(solution)/shard_map/ppermute | solution.py:21
  56.6 6.1 %copy-start = (bf16[8192,128]{1,0:T(8,128)(2,1)}, bf16[8192,128]{1,0:T(8,128)(2,1)S(1)}, u32[]{:S(2)}) copy-start(bf16[8192,128]{1,0:T(8,128)(2,1)S(1)} %constant_dynamic-update-slice_fusion) | copy-start | bytes 6291460
  58.5 4.3 %collective-permute-start.12 = (bf16[4,2048,128]{2,1,0:T(8,128)(2,1)S(1)}, bf16[4,2048,128]{2,1,0:T(8,128)(2,1)}, u32[]{:S(2)}, u32[]{:S(2)}) collective-permute-start(bf16[4,2048,128]{2,1,0:T(8,128)(2,1)S(1)} %bitcast.9), channel_id=1, source_target_pairs={{0,1},{1,0},{2,3},{3,2},{4,5},{5,4},{6,7},{7,6},{8,9},{9,8},{10,11... | collective-permute-start | bytes 6291464 | tf_op jit(solution)/shard_map/ppermute | solution.py:21
  58.5 16.2 %collective-permute-start.14 = (bf16[512,512]{1,0:T(8,128)(2,1)}, bf16[512,512]{1,0:T(8,128)(2,1)}, u32[]{:S(2)}, u32[]{:S(2)}) collective-permute-start(bf16[512,512]{1,0:T(8,128)(2,1)} %collective-permute-done.8.refs_3_), channel_id=1, source_target_pairs={{0,24},{8,0},{16,8},{24,16},{1,25},{9,1},{17,9},{25,17},{2,26},{10... | collective-permute-start | bytes 1572872 | tf_op jit(solution)/shard_map/ppermute | solution.py:21
  60.0 15.0 %collective-permute-start.13 = (bf16[512,512]{1,0:T(8,128)(2,1)}, bf16[512,512]{1,0:T(8,128)(2,1)}, u32[]{:S(2)}, u32[]{:S(2)}) collective-permute-start(bf16[512,512]{1,0:T(8,128)(2,1)} %collective-permute-done.7.refs_6_), channel_id=1, source_target_pairs={{0,8},{8,16},{16,24},{24,0},{1,9},{9,17},{17,25},{25,1},{2,10},{10... | collective-permute-start | bytes 1572872 | tf_op jit(solution)/shard_map/ppermute | solution.py:21
  68.3 24.8 %collective-permute-start.15 = (bf16[512,512]{1,0:T(8,128)(2,1)}, bf16[512,512]{1,0:T(8,128)(2,1)S(1)}, u32[]{:S(2)}, u32[]{:S(2)}) collective-permute-start(bf16[512,512]{1,0:T(8,128)(2,1)} %get-tuple-element.46), channel_id=1, source_target_pairs={{0,8},{8,16},{16,24},{24,0},{1,9},{9,17},{17,25},{25,1},{2,10},{10... | collective-permute-start | bytes 1572872 | tf_op jit(solution)/shard_map/ppermute | solution.py:21
  71.6 21.5 %collective-permute-start.16 = (bf16[512,512]{1,0:T(8,128)(2,1)}, bf16[512,512]{1,0:T(8,128)(2,1)S(1)}, u32[]{:S(2)}, u32[]{:S(2)}) collective-permute-start(bf16[512,512]{1,0:T(8,128)(2,1)} %get-tuple-element.47), channel_id=1, source_target_pairs={{0,24},{8,0},{16,8},{24,16},{1,25},{9,1},{17,9},{25,17},{2,26},{10... | collective-permute-start | bytes 1572872 | tf_op jit(solution)/shard_map/ppermute | solution.py:21
  80.8 19.9 %collective-permute-start.18 = (bf16[512,512]{1,0:T(8,128)(2,1)}, bf16[512,512]{1,0:T(8,128)(2,1)}, u32[]{:S(2)}, u32[]{:S(2)}) collective-permute-start(bf16[512,512]{1,0:T(8,128)(2,1)} %get-tuple-element.52), channel_id=1, source_target_pairs={{0,8},{8,16},{16,24},{24,0},{1,9},{9,17},{17,25},{25,1},{2,10},{10... | collective-permute-start | bytes 1572872 | tf_op jit(solution)/shard_map/ppermute | solution.py:21
  83.8 16.9 %collective-permute-start.19 = (bf16[512,512]{1,0:T(8,128)(2,1)}, bf16[512,512]{1,0:T(8,128)(2,1)}, u32[]{:S(2)}, u32[]{:S(2)}) collective-permute-start(bf16[512,512]{1,0:T(8,128)(2,1)} %get-tuple-element.53), channel_id=1, source_target_pairs={{0,24},{8,0},{16,8},{24,16},{1,25},{9,1},{17,9},{25,17},{2,26},{10... | collective-permute-start | bytes 1572872 | tf_op jit(solution)/shard_map/ppermute | solution.py:21
  100.7 3.4 %copy-start.1 = (bf16[8192,128]{1,0:T(8,128)(2,1)S(1)}, bf16[8192,128]{1,0:T(8,128)(2,1)}, u32[]{:S(2)}) copy-start(bf16[8192,128]{1,0:T(8,128)(2,1)} %copy-done) | copy-start | bytes 6291460
  100.7 3.4 %copy-start.15 = (s32[8]{0:T(128)S(1)}, s32[8]{0:T(128)}, u32[]{:S(2)}) copy-start(s32[8]{0:T(128)} %stack.35.place_ref) | copy-start | bytes 100
  100.7 13.8 %collective-permute-start.17 = (bf16[512,512]{1,0:T(8,128)(2,1)}, bf16[512,512]{1,0:T(8,128)(2,1)S(1)}, u32[]{:S(2)}, u32[]{:S(2)}) collective-permute-start(bf16[512,512]{1,0:T(8,128)(2,1)} %get-tuple-element.51), channel_id=1, source_target_pairs={{0,8},{8,16},{16,24},{24,0},{1,9},{9,17},{17,25},{25,1},{2,10},{10... | collective-permute-start | bytes 1572872 | tf_op jit(solution)/shard_map/ppermute | solution.py:21
  104.0 13.8 %collective-permute-start.20 = (bf16[512,512]{1,0:T(8,128)(2,1)}, bf16[512,512]{1,0:T(8,128)(2,1)S(1)}, u32[]{:S(2)}, u32[]{:S(2)}) collective-permute-start(bf16[512,512]{1,0:T(8,128)(2,1)} %get-tuple-element.54), channel_id=1, source_target_pairs={{0,24},{8,0},{16,8},{24,16},{1,25},{9,1},{17,9},{25,17},{2,26},{10... | collective-permute-start | bytes 1572872 | tf_op jit(solution)/shard_map/ppermute | solution.py:21
  104.1 1.6 copy-start.2
  105.6 12.2 %copy-start.7 = (bf16[512,1024]{1,0:T(8,128)(2,1)S(1)}, bf16[512,1024]{1,0:T(8,128)(2,1)}, u32[]{:S(2)}) copy-start(bf16[512,1024]{1,0:T(8,128)(2,1)} %refs_6_.1) | copy-start | bytes 3145732
  105.6 12.2 %copy-start.9 = (f32[512,1024]{1,0:T(8,128)S(1)}, f32[512,1024]{1,0:T(8,128)}, u32[]{:S(2)}) copy-start(f32[512,1024]{1,0:T(8,128)} %copy-done.8) | copy-start | bytes 6291460
  117.8 6.1 %copy-start.11 = (bf16[512,1024]{1,0:T(8,128)(2,1)S(1)}, bf16[512,1024]{1,0:T(8,128)(2,1)}, u32[]{:S(2)}) copy-start(bf16[512,1024]{1,0:T(8,128)(2,1)} %copy-done.10) | copy-start | bytes 3145732
  121.8 17.4 %copy-start.5 = (bf16[512,1024]{1,0:T(8,128)(2,1)S(1)}, bf16[512,1024]{1,0:T(8,128)(2,1)}, u32[]{:S(2)}) copy-start(bf16[512,1024]{1,0:T(8,128)(2,1)} %v_ref.7) | copy-start | bytes 3145732
  121.8 17.4 %collective-permute-start.24 = (bf16[128,1024]{1,0:T(8,128)(2,1)}, bf16[128,1024]{1,0:T(8,128)(2,1)}, u32[]{:S(2)}, u32[]{:S(2)}) collective-permute-start(bf16[128,1024]{1,0:T(8,128)(2,1)} %get-tuple-element.60), channel_id=1, source_target_pairs={{8,0},{16,8},{24,16},{32,24},{40,32},{48,40},{56,48},{64,56},{72,6... | collective-permute-start | bytes 786440 | tf_op jit(solution)/shard_map/ppermute | solution.py:27
  129.6 13.6 %collective-permute-start.21 = (f32[64,128]{1,0:T(8,128)S(1)}, f32[64,128]{1,0:T(8,128)S(1)}, u32[]{:S(2)}, u32[]{:S(2)}) collective-permute-start(f32[64,128]{1,0:T(8,128)S(1)} %filter_part.1), channel_id=1, source_target_pairs={{0,24},{8,0},{16,8},{24,16},{1,25},{9,1},{17,9},{25,17},{2,26},{10... | collective-permute-start | bytes 98312 | tf_op jit(solution)/shard_map/ppermute | solution.py:21
  129.7 13.6 %collective-permute-start.22 = (f32[64,128]{1,0:T(8,128)S(1)}, f32[64,128]{1,0:T(8,128)S(1)}, u32[]{:S(2)}, u32[]{:S(2)}) collective-permute-start(f32[64,128]{1,0:T(8,128)S(1)} %filter_part.1), channel_id=1, source_target_pairs={{0,16},{8,24},{16,0},{24,8},{1,17},{9,25},{17,1},{25,9},{2,18},{10... | collective-permute-start | bytes 98312 | tf_op jit(solution)/shard_map/ppermute | solution.py:21
  131.6 11.7 %collective-permute-start.23 = (f32[64,128]{1,0:T(8,128)S(1)}, f32[64,128]{1,0:T(8,128)S(1)}, u32[]{:S(2)}, u32[]{:S(2)}) collective-permute-start(f32[64,128]{1,0:T(8,128)S(1)} %filter_part.1), channel_id=1, source_target_pairs={{0,8},{8,16},{16,24},{24,0},{1,9},{9,17},{17,25},{25,1},{2,10},{10... | collective-permute-start | bytes 98312 | tf_op jit(solution)/shard_map/ppermute | solution.py:21
  143.3 18.6 %collective-permute-start.25 = (f32[64,128]{1,0:T(8,128)S(1)}, f32[64,128]{1,0:T(8,128)S(1)}, u32[]{:S(2)}, u32[]{:S(2)}) collective-permute-start(f32[64,128]{1,0:T(8,128)S(1)} %select_add_fusion.1), channel_id=1, source_target_pairs={{0,192},{32,224},{64,0},{96,32},{128,64},{160,96},{192,128},{224,1... | collective-permute-start | bytes 98312 | tf_op jit(solution)/shard_map/ppermute | solution.py:21
  152.1 9.8 %collective-permute-start.26 = (f32[64,128]{1,0:T(8,128)S(1)}, f32[64,128]{1,0:T(8,128)S(1)}, u32[]{:S(2)}, u32[]{:S(2)}) collective-permute-start(f32[64,128]{1,0:T(8,128)S(1)} %select_add_fusion.1), channel_id=1, source_target_pairs={{0,128},{32,160},{64,192},{96,224},{128,0},{160,32},{192,64},{224,... | collective-permute-start | bytes 98312 | tf_op jit(solution)/shard_map/ppermute | solution.py:21
  155.0 6.9 %collective-permute-start.27 = (f32[64,128]{1,0:T(8,128)S(1)}, f32[64,128]{1,0:T(8,128)S(1)}, u32[]{:S(2)}, u32[]{:S(2)}) collective-permute-start(f32[64,128]{1,0:T(8,128)S(1)} %select_add_fusion.1), channel_id=1, source_target_pairs={{0,64},{32,96},{64,128},{96,160},{128,192},{160,224},{192,0},{224,... | collective-permute-start | bytes 98312 | tf_op jit(solution)/shard_map/ppermute | solution.py:21
  161.9 4.0 %collective-permute-start.28 = (f32[64,128]{1,0:T(8,128)S(1)}, f32[64,128]{1,0:T(8,128)S(1)}, u32[]{:S(2)}, u32[]{:S(2)}) collective-permute-start(f32[64,128]{1,0:T(8,128)S(1)} %select_add_fusion), channel_id=1, source_target_pairs={{0,32},{32,0},{64,96},{96,64},{128,160},{160,128},{192,224},{224,1... | collective-permute-start | bytes 98312 | tf_op jit(solution)/shard_map/ppermute | solution.py:423
  (3 other events, 2.4 us)
Sparse Core Ops, SparseCore 0:
  17.4 43.7 all-gather.1
  100.8 47.9 reduce-scatter.1

commit v7 on v6

--- a/solution.py
+++ b/solution.py
@@ -139,63 +139,45 @@
     )(*pieces, later_than)
 
 
-def gate_body(place_ref, mine_ref, sib_ref, proj_ref, *refs):
+def gate_body(wanted, place_ref, mine_ref, sib_ref, proj_ref, *refs):
     added, outs = refs[:-2], refs[-2:]
     rows = proj_ref.shape[0] // 8
-    acc = None
-    for dy in range(4):
-        lhs = jnp.concatenate([mine_ref[dy], sib_ref[dy]], 1)
-        rhs = jnp.concatenate(
-            [
-                proj_ref[pl.ds(pl.multiple_of(place_ref[2 * dy + i] * rows, rows), rows), :]
-                for i in range(2)
-            ],
-            0,
-        )
-        term = jnp.dot(lhs, rhs, preferred_element_type=F32)
-        acc = term if acc is None else acc + term
-    second = pl.program_id(0) >= pl.num_programs(0) // 2
-    if added:
-        acc = acc + jnp.where(second, added[1][...], added[0][...]).astype(F32)
-    acc = acc.astype(outs[0].dtype)
-
-    @pl.when(jnp.logical_not(second))
-    def _():
-        outs[0][...] = acc
-
-    @pl.when(second)
-    def _():
-        outs[1][...] = acc
+    tokens, half = outs[0].shape
+    tile = 256
+    for n, (block, side) in enumerate(wanted):
+        at = pl.ds(block * tokens, tokens)
+        lhs = [jnp.concatenate([mine_ref[dy, at], sib_ref[dy, at]], 1) for dy in range(4)]
+        for start in range(0, half, tile):
+            cols = pl.ds(side * half + start, tile)
+            acc = None
+            for dy in range(4):
+                rhs = jnp.concatenate(
+                    [
+                        proj_ref[pl.ds(pl.multiple_of(place_ref[2 * dy + i] * rows, rows), rows), cols]
+                        for i in range(2)
+                    ],
+                    0,
+                )
+                term = jnp.dot(lhs[dy], rhs, preferred_element_type=F32)
+                acc = term if acc is None else acc + term
+            here = pl.ds(start, tile)
+            if added:
+                acc = acc + added[n][:, here].astype(F32)
+            outs[n][:, here] = acc.astype(outs[n].dtype)
+
+
+RESIDENT = pl.BlockSpec(memory_space=pltpu.VMEM)
 
 
 def gate_parts(place, mine, sib, proj, wanted, dtype, *added):
-    depth, width = proj.shape
+    width = proj.shape[1]
     tokens = mine.shape[1] // 4
-    tile = 256
-    steps = width // 2 // tile
-    (block0, half0), (block1, half1) = wanted
-    choose = lambda i, first, second: jnp.where(i < steps, first, second)
-    cot = pl.BlockSpec((4, tokens, depth // 8), lambda i, p: (0, choose(i, block0, block1), 0))
-    pair = [
-        pl.BlockSpec((tokens, tile), lambda i, p: (0, jnp.minimum(i, steps - 1))),
-        pl.BlockSpec((tokens, tile), lambda i, p: (0, jnp.maximum(i - steps, 0))),
-    ]
-    spec = pltpu.PrefetchScalarGridSpec(
-        num_scalar_prefetch=1,
-        grid=(2 * steps,),
-        in_specs=[
-            cot,
-            cot,
-            pl.BlockSpec((depth, tile), lambda i, p: (0, i % steps + choose(i, half0, half1) * steps)),
-        ]
-        + pair[: len(added)],
-        out_specs=pair,
-    )
-    return pl.pallas_call(
-        gate_body,
-        grid_spec=spec,
+    return pl.pallas_call(
+        functools.partial(gate_body, wanted),
+        in_specs=[pl.BlockSpec(memory_space=pltpu.SMEM)] + [RESIDENT] * (3 + len(added)),
+        out_specs=[RESIDENT] * 2,
         out_shape=[jax.ShapeDtypeStruct((tokens, width // 2), dtype)] * 2,
-        compiler_params=pltpu.CompilerParams(vmem_limit_bytes=(16 if dtype == F32 else 60) * MIB),
+        compiler_params=pltpu.CompilerParams(vmem_limit_bytes=14 * MIB),
         cost_estimate=LIGHT,
         name="grad_gate_parts",
     )(place, mine, sib, proj, *added)
@@ -203,40 +185,38 @@
 
 def proj_body(place_ref, mine_ref, sib_ref, *refs):
     gated_refs, out_ref = refs[:-1], refs[-1]
-    rows = mine_ref.shape[1]
+    rows = mine_ref.shape[2]
     tokens, half = gated_refs[0].shape
-    core = place_ref[0] % 2
-    for h in range(2):
-        acc = None
-        for d in range(4):
-            at = pl.ds(d * tokens, tokens)
-            lhs = jnp.concatenate([mine_ref[at, :], sib_ref[at, :]], 1)
-            term = lax.dot_general(
-                lhs, gated_refs[2 * d + h][...], (((0,), (0,)), ((), ())), preferred_element_type=F32
-            )
-            acc = term if acc is None else acc + term
-        acc = acc.astype(BF16)
-        cols = pl.ds(h * half, half)
-        out_ref[pl.ds(pl.multiple_of(core * rows, rows), rows), cols] = acc[:rows]
-        out_ref[pl.ds(pl.multiple_of((1 - core) * rows, rows), rows), cols] = acc[rows:]
+    for dy in range(4):
+        lhs = [
+            jnp.concatenate([mine_ref[dy, at], sib_ref[dy, at]], 1)
+            for at in (pl.ds(d * tokens, tokens) for d in range(4))
+        ]
+        for h in range(2):
+            acc = None
+            for d in range(4):
+                term = lax.dot_general(
+                    lhs[d],
+                    gated_refs[2 * d + h][...],
+                    (((0,), (0,)), ((), ())),
+                    preferred_element_type=F32,
+                )
+                acc = term if acc is None else acc + term
+            acc = acc.astype(BF16)
+            cols = pl.ds(h * half, half)
+            for i in range(2):
+                to = pl.ds(pl.multiple_of(place_ref[2 * dy + i] * rows, rows), rows)
+                out_ref[to, cols] = acc[i * rows : (i + 1) * rows]
 
 
 def proj_part(place, mine, sib, gated):
-    rows = mine.shape[2]
-    depth = 8 * rows
-    tokens, half = gated[0].shape
-    spec = pltpu.PrefetchScalarGridSpec(
-        num_scalar_prefetch=1,
-        grid=(4,),
-        in_specs=[pl.BlockSpec((None, 4 * tokens, rows), lambda i, p: (i, 0, 0))] * 2
-        + [pl.BlockSpec((tokens, half), lambda i, p: (0, 0))] * 8,
-        out_specs=pl.BlockSpec((2 * rows, 2 * half), lambda i, p: (p[2 * i] // 2, 0)),
-    )
+    half = gated[0].shape[1]
     return pl.pallas_call(
         proj_body,
-        grid_spec=spec,
-        out_shape=jax.ShapeDtypeStruct((depth, 2 * half), BF16),
-        compiler_params=pltpu.CompilerParams(vmem_limit_bytes=60 * MIB),
+        in_specs=[pl.BlockSpec(memory_space=pltpu.SMEM)] + [RESIDENT] * 10,
+        out_specs=RESIDENT,
+        out_shape=jax.ShapeDtypeStruct((8 * mine.shape[2], 2 * half), BF16),
+        compiler_params=pltpu.CompilerParams(vmem_limit_bytes=14 * MIB),
         cost_estimate=LIGHT,
         name="grad_proj_part",
     )(place, mine, sib, *gated)
@@ -400,7 +380,7 @@
 
     across = gate_parts(place, mine, sib, proj, ((2, 0), (2, 1)), BF16)
     far_a, far_b = send(across[0], "x", 1), send(across[1], "x", -1)
-    proj = after(proj, *across, *gated[4:6])
+    proj = after(proj, *across)
     beside = gate_parts(place, mine, sib, proj, ((1, 1), (3, 0)), BF16)
     from_left_b, from_right_a = send(beside[0], "x", 1), send(beside[1], "x", -1)
     gated[0] = after(gated[0], *beside)

time: 175 us -> 170 us (0.971)
  Pallas kernels: 57.1 us -> 44.8 us
  waiting for transfers between devices: 35.4 us -> 40.6 us
  local copies, waits for them, and re-layouts: 7.98 us -> 12 us
    pallas_call x5, Pallas kernels: 30.9 us -> 20.2 us  [the longest x4 13.7 us: gate_parts(): pl.pallas_call(functools.partial(gate_body, wanted), in_specs=[pl.BlockSp...]
    unnamed x44 -> x56, local copies, waits for them, and re-layouts: 5.4 us -> 10 us
    ppermute x26, waiting for transfers between devices: 26.2 us -> 30.6 us  [send(): lax.ppermute(value, axis, [(i, (i + by) % count) for i in range(count)])]
    ppermute x26, starting transfers between devices: 49.4 us -> 47.5 us  [send(): lax.ppermute(value, axis, [(i, (i + by) % count) for i in range(count)])]
  transfers between devices with their start and end apart: 31 -> 31, of which waited for: 12 -> 15; matrix products, arithmetic and copies ran while one was open for 2% -> 2% of each run, Pallas kernels for 33% -> 26%
where the time goes in v7:
time: 170 us; the launch traced here: 169 us
  starting transfers between devices  53.9 us (32%)
  Pallas kernels  44.8 us (26%)
  waiting for transfers between devices  40.6 us (24%)
  between operations  14.5 us (9%)
  local copies, waits for them, and re-layouts  12 us (7%)
  other arithmetic  3.09 us (2%)
    ppermute x26, starting transfers between devices, send(): lax.ppermute(value, axis, [(i, (i + by) % count) for i in range(count)])  47.5 us
    ppermute x26, waiting for transfers between devices, send(): lax.ppermute(value, axis, [(i, (i + by) % count) for i in range(count)])  30.6 us
    pallas_call x4, Pallas kernels, gate_parts(): pl.pallas_call(functools.partial(gate_body, wanted), in_specs=[pl.BlockSp...  13.7 us
    unnamed x56, local copies, waits for them, and re-layouts  10 us
    pallas_call x2, Pallas kernels, backward(): pl.pallas_call(functools.partial(backward_body, taps, groups), grid=(step...  8.05 us
    ppermute x2, waiting for transfers between devices, send_along_tokens(): return lax.ppermute(value, ('z', 'x'), pairs)  8.05 us
    pallas_call x2, Pallas kernels, forward(): pl.pallas_call(functools.partial(forward_body, taps, groups), grid=(steps...  6.91 us
    pallas_call x1, Pallas kernels, proj_part(): pl.pallas_call(proj_body, in_specs=[pl.BlockSpec(memory_space=pltpu.SMEM)...  6.51 us
  transfers between devices with their start and end apart: 31, of which 15 were waited for; matrix products, arithmetic and copies ran while one was open for 2% of the time, Pallas kernels for 26%

profile of v7, /device:TPU:6, one launch (start us, length us, event | category | flops | bytes accessed | tf_op | source)
XLA Modules:
  0.0 169.0 jit_solution(17455120734932389917)
XLA Ops:
  7.2 1.2 multiply_convert_fusion
  8.5 3.7 %collective-permute-start.3 = (bf16[128,1024]{1,0:T(8,128)(2,1)S(1)}, bf16[128,1024]{1,0:T(8,128)(2,1)S(1)}, u32[]{:S(2)}, u32[]{:S(2)}) collective-permute-start(bf16[128,1024]{1,0:T(8,128)(2,1)S(1)} %multiply_convert_fusion), channel_id=1, source_target_pairs={{0,8},{8,16},{16,24},{24,32},{32,40},{40,48},{48,56},{56,64},{64,7... | collective-permute-start | bytes 786440 | tf_op jit(solution)/shard_map/ppermute | solution.py:27
  13.7 1.4 collective-permute-start.1
  15.1 2.1 %collective-permute-start.2 = (bf16[512,128]{1,0:T(8,128)(2,1)S(1)}, bf16[512,128]{1,0:T(8,128)(2,1)S(1)}, u32[]{:S(2)}, u32[]{:S(2)}) collective-permute-start(bf16[512,128]{1,0:T(8,128)(2,1)S(1)} %get-tuple-element.71), channel_id=1, source_target_pairs={{0,8},{8,16},{16,24},{24,0},{1,9},{9,17},{17,25},{25,1},{2,10},{10... | collective-permute-start | bytes 393224 | tf_op jit(solution)/shard_map/ppermute | solution.py:21
  17.3 2.0 %collective-permute-done.3.rim_ref = bf16[128,1024]{1,0:T(8,128)(2,1)S(1)} collective-permute-done((bf16[128,1024]{1,0:T(8,128)(2,1)S(1)}, bf16[128,1024]{1,0:T(8,128)(2,1)S(1)}, u32[]{:S(2)}, u32[]{:S(2)}) %collective-permute-start.3) | collective-permute-done | bytes 262176 | tf_op jit(solution)/shard_map/ppermute | solution.py:27
  19.3 1.2 copy-done.6
  20.5 3.4 %conv_forward.2 = (f32[512,1024]{1,0:T(8,128)S(1)}, bf16[512,1024]{1,0:T(8,128)(2,1)S(1)}, bf16[512,512]{1,0:T(8,128)(2,1)S(1)}) custom-call(bf16[64,128]{1,0:T(8,128)(2,1)S(1)} %copy-done.23, bf16[512,1024]{1,0:T(8,128)(2,1)S(1)} %copy-done.3, bf16[512,1024]{1,0:T(8,128)(2,1)S(1)} %copy-done.4, bf16[512,1024]{1,0:T(8,128)(2,1)S(1)} %copy-done.6, ...), custom_call_target="tpu_custom_call" | custom-call | flops 1048576 | bytes 262144 | tf_op jit(solution)/shard_map/conv_forward/pallas_call | solution.py:105
  24.0 3.5 %conv_forward.3 = (f32[512,1024]{1,0:T(8,128)S(1)}, bf16[512,1024]{1,0:T(8,128)(2,1)S(1)}, bf16[512,512]{1,0:T(8,128)(2,1)S(1)}) custom-call(bf16[64,128]{1,0:T(8,128)(2,1)S(1)} %copy-done.23, bf16[512,1024]{1,0:T(8,128)(2,1)S(1)} %copy-done.3, bf16[512,1024]{1,0:T(8,128)(2,1)S(1)} %copy-done.4, ...), custom_call_target="tpu_custom_call", output_to_operand_aliasing={{0}: (5, {}), {1}: (6, {})} | custom-call | flops 1048576 | bytes 262144 | tf_op jit(solution)/shard_map/conv_forward/pallas_call | solution.py:105
  27.6 1.7 collective-permute-start.5
  29.2 1.7 collective-permute-start.4
  30.9 2.7 %collective-permute-start.10 = (bf16[512,512]{1,0:T(8,128)(2,1)S(1)}, bf16[512,512]{1,0:T(8,128)(2,1)S(1)}, u32[]{:S(2)}, u32[]{:S(2)}) collective-permute-start(bf16[512,512]{1,0:T(8,128)(2,1)S(1)} %get-tuple-element.68.refs_0_), channel_id=1, source_target_pairs={{0,24},{8,0},{16,8},{24,16},{1,25},{9,1},{17,9},{25,17},{2,26},{10... | collective-permute-start | bytes 1572872 | tf_op jit(solution)/shard_map/ppermute | solution.py:21
  33.6 2.0 %collective-permute-start.8 = (bf16[512,512]{1,0:T(8,128)(2,1)S(1)}, bf16[512,512]{1,0:T(8,128)(2,1)}, u32[]{:S(2)}, u32[]{:S(2)}) collective-permute-start(bf16[512,512]{1,0:T(8,128)(2,1)S(1)} %get-tuple-element.44.refs_4_.refs_1_), channel_id=1, source_target_pairs={{0,24},{8,0},{16,8},{24,16},{1,25},{9,1},{17,9},{25,17},{2,26},{10... | collective-permute-start | bytes 1572872 | tf_op jit(solution)/shard_map/ppermute | solution.py:21
  35.7 5.2 %collective-permute-done.5 = bf16[2048,128]{1,0:T(8,128)(2,1)S(1)} collective-permute-done((bf16[2048,128]{1,0:T(8,128)(2,1)S(1)}, bf16[2048,128]{1,0:T(8,128)(2,1)S(1)}, u32[]{:S(2)}, u32[]{:S(2)}) %collective-permute-start.5) | collective-permute-done | bytes 524320 | tf_op jit(solution)/shard_map/ppermute | solution.py:21
  41.3 3.0 %collective-permute-start.9 = (bf16[1024,128]{1,0:T(8,128)(2,1)S(1)}, bf16[1024,128]{1,0:T(8,128)(2,1)S(1)}, u32[]{:S(2)}, u32[]{:S(2)}) collective-permute-start(bf16[1024,128]{1,0:T(8,128)(2,1)S(1)} %slice.17), channel_id=1, source_target_pairs={{0,6},{2,0},{4,2},{6,4},{1,7},{3,1},{5,3},{7,5},{8,14},{10,8},{12,... | collective-permute-start | bytes 786440 | tf_op jit(solution)/shard_map/ppermute | solution.py:21
  44.3 2.6 %collective-permute-done.10.refs_2_ = bf16[512,512]{1,0:T(8,128)(2,1)S(1)} collective-permute-done((bf16[512,512]{1,0:T(8,128)(2,1)S(1)}, bf16[512,512]{1,0:T(8,128)(2,1)S(1)}, u32[]{:S(2)}, u32[]{:S(2)}) %collective-permute-start.10) | collective-permute-done | bytes 524320 | tf_op jit(solution)/shard_map/ppermute | solution.py:21
  47.0 2.1 %collective-permute-start.11 = (bf16[512,512]{1,0:T(8,128)(2,1)S(1)}, bf16[512,512]{1,0:T(8,128)(2,1)S(1)}, u32[]{:S(2)}, u32[]{:S(2)}) collective-permute-start(bf16[512,512]{1,0:T(8,128)(2,1)S(1)} %get-tuple-element.44.refs_4_.refs_1_), channel_id=1, source_target_pairs={{0,8},{8,16},{16,24},{24,0},{1,9},{9,17},{17,25},{25,1},{2,10},{10... | collective-permute-start | bytes 1572872 | tf_op jit(solution)/shard_map/ppermute | solution.py:21
  49.2 5.8 %collective-permute-done.8.refs_3_ = bf16[512,512]{1,0:T(8,128)(2,1)} collective-permute-done((bf16[512,512]{1,0:T(8,128)(2,1)S(1)}, bf16[512,512]{1,0:T(8,128)(2,1)}, u32[]{:S(2)}, u32[]{:S(2)}) %collective-permute-start.8) | collective-permute-done | bytes 524320 | tf_op jit(solution)/shard_map/ppermute | solution.py:21
  57.0 1.5 collective-permute-start.27
  58.6 2.1 %collective-permute-start.26 = (bf16[512,512]{1,0:T(8,128)(2,1)}, bf16[512,512]{1,0:T(8,128)(2,1)}, u32[]{:S(2)}, u32[]{:S(2)}) collective-permute-start(bf16[512,512]{1,0:T(8,128)(2,1)} %copy-done.17), channel_id=1, source_target_pairs={{0,8},{8,16},{16,24},{24,0},{1,9},{9,17},{17,25},{25,1},{2,10},{10... | collective-permute-start | bytes 1572872 | tf_op jit(solution)/shard_map/ppermute | solution.py:21
  61.4 1.6 copy-done
  63.0 3.7 %grad_gate_parts.4 = (bf16[512,512]{1,0:T(8,128)(2,1)}, bf16[512,512]{1,0:T(8,128)(2,1)}) custom-call(s32[8]{0:T(128)S(1)} %stack.35.place_ref, bf16[4,2048,128]{2,1,0:T(8,128)(2,1)S(1)} %bitcast.10, bf16[4,2048,128]{2,1,0:T(8,128)(2,1)} %collective-permute-done.12.sib_ref, bf16[1024,1024]{1,0:T(8,128)(2,1)S(1)} %copy-done), custom_call_target="tpu_custom_call" | custom-call | flops 1048576 | bytes 262144 | tf_op jit(solution)/shard_map/grad_gate_parts/pallas_call | solution.py:175
  66.7 3.2 %collective-permute-start.13 = (bf16[512,512]{1,0:T(8,128)(2,1)}, bf16[512,512]{1,0:T(8,128)(2,1)}, u32[]{:S(2)}, u32[]{:S(2)}) collective-permute-start(bf16[512,512]{1,0:T(8,128)(2,1)} %get-tuple-element.46), channel_id=1, source_target_pairs={{0,8},{8,16},{16,24},{24,0},{1,9},{9,17},{17,25},{25,1},{2,10},{10... | collective-permute-start | bytes 1572872 | tf_op jit(solution)/shard_map/ppermute | solution.py:21
  70.0 3.9 %grad_gate_parts.7 = (bf16[512,512]{1,0:T(8,128)(2,1)}, bf16[512,512]{1,0:T(8,128)(2,1)}) custom-call(s32[8]{0:T(128)S(1)} %stack.35.place_ref, bf16[4,2048,128]{2,1,0:T(8,128)(2,1)S(1)} %bitcast.11, bf16[4,2048,128]{2,1,0:T(8,128)(2,1)} %collective-permute-done.12.sib_ref, bf16[1024,1024]{1,0:T(8,128)(2,1)S(1)} %copy-done), custom_call_target="tpu_custom_call" | custom-call | flops 1048576 | bytes 262144 | tf_op jit(solution)/shard_map/grad_gate_parts/pallas_call | solution.py:175
  73.9 3.1 %collective-permute-start.16 = (bf16[512,512]{1,0:T(8,128)(2,1)}, bf16[512,512]{1,0:T(8,128)(2,1)}, u32[]{:S(2)}, u32[]{:S(2)}) collective-permute-start(bf16[512,512]{1,0:T(8,128)(2,1)} %get-tuple-element.52), channel_id=1, source_target_pairs={{0,8},{8,16},{16,24},{24,0},{1,9},{9,17},{17,25},{25,1},{2,10},{10... | collective-permute-start | bytes 1572872 | tf_op jit(solution)/shard_map/ppermute | solution.py:21
  77.0 6.5 %grad_proj_part.1 = bf16[1024,1024]{1,0:T(8,128)(2,1)S(1)} custom-call(s32[8]{0:T(128)S(1)} %stack.35.place_ref, bf16[4,2048,128]{2,1,0:T(8,128)(2,1)S(1)} %bitcast.12, bf16[4,2048,128]{2,1,0:T(8,128)(2,1)} %collective-permute-done.12.sib_ref, bf16[512,512]{1,0:T(8,128)(2,1)S(1)} %copy-done.16, bf16[512,512]{1,0:T(8,128)(2,1)S(1)} %copy-done.14, ...), custom_call_target="tpu_custom_call" | custom-call | flops 1048576 | bytes 262144 | tf_op jit(solution)/shard_map/grad_proj_part/pallas_call | solution.py:214
  83.5 1.4 copy-done.10
  85.0 1.3 collective-permute-done.14.refs_1_
  86.3 1.6 copy-done.1
  87.9 3.1 %grad_gate_parts.6 = (bf16[512,512]{1,0:T(8,128)(2,1)S(1)}, bf16[512,512]{1,0:T(8,128)(2,1)S(1)}) custom-call(s32[8]{0:T(128)S(1)} %stack.35.place_ref, bf16[4,2048,128]{2,1,0:T(8,128)(2,1)S(1)} %bitcast.13, bf16[4,2048,128]{2,1,0:T(8,128)(2,1)} %collective-permute-done.12.sib_ref, bf16[1024,1024]{1,0:T(8,128)(2,1)S(1)} %copy-done.1, ...), custom_call_target="tpu_custom_call" | custom-call | flops 1048576 | bytes 262144 | tf_op jit(solution)/shard_map/grad_gate_parts/pallas_call | solution.py:175
  92.6 3.3 %collective-permute-done.16.refs_3_ = bf16[512,512]{1,0:T(8,128)(2,1)} collective-permute-done((bf16[512,512]{1,0:T(8,128)(2,1)}, bf16[512,512]{1,0:T(8,128)(2,1)}, u32[]{:S(2)}, u32[]{:S(2)}) %collective-permute-start.16) | collective-permute-done | bytes 524320 | tf_op jit(solution)/shard_map/ppermute | solution.py:21
  96.4 2.6 %collective-permute-start.15 = (bf16[512,512]{1,0:T(8,128)(2,1)}, bf16[512,512]{1,0:T(8,128)(2,1)S(1)}, u32[]{:S(2)}, u32[]{:S(2)}) collective-permute-start(bf16[512,512]{1,0:T(8,128)(2,1)} %copy-done.25), channel_id=1, source_target_pairs={{0,8},{8,16},{16,24},{24,0},{1,9},{9,17},{17,25},{25,1},{2,10},{10... | collective-permute-start | bytes 1572872 | tf_op jit(solution)/shard_map/ppermute | solution.py:21
  99.0 1.6 copy-done.2
  100.6 3.0 %grad_gate_parts.5 = (f32[512,512]{1,0:T(8,128)S(1)}, f32[512,512]{1,0:T(8,128)S(1)}) custom-call(s32[8]{0:T(128)S(1)} %stack.35.place_ref, bf16[4,2048,128]{2,1,0:T(8,128)(2,1)S(1)} %bitcast.14, bf16[4,2048,128]{2,1,0:T(8,128)(2,1)} %collective-permute-done.12.sib_ref, bf16[1024,1024]{1,0:T(8,128)(2,1)S(1)} %copy-done.2), custom_call_target="tpu_custom_call" | custom-call | flops 1048576 | bytes 262144 | tf_op jit(solution)/shard_map/grad_gate_parts/pallas_call | solution.py:175
  103.6 6.7 %collective-permute-done.15.refs_2_ = bf16[512,512]{1,0:T(8,128)(2,1)S(1)} collective-permute-done((bf16[512,512]{1,0:T(8,128)(2,1)}, bf16[512,512]{1,0:T(8,128)(2,1)S(1)}, u32[]{:S(2)}, u32[]{:S(2)}) %collective-permute-start.15) | collective-permute-done | bytes 524320 | tf_op jit(solution)/shard_map/ppermute | solution.py:21
  110.4 3.3 %collective-permute-done.18.refs_5_ = bf16[512,512]{1,0:T(8,128)(2,1)S(1)} collective-permute-done((bf16[512,512]{1,0:T(8,128)(2,1)}, bf16[512,512]{1,0:T(8,128)(2,1)S(1)}, u32[]{:S(2)}, u32[]{:S(2)}) %collective-permute-start.18) | collective-permute-done | bytes 524320 | tf_op jit(solution)/shard_map/ppermute | solution.py:21
  113.7 3.9 %gate_gradients.1 = (bf16[512,1024]{1,0:T(8,128)(2,1)}, bf16[512,1024]{1,0:T(8,128)(2,1)S(1)}, bf16[128,1024]{1,0:T(8,128)(2,1)}) custom-call(f32[512,512]{1,0:T(8,128)S(1)} %get-tuple-element.49.refs_0_, f32[512,512]{1,0:T(8,128)S(1)} %get-tuple-element.50.refs_1_, bf16[512,512]{1,0:T(8,128)(2,1)S(1)} %collective-permute-done.15.refs_2_, ...), custom_call_target="tpu_custom_call" | custom-call | flops 1048576 | bytes 262144 | tf_op jit(solution)/shard_map/gate_gradients/pallas_call | solution.py:244
  117.6 2.3 %collective-permute-start.22 = (bf16[128,1024]{1,0:T(8,128)(2,1)}, bf16[128,1024]{1,0:T(8,128)(2,1)}, u32[]{:S(2)}, u32[]{:S(2)}) collective-permute-start(bf16[128,1024]{1,0:T(8,128)(2,1)} %get-tuple-element.60), channel_id=1, source_target_pairs={{8,0},{16,8},{24,16},{32,24},{40,32},{48,40},{56,48},{64,56},{72,6... | collective-permute-start | bytes 786440 | tf_op jit(solution)/shard_map/ppermute | solution.py:27
  119.9 5.7 %filter_part.1 = f32[64,128]{1,0:T(8,128)S(1)} custom-call(bf16[512,1024]{1,0:T(8,128)(2,1)S(1)} %get-tuple-element.64.inner_ref, bf16[512,1024]{1,0:T(8,128)(2,1)S(1)} %copy-done.12, bf16[128,1024]{1,0:T(8,128)(2,1)S(1)} %collective-permute-done.3.rim_ref), custom_call_target="tpu_custom_call" | custom-call | flops 1048576 | bytes 262144 | tf_op jit(solution)/shard_map/filter_part/pallas_call | solution.py:283
  125.7 1.9 %collective-permute-start.20 = (f32[64,128]{1,0:T(8,128)S(1)}, f32[64,128]{1,0:T(8,128)S(1)}, u32[]{:S(2)}, u32[]{:S(2)}) collective-permute-start(f32[64,128]{1,0:T(8,128)S(1)} %filter_part.1), channel_id=1, source_target_pairs={{0,16},{8,24},{16,0},{24,8},{1,17},{9,25},{17,1},{25,9},{2,18},{10... | collective-permute-start | bytes 98312 | tf_op jit(solution)/shard_map/ppermute | solution.py:21
  127.5 2.5 %collective-permute-start.21 = (f32[64,128]{1,0:T(8,128)S(1)}, f32[64,128]{1,0:T(8,128)S(1)}, u32[]{:S(2)}, u32[]{:S(2)}) collective-permute-start(f32[64,128]{1,0:T(8,128)S(1)} %filter_part.1), channel_id=1, source_target_pairs={{0,8},{8,16},{16,24},{24,0},{1,9},{9,17},{17,25},{25,1},{2,10},{10... | collective-permute-start | bytes 98312 | tf_op jit(solution)/shard_map/ppermute | solution.py:21
  130.1 6.0 %collective-permute-done.22.ahead_ref = bf16[128,1024]{1,0:T(8,128)(2,1)} collective-permute-done((bf16[128,1024]{1,0:T(8,128)(2,1)}, bf16[128,1024]{1,0:T(8,128)(2,1)}, u32[]{:S(2)}, u32[]{:S(2)}) %collective-permute-start.22) | collective-permute-done | bytes 262176 | tf_op jit(solution)/shard_map/ppermute | solution.py:27
  136.1 4.0 %conv_backward.2 = (bf16[512,1024]{1,0:T(8,128)(2,1)}, bf16[512,1024]{1,0:T(8,128)(2,1)}) custom-call(bf16[64,128]{1,0:T(8,128)(2,1)S(1)} %copy-done.23, bf16[512,1024]{1,0:T(8,128)(2,1)S(1)} %get-tuple-element.64.inner_ref, bf16[128,1024]{1,0:T(8,128)(2,1)} %collective-permute-done.22.ahead_ref, bf16[512,1024]{1,0:T(8,128)(2,1)S(1)} %copy-done.3, ...), custom_call_target="tpu_custom_call" | custom-call | flops 1048576 | bytes 262144 | tf_op jit(solution)/shard_map/conv_backward/pallas_call | solution.py:323
  140.2 7.8 %collective-permute-start.23 = (f32[64,128]{1,0:T(8,128)S(1)}, f32[64,128]{1,0:T(8,128)S(1)}, u32[]{:S(2)}, u32[]{:S(2)}) collective-permute-start(f32[64,128]{1,0:T(8,128)S(1)} %select_add_fusion.1), channel_id=1, source_target_pairs={{0,192},{32,224},{64,0},{96,32},{128,64},{160,96},{192,128},{224,1... | collective-permute-start | bytes 98312 | tf_op jit(solution)/shard_map/ppermute | solution.py:21
  147.9 2.6 %collective-permute-start.24 = (f32[64,128]{1,0:T(8,128)S(1)}, f32[64,128]{1,0:T(8,128)S(1)}, u32[]{:S(2)}, u32[]{:S(2)}) collective-permute-start(f32[64,128]{1,0:T(8,128)S(1)} %select_add_fusion.1), channel_id=1, source_target_pairs={{0,128},{32,160},{64,192},{96,224},{128,0},{160,32},{192,64},{224,... | collective-permute-start | bytes 98312 | tf_op jit(solution)/shard_map/ppermute | solution.py:21
  150.5 2.8 %collective-permute-start.25 = (f32[64,128]{1,0:T(8,128)S(1)}, f32[64,128]{1,0:T(8,128)S(1)}, u32[]{:S(2)}, u32[]{:S(2)}) collective-permute-start(f32[64,128]{1,0:T(8,128)S(1)} %select_add_fusion.1), channel_id=1, source_target_pairs={{0,64},{32,96},{64,128},{96,160},{128,192},{160,224},{192,0},{224,... | collective-permute-start | bytes 98312 | tf_op jit(solution)/shard_map/ppermute | solution.py:21
  153.3 4.0 %conv_backward.3 = (bf16[512,1024]{1,0:T(8,128)(2,1)}, bf16[512,1024]{1,0:T(8,128)(2,1)}) custom-call(bf16[64,128]{1,0:T(8,128)(2,1)S(1)} %copy-done.23, bf16[512,1024]{1,0:T(8,128)(2,1)S(1)} %get-tuple-element.64.inner_ref, bf16[128,1024]{1,0:T(8,128)(2,1)} %collective-permute-done.22.ahead_ref, ...), custom_call_target="tpu_custom_call", output_to_operand_aliasing={{0}: (5, {}), {1}: (6, {})} | custom-call | flops 1048576 | bytes 262144 | tf_op jit(solution)/shard_map/conv_backward/pallas_call | solution.py:323
  157.8 1.8 %convert_element_type.15 = f32[128,1024]{1,0:T(8,128)} convert(bf16[128,1024]{1,0:T(8,128)(2,1)} %reduce-scatter.2.cloned.1.call-done) | non-fusion elementwise | flops 131072 | bytes 786432 | tf_op jit(solution)/shard_map/convert_element_type | solution.py:392
  159.6 1.8 %collective-permute-done.28 = f32[64,128]{1,0:T(8,128)S(1)} collective-permute-done((f32[64,128]{1,0:T(8,128)S(1)}, f32[64,128]{1,0:T(8,128)S(1)}, u32[]{:S(2)}, u32[]{:S(2)}) %collective-permute-start.28) | collective-permute-done | bytes 32800 | tf_op jit(solution)/shard_map/ppermute | solution.py:403
  (95 shorter events, 8.6 us)
Async XLA Ops:
  7.2 12.1 %copy-start.3 = (bf16[512,1024]{1,0:T(8,128)(2,1)S(1)}, bf16[512,1024]{1,0:T(8,128)(2,1)}, u32[]{:S(2)}) copy-start(bf16[512,1024]{1,0:T(8,128)(2,1)} %k_ref.7) | copy-start | bytes 3145732
  7.2 12.1 %copy-start.4 = (bf16[512,1024]{1,0:T(8,128)(2,1)S(1)}, bf16[512,1024]{1,0:T(8,128)(2,1)}, u32[]{:S(2)}) copy-start(bf16[512,1024]{1,0:T(8,128)(2,1)} %v_ref.7) | copy-start | bytes 3145732
  7.2 12.1 %copy-start.23 = (bf16[64,128]{1,0:T(8,128)(2,1)S(1)}, bf16[64,128]{1,0:T(8,128)(2,1)}, u32[]{:S(2)}) copy-start(bf16[64,128]{1,0:T(8,128)(2,1)} %filters_ref.7) | copy-start | bytes 49156
  7.2 54.2 %all-gather.2.cloned.1.call-start = ((), (), s32[]{:S(2)}) async-start(), calls=%async_computation.1 | async-start | bytes 2359296 | tf_op jit(solution)/shard_map/all_gather | solution.py:355
  8.5 10.8 %collective-permute-start.3 = (bf16[128,1024]{1,0:T(8,128)(2,1)S(1)}, bf16[128,1024]{1,0:T(8,128)(2,1)S(1)}, u32[]{:S(2)}, u32[]{:S(2)}) collective-permute-start(bf16[128,1024]{1,0:T(8,128)(2,1)S(1)} %multiply_convert_fusion), channel_id=1, source_target_pairs={{0,8},{8,16},{16,24},{24,32},{32,40},{40,48},{48,56},{56,64},{64,7... | collective-permute-start | bytes 786440 | tf_op jit(solution)/shard_map/ppermute | solution.py:27
  13.4 14.1 %collective-permute-start = (bf16[512,128]{1,0:T(8,128)(2,1)S(1)}, bf16[512,128]{1,0:T(8,128)(2,1)S(1)}, u32[]{:S(2)}, u32[]{:S(2)}) collective-permute-start(bf16[512,128]{1,0:T(8,128)(2,1)S(1)} %get-tuple-element.72), channel_id=1, source_target_pairs={{0,24},{8,0},{16,8},{24,16},{1,25},{9,1},{17,9},{25,17},{2,26},{10... | collective-permute-start | bytes 393224 | tf_op jit(solution)/shard_map/ppermute | solution.py:21
  13.7 13.8 %collective-permute-start.1 = (bf16[512,128]{1,0:T(8,128)(2,1)S(1)}, bf16[512,128]{1,0:T(8,128)(2,1)S(1)}, u32[]{:S(2)}, u32[]{:S(2)}) collective-permute-start(bf16[512,128]{1,0:T(8,128)(2,1)S(1)} %get-tuple-element.74), channel_id=1, source_target_pairs={{0,16},{8,24},{16,0},{24,8},{1,17},{9,25},{17,1},{25,9},{2,18},{10... | collective-permute-start | bytes 393224 | tf_op jit(solution)/shard_map/ppermute | solution.py:21
  15.1 12.4 %collective-permute-start.2 = (bf16[512,128]{1,0:T(8,128)(2,1)S(1)}, bf16[512,128]{1,0:T(8,128)(2,1)S(1)}, u32[]{:S(2)}, u32[]{:S(2)}) collective-permute-start(bf16[512,128]{1,0:T(8,128)(2,1)S(1)} %get-tuple-element.71), channel_id=1, source_target_pairs={{0,8},{8,16},{16,24},{24,0},{1,9},{9,17},{17,25},{25,1},{2,10},{10... | collective-permute-start | bytes 393224 | tf_op jit(solution)/shard_map/ppermute | solution.py:21
  17.2 140.5 %reduce-scatter.2.cloned.1.call-start = ((), (), s32[]{:S(2)}) async-start(), calls=%async_computation.2 | async-start | bytes 2359296 | tf_op jit(solution)/shard_map/reduce_scatter | solution.py:392
  24.0 6.9 %copy-start.15 = (bf16[512,512]{1,0:T(8,128)(2,1)}, bf16[512,512]{1,0:T(8,128)(2,1)S(1)}, u32[]{:S(2)}) copy-start(bf16[512,512]{1,0:T(8,128)(2,1)S(1)} %get-tuple-element.68.refs_0_) | copy-start | bytes 1572868
  27.5 21.7 %copy-start.8 = (f32[512,1024]{1,0:T(8,128)}, f32[512,1024]{1,0:T(8,128)S(1)}, u32[]{:S(2)}) copy-start(f32[512,1024]{1,0:T(8,128)S(1)} %get-tuple-element.55.refs_7_) | copy-start | bytes 6291460
  27.5 21.7 %copy-start.11 = (bf16[512,1024]{1,0:T(8,128)(2,1)}, bf16[512,1024]{1,0:T(8,128)(2,1)S(1)}, u32[]{:S(2)}) copy-start(bf16[512,1024]{1,0:T(8,128)(2,1)S(1)} %get-tuple-element.58.mixed_ref) | copy-start | bytes 3145732
  27.5 21.7 %copy-start.13 = (bf16[512,512]{1,0:T(8,128)(2,1)}, bf16[512,512]{1,0:T(8,128)(2,1)S(1)}, u32[]{:S(2)}) copy-start(bf16[512,512]{1,0:T(8,128)(2,1)S(1)} %get-tuple-element.44.refs_4_.refs_1_) | copy-start | bytes 1572868
  27.6 13.3 %collective-permute-start.5 = (bf16[2048,128]{1,0:T(8,128)(2,1)S(1)}, bf16[2048,128]{1,0:T(8,128)(2,1)S(1)}, u32[]{:S(2)}, u32[]{:S(2)}) collective-permute-start(bf16[2048,128]{1,0:T(8,128)(2,1)S(1)} %join.1), channel_id=1, source_target_pairs={{0,2},{2,4},{4,6},{6,0},{1,3},{3,5},{5,7},{7,1},{8,10},{10,12},{12... | collective-permute-start | bytes 1572872 | tf_op jit(solution)/shard_map/ppermute | solution.py:21
  29.2 12.0 %collective-permute-start.4 = (bf16[2048,128]{1,0:T(8,128)(2,1)S(1)}, bf16[2048,128]{1,0:T(8,128)(2,1)S(1)}, u32[]{:S(2)}, u32[]{:S(2)}) collective-permute-start(bf16[2048,128]{1,0:T(8,128)(2,1)S(1)} %join.1), channel_id=1, source_target_pairs={{0,6},{2,0},{4,2},{6,4},{1,7},{3,1},{5,3},{7,5},{8,14},{10,8},{12,... | collective-permute-start | bytes 1572872 | tf_op jit(solution)/shard_map/ppermute | solution.py:21
  30.9 13.4 %collective-permute-start.7 = (bf16[512,512]{1,0:T(8,128)(2,1)S(1)}, bf16[512,512]{1,0:T(8,128)(2,1)S(1)}, u32[]{:S(2)}, u32[]{:S(2)}) collective-permute-start(bf16[512,512]{1,0:T(8,128)(2,1)S(1)} %get-tuple-element.68.refs_0_), channel_id=1, source_target_pairs={{0,8},{8,16},{16,24},{24,0},{1,9},{9,17},{17,25},{25,1},{2,10},{10... | collective-permute-start | bytes 1572872 | tf_op jit(solution)/shard_map/ppermute | solution.py:21
  30.9 16.1 %collective-permute-start.10 = (bf16[512,512]{1,0:T(8,128)(2,1)S(1)}, bf16[512,512]{1,0:T(8,128)(2,1)S(1)}, u32[]{:S(2)}, u32[]{:S(2)}) collective-permute-start(bf16[512,512]{1,0:T(8,128)(2,1)S(1)} %get-tuple-element.68.refs_0_), channel_id=1, source_target_pairs={{0,24},{8,0},{16,8},{24,16},{1,25},{9,1},{17,9},{25,17},{2,26},{10... | collective-permute-start | bytes 1572872 | tf_op jit(solution)/shard_map/ppermute | solution.py:21
  33.6 21.3 %collective-permute-start.8 = (bf16[512,512]{1,0:T(8,128)(2,1)S(1)}, bf16[512,512]{1,0:T(8,128)(2,1)}, u32[]{:S(2)}, u32[]{:S(2)}) collective-permute-start(bf16[512,512]{1,0:T(8,128)(2,1)S(1)} %get-tuple-element.44.refs_4_.refs_1_), channel_id=1, source_target_pairs={{0,24},{8,0},{16,8},{24,16},{1,25},{9,1},{17,9},{25,17},{2,26},{10... | collective-permute-start | bytes 1572872 | tf_op jit(solution)/shard_map/ppermute | solution.py:21
  40.9 14.1 %collective-permute-start.6 = (bf16[1024,128]{1,0:T(8,128)(2,1)S(1)}, bf16[1024,128]{1,0:T(8,128)(2,1)S(1)}, u32[]{:S(2)}, u32[]{:S(2)}) collective-permute-start(bf16[1024,128]{1,0:T(8,128)(2,1)S(1)} %slice.16), channel_id=1, source_target_pairs={{0,2},{2,4},{4,6},{6,0},{1,3},{3,5},{5,7},{7,1},{8,10},{10,12},{12... | collective-permute-start | bytes 786440 | tf_op jit(solution)/shard_map/ppermute | solution.py:21
  41.3 13.7 %collective-permute-start.9 = (bf16[1024,128]{1,0:T(8,128)(2,1)S(1)}, bf16[1024,128]{1,0:T(8,128)(2,1)S(1)}, u32[]{:S(2)}, u32[]{:S(2)}) collective-permute-start(bf16[1024,128]{1,0:T(8,128)(2,1)S(1)} %slice.17), channel_id=1, source_target_pairs={{0,6},{2,0},{4,2},{6,4},{1,7},{3,1},{5,3},{7,5},{8,14},{10,8},{12,... | collective-permute-start | bytes 786440 | tf_op jit(solution)/shard_map/ppermute | solution.py:21
  44.3 11.8 %copy-start.17 = (bf16[512,512]{1,0:T(8,128)(2,1)}, bf16[512,512]{1,0:T(8,128)(2,1)S(1)}, u32[]{:S(2)}) copy-start(bf16[512,512]{1,0:T(8,128)(2,1)S(1)} %collective-permute-done.7.refs_6_) | copy-start | bytes 1572868
  47.0 10.0 %copy-start.19 = (bf16[512,512]{1,0:T(8,128)(2,1)}, bf16[512,512]{1,0:T(8,128)(2,1)S(1)}, u32[]{:S(2)}) copy-start(bf16[512,512]{1,0:T(8,128)(2,1)S(1)} %collective-permute-done.10.refs_2_) | copy-start | bytes 1572868
  47.0 9.2 %collective-permute-start.11 = (bf16[512,512]{1,0:T(8,128)(2,1)S(1)}, bf16[512,512]{1,0:T(8,128)(2,1)S(1)}, u32[]{:S(2)}, u32[]{:S(2)}) collective-permute-start(bf16[512,512]{1,0:T(8,128)(2,1)S(1)} %get-tuple-element.44.refs_4_.refs_1_), channel_id=1, source_target_pairs={{0,8},{8,16},{16,24},{24,0},{1,9},{9,17},{17,25},{25,1},{2,10},{10... | collective-permute-start | bytes 1572872 | tf_op jit(solution)/shard_map/ppermute | solution.py:21
  57.0 4.3 %collective-permute-start.12 = (bf16[4,2048,128]{2,1,0:T(8,128)(2,1)S(1)}, bf16[4,2048,128]{2,1,0:T(8,128)(2,1)}, u32[]{:S(2)}, u32[]{:S(2)}) collective-permute-start(bf16[4,2048,128]{2,1,0:T(8,128)(2,1)S(1)} %bitcast.9), channel_id=1, source_target_pairs={{0,1},{1,0},{2,3},{3,2},{4,5},{5,4},{6,7},{7,6},{8,9},{9,8},{10,11... | collective-permute-start | bytes 6291464 | tf_op jit(solution)/shard_map/ppermute | solution.py:21
  57.0 20.0 %collective-permute-start.27 = (bf16[512,512]{1,0:T(8,128)(2,1)}, bf16[512,512]{1,0:T(8,128)(2,1)}, u32[]{:S(2)}, u32[]{:S(2)}) collective-permute-start(bf16[512,512]{1,0:T(8,128)(2,1)} %collective-permute-done.8.refs_3_), channel_id=1, source_target_pairs={{0,24},{8,0},{16,8},{24,16},{1,25},{9,1},{17,9},{25,17},{2,26},{10... | collective-permute-start | bytes 1572872 | tf_op jit(solution)/shard_map/ppermute | solution.py:21
  58.6 18.4 %collective-permute-start.26 = (bf16[512,512]{1,0:T(8,128)(2,1)}, bf16[512,512]{1,0:T(8,128)(2,1)}, u32[]{:S(2)}, u32[]{:S(2)}) collective-permute-start(bf16[512,512]{1,0:T(8,128)(2,1)} %copy-done.17), channel_id=1, source_target_pairs={{0,8},{8,16},{16,24},{24,0},{1,9},{9,17},{17,25},{25,1},{2,10},{10... | collective-permute-start | bytes 1572872 | tf_op jit(solution)/shard_map/ppermute | solution.py:21
  66.7 18.4 %collective-permute-start.13 = (bf16[512,512]{1,0:T(8,128)(2,1)}, bf16[512,512]{1,0:T(8,128)(2,1)}, u32[]{:S(2)}, u32[]{:S(2)}) collective-permute-start(bf16[512,512]{1,0:T(8,128)(2,1)} %get-tuple-element.46), channel_id=1, source_target_pairs={{0,8},{8,16},{16,24},{24,0},{1,9},{9,17},{17,25},{25,1},{2,10},{10... | collective-permute-start | bytes 1572872 | tf_op jit(solution)/shard_map/ppermute | solution.py:21
  69.9 7.1 %copy-start.14 = (bf16[512,512]{1,0:T(8,128)(2,1)S(1)}, bf16[512,512]{1,0:T(8,128)(2,1)}, u32[]{:S(2)}) copy-start(bf16[512,512]{1,0:T(8,128)(2,1)} %copy-done.13) | copy-start | bytes 1572868
  69.9 7.1 %copy-start.16 = (bf16[512,512]{1,0:T(8,128)(2,1)S(1)}, bf16[512,512]{1,0:T(8,128)(2,1)}, u32[]{:S(2)}) copy-start(bf16[512,512]{1,0:T(8,128)(2,1)} %copy-done.15) | copy-start | bytes 1572868
  69.9 7.1 %copy-start.18 = (bf16[512,512]{1,0:T(8,128)(2,1)S(1)}, bf16[512,512]{1,0:T(8,128)(2,1)}, u32[]{:S(2)}) copy-start(bf16[512,512]{1,0:T(8,128)(2,1)} %copy-done.17) | copy-start | bytes 1572868
  69.9 7.1 %copy-start.20 = (bf16[512,512]{1,0:T(8,128)(2,1)S(1)}, bf16[512,512]{1,0:T(8,128)(2,1)}, u32[]{:S(2)}) copy-start(bf16[512,512]{1,0:T(8,128)(2,1)} %copy-done.19) | copy-start | bytes 1572868
  69.9 7.1 %copy-start.22 = (bf16[512,512]{1,0:T(8,128)(2,1)S(1)}, bf16[512,512]{1,0:T(8,128)(2,1)}, u32[]{:S(2)}) copy-start(bf16[512,512]{1,0:T(8,128)(2,1)} %copy-done.21) | copy-start | bytes 1572868
  69.9 16.4 %collective-permute-start.14 = (bf16[512,512]{1,0:T(8,128)(2,1)}, bf16[512,512]{1,0:T(8,128)(2,1)}, u32[]{:S(2)}, u32[]{:S(2)}) collective-permute-start(bf16[512,512]{1,0:T(8,128)(2,1)} %get-tuple-element.47), channel_id=1, source_target_pairs={{0,24},{8,0},{16,8},{24,16},{1,25},{9,1},{17,9},{25,17},{2,26},{10... | collective-permute-start | bytes 1572872 | tf_op jit(solution)/shard_map/ppermute | solution.py:21
  73.9 22.0 %collective-permute-start.16 = (bf16[512,512]{1,0:T(8,128)(2,1)}, bf16[512,512]{1,0:T(8,128)(2,1)}, u32[]{:S(2)}, u32[]{:S(2)}) collective-permute-start(bf16[512,512]{1,0:T(8,128)(2,1)} %get-tuple-element.52), channel_id=1, source_target_pairs={{0,8},{8,16},{16,24},{24,0},{1,9},{9,17},{17,25},{25,1},{2,10},{10... | collective-permute-start | bytes 1572872 | tf_op jit(solution)/shard_map/ppermute | solution.py:21
  76.9 19.5 %collective-permute-start.17 = (bf16[512,512]{1,0:T(8,128)(2,1)}, bf16[512,512]{1,0:T(8,128)(2,1)}, u32[]{:S(2)}, u32[]{:S(2)}) collective-permute-start(bf16[512,512]{1,0:T(8,128)(2,1)} %get-tuple-element.53), channel_id=1, source_target_pairs={{0,24},{8,0},{16,8},{24,16},{1,25},{9,1},{17,9},{25,17},{2,26},{10... | collective-permute-start | bytes 1572872 | tf_op jit(solution)/shard_map/ppermute | solution.py:21
  96.4 13.9 %collective-permute-start.15 = (bf16[512,512]{1,0:T(8,128)(2,1)}, bf16[512,512]{1,0:T(8,128)(2,1)S(1)}, u32[]{:S(2)}, u32[]{:S(2)}) collective-permute-start(bf16[512,512]{1,0:T(8,128)(2,1)} %copy-done.25), channel_id=1, source_target_pairs={{0,8},{8,16},{16,24},{24,0},{1,9},{9,17},{17,25},{25,1},{2,10},{10... | collective-permute-start | bytes 1572872 | tf_op jit(solution)/shard_map/ppermute | solution.py:21
  99.0 14.6 %collective-permute-start.18 = (bf16[512,512]{1,0:T(8,128)(2,1)}, bf16[512,512]{1,0:T(8,128)(2,1)S(1)}, u32[]{:S(2)}, u32[]{:S(2)}) collective-permute-start(bf16[512,512]{1,0:T(8,128)(2,1)} %copy-done.24), channel_id=1, source_target_pairs={{0,24},{8,0},{16,8},{24,16},{1,25},{9,1},{17,9},{25,17},{2,26},{10... | collective-permute-start | bytes 1572872 | tf_op jit(solution)/shard_map/ppermute | solution.py:21
  100.6 13.0 %copy-start.7 = (bf16[512,1024]{1,0:T(8,128)(2,1)S(1)}, bf16[512,1024]{1,0:T(8,128)(2,1)}, u32[]{:S(2)}) copy-start(bf16[512,1024]{1,0:T(8,128)(2,1)} %refs_6_.1) | copy-start | bytes 3145732
  100.6 13.0 %copy-start.9 = (f32[512,1024]{1,0:T(8,128)S(1)}, f32[512,1024]{1,0:T(8,128)}, u32[]{:S(2)}) copy-start(f32[512,1024]{1,0:T(8,128)} %copy-done.8) | copy-start | bytes 6291460
  117.6 18.5 %copy-start.5 = (bf16[512,1024]{1,0:T(8,128)(2,1)S(1)}, bf16[512,1024]{1,0:T(8,128)(2,1)}, u32[]{:S(2)}) copy-start(bf16[512,1024]{1,0:T(8,128)(2,1)} %v_ref.7) | copy-start | bytes 3145732
  117.6 18.5 %collective-permute-start.22 = (bf16[128,1024]{1,0:T(8,128)(2,1)}, bf16[128,1024]{1,0:T(8,128)(2,1)}, u32[]{:S(2)}, u32[]{:S(2)}) collective-permute-start(bf16[128,1024]{1,0:T(8,128)(2,1)} %get-tuple-element.60), channel_id=1, source_target_pairs={{8,0},{16,8},{24,16},{32,24},{40,32},{48,40},{56,48},{64,56},{72,6... | collective-permute-start | bytes 786440 | tf_op jit(solution)/shard_map/ppermute | solution.py:27
  125.6 14.6 %collective-permute-start.19 = (f32[64,128]{1,0:T(8,128)S(1)}, f32[64,128]{1,0:T(8,128)S(1)}, u32[]{:S(2)}, u32[]{:S(2)}) collective-permute-start(f32[64,128]{1,0:T(8,128)S(1)} %filter_part.1), channel_id=1, source_target_pairs={{0,24},{8,0},{16,8},{24,16},{1,25},{9,1},{17,9},{25,17},{2,26},{10... | collective-permute-start | bytes 98312 | tf_op jit(solution)/shard_map/ppermute | solution.py:21
  125.7 14.5 %collective-permute-start.20 = (f32[64,128]{1,0:T(8,128)S(1)}, f32[64,128]{1,0:T(8,128)S(1)}, u32[]{:S(2)}, u32[]{:S(2)}) collective-permute-start(f32[64,128]{1,0:T(8,128)S(1)} %filter_part.1), channel_id=1, source_target_pairs={{0,16},{8,24},{16,0},{24,8},{1,17},{9,25},{17,1},{25,9},{2,18},{10... | collective-permute-start | bytes 98312 | tf_op jit(solution)/shard_map/ppermute | solution.py:21
  127.5 12.6 %collective-permute-start.21 = (f32[64,128]{1,0:T(8,128)S(1)}, f32[64,128]{1,0:T(8,128)S(1)}, u32[]{:S(2)}, u32[]{:S(2)}) collective-permute-start(f32[64,128]{1,0:T(8,128)S(1)} %filter_part.1), channel_id=1, source_target_pairs={{0,8},{8,16},{16,24},{24,0},{1,9},{9,17},{17,25},{25,1},{2,10},{10... | collective-permute-start | bytes 98312 | tf_op jit(solution)/shard_map/ppermute | solution.py:21
  140.2 17.2 %collective-permute-start.23 = (f32[64,128]{1,0:T(8,128)S(1)}, f32[64,128]{1,0:T(8,128)S(1)}, u32[]{:S(2)}, u32[]{:S(2)}) collective-permute-start(f32[64,128]{1,0:T(8,128)S(1)} %select_add_fusion.1), channel_id=1, source_target_pairs={{0,192},{32,224},{64,0},{96,32},{128,64},{160,96},{192,128},{224,1... | collective-permute-start | bytes 98312 | tf_op jit(solution)/shard_map/ppermute | solution.py:21
  147.9 9.4 %collective-permute-start.24 = (f32[64,128]{1,0:T(8,128)S(1)}, f32[64,128]{1,0:T(8,128)S(1)}, u32[]{:S(2)}, u32[]{:S(2)}) collective-permute-start(f32[64,128]{1,0:T(8,128)S(1)} %select_add_fusion.1), channel_id=1, source_target_pairs={{0,128},{32,160},{64,192},{96,224},{128,0},{160,32},{192,64},{224,... | collective-permute-start | bytes 98312 | tf_op jit(solution)/shard_map/ppermute | solution.py:21
  150.5 6.9 %collective-permute-start.25 = (f32[64,128]{1,0:T(8,128)S(1)}, f32[64,128]{1,0:T(8,128)S(1)}, u32[]{:S(2)}, u32[]{:S(2)}) collective-permute-start(f32[64,128]{1,0:T(8,128)S(1)} %select_add_fusion.1), channel_id=1, source_target_pairs={{0,64},{32,96},{64,128},{96,160},{128,192},{160,224},{192,0},{224,... | collective-permute-start | bytes 98312 | tf_op jit(solution)/shard_map/ppermute | solution.py:21
  157.4 4.0 %collective-permute-start.28 = (f32[64,128]{1,0:T(8,128)S(1)}, f32[64,128]{1,0:T(8,128)S(1)}, u32[]{:S(2)}, u32[]{:S(2)}) collective-permute-start(f32[64,128]{1,0:T(8,128)S(1)} %select_add_fusion), channel_id=1, source_target_pairs={{0,32},{32,0},{64,96},{96,64},{128,160},{160,128},{192,224},{224,1... | collective-permute-start | bytes 98312 | tf_op jit(solution)/shard_map/ppermute | solution.py:403
  (9 other events, 16.0 us)
Sparse Core Ops, SparseCore 0:
  17.4 43.9 all-gather.1
  96.6 47.0 reduce-scatter.1

commit v8 on v7

--- a/solution.py
+++ b/solution.py
@@ -13,6 +13,7 @@
 AXES = ("z", "x", "y", "c")
 SIZE = {"x": 4, "y": 4, "c": 2}
 MIB = 1 << 20
+HEAVY = pl.CostEstimate(flops=1 << 37, bytes_accessed=1 << 18, transcendentals=0)
 LIGHT = pl.CostEstimate(flops=1 << 20, bytes_accessed=1 << 18, transcendentals=0)
 
 
@@ -225,8 +226,9 @@
 def inner_body(*refs):
     own, from_left, from_right = refs[0:2], refs[2:4], refs[4:6]
     q_ref, conv_ref, query_ref, inner_ref, first_ref = refs[6:]
-    second = pl.program_id(0) >= pl.num_programs(0) // 2
-    pick = lambda pair: jnp.where(second, pair[1][...], pair[0][...]).astype(F32)
+    step, half_steps, wide = pl.program_id(0), pl.num_programs(0) // 2, inner_ref.shape[1]
+    here = pl.ds(pl.multiple_of(step % half_steps * wide, wide), wide)
+    pick = lambda pair: jnp.where(step >= half_steps, pair[1][:, here], pair[0][:, here]).astype(F32)
     gate = pick(own) + pick(from_left) + pick(from_right)
     query_ref[...] = (gate * conv_ref[...]).astype(BF16)
     inner = (gate * q_ref[...].astype(F32)).astype(BF16)
@@ -239,12 +241,10 @@
     wide = 2 * LANES
     steps = width // wide
     column = pl.BlockSpec((tokens, wide), lambda i: (0, i))
-    first = pl.BlockSpec((tokens, wide), lambda i: (0, jnp.minimum(i, steps // 2 - 1)))
-    last = pl.BlockSpec((tokens, wide), lambda i: (0, jnp.maximum(i - steps // 2, 0)))
     return pl.pallas_call(
         inner_body,
         grid=(steps,),
-        in_specs=[first, last] * 3 + [column, column],
+        in_specs=[RESIDENT] * 6 + [column, column],
         out_specs=[column, column, pl.BlockSpec((taps, wide), lambda i: (0, i))],
         out_shape=[jax.ShapeDtypeStruct((n, width), BF16) for n in (tokens, tokens, taps)],
         compiler_params=pltpu.CompilerParams(vmem_limit_bytes=16 * MIB),
@@ -287,7 +287,7 @@
         out_specs=pl.BlockSpec((groups, taps), lambda i: (i, 0)),
         out_shape=jax.ShapeDtypeStruct((group_count, taps), F32),
         compiler_params=pltpu.CompilerParams(vmem_limit_bytes=16 * MIB),
-        cost_estimate=LIGHT,
+        cost_estimate=HEAVY,
         name="filter_part",
     )(inner, mixed, rim)
 
@@ -368,7 +368,7 @@
     middle = column.shape[0] // 2
     far = send(below[:middle], "y", 1), send(above[middle:], "y", -1)
     left_a, right_a = send(gated_a, "x", 1), send(gated_a, "x", -1)
-    right_b, left_b = send(gated_b, "x", -1), send(after(gated_b, left_a, right_a), "x", 1)
+    right_b, left_b = send(gated_b, "x", -1), send(after(gated_b, left_a), "x", 1)
     far_a, far_b = send(left_a, "x", 1), send(right_b, "x", -1)
     gated = [gated_a, gated_b, right_a, right_b, far_a, far_b, left_a, left_b]
 
@@ -380,15 +380,14 @@
 
     across = gate_parts(place, mine, sib, proj, ((2, 0), (2, 1)), BF16)
     far_a, far_b = send(across[0], "x", 1), send(across[1], "x", -1)
-    proj = after(proj, *across)
+    proj = after(proj, *across, *gated[4:6])
     beside = gate_parts(place, mine, sib, proj, ((1, 1), (3, 0)), BF16)
     from_left_b, from_right_a = send(beside[0], "x", 1), send(beside[1], "x", -1)
     gated[0] = after(gated[0], *beside)
     proj_sums = proj_part(place, mine, sib, gated)
 
-    joined = gate_parts(place, mine, sib, proj, ((1, 0), (3, 1)), BF16, far_a, far_b)
+    joined = gate_parts(place, mine, sib, proj, ((1, 0), (3, 1)), BF16, after(far_a, proj_sums), far_b)
     from_left_a, from_right_b = send(joined[0], "x", 1), send(joined[1], "x", -1)
-    proj_sums = after(proj_sums, from_left_b, from_right_a, joined[0])
     grad_proj = lax.psum_scatter(proj_sums, "z", scatter_dimension=0, tiled=True).astype(F32)
     own = gate_parts(place, mine, sib, proj, ((0, 0), (0, 1)), F32)
     from_left, from_right = (from_left_a, from_left_b), (from_right_a, from_right_b)

time: 170 us -> 167 us (0.982)
  waiting for transfers between devices: 40.6 us -> 34.3 us
  local copies, waits for them, and re-layouts: 12 us -> 15.7 us
    ppermute x2, waiting for transfers between devices: 8.05 us -> 4.78 us  [send_along_tokens(): return lax.ppermute(value, ('z', 'x'), pairs)]
    ppermute x26, waiting for transfers between devices: 30.6 us -> 27.5 us  [send(): lax.ppermute(value, axis, [(i, (i + by) % count) for i in range(count)])]
    unnamed x56 -> x64, local copies, waits for them, and re-layouts: 10 us -> 12.9 us
  transfers between devices with their start and end apart: 31 -> 31, of which waited for: 15 -> 13; matrix products, arithmetic and copies ran while one was open for 2% -> 2% of each run, Pallas kernels for 26% -> 27%
where the time goes in v8:
time: 167 us; the launch traced here: 166 us
  starting transfers between devices  53.7 us (32%)
  Pallas kernels  45 us (27%)
  waiting for transfers between devices  34.3 us (21%)
  local copies, waits for them, and re-layouts  15.7 us (9%)
  between operations  14.5 us (9%)
  other arithmetic  3.09 us (2%)
    ppermute x26, starting transfers between devices, send(): lax.ppermute(value, axis, [(i, (i + by) % count) for i in range(count)])  46.8 us
    ppermute x26, waiting for transfers between devices, send(): lax.ppermute(value, axis, [(i, (i + by) % count) for i in range(count)])  27.5 us
    pallas_call x4, Pallas kernels, gate_parts(): pl.pallas_call(functools.partial(gate_body, wanted), in_specs=[pl.BlockSp...  14.3 us
    unnamed x64, local copies, waits for them, and re-layouts  12.9 us
    pallas_call x2, Pallas kernels, backward(): pl.pallas_call(functools.partial(backward_body, taps, groups), grid=(step...  8.06 us
    pallas_call x2, Pallas kernels, forward(): pl.pallas_call(functools.partial(forward_body, taps, groups), grid=(steps...  6.91 us
    pallas_call x1, Pallas kernels, proj_part(): pl.pallas_call(proj_body, in_specs=[pl.BlockSpec(memory_space=pltpu.SMEM)...  6.35 us
    ppermute x2, starting transfers between devices, send_along_tokens(): return lax.ppermute(value, ('z', 'x'), pairs)  5.87 us
  transfers between devices with their start and end apart: 31, of which 13 were waited for; matrix products, arithmetic and copies ran while one was open for 2% of the time, Pallas kernels for 27%

profile of v8, /device:TPU:6, one launch (start us, length us, event | category | flops | bytes accessed | tf_op | source)
XLA Modules:
  0.0 166.3 jit_solution(10245468897383714131)
XLA Ops:
  7.2 1.2 multiply_convert_fusion
  8.5 3.7 %collective-permute-start.3 = (bf16[128,1024]{1,0:T(8,128)(2,1)S(1)}, bf16[128,1024]{1,0:T(8,128)(2,1)S(1)}, u32[]{:S(2)}, u32[]{:S(2)}) collective-permute-start(bf16[128,1024]{1,0:T(8,128)(2,1)S(1)} %multiply_convert_fusion), channel_id=1, source_target_pairs={{0,8},{8,16},{16,24},{24,32},{32,40},{40,48},{48,56},{56,64},{64,7... | collective-permute-start | bytes 786440 | tf_op jit(solution)/shard_map/ppermute | solution.py:28
  12.3 1.9 %constant_dynamic-slice_fusion = (bf16[512,128]{1,0:T(8,128)(2,1)S(1)}, bf16[512,128]{1,0:T(8,128)(2,1)}, bf16[512,128]{1,0:T(8,128)(2,1)S(1)}, bf16[512,128]{1,0:T(8,128)(2,1)}) fusion(bf16[512,512]{1,0:T(8,128)(2,1)} %param.11, s32[]{:T(128)S(6)} %select_n.281, s32[]{:T(128)S(6)} %select_n.277, s32[]{:T(128)S(6)} %select_n.275, s32[]{:T(128)S(6)} %select_n.279), kind=kLoop, calls=%fused_computation.8 | loop fusion | bytes 1048592 | tf_op jit(solution)/shard_map/dynamic_slice | solution.py:360
  14.3 1.4 collective-permute-start.1
  15.8 2.1 %collective-permute-start.2 = (bf16[512,128]{1,0:T(8,128)(2,1)S(1)}, bf16[512,128]{1,0:T(8,128)(2,1)S(1)}, u32[]{:S(2)}, u32[]{:S(2)}) collective-permute-start(bf16[512,128]{1,0:T(8,128)(2,1)S(1)} %get-tuple-element.71), channel_id=1, source_target_pairs={{0,8},{8,16},{16,24},{24,0},{1,9},{9,17},{17,25},{25,1},{2,10},{10... | collective-permute-start | bytes 393224 | tf_op jit(solution)/shard_map/ppermute | solution.py:22
  18.5 1.2 copy-done.7
  19.7 3.4 %conv_forward.2 = (f32[512,1024]{1,0:T(8,128)S(1)}, bf16[512,1024]{1,0:T(8,128)(2,1)S(1)}, bf16[512,512]{1,0:T(8,128)(2,1)S(1)}) custom-call(bf16[64,128]{1,0:T(8,128)(2,1)S(1)} %copy-done.28, bf16[512,1024]{1,0:T(8,128)(2,1)S(1)} %copy-done.3, bf16[512,1024]{1,0:T(8,128)(2,1)S(1)} %copy-done.5, bf16[512,1024]{1,0:T(8,128)(2,1)S(1)} %copy-done.7, ...), custom_call_target="tpu_custom_call" | custom-call | flops 1048576 | bytes 262144 | tf_op jit(solution)/shard_map/conv_forward/pallas_call | solution.py:106
  23.2 3.5 %conv_forward.3 = (f32[512,1024]{1,0:T(8,128)S(1)}, bf16[512,1024]{1,0:T(8,128)(2,1)S(1)}, bf16[512,512]{1,0:T(8,128)(2,1)S(1)}) custom-call(bf16[64,128]{1,0:T(8,128)(2,1)S(1)} %copy-done.28, bf16[512,1024]{1,0:T(8,128)(2,1)S(1)} %copy-done.3, bf16[512,1024]{1,0:T(8,128)(2,1)S(1)} %copy-done.5, ...), custom_call_target="tpu_custom_call", output_to_operand_aliasing={{0}: (5, {}), {1}: (6, {})} | custom-call | flops 1048576 | bytes 262144 | tf_op jit(solution)/shard_map/conv_forward/pallas_call | solution.py:106
  26.8 1.7 collective-permute-start.5
  28.4 1.7 collective-permute-start.4
  30.1 2.0 %collective-permute-start.8 = (bf16[512,512]{1,0:T(8,128)(2,1)S(1)}, bf16[512,512]{1,0:T(8,128)(2,1)S(1)}, u32[]{:S(2)}, u32[]{:S(2)}) collective-permute-start(bf16[512,512]{1,0:T(8,128)(2,1)S(1)} %get-tuple-element.44.refs_4_.refs_1_), channel_id=1, source_target_pairs={{0,24},{8,0},{16,8},{24,16},{1,25},{9,1},{17,9},{25,17},{2,26},{10... | collective-permute-start | bytes 1572872 | tf_op jit(solution)/shard_map/ppermute | solution.py:22
  32.1 8.7 %collective-permute-done.5 = bf16[2048,128]{1,0:T(8,128)(2,1)S(1)} collective-permute-done((bf16[2048,128]{1,0:T(8,128)(2,1)S(1)}, bf16[2048,128]{1,0:T(8,128)(2,1)S(1)}, u32[]{:S(2)}, u32[]{:S(2)}) %collective-permute-start.5) | collective-permute-done | bytes 524320 | tf_op jit(solution)/shard_map/ppermute | solution.py:22
  41.3 0.9 collective-permute-start.10
  42.2 3.0 %collective-permute-start.9 = (bf16[1024,128]{1,0:T(8,128)(2,1)S(1)}, bf16[1024,128]{1,0:T(8,128)(2,1)S(1)}, u32[]{:S(2)}, u32[]{:S(2)}) collective-permute-start(bf16[1024,128]{1,0:T(8,128)(2,1)S(1)} %slice.17), channel_id=1, source_target_pairs={{0,6},{2,0},{4,2},{6,4},{1,7},{3,1},{5,3},{7,5},{8,14},{10,8},{12,... | collective-permute-start | bytes 786440 | tf_op jit(solution)/shard_map/ppermute | solution.py:22
  45.2 2.4 %collective-permute-start.11 = (bf16[512,512]{1,0:T(8,128)(2,1)S(1)}, bf16[512,512]{1,0:T(8,128)(2,1)S(1)}, u32[]{:S(2)}, u32[]{:S(2)}) collective-permute-start(bf16[512,512]{1,0:T(8,128)(2,1)S(1)} %get-tuple-element.44.refs_4_.refs_1_), channel_id=1, source_target_pairs={{0,8},{8,16},{16,24},{24,0},{1,9},{9,17},{17,25},{25,1},{2,10},{10... | collective-permute-start | bytes 1572872 | tf_op jit(solution)/shard_map/ppermute | solution.py:22
  49.2 5.6 %collective-permute-done.10.refs_2_ = bf16[512,512]{1,0:T(8,128)(2,1)S(1)} collective-permute-done((bf16[512,512]{1,0:T(8,128)(2,1)S(1)}, bf16[512,512]{1,0:T(8,128)(2,1)S(1)}, u32[]{:S(2)}, u32[]{:S(2)}) %collective-permute-start.10) | collective-permute-done | bytes 524320 | tf_op jit(solution)/shard_map/ppermute | solution.py:22
  57.8 2.9 %collective-permute-start.13 = (bf16[512,512]{1,0:T(8,128)(2,1)S(1)}, bf16[512,512]{1,0:T(8,128)(2,1)}, u32[]{:S(2)}, u32[]{:S(2)}) collective-permute-start(bf16[512,512]{1,0:T(8,128)(2,1)S(1)} %collective-permute-done.7.refs_6_), channel_id=1, source_target_pairs={{0,8},{8,16},{16,24},{24,0},{1,9},{9,17},{17,25},{25,1},{2,10},{10... | collective-permute-start | bytes 1572872 | tf_op jit(solution)/shard_map/ppermute | solution.py:22
  62.0 1.6 copy-done
  63.6 3.7 %grad_gate_parts.4 = (bf16[512,512]{1,0:T(8,128)(2,1)}, bf16[512,512]{1,0:T(8,128)(2,1)}) custom-call(s32[8]{0:T(128)S(1)} %stack.35.place_ref, bf16[4,2048,128]{2,1,0:T(8,128)(2,1)S(1)} %bitcast.10, bf16[4,2048,128]{2,1,0:T(8,128)(2,1)} %collective-permute-done.12.sib_ref, bf16[1024,1024]{1,0:T(8,128)(2,1)S(1)} %copy-done), custom_call_target="tpu_custom_call" | custom-call | flops 1048576 | bytes 262144 | tf_op jit(solution)/shard_map/grad_gate_parts/pallas_call | solution.py:176
  67.3 3.0 %collective-permute-start.15 = (bf16[512,512]{1,0:T(8,128)(2,1)}, bf16[512,512]{1,0:T(8,128)(2,1)}, u32[]{:S(2)}, u32[]{:S(2)}) collective-permute-start(bf16[512,512]{1,0:T(8,128)(2,1)} %get-tuple-element.46), channel_id=1, source_target_pairs={{0,8},{8,16},{16,24},{24,0},{1,9},{9,17},{17,25},{25,1},{2,10},{10... | collective-permute-start | bytes 1572872 | tf_op jit(solution)/shard_map/ppermute | solution.py:22
  70.4 3.2 %collective-permute-done.14.refs_5_ = bf16[512,512]{1,0:T(8,128)(2,1)} collective-permute-done((bf16[512,512]{1,0:T(8,128)(2,1)}, bf16[512,512]{1,0:T(8,128)(2,1)}, u32[]{:S(2)}, u32[]{:S(2)}) %collective-permute-start.14) | collective-permute-done | bytes 524320 | tf_op jit(solution)/shard_map/ppermute | solution.py:22
  73.6 3.7 %grad_gate_parts.6 = (bf16[512,512]{1,0:T(8,128)(2,1)}, bf16[512,512]{1,0:T(8,128)(2,1)}) custom-call(s32[8]{0:T(128)S(1)} %stack.35.place_ref, bf16[4,2048,128]{2,1,0:T(8,128)(2,1)S(1)} %bitcast.11, bf16[4,2048,128]{2,1,0:T(8,128)(2,1)} %collective-permute-done.12.sib_ref, bf16[1024,1024]{1,0:T(8,128)(2,1)S(1)} %copy-done), custom_call_target="tpu_custom_call" | custom-call | flops 1048576 | bytes 262144 | tf_op jit(solution)/shard_map/grad_gate_parts/pallas_call | solution.py:176
  77.3 3.1 %collective-permute-start.18 = (bf16[512,512]{1,0:T(8,128)(2,1)}, bf16[512,512]{1,0:T(8,128)(2,1)S(1)}, u32[]{:S(2)}, u32[]{:S(2)}) collective-permute-start(bf16[512,512]{1,0:T(8,128)(2,1)} %get-tuple-element.51), channel_id=1, source_target_pairs={{0,8},{8,16},{16,24},{24,0},{1,9},{9,17},{17,25},{25,1},{2,10},{10... | collective-permute-start | bytes 1572872 | tf_op jit(solution)/shard_map/ppermute | solution.py:22
  80.5 6.4 %grad_proj_part.1 = bf16[1024,1024]{1,0:T(8,128)(2,1)S(1)} custom-call(s32[8]{0:T(128)S(1)} %stack.35.place_ref, bf16[4,2048,128]{2,1,0:T(8,128)(2,1)S(1)} %bitcast.12, bf16[4,2048,128]{2,1,0:T(8,128)(2,1)} %collective-permute-done.12.sib_ref, bf16[512,512]{1,0:T(8,128)(2,1)S(1)} %copy-done.19, bf16[512,512]{1,0:T(8,128)(2,1)S(1)} %get-tuple-element.44.refs_4_.refs_1_, ...), custom_call_target="tpu_custom_call" | custom-call | flops 1048576 | bytes 262144 | tf_op jit(solution)/shard_map/grad_proj_part/pallas_call | solution.py:215
  86.9 1.4 copy-done.11
  88.3 1.6 copy-done.1
  89.8 3.9 %grad_gate_parts.7 = (bf16[512,512]{1,0:T(8,128)(2,1)}, bf16[512,512]{1,0:T(8,128)(2,1)}) custom-call(s32[8]{0:T(128)S(1)} %stack.35.place_ref, bf16[4,2048,128]{2,1,0:T(8,128)(2,1)S(1)} %bitcast.13, bf16[4,2048,128]{2,1,0:T(8,128)(2,1)} %collective-permute-done.12.sib_ref, bf16[1024,1024]{1,0:T(8,128)(2,1)S(1)} %copy-done.1, ...), custom_call_target="tpu_custom_call" | custom-call | flops 1048576 | bytes 262144 | tf_op jit(solution)/shard_map/grad_gate_parts/pallas_call | solution.py:176
  93.8 3.2 %collective-permute-start.17 = (bf16[512,512]{1,0:T(8,128)(2,1)}, bf16[512,512]{1,0:T(8,128)(2,1)S(1)}, u32[]{:S(2)}, u32[]{:S(2)}) collective-permute-start(bf16[512,512]{1,0:T(8,128)(2,1)} %get-tuple-element.55), channel_id=1, source_target_pairs={{0,8},{8,16},{16,24},{24,0},{1,9},{9,17},{17,25},{25,1},{2,10},{10... | collective-permute-start | bytes 1572872 | tf_op jit(solution)/shard_map/ppermute | solution.py:22
  97.0 1.6 copy-done.2
  98.6 3.0 %grad_gate_parts.5 = (f32[512,512]{1,0:T(8,128)S(1)}, f32[512,512]{1,0:T(8,128)S(1)}) custom-call(s32[8]{0:T(128)S(1)} %stack.35.place_ref, bf16[4,2048,128]{2,1,0:T(8,128)(2,1)S(1)} %bitcast.14, bf16[4,2048,128]{2,1,0:T(8,128)(2,1)} %collective-permute-done.12.sib_ref, bf16[1024,1024]{1,0:T(8,128)(2,1)S(1)} %copy-done.2), custom_call_target="tpu_custom_call" | custom-call | flops 1048576 | bytes 262144 | tf_op jit(solution)/shard_map/grad_gate_parts/pallas_call | solution.py:176
  102.4 5.0 %collective-permute-done.17.refs_2_ = bf16[512,512]{1,0:T(8,128)(2,1)S(1)} collective-permute-done((bf16[512,512]{1,0:T(8,128)(2,1)}, bf16[512,512]{1,0:T(8,128)(2,1)S(1)}, u32[]{:S(2)}, u32[]{:S(2)}) %collective-permute-start.17) | collective-permute-done | bytes 524320 | tf_op jit(solution)/shard_map/ppermute | solution.py:22
  108.2 2.6 %collective-permute-done.20.refs_5_ = bf16[512,512]{1,0:T(8,128)(2,1)} collective-permute-done((bf16[512,512]{1,0:T(8,128)(2,1)}, bf16[512,512]{1,0:T(8,128)(2,1)}, u32[]{:S(2)}, u32[]{:S(2)}) %collective-permute-start.20) | collective-permute-done | bytes 524320 | tf_op jit(solution)/shard_map/ppermute | solution.py:22
  110.9 1.0 copy-done.15
  111.9 1.0 copy-done.17
  113.0 3.6 %gate_gradients.1 = (bf16[512,1024]{1,0:T(8,128)(2,1)}, bf16[512,1024]{1,0:T(8,128)(2,1)S(1)}, bf16[128,1024]{1,0:T(8,128)(2,1)}) custom-call(f32[512,512]{1,0:T(8,128)S(1)} %get-tuple-element.49.refs_0_, f32[512,512]{1,0:T(8,128)S(1)} %get-tuple-element.50.refs_1_, bf16[512,512]{1,0:T(8,128)(2,1)S(1)} %copy-done.17, bf16[512,512]{1,0:T(8,128)(2,1)S(1)} %copy-done.15, ...), custom_call_target="tpu_custom_call" | custom-call | flops 1048576 | bytes 262144 | tf_op jit(solution)/shard_map/gate_gradients/pallas_call | solution.py:244
  116.5 2.1 %collective-permute-start.24 = (bf16[128,1024]{1,0:T(8,128)(2,1)}, bf16[128,1024]{1,0:T(8,128)(2,1)}, u32[]{:S(2)}, u32[]{:S(2)}) collective-permute-start(bf16[128,1024]{1,0:T(8,128)(2,1)} %get-tuple-element.62), channel_id=1, source_target_pairs={{8,0},{16,8},{24,16},{32,24},{40,32},{48,40},{56,48},{64,56},{72,6... | collective-permute-start | bytes 786440 | tf_op jit(solution)/shard_map/ppermute | solution.py:28
  118.7 5.7 %filter_part.1 = f32[64,128]{1,0:T(8,128)S(1)} custom-call(bf16[512,1024]{1,0:T(8,128)(2,1)S(1)} %get-tuple-element.66.inner_ref, bf16[512,1024]{1,0:T(8,128)(2,1)S(1)} %copy-done.13, bf16[128,1024]{1,0:T(8,128)(2,1)S(1)} %collective-permute-done.3.rim_ref), custom_call_target="tpu_custom_call" | custom-call | flops 137438953472 | bytes 262144 | tf_op jit(solution)/shard_map/filter_part/pallas_call | solution.py:283
  124.5 2.5 %collective-permute-start.22 = (f32[64,128]{1,0:T(8,128)S(1)}, f32[64,128]{1,0:T(8,128)S(1)}, u32[]{:S(2)}, u32[]{:S(2)}) collective-permute-start(f32[64,128]{1,0:T(8,128)S(1)} %filter_part.1), channel_id=1, source_target_pairs={{0,16},{8,24},{16,0},{24,8},{1,17},{9,25},{17,1},{25,9},{2,18},{10... | collective-permute-start | bytes 98312 | tf_op jit(solution)/shard_map/ppermute | solution.py:22
  127.0 2.5 %collective-permute-start.23 = (f32[64,128]{1,0:T(8,128)S(1)}, f32[64,128]{1,0:T(8,128)S(1)}, u32[]{:S(2)}, u32[]{:S(2)}) collective-permute-start(f32[64,128]{1,0:T(8,128)S(1)} %filter_part.1), channel_id=1, source_target_pairs={{0,8},{8,16},{16,24},{24,0},{1,9},{9,17},{17,25},{25,1},{2,10},{10... | collective-permute-start | bytes 98312 | tf_op jit(solution)/shard_map/ppermute | solution.py:22
  129.5 4.2 %collective-permute-done.24.ahead_ref = bf16[128,1024]{1,0:T(8,128)(2,1)} collective-permute-done((bf16[128,1024]{1,0:T(8,128)(2,1)}, bf16[128,1024]{1,0:T(8,128)(2,1)}, u32[]{:S(2)}, u32[]{:S(2)}) %collective-permute-start.24) | collective-permute-done | bytes 262176 | tf_op jit(solution)/shard_map/ppermute | solution.py:28
  133.8 4.0 %conv_backward.2 = (bf16[512,1024]{1,0:T(8,128)(2,1)}, bf16[512,1024]{1,0:T(8,128)(2,1)}) custom-call(bf16[64,128]{1,0:T(8,128)(2,1)S(1)} %copy-done.29, bf16[512,1024]{1,0:T(8,128)(2,1)S(1)} %get-tuple-element.66.inner_ref, bf16[128,1024]{1,0:T(8,128)(2,1)} %collective-permute-done.24.ahead_ref, bf16[512,1024]{1,0:T(8,128)(2,1)S(1)} %copy-done.4, ...), custom_call_target="tpu_custom_call" | custom-call | flops 1048576 | bytes 262144 | tf_op jit(solution)/shard_map/conv_backward/pallas_call | solution.py:323
  137.8 7.7 %collective-permute-start.25 = (f32[64,128]{1,0:T(8,128)S(1)}, f32[64,128]{1,0:T(8,128)S(1)}, u32[]{:S(2)}, u32[]{:S(2)}) collective-permute-start(f32[64,128]{1,0:T(8,128)S(1)} %select_add_fusion.1), channel_id=1, source_target_pairs={{0,192},{32,224},{64,0},{96,32},{128,64},{160,96},{192,128},{224,1... | collective-permute-start | bytes 98312 | tf_op jit(solution)/shard_map/ppermute | solution.py:22
  145.5 2.3 %collective-permute-start.26 = (f32[64,128]{1,0:T(8,128)S(1)}, f32[64,128]{1,0:T(8,128)S(1)}, u32[]{:S(2)}, u32[]{:S(2)}) collective-permute-start(f32[64,128]{1,0:T(8,128)S(1)} %select_add_fusion.1), channel_id=1, source_target_pairs={{0,128},{32,160},{64,192},{96,224},{128,0},{160,32},{192,64},{224,... | collective-permute-start | bytes 98312 | tf_op jit(solution)/shard_map/ppermute | solution.py:22
  147.8 2.8 %collective-permute-start.27 = (f32[64,128]{1,0:T(8,128)S(1)}, f32[64,128]{1,0:T(8,128)S(1)}, u32[]{:S(2)}, u32[]{:S(2)}) collective-permute-start(f32[64,128]{1,0:T(8,128)S(1)} %select_add_fusion.1), channel_id=1, source_target_pairs={{0,64},{32,96},{64,128},{96,160},{128,192},{160,224},{192,0},{224,... | collective-permute-start | bytes 98312 | tf_op jit(solution)/shard_map/ppermute | solution.py:22
  150.6 4.0 %conv_backward.3 = (bf16[512,1024]{1,0:T(8,128)(2,1)}, bf16[512,1024]{1,0:T(8,128)(2,1)}) custom-call(bf16[64,128]{1,0:T(8,128)(2,1)S(1)} %copy-done.29, bf16[512,1024]{1,0:T(8,128)(2,1)S(1)} %get-tuple-element.66.inner_ref, bf16[128,1024]{1,0:T(8,128)(2,1)} %collective-permute-done.24.ahead_ref, ...), custom_call_target="tpu_custom_call", output_to_operand_aliasing={{0}: (5, {}), {1}: (6, {})} | custom-call | flops 1048576 | bytes 262144 | tf_op jit(solution)/shard_map/conv_backward/pallas_call | solution.py:323
  154.7 1.0 collective-permute-start.28
  155.7 1.8 %convert_element_type.15 = f32[128,1024]{1,0:T(8,128)} convert(bf16[128,1024]{1,0:T(8,128)(2,1)} %reduce-scatter.2.cloned.1.call-done) | non-fusion elementwise | flops 131072 | bytes 786432 | tf_op jit(solution)/shard_map/convert_element_type | solution.py:391
  157.5 1.2 collective-permute-done.28
  (103 shorter events, 9.8 us)
Async XLA Ops:
  7.2 11.3 %copy-start.3 = (bf16[512,1024]{1,0:T(8,128)(2,1)S(1)}, bf16[512,1024]{1,0:T(8,128)(2,1)}, u32[]{:S(2)}) copy-start(bf16[512,1024]{1,0:T(8,128)(2,1)} %k_ref.7) | copy-start | bytes 3145732
  7.2 11.3 %copy-start.5 = (bf16[512,1024]{1,0:T(8,128)(2,1)S(1)}, bf16[512,1024]{1,0:T(8,128)(2,1)}, u32[]{:S(2)}) copy-start(bf16[512,1024]{1,0:T(8,128)(2,1)} %v_ref.7) | copy-start | bytes 3145732
  7.2 11.3 %copy-start.28 = (bf16[64,128]{1,0:T(8,128)(2,1)S(1)}, bf16[64,128]{1,0:T(8,128)(2,1)}, u32[]{:S(2)}) copy-start(bf16[64,128]{1,0:T(8,128)(2,1)} %filters_ref.7) | copy-start | bytes 49156
  7.2 54.8 %all-gather.2.cloned.1.call-start = ((), (), s32[]{:S(2)}) async-start(), calls=%async_computation.1 | async-start | bytes 2359296 | tf_op jit(solution)/shard_map/all_gather | solution.py:355
  8.5 10.0 %collective-permute-start.3 = (bf16[128,1024]{1,0:T(8,128)(2,1)S(1)}, bf16[128,1024]{1,0:T(8,128)(2,1)S(1)}, u32[]{:S(2)}, u32[]{:S(2)}) collective-permute-start(bf16[128,1024]{1,0:T(8,128)(2,1)S(1)} %multiply_convert_fusion), channel_id=1, source_target_pairs={{0,8},{8,16},{16,24},{24,32},{32,40},{40,48},{48,56},{56,64},{64,7... | collective-permute-start | bytes 786440 | tf_op jit(solution)/shard_map/ppermute | solution.py:28
  14.1 12.6 %collective-permute-start = (bf16[512,128]{1,0:T(8,128)(2,1)}, bf16[512,128]{1,0:T(8,128)(2,1)S(1)}, u32[]{:S(2)}, u32[]{:S(2)}) collective-permute-start(bf16[512,128]{1,0:T(8,128)(2,1)} %get-tuple-element.72), channel_id=1, source_target_pairs={{0,24},{8,0},{16,8},{24,16},{1,25},{9,1},{17,9},{25,17},{2,26},{10... | collective-permute-start | bytes 393224 | tf_op jit(solution)/shard_map/ppermute | solution.py:22
  14.3 12.4 %collective-permute-start.1 = (bf16[512,128]{1,0:T(8,128)(2,1)}, bf16[512,128]{1,0:T(8,128)(2,1)S(1)}, u32[]{:S(2)}, u32[]{:S(2)}) collective-permute-start(bf16[512,128]{1,0:T(8,128)(2,1)} %get-tuple-element.74), channel_id=1, source_target_pairs={{0,16},{8,24},{16,0},{24,8},{1,17},{9,25},{17,1},{25,9},{2,18},{10... | collective-permute-start | bytes 393224 | tf_op jit(solution)/shard_map/ppermute | solution.py:22
  15.8 11.0 %collective-permute-start.2 = (bf16[512,128]{1,0:T(8,128)(2,1)S(1)}, bf16[512,128]{1,0:T(8,128)(2,1)S(1)}, u32[]{:S(2)}, u32[]{:S(2)}) collective-permute-start(bf16[512,128]{1,0:T(8,128)(2,1)S(1)} %get-tuple-element.71), channel_id=1, source_target_pairs={{0,8},{8,16},{16,24},{24,0},{1,9},{9,17},{17,25},{25,1},{2,10},{10... | collective-permute-start | bytes 393224 | tf_op jit(solution)/shard_map/ppermute | solution.py:22
  17.9 137.8 %reduce-scatter.2.cloned.1.call-start = ((), (), s32[]{:S(2)}) async-start(), calls=%async_computation.2 | async-start | bytes 2359296 | tf_op jit(solution)/shard_map/reduce_scatter | solution.py:391
  23.2 18.1 %copy-start.18 = (bf16[512,512]{1,0:T(8,128)(2,1)}, bf16[512,512]{1,0:T(8,128)(2,1)S(1)}, u32[]{:S(2)}) copy-start(bf16[512,512]{1,0:T(8,128)(2,1)S(1)} %get-tuple-element.53.refs_0_) | copy-start | bytes 1572868
  26.7 21.1 %copy-start.9 = (f32[512,1024]{1,0:T(8,128)}, f32[512,1024]{1,0:T(8,128)S(1)}, u32[]{:S(2)}) copy-start(f32[512,1024]{1,0:T(8,128)S(1)} %get-tuple-element.57.refs_7_) | copy-start | bytes 6291460
  26.7 21.1 %copy-start.12 = (bf16[512,1024]{1,0:T(8,128)(2,1)}, bf16[512,1024]{1,0:T(8,128)(2,1)S(1)}, u32[]{:S(2)}) copy-start(bf16[512,1024]{1,0:T(8,128)(2,1)S(1)} %get-tuple-element.60.mixed_ref) | copy-start | bytes 3145732
  26.8 14.1 %collective-permute-start.5 = (bf16[2048,128]{1,0:T(8,128)(2,1)S(1)}, bf16[2048,128]{1,0:T(8,128)(2,1)S(1)}, u32[]{:S(2)}, u32[]{:S(2)}) collective-permute-start(bf16[2048,128]{1,0:T(8,128)(2,1)S(1)} %join.1), channel_id=1, source_target_pairs={{0,2},{2,4},{4,6},{6,0},{1,3},{3,5},{5,7},{7,1},{8,10},{10,12},{12... | collective-permute-start | bytes 1572872 | tf_op jit(solution)/shard_map/ppermute | solution.py:22
  28.4 13.8 %collective-permute-start.4 = (bf16[2048,128]{1,0:T(8,128)(2,1)S(1)}, bf16[2048,128]{1,0:T(8,128)(2,1)S(1)}, u32[]{:S(2)}, u32[]{:S(2)}) collective-permute-start(bf16[2048,128]{1,0:T(8,128)(2,1)S(1)} %join.1), channel_id=1, source_target_pairs={{0,6},{2,0},{4,2},{6,4},{1,7},{3,1},{5,3},{7,5},{8,14},{10,8},{12,... | collective-permute-start | bytes 1572872 | tf_op jit(solution)/shard_map/ppermute | solution.py:22
  30.1 15.2 %collective-permute-start.7 = (bf16[512,512]{1,0:T(8,128)(2,1)S(1)}, bf16[512,512]{1,0:T(8,128)(2,1)S(1)}, u32[]{:S(2)}, u32[]{:S(2)}) collective-permute-start(bf16[512,512]{1,0:T(8,128)(2,1)S(1)} %get-tuple-element.53.refs_0_), channel_id=1, source_target_pairs={{0,8},{8,16},{16,24},{24,0},{1,9},{9,17},{17,25},{25,1},{2,10},{10... | collective-permute-start | bytes 1572872 | tf_op jit(solution)/shard_map/ppermute | solution.py:22
  30.1 17.6 %collective-permute-start.8 = (bf16[512,512]{1,0:T(8,128)(2,1)S(1)}, bf16[512,512]{1,0:T(8,128)(2,1)S(1)}, u32[]{:S(2)}, u32[]{:S(2)}) collective-permute-start(bf16[512,512]{1,0:T(8,128)(2,1)S(1)} %get-tuple-element.44.refs_4_.refs_1_), channel_id=1, source_target_pairs={{0,24},{8,0},{16,8},{24,16},{1,25},{9,1},{17,9},{25,17},{2,26},{10... | collective-permute-start | bytes 1572872 | tf_op jit(solution)/shard_map/ppermute | solution.py:22
  40.9 7.7 %collective-permute-start.6 = (bf16[1024,128]{1,0:T(8,128)(2,1)S(1)}, bf16[1024,128]{1,0:T(8,128)(2,1)S(1)}, u32[]{:S(2)}, u32[]{:S(2)}) collective-permute-start(bf16[1024,128]{1,0:T(8,128)(2,1)S(1)} %slice.16), channel_id=1, source_target_pairs={{0,2},{2,4},{4,6},{6,0},{1,3},{3,5},{5,7},{7,1},{8,10},{10,12},{12... | collective-permute-start | bytes 786440 | tf_op jit(solution)/shard_map/ppermute | solution.py:22
  41.3 13.5 %collective-permute-start.10 = (bf16[512,512]{1,0:T(8,128)(2,1)S(1)}, bf16[512,512]{1,0:T(8,128)(2,1)S(1)}, u32[]{:S(2)}, u32[]{:S(2)}) collective-permute-start(bf16[512,512]{1,0:T(8,128)(2,1)S(1)} %get-tuple-element.53.refs_0_), channel_id=1, source_target_pairs={{0,24},{8,0},{16,8},{24,16},{1,25},{9,1},{17,9},{25,17},{2,26},{10... | collective-permute-start | bytes 1572872 | tf_op jit(solution)/shard_map/ppermute | solution.py:22
  42.2 6.9 %collective-permute-start.9 = (bf16[1024,128]{1,0:T(8,128)(2,1)S(1)}, bf16[1024,128]{1,0:T(8,128)(2,1)S(1)}, u32[]{:S(2)}, u32[]{:S(2)}) collective-permute-start(bf16[1024,128]{1,0:T(8,128)(2,1)S(1)} %slice.17), channel_id=1, source_target_pairs={{0,6},{2,0},{4,2},{6,4},{1,7},{3,1},{5,3},{7,5},{8,14},{10,8},{12,... | collective-permute-start | bytes 786440 | tf_op jit(solution)/shard_map/ppermute | solution.py:22
  45.2 22.0 %copy-start.20 = (bf16[512,512]{1,0:T(8,128)(2,1)}, bf16[512,512]{1,0:T(8,128)(2,1)S(1)}, u32[]{:S(2)}) copy-start(bf16[512,512]{1,0:T(8,128)(2,1)S(1)} %collective-permute-done.7.refs_6_) | copy-start | bytes 1572868
  45.2 10.9 %collective-permute-start.11 = (bf16[512,512]{1,0:T(8,128)(2,1)S(1)}, bf16[512,512]{1,0:T(8,128)(2,1)S(1)}, u32[]{:S(2)}, u32[]{:S(2)}) collective-permute-start(bf16[512,512]{1,0:T(8,128)(2,1)S(1)} %get-tuple-element.44.refs_4_.refs_1_), channel_id=1, source_target_pairs={{0,8},{8,16},{16,24},{24,0},{1,9},{9,17},{17,25},{25,1},{2,10},{10... | collective-permute-start | bytes 1572872 | tf_op jit(solution)/shard_map/ppermute | solution.py:22
  57.0 4.3 %collective-permute-start.12 = (bf16[4,2048,128]{2,1,0:T(8,128)(2,1)S(1)}, bf16[4,2048,128]{2,1,0:T(8,128)(2,1)}, u32[]{:S(2)}, u32[]{:S(2)}) collective-permute-start(bf16[4,2048,128]{2,1,0:T(8,128)(2,1)S(1)} %bitcast.9), channel_id=1, source_target_pairs={{0,1},{1,0},{2,3},{3,2},{4,5},{5,4},{6,7},{7,6},{8,9},{9,8},{10,11... | collective-permute-start | bytes 6291464 | tf_op jit(solution)/shard_map/ppermute | solution.py:22
  57.0 16.6 %collective-permute-start.14 = (bf16[512,512]{1,0:T(8,128)(2,1)}, bf16[512,512]{1,0:T(8,128)(2,1)}, u32[]{:S(2)}, u32[]{:S(2)}) collective-permute-start(bf16[512,512]{1,0:T(8,128)(2,1)} %copy-done.22), channel_id=1, source_target_pairs={{0,24},{8,0},{16,8},{24,16},{1,25},{9,1},{17,9},{25,17},{2,26},{10... | collective-permute-start | bytes 1572872 | tf_op jit(solution)/shard_map/ppermute | solution.py:22
  57.8 15.8 %collective-permute-start.13 = (bf16[512,512]{1,0:T(8,128)(2,1)S(1)}, bf16[512,512]{1,0:T(8,128)(2,1)}, u32[]{:S(2)}, u32[]{:S(2)}) collective-permute-start(bf16[512,512]{1,0:T(8,128)(2,1)S(1)} %collective-permute-done.7.refs_6_), channel_id=1, source_target_pairs={{0,8},{8,16},{16,24},{24,0},{1,9},{9,17},{17,25},{25,1},{2,10},{10... | collective-permute-start | bytes 1572872 | tf_op jit(solution)/shard_map/ppermute | solution.py:22
  67.3 21.0 %collective-permute-start.15 = (bf16[512,512]{1,0:T(8,128)(2,1)}, bf16[512,512]{1,0:T(8,128)(2,1)}, u32[]{:S(2)}, u32[]{:S(2)}) collective-permute-start(bf16[512,512]{1,0:T(8,128)(2,1)} %get-tuple-element.46), channel_id=1, source_target_pairs={{0,8},{8,16},{16,24},{24,0},{1,9},{9,17},{17,25},{25,1},{2,10},{10... | collective-permute-start | bytes 1572872 | tf_op jit(solution)/shard_map/ppermute | solution.py:22
  70.3 10.2 %copy-start.19 = (bf16[512,512]{1,0:T(8,128)(2,1)S(1)}, bf16[512,512]{1,0:T(8,128)(2,1)}, u32[]{:S(2)}) copy-start(bf16[512,512]{1,0:T(8,128)(2,1)} %copy-done.18) | copy-start | bytes 1572868
  70.3 10.2 %copy-start.21 = (bf16[512,512]{1,0:T(8,128)(2,1)S(1)}, bf16[512,512]{1,0:T(8,128)(2,1)}, u32[]{:S(2)}) copy-start(bf16[512,512]{1,0:T(8,128)(2,1)} %copy-done.20) | copy-start | bytes 1572868
  70.3 10.2 %copy-start.23 = (bf16[512,512]{1,0:T(8,128)(2,1)S(1)}, bf16[512,512]{1,0:T(8,128)(2,1)}, u32[]{:S(2)}) copy-start(bf16[512,512]{1,0:T(8,128)(2,1)} %copy-done.22) | copy-start | bytes 1572868
  70.3 10.2 %copy-start.25 = (bf16[512,512]{1,0:T(8,128)(2,1)S(1)}, bf16[512,512]{1,0:T(8,128)(2,1)}, u32[]{:S(2)}) copy-start(bf16[512,512]{1,0:T(8,128)(2,1)} %copy-done.24) | copy-start | bytes 1572868
  70.3 10.2 %copy-start.27 = (bf16[512,512]{1,0:T(8,128)(2,1)S(1)}, bf16[512,512]{1,0:T(8,128)(2,1)}, u32[]{:S(2)}) copy-start(bf16[512,512]{1,0:T(8,128)(2,1)} %copy-done.26) | copy-start | bytes 1572868
  70.3 18.0 %collective-permute-start.16 = (bf16[512,512]{1,0:T(8,128)(2,1)}, bf16[512,512]{1,0:T(8,128)(2,1)}, u32[]{:S(2)}, u32[]{:S(2)}) collective-permute-start(bf16[512,512]{1,0:T(8,128)(2,1)} %get-tuple-element.47), channel_id=1, source_target_pairs={{0,24},{8,0},{16,8},{24,16},{1,25},{9,1},{17,9},{25,17},{2,26},{10... | collective-permute-start | bytes 1572872 | tf_op jit(solution)/shard_map/ppermute | solution.py:22
  77.3 24.3 %collective-permute-start.18 = (bf16[512,512]{1,0:T(8,128)(2,1)}, bf16[512,512]{1,0:T(8,128)(2,1)S(1)}, u32[]{:S(2)}, u32[]{:S(2)}) collective-permute-start(bf16[512,512]{1,0:T(8,128)(2,1)} %get-tuple-element.51), channel_id=1, source_target_pairs={{0,8},{8,16},{16,24},{24,0},{1,9},{9,17},{17,25},{25,1},{2,10},{10... | collective-permute-start | bytes 1572872 | tf_op jit(solution)/shard_map/ppermute | solution.py:22
  80.4 22.0 %collective-permute-start.19 = (bf16[512,512]{1,0:T(8,128)(2,1)}, bf16[512,512]{1,0:T(8,128)(2,1)}, u32[]{:S(2)}, u32[]{:S(2)}) collective-permute-start(bf16[512,512]{1,0:T(8,128)(2,1)} %get-tuple-element.52), channel_id=1, source_target_pairs={{0,24},{8,0},{16,8},{24,16},{1,25},{9,1},{17,9},{25,17},{2,26},{10... | collective-permute-start | bytes 1572872 | tf_op jit(solution)/shard_map/ppermute | solution.py:22
  93.8 13.7 %collective-permute-start.17 = (bf16[512,512]{1,0:T(8,128)(2,1)}, bf16[512,512]{1,0:T(8,128)(2,1)S(1)}, u32[]{:S(2)}, u32[]{:S(2)}) collective-permute-start(bf16[512,512]{1,0:T(8,128)(2,1)} %get-tuple-element.55), channel_id=1, source_target_pairs={{0,8},{8,16},{16,24},{24,0},{1,9},{9,17},{17,25},{25,1},{2,10},{10... | collective-permute-start | bytes 1572872 | tf_op jit(solution)/shard_map/ppermute | solution.py:22
  97.0 13.9 %collective-permute-start.20 = (bf16[512,512]{1,0:T(8,128)(2,1)}, bf16[512,512]{1,0:T(8,128)(2,1)}, u32[]{:S(2)}, u32[]{:S(2)}) collective-permute-start(bf16[512,512]{1,0:T(8,128)(2,1)} %get-tuple-element.56), channel_id=1, source_target_pairs={{0,24},{8,0},{16,8},{24,16},{1,25},{9,1},{17,9},{25,17},{2,26},{10... | collective-permute-start | bytes 1572872 | tf_op jit(solution)/shard_map/ppermute | solution.py:22
  98.6 12.2 %copy-start.8 = (bf16[512,1024]{1,0:T(8,128)(2,1)S(1)}, bf16[512,1024]{1,0:T(8,128)(2,1)}, u32[]{:S(2)}) copy-start(bf16[512,1024]{1,0:T(8,128)(2,1)} %refs_6_.1) | copy-start | bytes 3145732
  98.6 12.2 %copy-start.10 = (f32[512,1024]{1,0:T(8,128)S(1)}, f32[512,1024]{1,0:T(8,128)}, u32[]{:S(2)}) copy-start(f32[512,1024]{1,0:T(8,128)} %copy-done.9) | copy-start | bytes 6291460
  116.5 17.2 %collective-permute-start.24 = (bf16[128,1024]{1,0:T(8,128)(2,1)}, bf16[128,1024]{1,0:T(8,128)(2,1)}, u32[]{:S(2)}, u32[]{:S(2)}) collective-permute-start(bf16[128,1024]{1,0:T(8,128)(2,1)} %get-tuple-element.62), channel_id=1, source_target_pairs={{8,0},{16,8},{24,16},{32,24},{40,32},{48,40},{56,48},{64,56},{72,6... | collective-permute-start | bytes 786440 | tf_op jit(solution)/shard_map/ppermute | solution.py:28
  118.7 15.1 %copy-start.4 = (bf16[512,1024]{1,0:T(8,128)(2,1)S(1)}, bf16[512,1024]{1,0:T(8,128)(2,1)}, u32[]{:S(2)}) copy-start(bf16[512,1024]{1,0:T(8,128)(2,1)} %k_ref.7) | copy-start | bytes 3145732
  118.7 15.1 %copy-start.6 = (bf16[512,1024]{1,0:T(8,128)(2,1)S(1)}, bf16[512,1024]{1,0:T(8,128)(2,1)}, u32[]{:S(2)}) copy-start(bf16[512,1024]{1,0:T(8,128)(2,1)} %v_ref.7) | copy-start | bytes 3145732
  118.7 15.1 %copy-start.29 = (bf16[64,128]{1,0:T(8,128)(2,1)S(1)}, bf16[64,128]{1,0:T(8,128)(2,1)}, u32[]{:S(2)}) copy-start(bf16[64,128]{1,0:T(8,128)(2,1)} %filters_ref.7) | copy-start | bytes 49156
  124.4 13.4 %collective-permute-start.21 = (f32[64,128]{1,0:T(8,128)S(1)}, f32[64,128]{1,0:T(8,128)S(1)}, u32[]{:S(2)}, u32[]{:S(2)}) collective-permute-start(f32[64,128]{1,0:T(8,128)S(1)} %filter_part.1), channel_id=1, source_target_pairs={{0,24},{8,0},{16,8},{24,16},{1,25},{9,1},{17,9},{25,17},{2,26},{10... | collective-permute-start | bytes 98312 | tf_op jit(solution)/shard_map/ppermute | solution.py:22
  124.5 13.3 %collective-permute-start.22 = (f32[64,128]{1,0:T(8,128)S(1)}, f32[64,128]{1,0:T(8,128)S(1)}, u32[]{:S(2)}, u32[]{:S(2)}) collective-permute-start(f32[64,128]{1,0:T(8,128)S(1)} %filter_part.1), channel_id=1, source_target_pairs={{0,16},{8,24},{16,0},{24,8},{1,17},{9,25},{17,1},{25,9},{2,18},{10... | collective-permute-start | bytes 98312 | tf_op jit(solution)/shard_map/ppermute | solution.py:22
  127.0 10.8 %collective-permute-start.23 = (f32[64,128]{1,0:T(8,128)S(1)}, f32[64,128]{1,0:T(8,128)S(1)}, u32[]{:S(2)}, u32[]{:S(2)}) collective-permute-start(f32[64,128]{1,0:T(8,128)S(1)} %filter_part.1), channel_id=1, source_target_pairs={{0,8},{8,16},{16,24},{24,0},{1,9},{9,17},{17,25},{25,1},{2,10},{10... | collective-permute-start | bytes 98312 | tf_op jit(solution)/shard_map/ppermute | solution.py:22
  137.8 16.8 %collective-permute-start.25 = (f32[64,128]{1,0:T(8,128)S(1)}, f32[64,128]{1,0:T(8,128)S(1)}, u32[]{:S(2)}, u32[]{:S(2)}) collective-permute-start(f32[64,128]{1,0:T(8,128)S(1)} %select_add_fusion.1), channel_id=1, source_target_pairs={{0,192},{32,224},{64,0},{96,32},{128,64},{160,96},{192,128},{224,1... | collective-permute-start | bytes 98312 | tf_op jit(solution)/shard_map/ppermute | solution.py:22
  145.5 9.1 %collective-permute-start.26 = (f32[64,128]{1,0:T(8,128)S(1)}, f32[64,128]{1,0:T(8,128)S(1)}, u32[]{:S(2)}, u32[]{:S(2)}) collective-permute-start(f32[64,128]{1,0:T(8,128)S(1)} %select_add_fusion.1), channel_id=1, source_target_pairs={{0,128},{32,160},{64,192},{96,224},{128,0},{160,32},{192,64},{224,... | collective-permute-start | bytes 98312 | tf_op jit(solution)/shard_map/ppermute | solution.py:22
  147.8 6.9 %collective-permute-start.27 = (f32[64,128]{1,0:T(8,128)S(1)}, f32[64,128]{1,0:T(8,128)S(1)}, u32[]{:S(2)}, u32[]{:S(2)}) collective-permute-start(f32[64,128]{1,0:T(8,128)S(1)} %select_add_fusion.1), channel_id=1, source_target_pairs={{0,64},{32,96},{64,128},{96,160},{128,192},{160,224},{192,0},{224,... | collective-permute-start | bytes 98312 | tf_op jit(solution)/shard_map/ppermute | solution.py:22
  154.7 4.0 %collective-permute-start.28 = (f32[64,128]{1,0:T(8,128)S(1)}, f32[64,128]{1,0:T(8,128)S(1)}, u32[]{:S(2)}, u32[]{:S(2)}) collective-permute-start(f32[64,128]{1,0:T(8,128)S(1)} %select_add_fusion), channel_id=1, source_target_pairs={{0,32},{32,0},{64,96},{96,64},{128,160},{160,128},{192,224},{224,1... | collective-permute-start | bytes 98312 | tf_op jit(solution)/shard_map/ppermute | solution.py:402
  (13 other events, 26.9 us)
Sparse Core Ops, SparseCore 0:
  18.0 43.9 all-gather.1
  97.2 46.9 reduce-scatter.1

commit v9 on v8

--- a/solution.py
+++ b/solution.py
@@ -44,8 +44,8 @@
 def group_tables(filters, reverse):
     taps = filters.shape[1]
     if reverse:
-        filters = jnp.dot(filters, anti_identity(taps), preferred_element_type=F32)
-    rows = jnp.concatenate([filters.astype(F32), jnp.zeros(filters.shape, F32)], 1)
+        filters = jnp.dot(filters.astype(BF16), anti_identity(taps), preferred_element_type=F32)
+    rows = jnp.concatenate([filters, jnp.zeros(filters.shape, F32)], 1)
     tables = [
         pltpu.roll(
             jnp.broadcast_to(rows[g : g + 1], (taps, 2 * taps)), int(reverse), 1, stride=1, stride_axis=0
@@ -247,7 +247,7 @@
         in_specs=[RESIDENT] * 6 + [column, column],
         out_specs=[column, column, pl.BlockSpec((taps, wide), lambda i: (0, i))],
         out_shape=[jax.ShapeDtypeStruct((n, width), BF16) for n in (tokens, tokens, taps)],
-        compiler_params=pltpu.CompilerParams(vmem_limit_bytes=16 * MIB),
+        compiler_params=pltpu.CompilerParams(vmem_limit_bytes=60 * MIB),
         cost_estimate=LIGHT,
         name="gate_gradients",
     )(*own, *from_left, *from_right, q, conv)
@@ -286,7 +286,7 @@
         in_specs=[column, column, pl.BlockSpec((taps, LANES), lambda i: (0, i))],
         out_specs=pl.BlockSpec((groups, taps), lambda i: (i, 0)),
         out_shape=jax.ShapeDtypeStruct((group_count, taps), F32),
-        compiler_params=pltpu.CompilerParams(vmem_limit_bytes=16 * MIB),
+        compiler_params=pltpu.CompilerParams(vmem_limit_bytes=60 * MIB),
         cost_estimate=HEAVY,
         name="filter_part",
     )(inner, mixed, rim)
@@ -351,6 +351,7 @@
     half = width // 2
     x, y, c = (lax.axis_index(a) for a in ("x", "y", "c"))
     part = cotangent.shape[1] // 4
+    filters = filters.astype(F32)
 
     proj = lax.all_gather(proj_out, "z", axis=0, tiled=True)
 

time: 167 us -> 167 us (level)
  waiting for transfers between devices: 34.3 us -> 30.8 us
  Pallas kernels: 45 us -> 47.3 us
  local copies, waits for them, and re-layouts: 15.7 us -> 14 us
    ppermute x2, waiting for transfers between devices: 4.78 us -> 2.45 us  [send_along_tokens(): return lax.ppermute(value, ('z', 'x'), pairs)]
    pallas_call x1, Pallas kernels: 5.69 us -> 7.93 us  [filter_part(): pl.pallas_call(functools.partial(filter_body, taps, groups), grid=(width...]
    pallas_call x1, Pallas kernels: 3.57 us -> 5.59 us  [gate_gradients(): pl.pallas_call(inner_body, grid=(steps,), in_specs=[RESIDENT] * 6 + [colu...]
    unnamed x64 -> x56, local copies, waits for them, and re-layouts: 12.9 us -> 11.2 us
  transfers between devices with their start and end apart: 31 -> 31, of which waited for: 13 -> 13; matrix products, arithmetic and copies ran while one was open for 2% -> 3% of each run, Pallas kernels for 27% -> 29%
where the time goes in v9:
time: 167 us; the launch traced here: 166 us
  starting transfers between devices  54.6 us (33%)
  Pallas kernels  47.3 us (28%)
  waiting for transfers between devices  30.8 us (18%)
  between operations  14.5 us (9%)
  local copies, waits for them, and re-layouts  14 us (8%)
  other arithmetic  4.62 us (3%)
    ppermute x26, starting transfers between devices, send(): lax.ppermute(value, axis, [(i, (i + by) % count) for i in range(count)])  47 us
    ppermute x26, waiting for transfers between devices, send(): lax.ppermute(value, axis, [(i, (i + by) % count) for i in range(count)])  27.4 us
    pallas_call x4, Pallas kernels, gate_parts(): pl.pallas_call(functools.partial(gate_body, wanted), in_specs=[pl.BlockSp...  13.4 us
    unnamed x56, local copies, waits for them, and re-layouts  11.2 us
    pallas_call x1, Pallas kernels, filter_part(): pl.pallas_call(functools.partial(filter_body, taps, groups), grid=(width...  7.93 us
    pallas_call x2, Pallas kernels, forward(): pl.pallas_call(functools.partial(forward_body, taps, groups), grid=(steps...  6.92 us
    pallas_call x2, Pallas kernels, backward(): pl.pallas_call(functools.partial(backward_body, taps, groups), grid=(step...  6.72 us
    pallas_call x1, Pallas kernels, proj_part(): pl.pallas_call(proj_body, in_specs=[pl.BlockSpec(memory_space=pltpu.SMEM)...  6.7 us
  transfers between devices with their start and end apart: 31, of which 13 were waited for; matrix products, arithmetic and copies ran while one was open for 3% of the time, Pallas kernels for 29%

profile of v9, /device:TPU:6, one launch (start us, length us, event | category | flops | bytes accessed | tf_op | source)
XLA Modules:
  0.0 165.7 jit_solution(12082067795344910758)
XLA Ops:
  7.2 1.2 multiply_convert_fusion
  8.5 3.7 %collective-permute-start.3 = (bf16[128,1024]{1,0:T(8,128)(2,1)S(1)}, bf16[128,1024]{1,0:T(8,128)(2,1)S(1)}, u32[]{:S(2)}, u32[]{:S(2)}) collective-permute-start(bf16[128,1024]{1,0:T(8,128)(2,1)S(1)} %multiply_convert_fusion), channel_id=1, source_target_pairs={{0,8},{8,16},{16,24},{24,32},{32,40},{40,48},{48,56},{56,64},{64,7... | collective-permute-start | bytes 786440 | tf_op jit(solution)/shard_map/ppermute | solution.py:28
  12.3 1.9 %constant_dynamic-slice_fusion = (bf16[512,128]{1,0:T(8,128)(2,1)S(1)}, bf16[512,128]{1,0:T(8,128)(2,1)}, bf16[512,128]{1,0:T(8,128)(2,1)S(1)}, bf16[512,128]{1,0:T(8,128)(2,1)}) fusion(bf16[512,512]{1,0:T(8,128)(2,1)} %param.11, s32[]{:T(128)S(6)} %select_n.281, s32[]{:T(128)S(6)} %select_n.277, s32[]{:T(128)S(6)} %select_n.275, s32[]{:T(128)S(6)} %select_n.279), kind=kLoop, calls=%fused_computation.8 | loop fusion | bytes 1048592 | tf_op jit(solution)/shard_map/dynamic_slice | solution.py:361
  14.3 1.4 collective-permute-start.1
  15.8 2.1 %collective-permute-start.2 = (bf16[512,128]{1,0:T(8,128)(2,1)S(1)}, bf16[512,128]{1,0:T(8,128)(2,1)S(1)}, u32[]{:S(2)}, u32[]{:S(2)}) collective-permute-start(bf16[512,128]{1,0:T(8,128)(2,1)S(1)} %get-tuple-element.71), channel_id=1, source_target_pairs={{0,8},{8,16},{16,24},{24,0},{1,9},{9,17},{17,25},{25,1},{2,10},{10... | collective-permute-start | bytes 393224 | tf_op jit(solution)/shard_map/ppermute | solution.py:22
  18.5 1.2 copy-done.7
  19.7 3.4 %conv_forward.2 = (f32[512,1024]{1,0:T(8,128)S(1)}, bf16[512,1024]{1,0:T(8,128)(2,1)S(1)}, bf16[512,512]{1,0:T(8,128)(2,1)S(1)}) custom-call(f32[64,128]{1,0:T(8,128)S(1)} %convert_element_type.18.filters_ref, bf16[512,1024]{1,0:T(8,128)(2,1)S(1)} %copy-done.3, bf16[512,1024]{1,0:T(8,128)(2,1)S(1)} %copy-done.5, bf16[512,1024]{1,0:T(8,128)(2,1)S(1)} %copy-done.7, ...), custom_call_target="tpu_custom_call" | custom-call | flops 1048576 | bytes 262144 | tf_op jit(solution)/shard_map/conv_forward/pallas_call | solution.py:106
  23.2 3.5 %conv_forward.3 = (f32[512,1024]{1,0:T(8,128)S(1)}, bf16[512,1024]{1,0:T(8,128)(2,1)S(1)}, bf16[512,512]{1,0:T(8,128)(2,1)S(1)}) custom-call(f32[64,128]{1,0:T(8,128)S(1)} %convert_element_type.18.filters_ref, bf16[512,1024]{1,0:T(8,128)(2,1)S(1)} %copy-done.3, bf16[512,1024]{1,0:T(8,128)(2,1)S(1)} %copy-done.5, ...), custom_call_target="tpu_custom_call", output_to_operand_aliasing={{0}: (5, {}), {1}: (6, {})} | custom-call | flops 1048576 | bytes 262144 | tf_op jit(solution)/shard_map/conv_forward/pallas_call | solution.py:106
  26.8 1.7 collective-permute-start.5
  28.4 1.7 %collective-permute-start.4 = (bf16[2048,128]{1,0:T(8,128)(2,1)S(1)}, bf16[2048,128]{1,0:T(8,128)(2,1)S(1)}, u32[]{:S(2)}, u32[]{:S(2)}) collective-permute-start(bf16[2048,128]{1,0:T(8,128)(2,1)S(1)} %join.1), channel_id=1, source_target_pairs={{0,6},{2,0},{4,2},{6,4},{1,7},{3,1},{5,3},{7,5},{8,14},{10,8},{12,... | collective-permute-start | bytes 1572872 | tf_op jit(solution)/shard_map/ppermute | solution.py:22
  30.2 1.9 %collective-permute-start.8 = (bf16[512,512]{1,0:T(8,128)(2,1)S(1)}, bf16[512,512]{1,0:T(8,128)(2,1)}, u32[]{:S(2)}, u32[]{:S(2)}) collective-permute-start(bf16[512,512]{1,0:T(8,128)(2,1)S(1)} %get-tuple-element.44.refs_4_.refs_1_), channel_id=1, source_target_pairs={{0,24},{8,0},{16,8},{24,16},{1,25},{9,1},{17,9},{25,17},{2,26},{10... | collective-permute-start | bytes 1572872 | tf_op jit(solution)/shard_map/ppermute | solution.py:22
  32.1 8.7 %collective-permute-done.5 = bf16[2048,128]{1,0:T(8,128)(2,1)S(1)} collective-permute-done((bf16[2048,128]{1,0:T(8,128)(2,1)S(1)}, bf16[2048,128]{1,0:T(8,128)(2,1)S(1)}, u32[]{:S(2)}, u32[]{:S(2)}) %collective-permute-start.5) | collective-permute-done | bytes 524320 | tf_op jit(solution)/shard_map/ppermute | solution.py:22
  41.3 0.9 collective-permute-start.10
  42.2 3.0 %collective-permute-start.9 = (bf16[1024,128]{1,0:T(8,128)(2,1)S(1)}, bf16[1024,128]{1,0:T(8,128)(2,1)S(1)}, u32[]{:S(2)}, u32[]{:S(2)}) collective-permute-start(bf16[1024,128]{1,0:T(8,128)(2,1)S(1)} %slice.17), channel_id=1, source_target_pairs={{0,6},{2,0},{4,2},{6,4},{1,7},{3,1},{5,3},{7,5},{8,14},{10,8},{12,... | collective-permute-start | bytes 786440 | tf_op jit(solution)/shard_map/ppermute | solution.py:22
  45.3 2.4 %collective-permute-start.11 = (bf16[512,512]{1,0:T(8,128)(2,1)S(1)}, bf16[512,512]{1,0:T(8,128)(2,1)S(1)}, u32[]{:S(2)}, u32[]{:S(2)}) collective-permute-start(bf16[512,512]{1,0:T(8,128)(2,1)S(1)} %get-tuple-element.44.refs_4_.refs_1_), channel_id=1, source_target_pairs={{0,8},{8,16},{16,24},{24,0},{1,9},{9,17},{17,25},{25,1},{2,10},{10... | collective-permute-start | bytes 1572872 | tf_op jit(solution)/shard_map/ppermute | solution.py:22
  49.3 5.6 %collective-permute-done.10.refs_2_ = bf16[512,512]{1,0:T(8,128)(2,1)S(1)} collective-permute-done((bf16[512,512]{1,0:T(8,128)(2,1)S(1)}, bf16[512,512]{1,0:T(8,128)(2,1)S(1)}, u32[]{:S(2)}, u32[]{:S(2)}) %collective-permute-start.10) | collective-permute-done | bytes 524320 | tf_op jit(solution)/shard_map/ppermute | solution.py:22
  54.9 0.8 copy-done.19
  57.8 3.0 %collective-permute-start.13 = (bf16[512,512]{1,0:T(8,128)(2,1)}, bf16[512,512]{1,0:T(8,128)(2,1)}, u32[]{:S(2)}, u32[]{:S(2)}) collective-permute-start(bf16[512,512]{1,0:T(8,128)(2,1)} %collective-permute-done.7.refs_6_), channel_id=1, source_target_pairs={{0,8},{8,16},{16,24},{24,0},{1,9},{9,17},{17,25},{25,1},{2,10},{10... | collective-permute-start | bytes 1572872 | tf_op jit(solution)/shard_map/ppermute | solution.py:22
  62.0 1.6 copy-done
  63.6 3.7 %grad_gate_parts.4 = (bf16[512,512]{1,0:T(8,128)(2,1)}, bf16[512,512]{1,0:T(8,128)(2,1)}) custom-call(s32[8]{0:T(128)S(1)} %stack.35.place_ref, bf16[4,2048,128]{2,1,0:T(8,128)(2,1)S(1)} %bitcast.10, bf16[4,2048,128]{2,1,0:T(8,128)(2,1)} %collective-permute-done.12.sib_ref, bf16[1024,1024]{1,0:T(8,128)(2,1)S(1)} %copy-done), custom_call_target="tpu_custom_call" | custom-call | flops 1048576 | bytes 262144 | tf_op jit(solution)/shard_map/grad_gate_parts/pallas_call | solution.py:176
  67.3 3.1 %collective-permute-start.15 = (bf16[512,512]{1,0:T(8,128)(2,1)}, bf16[512,512]{1,0:T(8,128)(2,1)S(1)}, u32[]{:S(2)}, u32[]{:S(2)}) collective-permute-start(bf16[512,512]{1,0:T(8,128)(2,1)} %get-tuple-element.46), channel_id=1, source_target_pairs={{0,8},{8,16},{16,24},{24,0},{1,9},{9,17},{17,25},{25,1},{2,10},{10... | collective-permute-start | bytes 1572872 | tf_op jit(solution)/shard_map/ppermute | solution.py:22
  70.4 3.3 %collective-permute-done.14.refs_5_ = bf16[512,512]{1,0:T(8,128)(2,1)} collective-permute-done((bf16[512,512]{1,0:T(8,128)(2,1)}, bf16[512,512]{1,0:T(8,128)(2,1)}, u32[]{:S(2)}, u32[]{:S(2)}) %collective-permute-start.14) | collective-permute-done | bytes 524320 | tf_op jit(solution)/shard_map/ppermute | solution.py:22
  73.8 3.7 %grad_gate_parts.6 = (bf16[512,512]{1,0:T(8,128)(2,1)}, bf16[512,512]{1,0:T(8,128)(2,1)}) custom-call(s32[8]{0:T(128)S(1)} %stack.35.place_ref, bf16[4,2048,128]{2,1,0:T(8,128)(2,1)S(1)} %bitcast.11, bf16[4,2048,128]{2,1,0:T(8,128)(2,1)} %collective-permute-done.12.sib_ref, bf16[1024,1024]{1,0:T(8,128)(2,1)S(1)} %copy-done), custom_call_target="tpu_custom_call" | custom-call | flops 1048576 | bytes 262144 | tf_op jit(solution)/shard_map/grad_gate_parts/pallas_call | solution.py:176
  77.4 3.3 %collective-permute-start.18 = (bf16[512,512]{1,0:T(8,128)(2,1)}, bf16[512,512]{1,0:T(8,128)(2,1)}, u32[]{:S(2)}, u32[]{:S(2)}) collective-permute-start(bf16[512,512]{1,0:T(8,128)(2,1)} %get-tuple-element.51), channel_id=1, source_target_pairs={{0,8},{8,16},{16,24},{24,0},{1,9},{9,17},{17,25},{25,1},{2,10},{10... | collective-permute-start | bytes 1572872 | tf_op jit(solution)/shard_map/ppermute | solution.py:22
  80.8 6.7 %grad_proj_part.1 = bf16[1024,1024]{1,0:T(8,128)(2,1)S(1)} custom-call(s32[8]{0:T(128)S(1)} %stack.35.place_ref, bf16[4,2048,128]{2,1,0:T(8,128)(2,1)S(1)} %bitcast.12, bf16[4,2048,128]{2,1,0:T(8,128)(2,1)} %collective-permute-done.12.sib_ref, bf16[512,512]{1,0:T(8,128)(2,1)S(1)} %copy-done.18, bf16[512,512]{1,0:T(8,128)(2,1)S(1)} %get-tuple-element.44.refs_4_.refs_1_, ...), custom_call_target="tpu_custom_call" | custom-call | flops 1048576 | bytes 262144 | tf_op jit(solution)/shard_map/grad_proj_part/pallas_call | solution.py:215
  87.5 1.4 copy-done.9
  88.9 1.6 copy-done.1
  90.5 3.2 %grad_gate_parts.7 = (bf16[512,512]{1,0:T(8,128)(2,1)}, bf16[512,512]{1,0:T(8,128)(2,1)S(1)}) custom-call(s32[8]{0:T(128)S(1)} %stack.35.place_ref, bf16[4,2048,128]{2,1,0:T(8,128)(2,1)S(1)} %bitcast.13, bf16[4,2048,128]{2,1,0:T(8,128)(2,1)} %collective-permute-done.12.sib_ref, bf16[1024,1024]{1,0:T(8,128)(2,1)S(1)} %copy-done.1, ...), custom_call_target="tpu_custom_call" | custom-call | flops 1048576 | bytes 262144 | tf_op jit(solution)/shard_map/grad_gate_parts/pallas_call | solution.py:176
  93.7 3.2 %collective-permute-start.17 = (bf16[512,512]{1,0:T(8,128)(2,1)}, bf16[512,512]{1,0:T(8,128)(2,1)S(1)}, u32[]{:S(2)}, u32[]{:S(2)}) collective-permute-start(bf16[512,512]{1,0:T(8,128)(2,1)} %get-tuple-element.55), channel_id=1, source_target_pairs={{0,8},{8,16},{16,24},{24,0},{1,9},{9,17},{17,25},{25,1},{2,10},{10... | collective-permute-start | bytes 1572872 | tf_op jit(solution)/shard_map/ppermute | solution.py:22
  96.9 1.6 copy-done.2
  98.5 2.9 %grad_gate_parts.5 = (f32[512,512]{1,0:T(8,128)S(1)}, f32[512,512]{1,0:T(8,128)S(1)}) custom-call(s32[8]{0:T(128)S(1)} %stack.35.place_ref, bf16[4,2048,128]{2,1,0:T(8,128)(2,1)S(1)} %bitcast.14, bf16[4,2048,128]{2,1,0:T(8,128)(2,1)} %collective-permute-done.12.sib_ref, bf16[1024,1024]{1,0:T(8,128)(2,1)S(1)} %copy-done.2), custom_call_target="tpu_custom_call" | custom-call | flops 1048576 | bytes 262144 | tf_op jit(solution)/shard_map/grad_gate_parts/pallas_call | solution.py:176
  101.4 1.0 copy-done.11
  102.4 1.0 copy-done.12
  103.3 4.0 %collective-permute-done.17.refs_2_ = bf16[512,512]{1,0:T(8,128)(2,1)S(1)} collective-permute-done((bf16[512,512]{1,0:T(8,128)(2,1)}, bf16[512,512]{1,0:T(8,128)(2,1)S(1)}, u32[]{:S(2)}, u32[]{:S(2)}) %collective-permute-start.17) | collective-permute-done | bytes 524320 | tf_op jit(solution)/shard_map/ppermute | solution.py:22
  107.3 3.2 %collective-permute-done.20.refs_5_ = bf16[512,512]{1,0:T(8,128)(2,1)} collective-permute-done((bf16[512,512]{1,0:T(8,128)(2,1)S(1)}, bf16[512,512]{1,0:T(8,128)(2,1)}, u32[]{:S(2)}, u32[]{:S(2)}) %collective-permute-start.20) | collective-permute-done | bytes 524320 | tf_op jit(solution)/shard_map/ppermute | solution.py:22
  110.5 5.6 %gate_gradients.1 = (bf16[512,1024]{1,0:T(8,128)(2,1)}, bf16[512,1024]{1,0:T(8,128)(2,1)}, bf16[128,1024]{1,0:T(8,128)(2,1)}) custom-call(f32[512,512]{1,0:T(8,128)} %copy-done.11, f32[512,512]{1,0:T(8,128)} %copy-done.12, bf16[512,512]{1,0:T(8,128)(2,1)} %copy-done.23, bf16[512,512]{1,0:T(8,128)(2,1)} %collective-permute-done.18.refs_3_, ...), custom_call_target="tpu_custom_call" | custom-call | flops 1048576 | bytes 262144 | tf_op jit(solution)/shard_map/gate_gradients/pallas_call | solution.py:244
  116.1 1.9 %collective-permute-start.24 = (bf16[128,1024]{1,0:T(8,128)(2,1)}, bf16[128,1024]{1,0:T(8,128)(2,1)S(1)}, u32[]{:S(2)}, u32[]{:S(2)}) collective-permute-start(bf16[128,1024]{1,0:T(8,128)(2,1)} %get-tuple-element.62), channel_id=1, source_target_pairs={{8,0},{16,8},{24,16},{32,24},{40,32},{48,40},{56,48},{64,56},{72,6... | collective-permute-start | bytes 786440 | tf_op jit(solution)/shard_map/ppermute | solution.py:28
  118.1 7.9 %filter_part.1 = f32[64,128]{1,0:T(8,128)} custom-call(bf16[512,1024]{1,0:T(8,128)(2,1)} %get-tuple-element.66.inner_ref, bf16[512,1024]{1,0:T(8,128)(2,1)} %copy-done.13, bf16[128,1024]{1,0:T(8,128)(2,1)} %copy-done.14), custom_call_target="tpu_custom_call" | custom-call | flops 137438953472 | bytes 262144 | tf_op jit(solution)/shard_map/filter_part/pallas_call | solution.py:283
  126.5 2.4 %collective-permute-start.22 = (f32[64,128]{1,0:T(8,128)}, f32[64,128]{1,0:T(8,128)}, u32[]{:S(2)}, u32[]{:S(2)}) collective-permute-start(f32[64,128]{1,0:T(8,128)} %filter_part.1), channel_id=1, source_target_pairs={{0,16},{8,24},{16,0},{24,8},{1,17},{9,25},{17,1},{25,9},{2,18},{10... | collective-permute-start | bytes 98312 | tf_op jit(solution)/shard_map/ppermute | solution.py:22
  128.9 2.5 %collective-permute-start.23 = (f32[64,128]{1,0:T(8,128)}, f32[64,128]{1,0:T(8,128)}, u32[]{:S(2)}, u32[]{:S(2)}) collective-permute-start(f32[64,128]{1,0:T(8,128)} %filter_part.1), channel_id=1, source_target_pairs={{0,8},{8,16},{16,24},{24,0},{1,9},{9,17},{17,25},{25,1},{2,10},{10... | collective-permute-start | bytes 98312 | tf_op jit(solution)/shard_map/ppermute | solution.py:22
  131.4 1.9 %collective-permute-done.24.ahead_ref = bf16[128,1024]{1,0:T(8,128)(2,1)S(1)} collective-permute-done((bf16[128,1024]{1,0:T(8,128)(2,1)}, bf16[128,1024]{1,0:T(8,128)(2,1)S(1)}, u32[]{:S(2)}, u32[]{:S(2)}) %collective-permute-start.24) | collective-permute-done | bytes 262176 | tf_op jit(solution)/shard_map/ppermute | solution.py:28
  133.3 3.4 %conv_backward.2 = (bf16[512,1024]{1,0:T(8,128)(2,1)}, bf16[512,1024]{1,0:T(8,128)(2,1)}) custom-call(f32[64,128]{1,0:T(8,128)S(1)} %copy-done.16, bf16[512,1024]{1,0:T(8,128)(2,1)S(1)} %copy-done.10, bf16[128,1024]{1,0:T(8,128)(2,1)S(1)} %collective-permute-done.24.ahead_ref, bf16[512,1024]{1,0:T(8,128)(2,1)S(1)} %copy-done.4, bf16[512,1024]{1,0:T(8,128)(2,1)S(1)} %copy-done.6), custom_call_target="tpu_custom_call" | custom-call | flops 1048576 | bytes 262144 | tf_op jit(solution)/shard_map/conv_backward/pallas_call | solution.py:323
  137.5 7.6 %collective-permute-start.25 = (f32[64,128]{1,0:T(8,128)S(1)}, f32[64,128]{1,0:T(8,128)S(1)}, u32[]{:S(2)}, u32[]{:S(2)}) collective-permute-start(f32[64,128]{1,0:T(8,128)S(1)} %select_add_fusion.1), channel_id=1, source_target_pairs={{0,192},{32,224},{64,0},{96,32},{128,64},{160,96},{192,128},{224,1... | collective-permute-start | bytes 98312 | tf_op jit(solution)/shard_map/ppermute | solution.py:22
  145.1 2.1 %collective-permute-start.26 = (f32[64,128]{1,0:T(8,128)S(1)}, f32[64,128]{1,0:T(8,128)S(1)}, u32[]{:S(2)}, u32[]{:S(2)}) collective-permute-start(f32[64,128]{1,0:T(8,128)S(1)} %select_add_fusion.1), channel_id=1, source_target_pairs={{0,128},{32,160},{64,192},{96,224},{128,0},{160,32},{192,64},{224,... | collective-permute-start | bytes 98312 | tf_op jit(solution)/shard_map/ppermute | solution.py:22
  147.2 2.8 %collective-permute-start.27 = (f32[64,128]{1,0:T(8,128)S(1)}, f32[64,128]{1,0:T(8,128)}, u32[]{:S(2)}, u32[]{:S(2)}) collective-permute-start(f32[64,128]{1,0:T(8,128)S(1)} %select_add_fusion.1), channel_id=1, source_target_pairs={{0,64},{32,96},{64,128},{96,160},{128,192},{160,224},{192,0},{224,... | collective-permute-start | bytes 98312 | tf_op jit(solution)/shard_map/ppermute | solution.py:22
  150.0 3.4 %conv_backward.3 = (bf16[512,1024]{1,0:T(8,128)(2,1)}, bf16[512,1024]{1,0:T(8,128)(2,1)}) custom-call(f32[64,128]{1,0:T(8,128)S(1)} %copy-done.16, bf16[512,1024]{1,0:T(8,128)(2,1)S(1)} %copy-done.10, bf16[128,1024]{1,0:T(8,128)(2,1)S(1)} %collective-permute-done.24.ahead_ref, ...), custom_call_target="tpu_custom_call", output_to_operand_aliasing={{0}: (5, {}), {1}: (6, {})} | custom-call | flops 1048576 | bytes 262144 | tf_op jit(solution)/shard_map/conv_backward/pallas_call | solution.py:323
  154.2 1.9 %collective-permute-start.28 = (f32[64,128]{1,0:T(8,128)S(1)}, f32[64,128]{1,0:T(8,128)S(1)}, u32[]{:S(2)}, u32[]{:S(2)}) collective-permute-start(f32[64,128]{1,0:T(8,128)S(1)} %select_add_fusion), channel_id=1, source_target_pairs={{0,32},{32,0},{64,96},{96,64},{128,160},{160,128},{192,224},{224,1... | collective-permute-start | bytes 98312 | tf_op jit(solution)/shard_map/ppermute | solution.py:403
  156.1 1.8 %convert_element_type.19 = f32[128,1024]{1,0:T(8,128)} convert(bf16[128,1024]{1,0:T(8,128)(2,1)} %reduce-scatter.2.cloned.1.call-done) | non-fusion elementwise | flops 131072 | bytes 786432 | tf_op jit(solution)/shard_map/convert_element_type | solution.py:392
  (96 shorter events, 9.5 us)
Async XLA Ops:
  7.2 11.3 %copy-start.3 = (bf16[512,1024]{1,0:T(8,128)(2,1)S(1)}, bf16[512,1024]{1,0:T(8,128)(2,1)}, u32[]{:S(2)}) copy-start(bf16[512,1024]{1,0:T(8,128)(2,1)} %k_ref.7) | copy-start | bytes 3145732
  7.2 11.3 %copy-start.5 = (bf16[512,1024]{1,0:T(8,128)(2,1)S(1)}, bf16[512,1024]{1,0:T(8,128)(2,1)}, u32[]{:S(2)}) copy-start(bf16[512,1024]{1,0:T(8,128)(2,1)} %v_ref.7) | copy-start | bytes 3145732
  7.2 10.7 %copy-start.25 = (bf16[64,128]{1,0:T(8,128)(2,1)S(1)}, bf16[64,128]{1,0:T(8,128)(2,1)}, u32[]{:S(2)}) copy-start(bf16[64,128]{1,0:T(8,128)(2,1)} %param.9) | copy-start | bytes 49156
  7.2 54.8 %all-gather.2.cloned.1.call-start = ((), (), s32[]{:S(2)}) async-start(), calls=%async_computation.1 | async-start | bytes 2359296 | tf_op jit(solution)/shard_map/all_gather | solution.py:356
  8.5 10.0 %collective-permute-start.3 = (bf16[128,1024]{1,0:T(8,128)(2,1)S(1)}, bf16[128,1024]{1,0:T(8,128)(2,1)S(1)}, u32[]{:S(2)}, u32[]{:S(2)}) collective-permute-start(bf16[128,1024]{1,0:T(8,128)(2,1)S(1)} %multiply_convert_fusion), channel_id=1, source_target_pairs={{0,8},{8,16},{16,24},{24,32},{32,40},{40,48},{48,56},{56,64},{64,7... | collective-permute-start | bytes 786440 | tf_op jit(solution)/shard_map/ppermute | solution.py:28
  14.1 12.6 %collective-permute-start = (bf16[512,128]{1,0:T(8,128)(2,1)}, bf16[512,128]{1,0:T(8,128)(2,1)S(1)}, u32[]{:S(2)}, u32[]{:S(2)}) collective-permute-start(bf16[512,128]{1,0:T(8,128)(2,1)} %get-tuple-element.72), channel_id=1, source_target_pairs={{0,24},{8,0},{16,8},{24,16},{1,25},{9,1},{17,9},{25,17},{2,26},{10... | collective-permute-start | bytes 393224 | tf_op jit(solution)/shard_map/ppermute | solution.py:22
  14.3 12.4 %collective-permute-start.1 = (bf16[512,128]{1,0:T(8,128)(2,1)}, bf16[512,128]{1,0:T(8,128)(2,1)S(1)}, u32[]{:S(2)}, u32[]{:S(2)}) collective-permute-start(bf16[512,128]{1,0:T(8,128)(2,1)} %get-tuple-element.74), channel_id=1, source_target_pairs={{0,16},{8,24},{16,0},{24,8},{1,17},{9,25},{17,1},{25,9},{2,18},{10... | collective-permute-start | bytes 393224 | tf_op jit(solution)/shard_map/ppermute | solution.py:22
  15.8 11.0 %collective-permute-start.2 = (bf16[512,128]{1,0:T(8,128)(2,1)S(1)}, bf16[512,128]{1,0:T(8,128)(2,1)S(1)}, u32[]{:S(2)}, u32[]{:S(2)}) collective-permute-start(bf16[512,128]{1,0:T(8,128)(2,1)S(1)} %get-tuple-element.71), channel_id=1, source_target_pairs={{0,8},{8,16},{16,24},{24,0},{1,9},{9,17},{17,25},{25,1},{2,10},{10... | collective-permute-start | bytes 393224 | tf_op jit(solution)/shard_map/ppermute | solution.py:22
  17.9 138.2 %reduce-scatter.2.cloned.1.call-start = ((), (), s32[]{:S(2)}) async-start(), calls=%async_computation.2 | async-start | bytes 2359296 | tf_op jit(solution)/shard_map/reduce_scatter | solution.py:392
  17.9 8.7 %copy-start.15 = (f32[64,128]{1,0:T(8,128)}, f32[64,128]{1,0:T(8,128)S(1)}, u32[]{:S(2)}) copy-start(f32[64,128]{1,0:T(8,128)S(1)} %convert_element_type.18.filters_ref) | copy-start | bytes 98308
  19.7 7.0 %copy-start.14 = (bf16[128,1024]{1,0:T(8,128)(2,1)}, bf16[128,1024]{1,0:T(8,128)(2,1)S(1)}, u32[]{:S(2)}) copy-start(bf16[128,1024]{1,0:T(8,128)(2,1)S(1)} %collective-permute-done.3.rim_ref) | copy-start | bytes 786436
  23.1 18.2 %copy-start.17 = (bf16[512,512]{1,0:T(8,128)(2,1)}, bf16[512,512]{1,0:T(8,128)(2,1)S(1)}, u32[]{:S(2)}) copy-start(bf16[512,512]{1,0:T(8,128)(2,1)S(1)} %get-tuple-element.53.refs_0_) | copy-start | bytes 1572868
  26.7 21.1 %copy-start.8 = (f32[512,1024]{1,0:T(8,128)}, f32[512,1024]{1,0:T(8,128)S(1)}, u32[]{:S(2)}) copy-start(f32[512,1024]{1,0:T(8,128)S(1)} %get-tuple-element.57.refs_7_) | copy-start | bytes 6291460
  26.7 21.1 %copy-start.13 = (bf16[512,1024]{1,0:T(8,128)(2,1)}, bf16[512,1024]{1,0:T(8,128)(2,1)S(1)}, u32[]{:S(2)}) copy-start(bf16[512,1024]{1,0:T(8,128)(2,1)S(1)} %get-tuple-element.60.mixed_ref) | copy-start | bytes 3145732
  26.8 14.1 %collective-permute-start.5 = (bf16[2048,128]{1,0:T(8,128)(2,1)S(1)}, bf16[2048,128]{1,0:T(8,128)(2,1)S(1)}, u32[]{:S(2)}, u32[]{:S(2)}) collective-permute-start(bf16[2048,128]{1,0:T(8,128)(2,1)S(1)} %join.1), channel_id=1, source_target_pairs={{0,2},{2,4},{4,6},{6,0},{1,3},{3,5},{5,7},{7,1},{8,10},{10,12},{12... | collective-permute-start | bytes 1572872 | tf_op jit(solution)/shard_map/ppermute | solution.py:22
  28.4 13.8 %collective-permute-start.4 = (bf16[2048,128]{1,0:T(8,128)(2,1)S(1)}, bf16[2048,128]{1,0:T(8,128)(2,1)S(1)}, u32[]{:S(2)}, u32[]{:S(2)}) collective-permute-start(bf16[2048,128]{1,0:T(8,128)(2,1)S(1)} %join.1), channel_id=1, source_target_pairs={{0,6},{2,0},{4,2},{6,4},{1,7},{3,1},{5,3},{7,5},{8,14},{10,8},{12,... | collective-permute-start | bytes 1572872 | tf_op jit(solution)/shard_map/ppermute | solution.py:22
  30.1 15.2 %collective-permute-start.7 = (bf16[512,512]{1,0:T(8,128)(2,1)S(1)}, bf16[512,512]{1,0:T(8,128)(2,1)}, u32[]{:S(2)}, u32[]{:S(2)}) collective-permute-start(bf16[512,512]{1,0:T(8,128)(2,1)S(1)} %get-tuple-element.53.refs_0_), channel_id=1, source_target_pairs={{0,8},{8,16},{16,24},{24,0},{1,9},{9,17},{17,25},{25,1},{2,10},{10... | collective-permute-start | bytes 1572872 | tf_op jit(solution)/shard_map/ppermute | solution.py:22
  30.2 17.6 %collective-permute-start.8 = (bf16[512,512]{1,0:T(8,128)(2,1)S(1)}, bf16[512,512]{1,0:T(8,128)(2,1)}, u32[]{:S(2)}, u32[]{:S(2)}) collective-permute-start(bf16[512,512]{1,0:T(8,128)(2,1)S(1)} %get-tuple-element.44.refs_4_.refs_1_), channel_id=1, source_target_pairs={{0,24},{8,0},{16,8},{24,16},{1,25},{9,1},{17,9},{25,17},{2,26},{10... | collective-permute-start | bytes 1572872 | tf_op jit(solution)/shard_map/ppermute | solution.py:22
  40.9 7.7 %collective-permute-start.6 = (bf16[1024,128]{1,0:T(8,128)(2,1)S(1)}, bf16[1024,128]{1,0:T(8,128)(2,1)S(1)}, u32[]{:S(2)}, u32[]{:S(2)}) collective-permute-start(bf16[1024,128]{1,0:T(8,128)(2,1)S(1)} %slice.16), channel_id=1, source_target_pairs={{0,2},{2,4},{4,6},{6,0},{1,3},{3,5},{5,7},{7,1},{8,10},{10,12},{12... | collective-permute-start | bytes 786440 | tf_op jit(solution)/shard_map/ppermute | solution.py:22
  41.3 13.6 %collective-permute-start.10 = (bf16[512,512]{1,0:T(8,128)(2,1)S(1)}, bf16[512,512]{1,0:T(8,128)(2,1)S(1)}, u32[]{:S(2)}, u32[]{:S(2)}) collective-permute-start(bf16[512,512]{1,0:T(8,128)(2,1)S(1)} %get-tuple-element.53.refs_0_), channel_id=1, source_target_pairs={{0,24},{8,0},{16,8},{24,16},{1,25},{9,1},{17,9},{25,17},{2,26},{10... | collective-permute-start | bytes 1572872 | tf_op jit(solution)/shard_map/ppermute | solution.py:22
  42.2 6.9 %collective-permute-start.9 = (bf16[1024,128]{1,0:T(8,128)(2,1)S(1)}, bf16[1024,128]{1,0:T(8,128)(2,1)S(1)}, u32[]{:S(2)}, u32[]{:S(2)}) collective-permute-start(bf16[1024,128]{1,0:T(8,128)(2,1)S(1)} %slice.17), channel_id=1, source_target_pairs={{0,6},{2,0},{4,2},{6,4},{1,7},{3,1},{5,3},{7,5},{8,14},{10,8},{12,... | collective-permute-start | bytes 786440 | tf_op jit(solution)/shard_map/ppermute | solution.py:22
  45.3 11.1 %collective-permute-start.11 = (bf16[512,512]{1,0:T(8,128)(2,1)S(1)}, bf16[512,512]{1,0:T(8,128)(2,1)S(1)}, u32[]{:S(2)}, u32[]{:S(2)}) collective-permute-start(bf16[512,512]{1,0:T(8,128)(2,1)S(1)} %get-tuple-element.44.refs_4_.refs_1_), channel_id=1, source_target_pairs={{0,8},{8,16},{16,24},{24,0},{1,9},{9,17},{17,25},{25,1},{2,10},{10... | collective-permute-start | bytes 1572872 | tf_op jit(solution)/shard_map/ppermute | solution.py:22
  57.2 4.3 %collective-permute-start.12 = (bf16[4,2048,128]{2,1,0:T(8,128)(2,1)S(1)}, bf16[4,2048,128]{2,1,0:T(8,128)(2,1)}, u32[]{:S(2)}, u32[]{:S(2)}) collective-permute-start(bf16[4,2048,128]{2,1,0:T(8,128)(2,1)S(1)} %bitcast.9), channel_id=1, source_target_pairs={{0,1},{1,0},{2,3},{3,2},{4,5},{5,4},{6,7},{7,6},{8,9},{9,8},{10,11... | collective-permute-start | bytes 6291464 | tf_op jit(solution)/shard_map/ppermute | solution.py:22
  57.2 16.6 %collective-permute-start.14 = (bf16[512,512]{1,0:T(8,128)(2,1)}, bf16[512,512]{1,0:T(8,128)(2,1)}, u32[]{:S(2)}, u32[]{:S(2)}) collective-permute-start(bf16[512,512]{1,0:T(8,128)(2,1)} %collective-permute-done.8.refs_3_), channel_id=1, source_target_pairs={{0,24},{8,0},{16,8},{24,16},{1,25},{9,1},{17,9},{25,17},{2,26},{10... | collective-permute-start | bytes 1572872 | tf_op jit(solution)/shard_map/ppermute | solution.py:22
  57.8 15.9 %collective-permute-start.13 = (bf16[512,512]{1,0:T(8,128)(2,1)}, bf16[512,512]{1,0:T(8,128)(2,1)}, u32[]{:S(2)}, u32[]{:S(2)}) collective-permute-start(bf16[512,512]{1,0:T(8,128)(2,1)} %collective-permute-done.7.refs_6_), channel_id=1, source_target_pairs={{0,8},{8,16},{16,24},{24,0},{1,9},{9,17},{17,25},{25,1},{2,10},{10... | collective-permute-start | bytes 1572872 | tf_op jit(solution)/shard_map/ppermute | solution.py:22
  67.3 21.6 %collective-permute-start.15 = (bf16[512,512]{1,0:T(8,128)(2,1)}, bf16[512,512]{1,0:T(8,128)(2,1)S(1)}, u32[]{:S(2)}, u32[]{:S(2)}) collective-permute-start(bf16[512,512]{1,0:T(8,128)(2,1)} %get-tuple-element.46), channel_id=1, source_target_pairs={{0,8},{8,16},{16,24},{24,0},{1,9},{9,17},{17,25},{25,1},{2,10},{10... | collective-permute-start | bytes 1572872 | tf_op jit(solution)/shard_map/ppermute | solution.py:22
  70.4 10.4 %copy-start.18 = (bf16[512,512]{1,0:T(8,128)(2,1)S(1)}, bf16[512,512]{1,0:T(8,128)(2,1)}, u32[]{:S(2)}) copy-start(bf16[512,512]{1,0:T(8,128)(2,1)} %copy-done.17) | copy-start | bytes 1572868
  70.4 10.4 %copy-start.20 = (bf16[512,512]{1,0:T(8,128)(2,1)S(1)}, bf16[512,512]{1,0:T(8,128)(2,1)}, u32[]{:S(2)}) copy-start(bf16[512,512]{1,0:T(8,128)(2,1)} %copy-done.19) | copy-start | bytes 1572868
  70.4 10.4 %copy-start.22 = (bf16[512,512]{1,0:T(8,128)(2,1)S(1)}, bf16[512,512]{1,0:T(8,128)(2,1)}, u32[]{:S(2)}) copy-start(bf16[512,512]{1,0:T(8,128)(2,1)} %copy-done.21) | copy-start | bytes 1572868
  70.4 18.5 %collective-permute-start.16 = (bf16[512,512]{1,0:T(8,128)(2,1)}, bf16[512,512]{1,0:T(8,128)(2,1)}, u32[]{:S(2)}, u32[]{:S(2)}) collective-permute-start(bf16[512,512]{1,0:T(8,128)(2,1)} %get-tuple-element.47), channel_id=1, source_target_pairs={{0,24},{8,0},{16,8},{24,16},{1,25},{9,1},{17,9},{25,17},{2,26},{10... | collective-permute-start | bytes 1572872 | tf_op jit(solution)/shard_map/ppermute | solution.py:22
  77.4 25.9 %collective-permute-start.18 = (bf16[512,512]{1,0:T(8,128)(2,1)}, bf16[512,512]{1,0:T(8,128)(2,1)}, u32[]{:S(2)}, u32[]{:S(2)}) collective-permute-start(bf16[512,512]{1,0:T(8,128)(2,1)} %get-tuple-element.51), channel_id=1, source_target_pairs={{0,8},{8,16},{16,24},{24,0},{1,9},{9,17},{17,25},{25,1},{2,10},{10... | collective-permute-start | bytes 1572872 | tf_op jit(solution)/shard_map/ppermute | solution.py:22
  80.8 22.6 %collective-permute-start.19 = (bf16[512,512]{1,0:T(8,128)(2,1)}, bf16[512,512]{1,0:T(8,128)(2,1)}, u32[]{:S(2)}, u32[]{:S(2)}) collective-permute-start(bf16[512,512]{1,0:T(8,128)(2,1)} %get-tuple-element.52), channel_id=1, source_target_pairs={{0,24},{8,0},{16,8},{24,16},{1,25},{9,1},{17,9},{25,17},{2,26},{10... | collective-permute-start | bytes 1572872 | tf_op jit(solution)/shard_map/ppermute | solution.py:22
  93.7 13.7 %collective-permute-start.17 = (bf16[512,512]{1,0:T(8,128)(2,1)}, bf16[512,512]{1,0:T(8,128)(2,1)S(1)}, u32[]{:S(2)}, u32[]{:S(2)}) collective-permute-start(bf16[512,512]{1,0:T(8,128)(2,1)} %get-tuple-element.55), channel_id=1, source_target_pairs={{0,8},{8,16},{16,24},{24,0},{1,9},{9,17},{17,25},{25,1},{2,10},{10... | collective-permute-start | bytes 1572872 | tf_op jit(solution)/shard_map/ppermute | solution.py:22
  96.9 13.6 %collective-permute-start.20 = (bf16[512,512]{1,0:T(8,128)(2,1)S(1)}, bf16[512,512]{1,0:T(8,128)(2,1)}, u32[]{:S(2)}, u32[]{:S(2)}) collective-permute-start(bf16[512,512]{1,0:T(8,128)(2,1)S(1)} %get-tuple-element.56), channel_id=1, source_target_pairs={{0,24},{8,0},{16,8},{24,16},{1,25},{9,1},{17,9},{25,17},{2,26},{10... | collective-permute-start | bytes 1572872 | tf_op jit(solution)/shard_map/ppermute | solution.py:22
  107.3 3.2 %copy-start.23 = (bf16[512,512]{1,0:T(8,128)(2,1)}, bf16[512,512]{1,0:T(8,128)(2,1)S(1)}, u32[]{:S(2)}) copy-start(bf16[512,512]{1,0:T(8,128)(2,1)S(1)} %collective-permute-done.17.refs_2_) | copy-start | bytes 1572868
  116.1 17.2 %collective-permute-start.24 = (bf16[128,1024]{1,0:T(8,128)(2,1)}, bf16[128,1024]{1,0:T(8,128)(2,1)S(1)}, u32[]{:S(2)}, u32[]{:S(2)}) collective-permute-start(bf16[128,1024]{1,0:T(8,128)(2,1)} %get-tuple-element.62), channel_id=1, source_target_pairs={{8,0},{16,8},{24,16},{32,24},{40,32},{48,40},{56,48},{64,56},{72,6... | collective-permute-start | bytes 786440 | tf_op jit(solution)/shard_map/ppermute | solution.py:28
  118.1 15.3 %copy-start.4 = (bf16[512,1024]{1,0:T(8,128)(2,1)S(1)}, bf16[512,1024]{1,0:T(8,128)(2,1)}, u32[]{:S(2)}) copy-start(bf16[512,1024]{1,0:T(8,128)(2,1)} %k_ref.7) | copy-start | bytes 3145732
  118.1 15.3 %copy-start.6 = (bf16[512,1024]{1,0:T(8,128)(2,1)S(1)}, bf16[512,1024]{1,0:T(8,128)(2,1)}, u32[]{:S(2)}) copy-start(bf16[512,1024]{1,0:T(8,128)(2,1)} %v_ref.7) | copy-start | bytes 3145732
  118.1 15.2 %copy-start.10 = (bf16[512,1024]{1,0:T(8,128)(2,1)S(1)}, bf16[512,1024]{1,0:T(8,128)(2,1)}, u32[]{:S(2)}) copy-start(bf16[512,1024]{1,0:T(8,128)(2,1)} %get-tuple-element.66.inner_ref) | copy-start | bytes 3145732
  118.1 15.2 %copy-start.16 = (f32[64,128]{1,0:T(8,128)S(1)}, f32[64,128]{1,0:T(8,128)}, u32[]{:S(2)}) copy-start(f32[64,128]{1,0:T(8,128)} %copy-done.15) | copy-start | bytes 98308
  126.0 10.7 %copy-start.24 = (f32[64,128]{1,0:T(8,128)S(1)}, f32[64,128]{1,0:T(8,128)}, u32[]{:S(2)}) copy-start(f32[64,128]{1,0:T(8,128)} %filter_part.1) | copy-start | bytes 98308
  126.0 10.7 %collective-permute-start.21 = (f32[64,128]{1,0:T(8,128)}, f32[64,128]{1,0:T(8,128)S(1)}, u32[]{:S(2)}, u32[]{:S(2)}) collective-permute-start(f32[64,128]{1,0:T(8,128)} %filter_part.1), channel_id=1, source_target_pairs={{0,24},{8,0},{16,8},{24,16},{1,25},{9,1},{17,9},{25,17},{2,26},{10... | collective-permute-start | bytes 98312 | tf_op jit(solution)/shard_map/ppermute | solution.py:22
  126.5 10.2 %collective-permute-start.22 = (f32[64,128]{1,0:T(8,128)}, f32[64,128]{1,0:T(8,128)}, u32[]{:S(2)}, u32[]{:S(2)}) collective-permute-start(f32[64,128]{1,0:T(8,128)} %filter_part.1), channel_id=1, source_target_pairs={{0,16},{8,24},{16,0},{24,8},{1,17},{9,25},{17,1},{25,9},{2,18},{10... | collective-permute-start | bytes 98312 | tf_op jit(solution)/shard_map/ppermute | solution.py:22
  128.9 7.9 %collective-permute-start.23 = (f32[64,128]{1,0:T(8,128)}, f32[64,128]{1,0:T(8,128)}, u32[]{:S(2)}, u32[]{:S(2)}) collective-permute-start(f32[64,128]{1,0:T(8,128)} %filter_part.1), channel_id=1, source_target_pairs={{0,8},{8,16},{16,24},{24,0},{1,9},{9,17},{17,25},{25,1},{2,10},{10... | collective-permute-start | bytes 98312 | tf_op jit(solution)/shard_map/ppermute | solution.py:22
  137.5 15.8 %collective-permute-start.25 = (f32[64,128]{1,0:T(8,128)S(1)}, f32[64,128]{1,0:T(8,128)S(1)}, u32[]{:S(2)}, u32[]{:S(2)}) collective-permute-start(f32[64,128]{1,0:T(8,128)S(1)} %select_add_fusion.1), channel_id=1, source_target_pairs={{0,192},{32,224},{64,0},{96,32},{128,64},{160,96},{192,128},{224,1... | collective-permute-start | bytes 98312 | tf_op jit(solution)/shard_map/ppermute | solution.py:22
  145.1 8.3 %collective-permute-start.26 = (f32[64,128]{1,0:T(8,128)S(1)}, f32[64,128]{1,0:T(8,128)S(1)}, u32[]{:S(2)}, u32[]{:S(2)}) collective-permute-start(f32[64,128]{1,0:T(8,128)S(1)} %select_add_fusion.1), channel_id=1, source_target_pairs={{0,128},{32,160},{64,192},{96,224},{128,0},{160,32},{192,64},{224,... | collective-permute-start | bytes 98312 | tf_op jit(solution)/shard_map/ppermute | solution.py:22
  147.2 6.2 %collective-permute-start.27 = (f32[64,128]{1,0:T(8,128)S(1)}, f32[64,128]{1,0:T(8,128)}, u32[]{:S(2)}, u32[]{:S(2)}) collective-permute-start(f32[64,128]{1,0:T(8,128)S(1)} %select_add_fusion.1), channel_id=1, source_target_pairs={{0,64},{32,96},{64,128},{96,160},{128,192},{160,224},{192,0},{224,... | collective-permute-start | bytes 98312 | tf_op jit(solution)/shard_map/ppermute | solution.py:22
  154.2 4.0 %collective-permute-start.28 = (f32[64,128]{1,0:T(8,128)S(1)}, f32[64,128]{1,0:T(8,128)S(1)}, u32[]{:S(2)}, u32[]{:S(2)}) collective-permute-start(f32[64,128]{1,0:T(8,128)S(1)} %select_add_fusion), channel_id=1, source_target_pairs={{0,32},{32,0},{64,96},{96,64},{128,160},{160,128},{192,224},{224,1... | collective-permute-start | bytes 98312 | tf_op jit(solution)/shard_map/ppermute | solution.py:403
  (9 other events, 11.0 us)
Sparse Core Ops, SparseCore 0:
  18.0 43.9 all-gather.1
  97.1 46.5 reduce-scatter.1
